TPU v7x, 512 devices: a whole 4x8x8 slice. The times are simulated.
512 devices in a mesh: row: 32 (over y, x), col: 16 (over z, core).
Axes of the slice: x: 4, y: 8, z: 8, core: 2. Of those that a mesh axis runs over, the one named last changes fastest.
Arguments:
- features: bfloat16 [65536, 512], P(('col', 'row')), may hold values from -6 to 6
- weight: bfloat16 [512, 512], replicated, may hold values from -0.25 to 0.25
- cotangent: bfloat16 [65536, 512], P(('row', 'col')), may hold values from -6 to 6
- tile_values: bfloat16 [32, 16, 8, 128, 128], P('row', 'col'), may hold values from -0.1875 to 0.1875
- tile_rows: int32 [32, 16, 8], P('row', 'col'), may hold values from 0 to 15
- tile_cols: int32 [32, 16, 8], P('row', 'col'), may hold values from 0 to 31
- tile_valid: int32 [32, 16, 8], P('row', 'col'), may hold values from 0 to 1, as said below
Outputs:
- activations: bfloat16 [65536, 512], P(('row', 'col'))
- input_grad: bfloat16 [65536, 512], P(('col', 'row'))
- weight_grad: float32 [512, 512], replicated
Inputs may be any that keep to these rules, and one draw needn't show every extreme that they name: `tile_valid`: in each grid block the valid slots come first; every block has at least one, and some block has all 8.
All inputs are finite; a program needn't handle non-finite values.
Results may differ from a plain program's by a relative error of at most 0.02.
Values may be sent and summed in bfloat16 or wider, within the bound.
No kernel may reach another device: no remote copies, remote signals or barrier semaphores. Data moves between devices by JAX's collectives and lax.ppermute only.
A program may use at most 64 MiB of HBM per device.

v0:
```python
import math

import jax
import jax.numpy as jnp
from jax import lax
from jax.sharding import PartitionSpec as P


def tile_block(values, out_index, in_index, valid_flags, panel, out_count, transposed):
    tile_size = values.shape[-1]
    width = panel.shape[-1]
    slots = values.shape[0]
    group = math.gcd(slots, 8)
    turns = slots // group
    blocks = panel.reshape(-1, tile_size, width)
    form = "sji,sjf->sif" if transposed else "sij,sjf->sif"

    def add_group(total, slot_group):
        group_values, group_out, group_in, group_valid = slot_group
        products = jnp.einsum(
            form, group_values, blocks[group_in], preferred_element_type=jnp.float32
        )
        products = jnp.where(group_valid[:, None, None] > 0, products, 0.0)
        return (total.at[group_out].add(products), None)

    inputs = (
        values.reshape(turns, group, tile_size, tile_size),
        out_index.reshape(turns, group),
        in_index.reshape(turns, group),
        valid_flags.reshape(turns, group),
    )
    total, unused = lax.scan(
        add_group, jnp.zeros((out_count, tile_size, width), jnp.float32), inputs
    )
    return total.reshape(out_count * tile_size, width)


def body(features, weight, cotangent, tile_values, tile_rows, tile_cols, tile_valid):
    node_local = features.shape[0]
    tile_size = tile_values.shape[-1]
    row_count = lax.axis_size("row")
    col_count = lax.axis_size("col")
    values = tile_values.reshape(-1, tile_size, tile_size)
    rows_local = tile_rows.reshape(-1)
    cols_local = tile_cols.reshape(-1)
    valid_local = tile_valid.reshape(-1)
    row_tiles = node_local * col_count // tile_size
    col_tiles = node_local * row_count // tile_size
    projected = jnp.dot(features, weight, preferred_element_type=jnp.float32).astype(jnp.bfloat16)
    panel = lax.all_gather(projected, "row", axis=0, tiled=True)
    forward_term = tile_block(values, rows_local, cols_local, valid_local, panel, row_tiles, False)
    aggregated = lax.psum_scatter(
        forward_term.astype(jnp.bfloat16), "col", scatter_dimension=0, tiled=True
    ).astype(jnp.float32)
    activations = jax.nn.silu(aggregated).astype(jnp.bfloat16)
    sig = jax.nn.sigmoid(aggregated)
    grad_pre = (cotangent.astype(jnp.float32) * sig * (1.0 + aggregated * (1.0 - sig))).astype(
        jnp.bfloat16
    )
    grad_panel = lax.all_gather(grad_pre, "col", axis=0, tiled=True)
    backward_term = tile_block(
        values, cols_local, rows_local, valid_local, grad_panel, col_tiles, True
    )
    grad_projected = lax.psum_scatter(
        backward_term.astype(jnp.bfloat16), "row", scatter_dimension=0, tiled=True
    )
    input_grad = lax.dot_general(
        grad_projected, weight, (((1,), (1,)), ((), ())), preferred_element_type=jnp.float32
    ).astype(jnp.bfloat16)
    weight_part = lax.dot_general(
        features, grad_projected, (((0,), (0,)), ((), ())), preferred_element_type=jnp.float32
    )
    node_total = node_local * row_count * col_count
    weight_total = lax.psum(weight_part, ("row", "col"))
    weight_grad = weight_total * (1.0 / math.sqrt(node_total))
    return (activations, input_grad, weight_grad)


def solution(mesh):
    placed = (
        P(("col", "row"), None),
        P(),
        P(("row", "col"), None),
        P("row", "col", None, None, None),
        P("row", "col", None),
        P("row", "col", None),
        P("row", "col", None),
    )
    return jax.shard_map(
        body,
        mesh=mesh,
        in_specs=placed,
        out_specs=(P(("row", "col"), None), P(("col", "row"), None), P()),
        check_vma=False,
    )
```

profile of v0, /device:TPU:1, one launch (start us, length us, event | category | flops | bytes accessed | tf_op | source)
XLA Modules:
  0.0 757.6 jit_solution(9567418407756087645)
XLA Ops:
  7.2 0.0 copy-start
  7.2 0.0 copy-start.1
  7.2 0.0 all-gather.3.cloned.1.call-start
  7.2 1.0 copy-done
  8.2 1.8 convolution_convert_fusion.1
  10.0 0.0 all-gather.3.cloned.1.call-update
  10.0 0.0 reduce-scatter.3.cloned.1.call-start
  10.1 0.7 fusion.10
  10.8 0.7 fusion.9
  11.4 0.7 compare_bitcast_fusion
  12.1 89.7 %all-gather.3.cloned.1.call-done = bf16[4096,512]{1,0:T(8,128)(2,1)} async-done(((bf16[128,512]{1,0:T(8,128)(2,1)}), bf16[4096,512]{1,0:T(8,128)(2,1)}) %all-gather.3.cloned.1.call-update) | async-done | bytes 4194320 | tf_op jit(solution)/shard_map/all_gather | solution.py:50
  101.7 2.8 gather_fusion
  104.5 0.0 copy-done.1
  104.5 1.9 select_bitcast_fusion.1
  106.4 1.9 copy.14
  108.4 2.5 broadcast_in_dim.42
  110.8 4.3 scatter_fusion
  115.1 3.8 convert_element_type.31
  118.9 0.0 copy-start.4
  118.9 0.0 reduce-scatter.3.cloned.1.call-update
  118.9 0.0 all-gather.5.cloned.1.call-start
  119.0 60.2 %reduce-scatter.3.cloned.1.call-done = bf16[128,512]{1,0:T(8,128)(2,1)} async-done(((bf16[2048,512]{1,0:T(8,128)(2,1)}), bf16[128,512]{1,0:T(8,128)(2,1)}) %reduce-scatter.3.cloned.1.call-update) | async-done | bytes 131088 | tf_op jit(solution)/shard_map/reduce_scatter | solution.py:52
  179.2 0.0 copy-done.4
  179.2 1.7 fusion.6
  180.9 0.0 all-gather.5.cloned.1.call-update
  180.9 0.0 reduce-scatter.5.cloned.1.call-start
  181.0 45.1 %all-gather.5.cloned.1.call-done = bf16[2048,512]{1,0:T(8,128)(2,1)} async-done(((bf16[128,512]{1,0:T(8,128)(2,1)}), bf16[2048,512]{1,0:T(8,128)(2,1)}) %all-gather.5.cloned.1.call-update) | async-done | bytes 2097168 | tf_op jit(solution)/shard_map/all_gather | solution.py:60
  226.1 2.2 gather_fusion.1
  228.3 1.9 select_bitcast_fusion
  230.2 1.9 copy.16
  232.1 4.3 broadcast_in_dim.45
  236.4 4.3 scatter_fusion.1
  240.7 6.0 convert_element_type.37
  246.7 0.0 copy-start.2
  246.7 0.0 reduce-scatter.5.cloned.1.call-update
  246.7 0.0 all-reduce.2.cloned.1.call-start
  246.8 219.3 %reduce-scatter.5.cloned.1.call-done = bf16[128,512]{1,0:T(8,128)(2,1)} async-done(((bf16[4096,512]{1,0:T(8,128)(2,1)}), bf16[128,512]{1,0:T(8,128)(2,1)}) %reduce-scatter.5.cloned.1.call-update) | async-done | bytes 131088 | tf_op jit(solution)/shard_map/reduce_scatter | solution.py:64
  466.1 0.0 copy-done.2
  466.1 0.0 copy-start.3
  466.1 2.3 convolution_bitcast_fusion
  468.4 0.0 all-reduce.2.cloned.1.call-update
  468.4 0.0 copy-done.3
  468.4 1.0 convolution_convert_fusion
  469.4 279.1 %all-reduce.2.cloned.1.call-done = f32[512,512]{0,1:T(8,128)} async-done(((f32[512,512]{0,1:T(8,128)}), f32[512,512]{0,1:T(8,128)}) %all-reduce.2.cloned.1.call-update) | async-done | bytes 1048592 | tf_op jit(solution)/shard_map/psum | solution.py:74
  748.5 1.3 broadcast_multiply_fusion
  749.8 1.3 copy.17
  (2 shorter events, 0.0 us)
Async XLA Ops:
  7.2 1.0 copy-start
  7.2 97.4 %copy-start.1 = (bf16[1,1,8,128,128]{4,3,2,1,0:T(8,128)(2,1)S(1)}, bf16[1,1,8,128,128]{4,3,2,1,0:T(8,128)(2,1)}, u32[]{:S(2)}) copy-start(bf16[1,1,8,128,128]{4,3,2,1,0:T(8,128)(2,1)} %param.10) | copy-start | bytes 786436
  7.2 94.5 %all-gather.3.cloned.1.call-start = ((), (), s32[]{:S(2)}) async-start(), calls=%async_computation.2 | async-start | bytes 4325376 | tf_op jit(solution)/shard_map/all_gather | solution.py:50
  10.0 169.1 %reduce-scatter.3.cloned.1.call-start = ((), (), s32[]{:S(2)}) async-start(), calls=%async_computation.3 | async-start | bytes 2228224 | tf_op jit(solution)/shard_map/reduce_scatter | solution.py:52
  118.9 60.3 %copy-start.4 = (bf16[128,512]{1,0:T(8,128)(2,1)S(1)}, bf16[128,512]{1,0:T(8,128)(2,1)}, u32[]{:S(2)}) copy-start(bf16[128,512]{1,0:T(8,128)(2,1)} %param.9) | copy-start | bytes 393220
  118.9 107.1 %all-gather.5.cloned.1.call-start = ((), (), s32[]{:S(2)}) async-start(), calls=%async_computation.4 | async-start | bytes 2228224 | tf_op jit(solution)/shard_map/all_gather | solution.py:60
  180.9 285.2 %reduce-scatter.5.cloned.1.call-start = ((), (), s32[]{:S(2)}) async-start(), calls=%async_computation.5 | async-start | bytes 4325376 | tf_op jit(solution)/shard_map/reduce_scatter | solution.py:64
  246.7 219.4 %copy-start.2 = (bf16[128,512]{1,0:T(8,128)(2,1)S(1)}, bf16[128,512]{1,0:T(8,128)(2,1)}, u32[]{:S(2)}) copy-start(bf16[128,512]{1,0:T(8,128)(2,1)} %param.7) | copy-start | bytes 393220
  246.7 501.7 %all-reduce.2.cloned.1.call-start = ((), (), s32[]{:S(2)}) async-start(), calls=%async_computation.6 | async-start | bytes 2097152 | tf_op jit(solution)/shard_map/psum | solution.py:74
  466.1 2.3 copy-start.3
Sparse Core Ops, SparseCore 0:
  11.8 89.9 all-gather.2
  119.1 60.0 reduce-scatter.2
  181.9 44.1 all-gather.4
  246.9 219.1 reduce-scatter.4
  472.4 276.0 all-reduce.1
where the time goes:
time: 758 us
  waiting for transfers between devices  693 us (91%)
  other arithmetic  23.4 us (3%)
  local copies, waits for them, and re-layouts  17.9 us (2%)
  between operations  13.9 us (2%)
  matrix products  8.83 us (1%)
    psum x1, waiting for transfers between devices, body(): weight_total = lax.psum(weight_part, ('row', 'col'))  279 us
    reduce_scatter x1, waiting for transfers between devices, body(): lax.psum_scatter(backward_term.astype(jnp.bfloat16), 'row', scatter_dimen...  219 us
    all_gather x1, waiting for transfers between devices, body(): panel = lax.all_gather(projected, 'row', axis=0, tiled=True)  89.7 us
    reduce_scatter x1, waiting for transfers between devices, body(): lax.psum_scatter(forward_term.astype(jnp.bfloat16), 'col', scatter_dimens...  60.2 us
    all_gather x1, waiting for transfers between devices, body(): grad_panel = lax.all_gather(grad_pre, 'col', axis=0, tiled=True)  45.1 us
  transfers between devices with their start and end apart: 5, of which 5 were waited for; matrix products, arithmetic and copies ran while one was open for 0% of the time, Pallas kernels for 0%

commit v1 on v0

v1 whole, which is shorter than its diff:
```python
import math

import jax
import jax.numpy as jnp
from jax import lax
from jax.experimental import pallas as pl
from jax.experimental.pallas import tpu as pltpu
from jax.sharding import Mesh, PartitionSpec as P

Y, X, Z, CORES = 8, 4, 8, 2
TILE = 128
SLOTS = 8
WIDTH = 512
CHUNK = WIDTH // X
ROW_TILES = Z * CORES
COL_TILES = Y * X
INDEX_ROWS = 16
BF16 = jnp.bfloat16
F32 = jnp.float32


def params():
    return pltpu.CompilerParams(vmem_limit_bytes=24 * 1024 * 1024)


def vmem():
    return pl.BlockSpec(memory_space=pltpu.VMEM)


def smem():
    return pl.BlockSpec(memory_space=pltpu.SMEM)


def forward_tiles(core_ref, index_ref, tiles_ref, panel_ref, mine_ref, other_ref, total):
    block = pl.program_id(0)
    core = core_ref[0]
    total[...] = jnp.zeros_like(total)
    for slot in range(SLOTS):
        row = index_ref[block, slot]
        col = index_ref[block, SLOTS + slot]
        valid = index_ref[block, 2 * SLOTS + slot]
        product = jnp.dot(
            tiles_ref[0, slot * TILE : (slot + 1) * TILE, :], panel_ref[col], preferred_element_type=F32
        )
        total[row] += jnp.where(valid > 0, product, 0.0)
    for pair in range(Z):
        mine_ref[0, pair] = total[2 * pair + core].astype(BF16)
        other_ref[0, pair] = total[2 * pair + 1 - core].astype(BF16)


def middle(parts_ref, weight_ref, cotangent_ref, act_ref, grad_ref, weight_part_ref):
    chunks = []
    for chunk in range(X):
        total = parts_ref[chunk * Z].astype(F32)
        for z in range(1, Z):
            total += parts_ref[chunk * Z + z].astype(F32)
        chunks.append(total)
    summed = jnp.concatenate(chunks, axis=1)
    high = summed.astype(BF16)
    low = (summed - high.astype(F32)).astype(BF16)
    weight = weight_ref[...]
    aggregated = jnp.dot(high, weight, preferred_element_type=F32) + jnp.dot(
        low, weight, preferred_element_type=F32
    )
    sig = jax.nn.sigmoid(aggregated)
    act_ref[...] = (aggregated * sig).astype(BF16)
    grad = (cotangent_ref[...].astype(F32) * sig * (1.0 + aggregated * (1.0 - sig))).astype(BF16)
    for chunk in range(X):
        piece = grad[:, chunk * CHUNK : (chunk + 1) * CHUNK]
        for z in range(Z):
            grad_ref[chunk * Z + z] = piece
    weight_part_ref[...] = lax.dot_general(
        high, grad, (((0,), (0,)), ((), ())), preferred_element_type=F32
    ).astype(BF16)


def backward_tiles(core_ref, index_ref, tiles_ref, mine_ref, other_ref, out_ref, total):
    core = core_ref[0]
    total[...] = jnp.zeros_like(total)
    for block in range(X):
        for slot in range(SLOTS):
            row = index_ref[block, slot]
            col = index_ref[block, SLOTS + slot]
            valid = index_ref[block, 2 * SLOTS + slot]
            at = block * Z + row // 2
            panel = jnp.where(row % 2 == core, mine_ref[at], other_ref[at])
            product = lax.dot_general(
                tiles_ref[block, slot * TILE : (slot + 1) * TILE, :],
                panel,
                (((0,), (0,)), ((), ())),
                preferred_element_type=F32,
            )
            total[col] += jnp.where(valid > 0, product, 0.0)
    for tile in range(COL_TILES):
        out_ref[tile] = total[tile].astype(BF16)


def last(parts_ref, weight_ref, out_ref):
    chunks = []
    for chunk in range(X):
        total = parts_ref[chunk].astype(F32)
        for y in range(1, Y):
            total += parts_ref[y * X + chunk].astype(F32)
        chunks.append(total)
    summed = jnp.concatenate(chunks, axis=1).astype(BF16)
    out_ref[...] = lax.dot_general(
        summed, weight_ref[...], (((1,), (1,)), ((), ())), preferred_element_type=F32
    ).astype(BF16)


def body(features, weight, cotangent, tile_values, tile_rows, tile_cols, tile_valid):
    core = lax.axis_index("core").astype(jnp.int32)[None]

    index = jnp.concatenate(
        [tile_rows.reshape(-1), tile_cols.reshape(-1), tile_valid.reshape(-1)]
    ).astype(BF16)
    index = jnp.pad(index[None, :], ((0, INDEX_ROWS - 1), (0, TILE - 3 * SLOTS)))
    tiles = jnp.concatenate([tile_values.reshape(SLOTS * TILE, TILE), index], axis=0)
    tiles = lax.all_gather(tiles, "x", axis=0)
    index = tiles[:, SLOTS * TILE, : 3 * SLOTS].astype(jnp.int32)
    limit = jnp.repeat(jnp.array([ROW_TILES - 1, COL_TILES - 1, 1], jnp.int32), SLOTS)
    index = jnp.clip(index, 0, limit[None, :])

    chunks = features.reshape(TILE, X, CHUNK).transpose(1, 0, 2)
    chunks = jnp.broadcast_to(chunks[None], (Y, X, TILE, CHUNK)).reshape(COL_TILES, TILE, CHUNK)
    panel = lax.all_to_all(chunks, ("y", "x"), 0, 0, tiled=True)

    rows = SLOTS * TILE + INDEX_ROWS
    mine, other = pl.pallas_call(
        forward_tiles,
        grid=(X,),
        in_specs=[
            smem(),
            smem(),
            pl.BlockSpec((1, rows, TILE), lambda i: (i, 0, 0)),
            pl.BlockSpec((COL_TILES, TILE, CHUNK), lambda i: (0, 0, 0)),
        ],
        out_specs=[pl.BlockSpec((1, Z, TILE, CHUNK), lambda i: (i, 0, 0, 0))] * 2,
        out_shape=[jax.ShapeDtypeStruct((X, Z, TILE, CHUNK), BF16)] * 2,
        scratch_shapes=[pltpu.VMEM((ROW_TILES, TILE, CHUNK), F32)],
        compiler_params=params(),
        name="forward_tiles",
    )(core, index, tiles, panel)

    swap = [(0, 1), (1, 0)]
    term = (mine.astype(F32) + lax.ppermute(other, "core", swap).astype(F32)).astype(BF16)
    parts = lax.all_to_all(term.reshape(X * Z, TILE, CHUNK), ("x", "z"), 0, 0, tiled=True)

    activations, grad, weight_part = pl.pallas_call(
        middle,
        in_specs=[vmem()] * 3,
        out_specs=[vmem()] * 3,
        out_shape=[
            jax.ShapeDtypeStruct((TILE, WIDTH), BF16),
            jax.ShapeDtypeStruct((X * Z, TILE, CHUNK), BF16),
            jax.ShapeDtypeStruct((WIDTH, WIDTH), BF16),
        ],
        compiler_params=params(),
        name="middle",
    )(parts, weight, cotangent)

    grad_mine = lax.all_to_all(grad, ("x", "z"), 0, 0, tiled=True)
    grad_other = lax.ppermute(grad_mine, "core", swap)

    group = Y * X * CORES
    share = WIDTH // group
    pieces = lax.all_to_all(
        weight_part.reshape(group, share, WIDTH), ("y", "x", "core"), 0, 0, tiled=True
    )
    piece = pieces.astype(F32).sum(0).astype(BF16)
    piece = lax.all_to_all(
        jnp.broadcast_to(piece[None], (Z, share, WIDTH)), "z", 0, 0, tiled=True
    )
    piece = piece.astype(F32).sum(0).astype(BF16)
    whole = lax.all_to_all(
        jnp.broadcast_to(piece[None], (group, share, WIDTH)), ("y", "x", "core"), 0, 0, tiled=True
    )
    nodes = TILE * Y * X * Z * CORES
    weight_grad = whole.reshape(WIDTH, WIDTH).astype(F32) * (1.0 / math.sqrt(nodes))

    back = pl.pallas_call(
        backward_tiles,
        in_specs=[smem(), smem(), vmem(), vmem(), vmem()],
        out_specs=vmem(),
        out_shape=jax.ShapeDtypeStruct((COL_TILES, TILE, CHUNK), BF16),
        scratch_shapes=[pltpu.VMEM((COL_TILES, TILE, CHUNK), F32)],
        compiler_params=params(),
        name="backward_tiles",
    )(core, index, tiles, grad_mine, grad_other)
    back = lax.all_to_all(back, ("y", "x"), 0, 0, tiled=True)

    input_grad = pl.pallas_call(
        last,
        in_specs=[vmem()] * 2,
        out_specs=vmem(),
        out_shape=jax.ShapeDtypeStruct((TILE, WIDTH), BF16),
        compiler_params=params(),
        name="last",
    )(back, weight)
    return (activations, input_grad, weight_grad)


def solution(mesh):
    axes = Mesh(mesh.devices.reshape(Y, X, Z, CORES), ("y", "x", "z", "core"))
    row, col = ("y", "x"), ("z", "core")
    placed = (
        P(col + row, None),
        P(),
        P(row + col, None),
        P(row, col, None, None, None),
        P(row, col, None),
        P(row, col, None),
        P(row, col, None),
    )
    return jax.shard_map(
        body,
        mesh=axes,
        in_specs=placed,
        out_specs=(P(row + col, None), P(col + row, None), P()),
        check_vma=False,
    )
```

time: 758 us -> 237 us (0.31)
  waiting for transfers between devices: 693 us -> 96.2 us
  blocking collectives: 0 us -> 63.7 us
  starting transfers between devices: 0.21 us -> 42.6 us
  other arithmetic: 23.4 us -> 5.39 us
  local copies, waits for them, and re-layouts: 17.9 us -> 5.03 us
  matrix products: 8.83 us -> 0 us
    reduce_scatter x2 -> x0, waiting for transfers between devices: 279 us -> none  [the longest x1 219 us: body(): lax.psum_scatter(backward_term.astype(jnp.bfloat16), 'row', scatter_dimen...]
    psum x1 -> x0, waiting for transfers between devices: 279 us -> none  [body(): weight_total = lax.psum(weight_part, ('row', 'col'))]
    all_gather x2 -> x1, waiting for transfers between devices: 135 us -> 27.4 us  [body(): tiles = lax.all_gather(tiles, 'x', axis=0)]
    all_to_all x0 -> x5, waiting for transfers between devices: none -> 66.5 us  [the longest x1 25 us: body(): back = lax.all_to_all(back, ('y', 'x'), 0, 0, tiled=True)]
    all_to_all x0 -> x2, blocking collectives: none -> 63.7 us  [the longest x1 38.3 us: body(): lax.all_to_all(term.reshape(X * Z, TILE, CHUNK), ('x', 'z'), 0, 0, tiled=...]
    all_to_all x0 -> x5, starting transfers between devices: none -> 35 us  [the longest x1 10.6 us: body(): panel = lax.all_to_all(chunks, ('y', 'x'), 0, 0, tiled=True)]
    convert_element_type x3 -> x1, other arithmetic: 11.5 us -> 0.37 us  [body(): (mine.astype(F32) + lax.ppermute(other, 'core', swap).astype(F32)).astype...]
    dot_general x5 -> x0, matrix products: 8.83 us -> none  [the longest x2 3.81 us: add_group(): jnp.einsum(form, group_values, blocks[group_in], preferred_element_type=j...]
  transfers between devices with their start and end apart: 5 -> 8, of which waited for: 5 -> 6; matrix products, arithmetic and copies ran while one was open for 0% -> 2% of each run, Pallas kernels for 0% -> 1%
where the time goes in v1:
time: 237 us; the launch traced here: 235 us
  waiting for transfers between devices  96.2 us (41%)
  blocking collectives  63.7 us (27%)
  starting transfers between devices  42.6 us (18%)
  between operations  14.2 us (6%)
  Pallas kernels  7.41 us (3%)
  other arithmetic  5.39 us (2%)
  local copies, waits for them, and re-layouts  5.03 us (2%)
    all_to_all x1, blocking collectives, body(): lax.all_to_all(term.reshape(X * Z, TILE, CHUNK), ('x', 'z'), 0, 0, tiled=...  38.3 us
    all_gather x1, waiting for transfers between devices, body(): tiles = lax.all_gather(tiles, 'x', axis=0)  27.4 us
    all_to_all x1, blocking collectives, body(): lax.all_to_all(weight_part.reshape(group, share, WIDTH), ('y', 'x', 'core...  25.4 us
    all_to_all x1, waiting for transfers between devices, body(): back = lax.all_to_all(back, ('y', 'x'), 0, 0, tiled=True)  25 us
    all_to_all x1, waiting for transfers between devices, body(): grad_mine = lax.all_to_all(grad, ('x', 'z'), 0, 0, tiled=True)  24.7 us
    all_to_all x1, waiting for transfers between devices, body(): lax.all_to_all(jnp.broadcast_to(piece[None], (group, share, WIDTH)), ('y'...  14.6 us
    all_to_all x1, starting transfers between devices, body(): panel = lax.all_to_all(chunks, ('y', 'x'), 0, 0, tiled=True)  10.6 us
    all_to_all x1, starting transfers between devices, body(): lax.all_to_all(jnp.broadcast_to(piece[None], (group, share, WIDTH)), ('y'...  8.48 us
  transfers between devices with their start and end apart: 8, of which 6 were waited for; matrix products, arithmetic and copies ran while one was open for 2% of the time, Pallas kernels for 1%

profile of v1, /device:TPU:1, one launch (start us, length us, event | category | flops | bytes accessed | tf_op | source)
XLA Modules:
  0.0 234.5 jit_solution(15961366666584147488)
XLA Ops:
  7.2 0.0 all-gather.3.cloned.1.call-start
  7.2 0.7 convert_bitcast_fusion.2
  7.9 0.7 convert_bitcast_fusion
  8.5 0.1 fusion.8
  8.6 1.7 pad_maximum_fusion
  10.3 0.0 all-gather.3.cloned.1.call-update
  10.3 0.9 reshape.84
  11.3 1.2 broadcast_in_dim.12
  12.5 0.0 copy-start.4
  12.5 10.6 %all-to-all-start = ((bf16[32,128,128]{2,1,0:T(8,128)(2,1)}), bf16[32,128,128]{2,1,0:T(8,128)(2,1)S(1)}, u32[]{:S(2)}, u32[]{:S(2)}) async-start(bf16[32,128,128]{2,1,0:T(8,128)(2,1)} %bitcast.8), calls=%async_computation | async-start | bytes 2097152 | tf_op jit(solution)/shard_map/all_to_all | solution.py:126
  23.1 0.0 copy-done.4
  23.2 0.1 broadcast_in_dim.11
  23.2 0.1 min.14
  23.3 27.4 %all-gather.3.cloned.1.call-done = bf16[4160,128]{1,0:T(8,128)(2,1)} async-done(((bf16[1040,128]{1,0:T(8,128)(2,1)}), bf16[4160,128]{1,0:T(8,128)(2,1)}) %all-gather.3.cloned.1.call-update) | async-done | bytes 1064976 | tf_op jit(solution)/shard_map/all_gather | solution.py:119
  50.7 0.7 fusion.9
  51.4 0.0 all-to-all-done.panel_ref
  51.4 0.0 copy-start
  51.4 1.2 copy-done
  52.7 1.8 forward_tiles.1
  54.5 2.7 %collective-permute-start = (bf16[4,8,128,128]{3,2,1,0:T(8,128)(2,1)S(1)}, bf16[4,8,128,128]{3,2,1,0:T(8,128)(2,1)S(1)}, u32[]{:S(2)}, u32[]{:S(2)}) collective-permute-start(bf16[4,8,128,128]{3,2,1,0:T(8,128)(2,1)S(1)} %get-tuple-element.9), channel_id=1, source_target_pairs={{0,1},{1,0},{2,3},{3,2},{4,5},{5,4},{6,7},{7,6},{8,9},{9,8},{10,11... | collective-permute-start | bytes 3145736 | tf_op jit(solution)/shard_map/ppermute | solution.py:146
  57.1 2.3 collective-permute-done
  59.4 0.4 add_convert_fusion
  59.8 0.0 copy-start.2
  59.8 0.0 copy-start.3
  59.8 38.3 %all_to_all.35.parts_ref = bf16[32,128,128]{2,1,0:T(8,128)(2,1)S(1)} all-to-all(bf16[32,128,128]{2,1,0:T(8,128)(2,1)S(1)} %bitcast.20), channel_id=1, replica_groups=mesh['y'=8,'x'=4,'z'=8,'core'=2] {'x','z'}, dimensions={0} | all-to-all | bytes 2097152 | tf_op jit(solution)/shard_map/all_to_all | solution.py:147
  98.1 0.0 copy-done.2
  98.1 0.0 copy-done.3
  98.1 1.5 middle.1
  99.6 25.4 %all_to_all.36 = bf16[64,8,512]{2,1,0:T(8,128)(2,1)S(1)} all-to-all(bf16[64,8,512]{2,1,0:T(8,128)(2,1)S(1)} %bitcast.19), channel_id=1, replica_groups=mesh['y'=8,'x'=4,'z'=8,'core'=2] {'y','x','core'}, dimensions={0} | all-to-all | bytes 1048576 | tf_op jit(solution)/shard_map/all_to_all | solution.py:167
  125.0 5.9 %all-to-all-start.2 = ((bf16[32,128,128]{2,1,0:T(8,128)(2,1)}), bf16[32,128,128]{2,1,0:T(8,128)(2,1)S(1)}, u32[]{:S(2)}, u32[]{:S(2)}) async-start(bf16[32,128,128]{2,1,0:T(8,128)(2,1)} %get-tuple-element.11), calls=%async_computation.2 | async-start | bytes 2097152 | tf_op jit(solution)/shard_map/all_to_all | solution.py:162
  131.0 0.0 copy-start.1
  131.0 0.1 reduce_sum.24
  131.1 24.7 %all-to-all-done.2.mine_ref = bf16[32,128,128]{2,1,0:T(8,128)(2,1)S(1)} async-done(((bf16[32,128,128]{2,1,0:T(8,128)(2,1)}), bf16[32,128,128]{2,1,0:T(8,128)(2,1)S(1)}, u32[]{:S(2)}, u32[]{:S(2)}) %all-to-all-start.2) | async-done | bytes 1048608 | tf_op jit(solution)/shard_map/all_to_all | solution.py:162
  155.8 0.6 broadcast_in_dim.13
  156.4 5.4 %all-to-all-start.5 = ((bf16[8,8,512]{2,1,0:T(8,128)(2,1)}), bf16[8,8,512]{2,1,0:T(8,128)(2,1)S(1)}, u32[]{:S(2)}, u32[]{:S(2)}) async-start(bf16[8,8,512]{2,1,0:T(8,128)(2,1)} %broadcast_in_dim.13), calls=%async_computation.5 | async-start | bytes 131072 | tf_op jit(solution)/shard_map/all_to_all | solution.py:171
  161.8 4.9 %collective-permute-start.1 = (bf16[32,128,128]{2,1,0:T(8,128)(2,1)S(1)}, bf16[32,128,128]{2,1,0:T(8,128)(2,1)}, u32[]{:S(2)}, u32[]{:S(2)}) collective-permute-start(bf16[32,128,128]{2,1,0:T(8,128)(2,1)S(1)} %all-to-all-done.2.mine_ref), channel_id=1, source_target_pairs={{0,1},{1,0},{2,3},{3,2},{4,5},{5,4},{6,7},{7,6},{8,9},{9,8},{10,11... | collective-permute-start | bytes 3145736 | tf_op jit(solution)/shard_map/ppermute | solution.py:163
  166.8 2.3 all-to-all-done.5
  169.1 0.8 broadcast_in_dim.14
  169.9 8.5 %all-to-all-start.6 = ((bf16[64,8,512]{2,1,0:T(8,128)(2,1)}), bf16[64,8,512]{2,1,0:T(8,128)(2,1)S(1)}, u32[]{:S(2)}, u32[]{:S(2)}) async-start(bf16[64,8,512]{2,1,0:T(8,128)(2,1)} %broadcast_in_dim.14), calls=%async_computation.6 | async-start | bytes 1048576 | tf_op jit(solution)/shard_map/all_to_all | solution.py:175
  178.4 0.0 collective-permute-done.1.other_ref
  178.4 0.0 copy-done.1
  178.4 3.1 %backward_tiles.1 = bf16[32,128,128]{2,1,0:T(8,128)(2,1)} custom-call(s32[1]{0:T(128)} %bitcast.core_ref, s32[4,24]{1,0:T(4,128)S(1)} %broadcast_minimum_fusion.index_ref, bf16[4,1040,128]{2,1,0:T(8,128)(2,1)S(1)} %bitcast.18, bf16[32,128,128]{2,1,0:T(8,128)(2,1)S(1)} %all-to-all-done.2.mine_ref, bf16[32,128,128]{2,1,0:T(8,128)(2,1)} %collective-permute-done.1.other_ref), custom_call_target="tpu_custom_call" | custom-call | tf_op jit(solution)/shard_map/backward_tiles/pallas_call | solution.py:181
  181.5 14.6 %all-to-all-done.6 = bf16[64,8,512]{2,1,0:T(8,128)(2,1)S(1)} async-done(((bf16[64,8,512]{2,1,0:T(8,128)(2,1)}), bf16[64,8,512]{2,1,0:T(8,128)(2,1)S(1)}, u32[]{:S(2)}, u32[]{:S(2)}) %all-to-all-start.6) | async-done | bytes 524320 | tf_op jit(solution)/shard_map/all_to_all | solution.py:175
  196.1 4.5 %all-to-all-start.3 = ((bf16[32,128,128]{2,1,0:T(8,128)(2,1)}), bf16[32,128,128]{2,1,0:T(8,128)(2,1)S(1)}, u32[]{:S(2)}, u32[]{:S(2)}) async-start(bf16[32,128,128]{2,1,0:T(8,128)(2,1)} %backward_tiles.1), calls=%async_computation.3 | async-start | bytes 2097152 | tf_op jit(solution)/shard_map/all_to_all | solution.py:190
  200.6 1.1 multiply_bitcast_fusion
  201.7 25.0 %all-to-all-done.3.parts_ref = bf16[32,128,128]{2,1,0:T(8,128)(2,1)S(1)} async-done(((bf16[32,128,128]{2,1,0:T(8,128)(2,1)}), bf16[32,128,128]{2,1,0:T(8,128)(2,1)S(1)}, u32[]{:S(2)}, u32[]{:S(2)}) %all-to-all-start.3) | async-done | bytes 1048608 | tf_op jit(solution)/shard_map/all_to_all | solution.py:190
  226.7 1.0 last.1
  (3 shorter events, 0.0 us)
Async XLA Ops:
  7.2 43.6 %all-gather.3.cloned.1.call-start = ((), (), s32[]{:S(2)}) async-start(), calls=%async_computation.7 | async-start | bytes 1331200 | tf_op jit(solution)/shard_map/all_gather | solution.py:119
  12.5 10.6 %copy-start.4 = (s32[3]{0:T(128)S(1)}, s32[3]{0:T(128)}, u32[]{:S(2)}) copy-start(s32[3]{0:T(128)} %constant.15.clone) | copy-start | bytes 40
  12.5 38.9 %all-to-all-start = ((bf16[32,128,128]{2,1,0:T(8,128)(2,1)}), bf16[32,128,128]{2,1,0:T(8,128)(2,1)S(1)}, u32[]{:S(2)}, u32[]{:S(2)}) async-start(bf16[32,128,128]{2,1,0:T(8,128)(2,1)} %bitcast.8), calls=%async_computation | async-start | bytes 2097152 | tf_op jit(solution)/shard_map/all_to_all | solution.py:126
  51.4 1.2 copy-start
  54.5 4.9 %collective-permute-start = (bf16[4,8,128,128]{3,2,1,0:T(8,128)(2,1)S(1)}, bf16[4,8,128,128]{3,2,1,0:T(8,128)(2,1)S(1)}, u32[]{:S(2)}, u32[]{:S(2)}) collective-permute-start(bf16[4,8,128,128]{3,2,1,0:T(8,128)(2,1)S(1)} %get-tuple-element.9), channel_id=1, source_target_pairs={{0,1},{1,0},{2,3},{3,2},{4,5},{5,4},{6,7},{7,6},{8,9},{9,8},{10,11... | collective-permute-start | bytes 3145736 | tf_op jit(solution)/shard_map/ppermute | solution.py:146
  59.8 38.3 %copy-start.2 = (bf16[512,512]{1,0:T(8,128)(2,1)S(1)}, bf16[512,512]{1,0:T(8,128)(2,1)}, u32[]{:S(2)}) copy-start(bf16[512,512]{1,0:T(8,128)(2,1)} %weight_ref.3) | copy-start | bytes 1572868
  59.8 38.3 %copy-start.3 = (bf16[128,512]{1,0:T(8,128)(2,1)S(1)}, bf16[128,512]{1,0:T(8,128)(2,1)}, u32[]{:S(2)}) copy-start(bf16[128,512]{1,0:T(8,128)(2,1)} %cotangent_ref.1) | copy-start | bytes 393220
  125.0 30.8 %all-to-all-start.2 = ((bf16[32,128,128]{2,1,0:T(8,128)(2,1)}), bf16[32,128,128]{2,1,0:T(8,128)(2,1)S(1)}, u32[]{:S(2)}, u32[]{:S(2)}) async-start(bf16[32,128,128]{2,1,0:T(8,128)(2,1)} %get-tuple-element.11), calls=%async_computation.2 | async-start | bytes 2097152 | tf_op jit(solution)/shard_map/all_to_all | solution.py:162
  131.0 47.5 %copy-start.1 = (bf16[4160,128]{1,0:T(8,128)(2,1)S(1)}, bf16[4160,128]{1,0:T(8,128)(2,1)}, u32[]{:S(2)}) copy-start(bf16[4160,128]{1,0:T(8,128)(2,1)} %all-gather.3.cloned.1.call-done) | copy-start | bytes 3194884
  156.4 12.7 %all-to-all-start.5 = ((bf16[8,8,512]{2,1,0:T(8,128)(2,1)}), bf16[8,8,512]{2,1,0:T(8,128)(2,1)S(1)}, u32[]{:S(2)}, u32[]{:S(2)}) async-start(bf16[8,8,512]{2,1,0:T(8,128)(2,1)} %broadcast_in_dim.13), calls=%async_computation.5 | async-start | bytes 131072 | tf_op jit(solution)/shard_map/all_to_all | solution.py:171
  161.8 16.6 %collective-permute-start.1 = (bf16[32,128,128]{2,1,0:T(8,128)(2,1)S(1)}, bf16[32,128,128]{2,1,0:T(8,128)(2,1)}, u32[]{:S(2)}, u32[]{:S(2)}) collective-permute-start(bf16[32,128,128]{2,1,0:T(8,128)(2,1)S(1)} %all-to-all-done.2.mine_ref), channel_id=1, source_target_pairs={{0,1},{1,0},{2,3},{3,2},{4,5},{5,4},{6,7},{7,6},{8,9},{9,8},{10,11... | collective-permute-start | bytes 3145736 | tf_op jit(solution)/shard_map/ppermute | solution.py:163
  169.9 26.2 %all-to-all-start.6 = ((bf16[64,8,512]{2,1,0:T(8,128)(2,1)}), bf16[64,8,512]{2,1,0:T(8,128)(2,1)S(1)}, u32[]{:S(2)}, u32[]{:S(2)}) async-start(bf16[64,8,512]{2,1,0:T(8,128)(2,1)} %broadcast_in_dim.14), calls=%async_computation.6 | async-start | bytes 1048576 | tf_op jit(solution)/shard_map/all_to_all | solution.py:175
  196.1 30.6 %all-to-all-start.3 = ((bf16[32,128,128]{2,1,0:T(8,128)(2,1)}), bf16[32,128,128]{2,1,0:T(8,128)(2,1)S(1)}, u32[]{:S(2)}, u32[]{:S(2)}) async-start(bf16[32,128,128]{2,1,0:T(8,128)(2,1)} %backward_tiles.1), calls=%async_computation.3 | async-start | bytes 2097152 | tf_op jit(solution)/shard_map/all_to_all | solution.py:190
Sparse Core Ops, SparseCore 0:
  10.4 40.2 all-gather.2

commit v2 on v1

v2 whole, which is shorter than its diff:
```python
import math

import jax
import jax.numpy as jnp
from jax import lax
from jax.experimental import pallas as pl
from jax.experimental.pallas import tpu as pltpu
from jax.sharding import Mesh, PartitionSpec as P

Y, X, Z, CORES = 8, 4, 8, 2
TILE = 128
SLOTS = 8
WIDTH = 512
CHUNK = WIDTH // X
ROW_TILES = Z * CORES
COL_TILES = Y * X
INDEX_ROWS = 16
BF16 = jnp.bfloat16
F32 = jnp.float32


def params():
    return pltpu.CompilerParams(vmem_limit_bytes=24 * 1024 * 1024)


def vmem():
    return pl.BlockSpec(memory_space=pltpu.VMEM)


def smem():
    return pl.BlockSpec(memory_space=pltpu.SMEM)


def spread(features_ref, out_ref):
    for chunk in range(X):
        piece = features_ref[:, chunk * CHUNK : (chunk + 1) * CHUNK]
        for y in range(Y):
            out_ref[y * X + chunk] = piece


def forward_tiles(place_ref, index_ref, panel_ref, *refs):
    tiles_refs, (mine_ref, other_ref, total) = refs[:X], refs[X:]
    core = place_ref[0]
    for step in range(X):
        block = place_ref[1] ^ step
        total[...] = jnp.zeros_like(total)
        for slot in range(SLOTS):
            row = index_ref[step, slot]
            col = index_ref[step, SLOTS + slot]
            valid = index_ref[step, 2 * SLOTS + slot]
            tile = tiles_refs[step][slot * TILE : (slot + 1) * TILE, :]
            product = jnp.dot(tile, panel_ref[col], preferred_element_type=F32)
            total[row] += jnp.where(valid > 0, product, 0.0)
        for pair in range(Z):
            mine_ref[block * Z + pair] = total[2 * pair + core].astype(BF16)
            other_ref[block * Z + pair] = total[2 * pair + 1 - core].astype(BF16)


def middle(core_ref, parts_ref, weight_ref, cotangent_ref, act_ref, grad_ref, keep_ref, send_ref):
    chunks = []
    for chunk in range(X):
        total = parts_ref[chunk * Z].astype(F32)
        for z in range(1, Z):
            total += parts_ref[chunk * Z + z].astype(F32)
        chunks.append(total)
    summed = jnp.concatenate(chunks, axis=1)
    high = summed.astype(BF16)
    low = (summed - high.astype(F32)).astype(BF16)
    weight = weight_ref[...]
    aggregated = jnp.dot(high, weight, preferred_element_type=F32) + jnp.dot(
        low, weight, preferred_element_type=F32
    )
    sig = jax.nn.sigmoid(aggregated)
    act_ref[...] = (aggregated * sig).astype(BF16)
    grad = (cotangent_ref[...].astype(F32) * sig * (1.0 + aggregated * (1.0 - sig))).astype(BF16)
    for chunk in range(X):
        piece = grad[:, chunk * CHUNK : (chunk + 1) * CHUNK]
        for z in range(Z):
            grad_ref[chunk * Z + z] = piece
    weight_part = lax.dot_general(
        high, grad, (((0,), (0,)), ((), ())), preferred_element_type=F32
    ).astype(BF16)
    low_half, high_half = weight_part[: WIDTH // 2], weight_part[WIDTH // 2 :]
    upper = core_ref[0] == 1
    keep_ref[...] = jnp.where(upper, high_half, low_half)
    send_ref[...] = jnp.where(upper, low_half, high_half)


def backward_tiles(place_ref, index_ref, mine_ref, other_ref, *refs):
    tiles_refs, (out_ref, total) = refs[:X], refs[X:]
    core = place_ref[0]
    total[...] = jnp.zeros_like(total)
    for step in range(X):
        block = place_ref[1] ^ step
        for slot in range(SLOTS):
            row = index_ref[step, slot]
            col = index_ref[step, SLOTS + slot]
            valid = index_ref[step, 2 * SLOTS + slot]
            at = block * Z + row // 2
            panel = jnp.where(row % 2 == core, mine_ref[at], other_ref[at])
            tile = tiles_refs[step][slot * TILE : (slot + 1) * TILE, :]
            product = lax.dot_general(
                tile, panel, (((0,), (0,)), ((), ())), preferred_element_type=F32
            )
            total[col] += jnp.where(valid > 0, product, 0.0)
    for tile in range(COL_TILES):
        out_ref[tile] = total[tile].astype(BF16)


def last(parts_ref, weight_ref, out_ref):
    chunks = []
    for chunk in range(X):
        total = parts_ref[chunk].astype(F32)
        for y in range(1, Y):
            total += parts_ref[y * X + chunk].astype(F32)
        chunks.append(total)
    summed = jnp.concatenate(chunks, axis=1).astype(BF16)
    out_ref[...] = lax.dot_general(
        summed, weight_ref[...], (((1,), (1,)), ((), ())), preferred_element_type=F32
    ).astype(BF16)


def exchange(array, axis, distance):
    size = lax.axis_size(axis)
    return lax.ppermute(array, axis, [(i, i ^ distance) for i in range(size)])


def halve(array, axis, distance):
    upper = jnp.minimum(lax.axis_index(axis) & distance, 1)
    halves = array.reshape(2, array.shape[0] // 2, array.shape[1])
    send = lax.dynamic_index_in_dim(halves, 1 - upper, 0, keepdims=False)
    keep = lax.dynamic_index_in_dim(halves, upper, 0, keepdims=False)
    return (keep.astype(F32) + exchange(send, axis, distance).astype(F32)).astype(BF16)


def body(features, weight, cotangent, tile_values, tile_rows, tile_cols, tile_valid):
    place = jnp.stack([lax.axis_index("core"), lax.axis_index("x")]).astype(jnp.int32)

    chunks = pl.pallas_call(
        spread,
        in_specs=[vmem()],
        out_specs=vmem(),
        out_shape=jax.ShapeDtypeStruct((COL_TILES, TILE, CHUNK), BF16),
        compiler_params=params(),
        name="spread",
    )(features)
    panel = lax.all_to_all(chunks, ("y", "x"), 0, 0, tiled=True)

    index = jnp.concatenate(
        [tile_rows.reshape(-1), tile_cols.reshape(-1), tile_valid.reshape(-1)]
    ).astype(BF16)
    index = jnp.pad(index[None, :], ((0, INDEX_ROWS - 1), (0, TILE - 3 * SLOTS)))
    tiles = jnp.concatenate([tile_values.reshape(SLOTS * TILE, TILE), index], axis=0)
    tiles = [tiles] + [exchange(tiles, "x", distance) for distance in range(1, X)]
    index = jnp.stack([t[SLOTS * TILE, : 3 * SLOTS] for t in tiles]).astype(jnp.int32)
    limit = jnp.repeat(jnp.array([ROW_TILES - 1, COL_TILES - 1, 1], jnp.int32), SLOTS)
    index = jnp.clip(index, 0, limit[None, :])

    mine, other = pl.pallas_call(
        forward_tiles,
        in_specs=[smem(), smem()] + [vmem()] * (1 + X),
        out_specs=[vmem()] * 2,
        out_shape=[jax.ShapeDtypeStruct((X * Z, TILE, CHUNK), BF16)] * 2,
        scratch_shapes=[pltpu.VMEM((ROW_TILES, TILE, CHUNK), F32)],
        compiler_params=params(),
        name="forward_tiles",
    )(place, index, panel, *tiles)
    term = (mine.astype(F32) + exchange(other, "core", 1).astype(F32)).astype(BF16)
    parts = lax.all_to_all(term, ("x", "z"), 0, 0, tiled=True)

    half = WIDTH // CORES
    activations, grad, weight_keep, weight_send = pl.pallas_call(
        middle,
        in_specs=[smem()] + [vmem()] * 3,
        out_specs=[vmem()] * 4,
        out_shape=[
            jax.ShapeDtypeStruct((TILE, WIDTH), BF16),
            jax.ShapeDtypeStruct((X * Z, TILE, CHUNK), BF16),
            jax.ShapeDtypeStruct((half, WIDTH), BF16),
            jax.ShapeDtypeStruct((half, WIDTH), BF16),
        ],
        compiler_params=params(),
        name="middle",
    )(place, parts, weight, cotangent)

    grad_mine = lax.all_to_all(grad, ("x", "z"), 0, 0, tiled=True)
    piece = weight_keep.astype(F32) + exchange(weight_send, "core", 1).astype(F32)
    piece = piece.astype(BF16)
    for distance in (1, 2, 4):
        piece = halve(piece, "y", distance)
    grad_mine, piece = lax.optimization_barrier((grad_mine, piece))

    grad_other = exchange(grad_mine, "core", 1)
    back = pl.pallas_call(
        backward_tiles,
        in_specs=[smem(), smem()] + [vmem()] * (2 + X),
        out_specs=vmem(),
        out_shape=jax.ShapeDtypeStruct((COL_TILES, TILE, CHUNK), BF16),
        scratch_shapes=[pltpu.VMEM((COL_TILES, TILE, CHUNK), F32)],
        compiler_params=params(),
        name="backward_tiles",
    )(place, index, grad_mine, grad_other, *tiles)
    back, piece = lax.optimization_barrier((back, piece.astype(F32)))
    back = lax.all_to_all(back, ("y", "x"), 0, 0, tiled=True)
    for axis, distance in (("z", 1), ("z", 2), ("z", 4), ("x", 1), ("x", 2)):
        piece = piece + exchange(piece, axis, distance)
    back, piece = lax.optimization_barrier((back, piece))

    input_grad = pl.pallas_call(
        last,
        in_specs=[vmem()] * 2,
        out_specs=vmem(),
        out_shape=jax.ShapeDtypeStruct((TILE, WIDTH), BF16),
        compiler_params=params(),
        name="last",
    )(back, weight)

    share = WIDTH // (Y * CORES)
    piece = jnp.broadcast_to(piece.astype(BF16)[None], (Y * CORES, share, WIDTH))
    whole = lax.all_to_all(piece, ("y", "core"), 0, 0, tiled=True)
    whole = whole.reshape(2, 2, 2, CORES, share, WIDTH).transpose(3, 2, 1, 0, 4, 5)
    nodes = TILE * Y * X * Z * CORES
    weight_grad = whole.reshape(WIDTH, WIDTH).astype(F32) * (1.0 / math.sqrt(nodes))
    return (activations, input_grad, weight_grad)


def solution(mesh):
    axes = Mesh(mesh.devices.reshape(Y, X, Z, CORES), ("y", "x", "z", "core"))
    row, col = ("y", "x"), ("z", "core")
    placed = (
        P(col + row, None),
        P(),
        P(row + col, None),
        P(row, col, None, None, None),
        P(row, col, None),
        P(row, col, None),
        P(row, col, None),
    )
    return jax.shard_map(
        body,
        mesh=axes,
        in_specs=placed,
        out_specs=(P(row + col, None), P(col + row, None), P()),
        check_vma=False,
    )
```

time: 237 us -> 207 us (0.87)
  starting transfers between devices: 42.6 us -> 89.4 us
  waiting for transfers between devices: 96.2 us -> 64.4 us
  blocking collectives: 63.7 us -> 38.3 us
  between operations: 14.2 us -> 1 us
  other arithmetic: 5.39 us -> 0.96 us
    ppermute x2 -> x14, waiting for transfers between devices: 2.27 us -> 48.1 us  [exchange(): return lax.ppermute(array, axis, [(i, i ^ distance) for i in range(size)])]
    ppermute x2 -> x14, starting transfers between devices: 7.6 us -> 51.8 us  [exchange(): return lax.ppermute(array, axis, [(i, i ^ distance) for i in range(size)])]
    all_gather x1 -> x0, waiting for transfers between devices: 27.4 us -> none  [body(): tiles = lax.all_gather(tiles, 'x', axis=0)]
    all_to_all x2 -> x1, blocking collectives: 63.7 us -> 38.3 us  [body(): parts = lax.all_to_all(term, ('x', 'z'), 0, 0, tiled=True)]
    all_to_all x1, waiting for transfers between devices: 25 us -> 0.01 us  [body(): back = lax.all_to_all(back, ('y', 'x'), 0, 0, tiled=True)]
    all_to_all x1, waiting for transfers between devices: 24.7 us -> 0.01 us  [body(): grad_mine = lax.all_to_all(grad, ('x', 'z'), 0, 0, tiled=True)]
    all_to_all x2 -> x1, starting transfers between devices: 13.9 us -> 12.2 us  [body(): whole = lax.all_to_all(piece, ('y', 'core'), 0, 0, tiled=True)]
    all_to_all x2 -> x1, waiting for transfers between devices: 16.9 us -> 16.4 us  [body(): whole = lax.all_to_all(piece, ('y', 'core'), 0, 0, tiled=True)]
  transfers between devices with their start and end apart: 8 -> 18, of which waited for: 6 -> 14; matrix products, arithmetic and copies ran while one was open for 2% -> 0% of each run, Pallas kernels for 1% -> 0%
where the time goes in v2:
time: 207 us; the launch traced here: 206 us
  starting transfers between devices  89.4 us (43%)
  waiting for transfers between devices  64.4 us (31%)
  blocking collectives  38.3 us (19%)
  Pallas kernels  7.64 us (4%)
  local copies, waits for them, and re-layouts  4.02 us (2%)
    ppermute x14, starting transfers between devices, exchange(): return lax.ppermute(array, axis, [(i, i ^ distance) for i in range(size)])  51.8 us
    ppermute x14, waiting for transfers between devices, exchange(): return lax.ppermute(array, axis, [(i, i ^ distance) for i in range(size)])  48.1 us
    all_to_all x1, blocking collectives, body(): parts = lax.all_to_all(term, ('x', 'z'), 0, 0, tiled=True)  38.3 us
    all_to_all x1, waiting for transfers between devices, body(): whole = lax.all_to_all(piece, ('y', 'core'), 0, 0, tiled=True)  16.4 us
    all_to_all x1, starting transfers between devices, body(): whole = lax.all_to_all(piece, ('y', 'core'), 0, 0, tiled=True)  12.2 us
    all_to_all x1, starting transfers between devices, body(): panel = lax.all_to_all(chunks, ('y', 'x'), 0, 0, tiled=True)  10.6 us
    all_to_all x1, starting transfers between devices, body(): grad_mine = lax.all_to_all(grad, ('x', 'z'), 0, 0, tiled=True)  7.95 us
    all_to_all x1, starting transfers between devices, body(): back = lax.all_to_all(back, ('y', 'x'), 0, 0, tiled=True)  6.78 us
  transfers between devices with their start and end apart: 18, of which 14 were waited for; matrix products, arithmetic and copies ran while one was open for 0% of the time, Pallas kernels for 0%

profile of v2, /device:TPU:1, one launch (start us, length us, event | category | flops | bytes accessed | tf_op | source)
XLA Modules:
  0.0 205.7 jit_solution(14990250743243233413)
XLA Ops:
  0.6 0.0 copy-start.2
  0.6 0.9 copy-done.2
  1.5 1.1 spread.1
  2.7 0.0 copy-start.5
  2.7 10.6 %all-to-all-start = ((bf16[32,128,128]{2,1,0:T(8,128)(2,1)}), bf16[32,128,128]{2,1,0:T(8,128)(2,1)S(1)}, u32[]{:S(2)}, u32[]{:S(2)}) async-start(bf16[32,128,128]{2,1,0:T(8,128)(2,1)} %spread.1), calls=%async_computation | async-start | bytes 2097152 | tf_op jit(solution)/shard_map/all_to_all | solution.py:147
  13.3 0.0 copy-done.8
  13.3 0.0 copy-done.6
  13.3 0.0 copy-done.7
  13.4 0.1 fusion.11
  13.5 0.0 copy-done.4
  13.5 4.3 %collective-permute-start.2 = (bf16[1040,128]{1,0:T(8,128)(2,1)S(1)}, bf16[1040,128]{1,0:T(8,128)(2,1)S(1)}, u32[]{:S(2)}, u32[]{:S(2)}) collective-permute-start(bf16[1040,128]{1,0:T(8,128)(2,1)S(1)} %pad_maximum_fusion.refs_0_), channel_id=1, source_target_pairs={{0,48},{16,32},{32,16},{48,0},{1,49},{17,33},{33,17},{49,1},{2,50}... | collective-permute-start | bytes 798728 | tf_op jit(solution)/shard_map/ppermute | solution.py:125
  17.8 2.5 %collective-permute-start.1 = (bf16[1040,128]{1,0:T(8,128)(2,1)S(1)}, bf16[1040,128]{1,0:T(8,128)(2,1)S(1)}, u32[]{:S(2)}, u32[]{:S(2)}) collective-permute-start(bf16[1040,128]{1,0:T(8,128)(2,1)S(1)} %pad_maximum_fusion.refs_0_), channel_id=1, source_target_pairs={{0,32},{16,48},{32,0},{48,16},{1,33},{17,49},{33,1},{49,17},{2,34}... | collective-permute-start | bytes 798728 | tf_op jit(solution)/shard_map/ppermute | solution.py:125
  20.3 2.1 %collective-permute-start = (bf16[1040,128]{1,0:T(8,128)(2,1)S(1)}, bf16[1040,128]{1,0:T(8,128)(2,1)S(1)}, u32[]{:S(2)}, u32[]{:S(2)}) collective-permute-start(bf16[1040,128]{1,0:T(8,128)(2,1)S(1)} %pad_maximum_fusion.refs_0_), channel_id=1, source_target_pairs={{0,16},{16,0},{32,48},{48,32},{1,17},{17,1},{33,49},{49,33},{2,18}... | collective-permute-start | bytes 798728 | tf_op jit(solution)/shard_map/ppermute | solution.py:125
  22.5 0.0 copy-done.5
  22.5 0.1 broadcast_in_dim.4
  22.6 0.1 min.23
  22.7 0.1 pad_add_fusion.place_ref.core_ref
  22.7 14.6 %collective-permute-done.2.refs_3_ = bf16[1040,128]{1,0:T(8,128)(2,1)S(1)} collective-permute-done((bf16[1040,128]{1,0:T(8,128)(2,1)S(1)}, bf16[1040,128]{1,0:T(8,128)(2,1)S(1)}, u32[]{:S(2)}, u32[]{:S(2)}) %collective-permute-start.2) | collective-permute-done | bytes 266272 | tf_op jit(solution)/shard_map/ppermute | solution.py:125
  37.4 0.0 collective-permute-done.1.refs_2_
  37.4 3.7 %collective-permute-done.refs_1_ = bf16[1040,128]{1,0:T(8,128)(2,1)S(1)} collective-permute-done((bf16[1040,128]{1,0:T(8,128)(2,1)S(1)}, bf16[1040,128]{1,0:T(8,128)(2,1)S(1)}, u32[]{:S(2)}, u32[]{:S(2)}) %collective-permute-start) | collective-permute-done | bytes 266272 | tf_op jit(solution)/shard_map/ppermute | solution.py:125
  41.1 0.1 maximum_minimum_fusion.index_ref
  41.2 0.0 all-to-all-done.panel_ref
  41.2 1.5 forward_tiles.1
  42.7 3.1 %collective-permute-start.3 = (bf16[32,128,128]{2,1,0:T(8,128)(2,1)S(1)}, bf16[32,128,128]{2,1,0:T(8,128)(2,1)S(1)}, u32[]{:S(2)}, u32[]{:S(2)}) collective-permute-start(bf16[32,128,128]{2,1,0:T(8,128)(2,1)S(1)} %get-tuple-element.16), channel_id=1, source_target_pairs={{0,1},{1,0},{2,3},{3,2},{4,5},{5,4},{6,7},{7,6},{8,9},{9,8},{10,11... | collective-permute-start | bytes 3145736 | tf_op jit(solution)/shard_map/ppermute | solution.py:125
  45.8 2.3 %collective-permute-done.3 = bf16[32,128,128]{2,1,0:T(8,128)(2,1)S(1)} collective-permute-done((bf16[32,128,128]{2,1,0:T(8,128)(2,1)S(1)}, bf16[32,128,128]{2,1,0:T(8,128)(2,1)S(1)}, u32[]{:S(2)}, u32[]{:S(2)}) %collective-permute-start.3) | collective-permute-done | bytes 1048608 | tf_op jit(solution)/shard_map/ppermute | solution.py:125
  48.1 0.4 add_convert_fusion
  48.4 0.0 copy-start
  48.4 0.0 copy-start.3
  48.5 38.3 %all_to_all.25.parts_ref = bf16[32,128,128]{2,1,0:T(8,128)(2,1)S(1)} all-to-all(bf16[32,128,128]{2,1,0:T(8,128)(2,1)S(1)} %add_convert_fusion), channel_id=1, replica_groups=mesh['y'=8,'x'=4,'z'=8,'core'=2] {'x','z'}, dimensions={0} | all-to-all | bytes 2097152 | tf_op jit(solution)/shard_map/all_to_all | solution.py:169
  86.7 0.0 copy-done
  86.7 1.7 middle.1
  88.4 1.0 copy-done.1
  89.4 7.9 %all-to-all-start.2 = ((bf16[32,128,128]{2,1,0:T(8,128)(2,1)}), bf16[32,128,128]{2,1,0:T(8,128)(2,1)S(1)}, u32[]{:S(2)}, u32[]{:S(2)}) async-start(bf16[32,128,128]{2,1,0:T(8,128)(2,1)} %copy-done.1), calls=%async_computation.2 | async-start | bytes 2097152 | tf_op jit(solution)/shard_map/all_to_all | solution.py:186
  97.4 3.4 %collective-permute-start.4 = (bf16[256,512]{1,0:T(8,128)(2,1)S(1)}, bf16[256,512]{1,0:T(8,128)(2,1)S(1)}, u32[]{:S(2)}, u32[]{:S(2)}) collective-permute-start(bf16[256,512]{1,0:T(8,128)(2,1)S(1)} %get-tuple-element.20), channel_id=1, source_target_pairs={{0,1},{1,0},{2,3},{3,2},{4,5},{5,4},{6,7},{7,6},{8,9},{9,8},{10,11... | collective-permute-start | bytes 786440 | tf_op jit(solution)/shard_map/ppermute | solution.py:125
  100.8 1.1 collective-permute-done.4
  101.9 0.1 add_convert_fusion.1
  102.0 2.2 %collective-permute-start.5 = (bf16[128,512]{1,0:T(8,128)(2,1)S(1)}, bf16[128,512]{1,0:T(8,128)(2,1)S(1)}, u32[]{:S(2)}, u32[]{:S(2)}) collective-permute-start(bf16[128,512]{1,0:T(8,128)(2,1)S(1)} %dynamic-slice_bitcast_fusion), channel_id=1, source_target_pairs={{0,64},{64,0},{128,192},{192,128},{256,320},{320,256},{384,448},{4... | collective-permute-start | bytes 393224 | tf_op jit(solution)/shard_map/ppermute | solution.py:125
  104.3 4.4 %collective-permute-done.5 = bf16[128,512]{1,0:T(8,128)(2,1)S(1)} collective-permute-done((bf16[128,512]{1,0:T(8,128)(2,1)S(1)}, bf16[128,512]{1,0:T(8,128)(2,1)S(1)}, u32[]{:S(2)}, u32[]{:S(2)}) %collective-permute-start.5) | collective-permute-done | bytes 131104 | tf_op jit(solution)/shard_map/ppermute | solution.py:125
  108.7 3.0 %collective-permute-start.6 = (bf16[64,512]{1,0:T(8,128)(2,1)S(1)}, bf16[64,512]{1,0:T(8,128)(2,1)S(1)}, u32[]{:S(2)}, u32[]{:S(2)}) collective-permute-start(bf16[64,512]{1,0:T(8,128)(2,1)S(1)} %dynamic-slice_bitcast_fusion.1), channel_id=1, source_target_pairs={{0,128},{64,192},{128,0},{192,64},{256,384},{320,448},{384,256},{4... | collective-permute-start | bytes 196616 | tf_op jit(solution)/shard_map/ppermute | solution.py:125
  111.7 3.9 %collective-permute-done.6 = bf16[64,512]{1,0:T(8,128)(2,1)S(1)} collective-permute-done((bf16[64,512]{1,0:T(8,128)(2,1)S(1)}, bf16[64,512]{1,0:T(8,128)(2,1)S(1)}, u32[]{:S(2)}, u32[]{:S(2)}) %collective-permute-start.6) | collective-permute-done | bytes 65568 | tf_op jit(solution)/shard_map/ppermute | solution.py:125
  115.6 4.3 %collective-permute-start.7 = (bf16[32,512]{1,0:T(8,128)(2,1)S(1)}, bf16[32,512]{1,0:T(8,128)(2,1)S(1)}, u32[]{:S(2)}, u32[]{:S(2)}) collective-permute-start(bf16[32,512]{1,0:T(8,128)(2,1)S(1)} %dynamic-slice_bitcast_fusion.2), channel_id=1, source_target_pairs={{0,256},{64,320},{128,384},{192,448},{256,0},{320,64},{384,128},{4... | collective-permute-start | bytes 98312 | tf_op jit(solution)/shard_map/ppermute | solution.py:125
  119.9 4.3 %collective-permute-done.7 = bf16[32,512]{1,0:T(8,128)(2,1)S(1)} collective-permute-done((bf16[32,512]{1,0:T(8,128)(2,1)S(1)}, bf16[32,512]{1,0:T(8,128)(2,1)S(1)}, u32[]{:S(2)}, u32[]{:S(2)}) %collective-permute-start.7) | collective-permute-done | bytes 32800 | tf_op jit(solution)/shard_map/ppermute | solution.py:125
  124.2 0.0 all-to-all-done.2.mine_ref
  124.2 5.1 %collective-permute-start.8 = (bf16[32,128,128]{2,1,0:T(8,128)(2,1)S(1)}, bf16[32,128,128]{2,1,0:T(8,128)(2,1)S(1)}, u32[]{:S(2)}, u32[]{:S(2)}) collective-permute-start(bf16[32,128,128]{2,1,0:T(8,128)(2,1)S(1)} %all-to-all-done.2.mine_ref), channel_id=1, source_target_pairs={{0,1},{1,0},{2,3},{3,2},{4,5},{5,4},{6,7},{7,6},{8,9},{9,8},{10,11... | collective-permute-start | bytes 3145736 | tf_op jit(solution)/shard_map/ppermute | solution.py:125
  129.4 2.2 %collective-permute-done.8.other_ref = bf16[32,128,128]{2,1,0:T(8,128)(2,1)S(1)} collective-permute-done((bf16[32,128,128]{2,1,0:T(8,128)(2,1)S(1)}, bf16[32,128,128]{2,1,0:T(8,128)(2,1)S(1)}, u32[]{:S(2)}, u32[]{:S(2)}) %collective-permute-start.8) | collective-permute-done | bytes 1048608 | tf_op jit(solution)/shard_map/ppermute | solution.py:125
  131.6 2.4 %backward_tiles.1 = bf16[32,128,128]{2,1,0:T(8,128)(2,1)} custom-call(s32[2]{0:T(128)S(1)} %pad_add_fusion.place_ref.core_ref, s32[4,24]{1,0:T(4,128)S(1)} %maximum_minimum_fusion.index_ref, bf16[32,128,128]{2,1,0:T(8,128)(2,1)S(1)} %all-to-all-done.2.mine_ref, bf16[32,128,128]{2,1,0:T(8,128)(2,1)S(1)} %collective-permute-done.8.other_ref, ...), custom_call_target="tpu_custom_call" | custom-call | tf_op jit(solution)/shard_map/backward_tiles/pallas_call | solution.py:194
  134.0 6.8 %all-to-all-start.3 = ((bf16[32,128,128]{2,1,0:T(8,128)(2,1)}), bf16[32,128,128]{2,1,0:T(8,128)(2,1)S(1)}, u32[]{:S(2)}, u32[]{:S(2)}) async-start(bf16[32,128,128]{2,1,0:T(8,128)(2,1)} %backward_tiles.1), calls=%async_computation.3 | async-start | bytes 2097152 | tf_op jit(solution)/shard_map/all_to_all | solution.py:204
  140.8 3.1 %collective-permute-start.9 = (f32[32,512]{1,0:T(8,128)S(1)}, f32[32,512]{1,0:T(8,128)S(1)}, u32[]{:S(2)}, u32[]{:S(2)}) collective-permute-start(f32[32,512]{1,0:T(8,128)S(1)} %convert_element_type.98), channel_id=1, source_target_pairs={{0,2},{2,0},{4,6},{6,4},{8,10},{10,8},{12,14},{14,12},{1,3},{3,1},... | collective-permute-start | bytes 196616 | tf_op jit(solution)/shard_map/ppermute | solution.py:125
  143.9 2.2 %collective-permute-done.9 = f32[32,512]{1,0:T(8,128)S(1)} collective-permute-done((f32[32,512]{1,0:T(8,128)S(1)}, f32[32,512]{1,0:T(8,128)S(1)}, u32[]{:S(2)}, u32[]{:S(2)}) %collective-permute-start.9) | collective-permute-done | bytes 65568 | tf_op jit(solution)/shard_map/ppermute | solution.py:125
  146.1 4.0 %collective-permute-start.10 = (f32[32,512]{1,0:T(8,128)S(1)}, f32[32,512]{1,0:T(8,128)S(1)}, u32[]{:S(2)}, u32[]{:S(2)}) collective-permute-start(f32[32,512]{1,0:T(8,128)S(1)} %add.67), channel_id=1, source_target_pairs={{0,4},{2,6},{4,0},{6,2},{8,12},{10,14},{12,8},{14,10},{1,5},{3,7},... | collective-permute-start | bytes 196616 | tf_op jit(solution)/shard_map/ppermute | solution.py:125
  150.1 2.2 %collective-permute-done.10 = f32[32,512]{1,0:T(8,128)S(1)} collective-permute-done((f32[32,512]{1,0:T(8,128)S(1)}, f32[32,512]{1,0:T(8,128)S(1)}, u32[]{:S(2)}, u32[]{:S(2)}) %collective-permute-start.10) | collective-permute-done | bytes 65568 | tf_op jit(solution)/shard_map/ppermute | solution.py:125
  152.3 7.7 %collective-permute-start.11 = (f32[32,512]{1,0:T(8,128)S(1)}, f32[32,512]{1,0:T(8,128)S(1)}, u32[]{:S(2)}, u32[]{:S(2)}) collective-permute-start(f32[32,512]{1,0:T(8,128)S(1)} %add.68), channel_id=1, source_target_pairs={{0,8},{2,10},{4,12},{6,14},{8,0},{10,2},{12,4},{14,6},{1,9},{3,11}... | collective-permute-start | bytes 196616 | tf_op jit(solution)/shard_map/ppermute | solution.py:125
  160.0 1.9 collective-permute-done.11
  162.0 2.9 %collective-permute-start.12 = (f32[32,512]{1,0:T(8,128)S(1)}, f32[32,512]{1,0:T(8,128)S(1)}, u32[]{:S(2)}, u32[]{:S(2)}) collective-permute-start(f32[32,512]{1,0:T(8,128)S(1)} %add.69), channel_id=1, source_target_pairs={{0,16},{16,0},{32,48},{48,32},{1,17},{17,1},{33,49},{49,33},{2,18}... | collective-permute-start | bytes 196616 | tf_op jit(solution)/shard_map/ppermute | solution.py:125
  164.9 2.5 %collective-permute-done.12 = f32[32,512]{1,0:T(8,128)S(1)} collective-permute-done((f32[32,512]{1,0:T(8,128)S(1)}, f32[32,512]{1,0:T(8,128)S(1)}, u32[]{:S(2)}, u32[]{:S(2)}) %collective-permute-start.12) | collective-permute-done | bytes 65568 | tf_op jit(solution)/shard_map/ppermute | solution.py:125
  167.4 4.0 %collective-permute-start.13 = (f32[32,512]{1,0:T(8,128)S(1)}, f32[32,512]{1,0:T(8,128)S(1)}, u32[]{:S(2)}, u32[]{:S(2)}) collective-permute-start(f32[32,512]{1,0:T(8,128)S(1)} %add.70), channel_id=1, source_target_pairs={{0,32},{16,48},{32,0},{48,16},{1,33},{17,49},{33,1},{49,17},{2,34}... | collective-permute-start | bytes 196616 | tf_op jit(solution)/shard_map/ppermute | solution.py:125
  171.4 2.7 %collective-permute-done.13 = f32[32,512]{1,0:T(8,128)S(1)} collective-permute-done((f32[32,512]{1,0:T(8,128)S(1)}, f32[32,512]{1,0:T(8,128)S(1)}, u32[]{:S(2)}, u32[]{:S(2)}) %collective-permute-start.13) | collective-permute-done | bytes 65568 | tf_op jit(solution)/shard_map/ppermute | solution.py:125
  174.1 0.0 all-to-all-done.3.parts_ref
  174.1 0.8 broadcast_in_dim.5
  175.0 12.2 %all-to-all-start.4 = ((bf16[16,32,512]{2,1,0:T(8,128)(2,1)}), bf16[16,32,512]{2,1,0:T(8,128)(2,1)S(1)}, u32[]{:S(2)}, u32[]{:S(2)}) async-start(bf16[16,32,512]{2,1,0:T(8,128)(2,1)} %broadcast_in_dim.5), calls=%async_computation.4 | async-start | bytes 1048576 | tf_op jit(solution)/shard_map/all_to_all | solution.py:220
  187.2 1.0 last.1
  188.2 16.4 %all-to-all-done.4 = bf16[16,32,512]{2,1,0:T(8,128)(2,1)S(1)} async-done(((bf16[16,32,512]{2,1,0:T(8,128)(2,1)}), bf16[16,32,512]{2,1,0:T(8,128)(2,1)S(1)}, u32[]{:S(2)}, u32[]{:S(2)}) %all-to-all-start.4) | async-done | bytes 524320 | tf_op jit(solution)/shard_map/all_to_all | solution.py:220
  204.5 0.1 convert_multiply_fusion
  204.7 1.1 copy.11
  (24 shorter events, 0.2 us)
Async XLA Ops:
  0.6 0.9 copy-start.2
  2.6 10.7 %copy-start.8 = (s32[1,1,8]{2,1,0:T(1,128)S(1)}, s32[1,1,8]{2,1,0:T(1,128)}, u32[]{:S(2)}) copy-start(s32[1,1,8]{2,1,0:T(1,128)} %param.12) | copy-start | bytes 100
  2.6 10.7 %copy-start.6 = (s32[1,1,8]{2,1,0:T(1,128)S(1)}, s32[1,1,8]{2,1,0:T(1,128)}, u32[]{:S(2)}) copy-start(s32[1,1,8]{2,1,0:T(1,128)} %param.14) | copy-start | bytes 100
  2.6 10.7 %copy-start.7 = (s32[1,1,8]{2,1,0:T(1,128)S(1)}, s32[1,1,8]{2,1,0:T(1,128)}, u32[]{:S(2)}) copy-start(s32[1,1,8]{2,1,0:T(1,128)} %param.13) | copy-start | bytes 100
  2.6 10.8 %copy-start.4 = (bf16[1,1,8,128,128]{4,3,2,1,0:T(8,128)(2,1)S(1)}, bf16[1,1,8,128,128]{4,3,2,1,0:T(8,128)(2,1)}, u32[]{:S(2)}) copy-start(bf16[1,1,8,128,128]{4,3,2,1,0:T(8,128)(2,1)} %param.11) | copy-start | bytes 786436
  2.7 19.8 %copy-start.5 = (s32[3]{0:T(128)S(1)}, s32[3]{0:T(128)}, u32[]{:S(2)}) copy-start(s32[3]{0:T(128)} %constant.52.clone) | copy-start | bytes 40
  2.7 38.5 %all-to-all-start = ((bf16[32,128,128]{2,1,0:T(8,128)(2,1)}), bf16[32,128,128]{2,1,0:T(8,128)(2,1)S(1)}, u32[]{:S(2)}, u32[]{:S(2)}) async-start(bf16[32,128,128]{2,1,0:T(8,128)(2,1)} %spread.1), calls=%async_computation | async-start | bytes 2097152 | tf_op jit(solution)/shard_map/all_to_all | solution.py:147
  13.5 23.9 %collective-permute-start.2 = (bf16[1040,128]{1,0:T(8,128)(2,1)S(1)}, bf16[1040,128]{1,0:T(8,128)(2,1)S(1)}, u32[]{:S(2)}, u32[]{:S(2)}) collective-permute-start(bf16[1040,128]{1,0:T(8,128)(2,1)S(1)} %pad_maximum_fusion.refs_0_), channel_id=1, source_target_pairs={{0,48},{16,32},{32,16},{48,0},{1,49},{17,33},{33,17},{49,1},{2,50}... | collective-permute-start | bytes 798728 | tf_op jit(solution)/shard_map/ppermute | solution.py:125
  17.8 19.5 %collective-permute-start.1 = (bf16[1040,128]{1,0:T(8,128)(2,1)S(1)}, bf16[1040,128]{1,0:T(8,128)(2,1)S(1)}, u32[]{:S(2)}, u32[]{:S(2)}) collective-permute-start(bf16[1040,128]{1,0:T(8,128)(2,1)S(1)} %pad_maximum_fusion.refs_0_), channel_id=1, source_target_pairs={{0,32},{16,48},{32,0},{48,16},{1,33},{17,49},{33,1},{49,17},{2,34}... | collective-permute-start | bytes 798728 | tf_op jit(solution)/shard_map/ppermute | solution.py:125
  20.3 20.7 %collective-permute-start = (bf16[1040,128]{1,0:T(8,128)(2,1)S(1)}, bf16[1040,128]{1,0:T(8,128)(2,1)S(1)}, u32[]{:S(2)}, u32[]{:S(2)}) collective-permute-start(bf16[1040,128]{1,0:T(8,128)(2,1)S(1)} %pad_maximum_fusion.refs_0_), channel_id=1, source_target_pairs={{0,16},{16,0},{32,48},{48,32},{1,17},{17,1},{33,49},{49,33},{2,18}... | collective-permute-start | bytes 798728 | tf_op jit(solution)/shard_map/ppermute | solution.py:125
  42.7 5.4 %collective-permute-start.3 = (bf16[32,128,128]{2,1,0:T(8,128)(2,1)S(1)}, bf16[32,128,128]{2,1,0:T(8,128)(2,1)S(1)}, u32[]{:S(2)}, u32[]{:S(2)}) collective-permute-start(bf16[32,128,128]{2,1,0:T(8,128)(2,1)S(1)} %get-tuple-element.16), channel_id=1, source_target_pairs={{0,1},{1,0},{2,3},{3,2},{4,5},{5,4},{6,7},{7,6},{8,9},{9,8},{10,11... | collective-permute-start | bytes 3145736 | tf_op jit(solution)/shard_map/ppermute | solution.py:125
  48.4 38.3 %copy-start = (bf16[512,512]{1,0:T(8,128)(2,1)S(1)}, bf16[512,512]{1,0:T(8,128)(2,1)}, u32[]{:S(2)}) copy-start(bf16[512,512]{1,0:T(8,128)(2,1)} %weight_ref.3) | copy-start | bytes 1572868
  48.4 38.3 %copy-start.3 = (bf16[128,512]{1,0:T(8,128)(2,1)S(1)}, bf16[128,512]{1,0:T(8,128)(2,1)}, u32[]{:S(2)}) copy-start(bf16[128,512]{1,0:T(8,128)(2,1)} %cotangent_ref.1) | copy-start | bytes 393220
  88.4 1.0 copy-start.1
  89.4 34.8 %all-to-all-start.2 = ((bf16[32,128,128]{2,1,0:T(8,128)(2,1)}), bf16[32,128,128]{2,1,0:T(8,128)(2,1)S(1)}, u32[]{:S(2)}, u32[]{:S(2)}) async-start(bf16[32,128,128]{2,1,0:T(8,128)(2,1)} %copy-done.1), calls=%async_computation.2 | async-start | bytes 2097152 | tf_op jit(solution)/shard_map/all_to_all | solution.py:186
  97.4 4.6 %collective-permute-start.4 = (bf16[256,512]{1,0:T(8,128)(2,1)S(1)}, bf16[256,512]{1,0:T(8,128)(2,1)S(1)}, u32[]{:S(2)}, u32[]{:S(2)}) collective-permute-start(bf16[256,512]{1,0:T(8,128)(2,1)S(1)} %get-tuple-element.20), channel_id=1, source_target_pairs={{0,1},{1,0},{2,3},{3,2},{4,5},{5,4},{6,7},{7,6},{8,9},{9,8},{10,11... | collective-permute-start | bytes 786440 | tf_op jit(solution)/shard_map/ppermute | solution.py:125
  102.0 6.6 %collective-permute-start.5 = (bf16[128,512]{1,0:T(8,128)(2,1)S(1)}, bf16[128,512]{1,0:T(8,128)(2,1)S(1)}, u32[]{:S(2)}, u32[]{:S(2)}) collective-permute-start(bf16[128,512]{1,0:T(8,128)(2,1)S(1)} %dynamic-slice_bitcast_fusion), channel_id=1, source_target_pairs={{0,64},{64,0},{128,192},{192,128},{256,320},{320,256},{384,448},{4... | collective-permute-start | bytes 393224 | tf_op jit(solution)/shard_map/ppermute | solution.py:125
  108.7 6.9 %collective-permute-start.6 = (bf16[64,512]{1,0:T(8,128)(2,1)S(1)}, bf16[64,512]{1,0:T(8,128)(2,1)S(1)}, u32[]{:S(2)}, u32[]{:S(2)}) collective-permute-start(bf16[64,512]{1,0:T(8,128)(2,1)S(1)} %dynamic-slice_bitcast_fusion.1), channel_id=1, source_target_pairs={{0,128},{64,192},{128,0},{192,64},{256,384},{320,448},{384,256},{4... | collective-permute-start | bytes 196616 | tf_op jit(solution)/shard_map/ppermute | solution.py:125
  115.6 8.6 %collective-permute-start.7 = (bf16[32,512]{1,0:T(8,128)(2,1)S(1)}, bf16[32,512]{1,0:T(8,128)(2,1)S(1)}, u32[]{:S(2)}, u32[]{:S(2)}) collective-permute-start(bf16[32,512]{1,0:T(8,128)(2,1)S(1)} %dynamic-slice_bitcast_fusion.2), channel_id=1, source_target_pairs={{0,256},{64,320},{128,384},{192,448},{256,0},{320,64},{384,128},{4... | collective-permute-start | bytes 98312 | tf_op jit(solution)/shard_map/ppermute | solution.py:125
  124.2 7.4 %collective-permute-start.8 = (bf16[32,128,128]{2,1,0:T(8,128)(2,1)S(1)}, bf16[32,128,128]{2,1,0:T(8,128)(2,1)S(1)}, u32[]{:S(2)}, u32[]{:S(2)}) collective-permute-start(bf16[32,128,128]{2,1,0:T(8,128)(2,1)S(1)} %all-to-all-done.2.mine_ref), channel_id=1, source_target_pairs={{0,1},{1,0},{2,3},{3,2},{4,5},{5,4},{6,7},{7,6},{8,9},{9,8},{10,11... | collective-permute-start | bytes 3145736 | tf_op jit(solution)/shard_map/ppermute | solution.py:125
  134.0 40.1 %all-to-all-start.3 = ((bf16[32,128,128]{2,1,0:T(8,128)(2,1)}), bf16[32,128,128]{2,1,0:T(8,128)(2,1)S(1)}, u32[]{:S(2)}, u32[]{:S(2)}) async-start(bf16[32,128,128]{2,1,0:T(8,128)(2,1)} %backward_tiles.1), calls=%async_computation.3 | async-start | bytes 2097152 | tf_op jit(solution)/shard_map/all_to_all | solution.py:204
  140.8 5.3 %collective-permute-start.9 = (f32[32,512]{1,0:T(8,128)S(1)}, f32[32,512]{1,0:T(8,128)S(1)}, u32[]{:S(2)}, u32[]{:S(2)}) collective-permute-start(f32[32,512]{1,0:T(8,128)S(1)} %convert_element_type.98), channel_id=1, source_target_pairs={{0,2},{2,0},{4,6},{6,4},{8,10},{10,8},{12,14},{14,12},{1,3},{3,1},... | collective-permute-start | bytes 196616 | tf_op jit(solution)/shard_map/ppermute | solution.py:125
  146.1 6.2 %collective-permute-start.10 = (f32[32,512]{1,0:T(8,128)S(1)}, f32[32,512]{1,0:T(8,128)S(1)}, u32[]{:S(2)}, u32[]{:S(2)}) collective-permute-start(f32[32,512]{1,0:T(8,128)S(1)} %add.67), channel_id=1, source_target_pairs={{0,4},{2,6},{4,0},{6,2},{8,12},{10,14},{12,8},{14,10},{1,5},{3,7},... | collective-permute-start | bytes 196616 | tf_op jit(solution)/shard_map/ppermute | solution.py:125
  152.3 9.7 %collective-permute-start.11 = (f32[32,512]{1,0:T(8,128)S(1)}, f32[32,512]{1,0:T(8,128)S(1)}, u32[]{:S(2)}, u32[]{:S(2)}) collective-permute-start(f32[32,512]{1,0:T(8,128)S(1)} %add.68), channel_id=1, source_target_pairs={{0,8},{2,10},{4,12},{6,14},{8,0},{10,2},{12,4},{14,6},{1,9},{3,11}... | collective-permute-start | bytes 196616 | tf_op jit(solution)/shard_map/ppermute | solution.py:125
  162.0 5.4 %collective-permute-start.12 = (f32[32,512]{1,0:T(8,128)S(1)}, f32[32,512]{1,0:T(8,128)S(1)}, u32[]{:S(2)}, u32[]{:S(2)}) collective-permute-start(f32[32,512]{1,0:T(8,128)S(1)} %add.69), channel_id=1, source_target_pairs={{0,16},{16,0},{32,48},{48,32},{1,17},{17,1},{33,49},{49,33},{2,18}... | collective-permute-start | bytes 196616 | tf_op jit(solution)/shard_map/ppermute | solution.py:125
  167.4 6.7 %collective-permute-start.13 = (f32[32,512]{1,0:T(8,128)S(1)}, f32[32,512]{1,0:T(8,128)S(1)}, u32[]{:S(2)}, u32[]{:S(2)}) collective-permute-start(f32[32,512]{1,0:T(8,128)S(1)} %add.70), channel_id=1, source_target_pairs={{0,32},{16,48},{32,0},{48,16},{1,33},{17,49},{33,1},{49,17},{2,34}... | collective-permute-start | bytes 196616 | tf_op jit(solution)/shard_map/ppermute | solution.py:125
  175.0 29.5 %all-to-all-start.4 = ((bf16[16,32,512]{2,1,0:T(8,128)(2,1)}), bf16[16,32,512]{2,1,0:T(8,128)(2,1)S(1)}, u32[]{:S(2)}, u32[]{:S(2)}) async-start(bf16[16,32,512]{2,1,0:T(8,128)(2,1)} %broadcast_in_dim.5), calls=%async_computation.4 | async-start | bytes 1048576 | tf_op jit(solution)/shard_map/all_to_all | solution.py:220

commit v3 on v2

--- a/solution.py
+++ b/solution.py
@@ -14,7 +14,6 @@
 CHUNK = WIDTH // X
 ROW_TILES = Z * CORES
 COL_TILES = Y * X
-INDEX_ROWS = 16
 BF16 = jnp.bfloat16
 F32 = jnp.float32
 
@@ -120,6 +119,17 @@
     ).astype(BF16)
 
 
+def place_rows(place_ref, mine_ref, other_ref, out_ref):
+    core = place_ref[0]
+    half, share = WIDTH // CORES, WIDTH // (Y * CORES)
+    scale = 1.0 / math.sqrt(TILE * Y * X * Z * CORES)
+    for y in range(Y):
+        at = (y & 1) * 4 * share + (y >> 1 & 1) * 2 * share + (y >> 2) * share
+        for side, ref in ((core, mine_ref), (1 - core, other_ref)):
+            start = pl.multiple_of(side * half + at, share)
+            out_ref[pl.ds(start, share), :] = ref[y].astype(F32) * scale
+
+
 def exchange(array, axis, distance):
     size = lax.axis_size(axis)
     return lax.ppermute(array, axis, [(i, i ^ distance) for i in range(size)])
@@ -146,15 +156,10 @@
     )(features)
     panel = lax.all_to_all(chunks, ("y", "x"), 0, 0, tiled=True)
 
-    index = jnp.concatenate(
-        [tile_rows.reshape(-1), tile_cols.reshape(-1), tile_valid.reshape(-1)]
-    ).astype(BF16)
-    index = jnp.pad(index[None, :], ((0, INDEX_ROWS - 1), (0, TILE - 3 * SLOTS)))
-    tiles = jnp.concatenate([tile_values.reshape(SLOTS * TILE, TILE), index], axis=0)
+    tiles = tile_values.reshape(SLOTS * TILE, TILE)
     tiles = [tiles] + [exchange(tiles, "x", distance) for distance in range(1, X)]
-    index = jnp.stack([t[SLOTS * TILE, : 3 * SLOTS] for t in tiles]).astype(jnp.int32)
-    limit = jnp.repeat(jnp.array([ROW_TILES - 1, COL_TILES - 1, 1], jnp.int32), SLOTS)
-    index = jnp.clip(index, 0, limit[None, :])
+    index = jnp.concatenate([tile_rows, tile_cols, tile_valid], axis=2).reshape(1, 3 * SLOTS)
+    index = jnp.concatenate([index] + [exchange(index, "x", distance) for distance in range(1, X)])
 
     mine, other = pl.pallas_call(
         forward_tiles,
@@ -191,6 +196,8 @@
     grad_mine, piece = lax.optimization_barrier((grad_mine, piece))
 
     grad_other = exchange(grad_mine, "core", 1)
+    piece = piece.astype(F32)
+    piece = piece + exchange(piece, "z", 1)
     back = pl.pallas_call(
         backward_tiles,
         in_specs=[smem(), smem()] + [vmem()] * (2 + X),
@@ -200,9 +207,9 @@
         compiler_params=params(),
         name="backward_tiles",
     )(place, index, grad_mine, grad_other, *tiles)
-    back, piece = lax.optimization_barrier((back, piece.astype(F32)))
+    back, piece = lax.optimization_barrier((back, piece))
     back = lax.all_to_all(back, ("y", "x"), 0, 0, tiled=True)
-    for axis, distance in (("z", 1), ("z", 2), ("z", 4), ("x", 1), ("x", 2)):
+    for axis, distance in (("z", 2), ("z", 4), ("x", 1), ("x", 2)):
         piece = piece + exchange(piece, axis, distance)
     back, piece = lax.optimization_barrier((back, piece))
 
@@ -216,11 +223,16 @@
     )(back, weight)
 
     share = WIDTH // (Y * CORES)
-    piece = jnp.broadcast_to(piece.astype(BF16)[None], (Y * CORES, share, WIDTH))
-    whole = lax.all_to_all(piece, ("y", "core"), 0, 0, tiled=True)
-    whole = whole.reshape(2, 2, 2, CORES, share, WIDTH).transpose(3, 2, 1, 0, 4, 5)
-    nodes = TILE * Y * X * Z * CORES
-    weight_grad = whole.reshape(WIDTH, WIDTH).astype(F32) * (1.0 / math.sqrt(nodes))
+    piece = jnp.broadcast_to(piece.astype(BF16)[None], (Y, share, WIDTH))
+    whole = lax.all_to_all(piece, "y", 0, 0, tiled=True)
+    weight_grad = pl.pallas_call(
+        place_rows,
+        in_specs=[smem()] + [vmem()] * 2,
+        out_specs=vmem(),
+        out_shape=jax.ShapeDtypeStruct((WIDTH, WIDTH), F32),
+        compiler_params=params(),
+        name="place_rows",
+    )(place, whole, exchange(whole, "core", 1))
     return (activations, input_grad, weight_grad)
 
 

time: 207 us -> 207 us (level)
  waiting for transfers between devices: 64.4 us -> 41.1 us
  blocking collectives: 38.3 us -> 50.9 us
  starting transfers between devices: 89.4 us -> 102 us
  local copies, waits for them, and re-layouts: 4.02 us -> 0.99 us
    ppermute x14 -> x18, starting transfers between devices: 51.8 us -> 74 us  [exchange(): return lax.ppermute(array, axis, [(i, i ^ distance) for i in range(size)])]
    all_to_all x1 -> x0, waiting for transfers between devices: 16.4 us -> none  [body(): whole = lax.all_to_all(piece, ('y', 'core'), 0, 0, tiled=True)]
    all_to_all x0 -> x1, blocking collectives: none -> 15.3 us  [body(): whole = lax.all_to_all(piece, 'y', 0, 0, tiled=True)]
    all_to_all x1 -> x0, starting transfers between devices: 12.2 us -> none  [body(): whole = lax.all_to_all(piece, ('y', 'core'), 0, 0, tiled=True)]
    ppermute x14 -> x18, waiting for transfers between devices: 48.1 us -> 41.1 us  [exchange(): return lax.ppermute(array, axis, [(i, i ^ distance) for i in range(size)])]
    all_to_all x1, blocking collectives: 38.3 us -> 35.6 us  [body(): parts = lax.all_to_all(term, ('x', 'z'), 0, 0, tiled=True)]
    all_to_all x1, starting transfers between devices: 6.78 us -> 9.12 us  [body(): back = lax.all_to_all(back, ('y', 'x'), 0, 0, tiled=True)]
  transfers between devices with their start and end apart: 18 -> 21, of which waited for: 14 -> 13; matrix products, arithmetic and copies ran while one was open for 0% -> 0% of each run, Pallas kernels for 0% -> 0%
where the time goes in v3:
time: 207 us; the launch traced here: 206 us
  starting transfers between devices  102 us (49%)
  blocking collectives  50.9 us (25%)
  waiting for transfers between devices  41.1 us (20%)
  Pallas kernels  9.58 us (5%)
    ppermute x18, starting transfers between devices, exchange(): return lax.ppermute(array, axis, [(i, i ^ distance) for i in range(size)])  74 us
    ppermute x18, waiting for transfers between devices, exchange(): return lax.ppermute(array, axis, [(i, i ^ distance) for i in range(size)])  41.1 us
    all_to_all x1, blocking collectives, body(): parts = lax.all_to_all(term, ('x', 'z'), 0, 0, tiled=True)  35.6 us
    all_to_all x1, blocking collectives, body(): whole = lax.all_to_all(piece, 'y', 0, 0, tiled=True)  15.3 us
    all_to_all x1, starting transfers between devices, body(): panel = lax.all_to_all(chunks, ('y', 'x'), 0, 0, tiled=True)  10.6 us
    all_to_all x1, starting transfers between devices, body(): back = lax.all_to_all(back, ('y', 'x'), 0, 0, tiled=True)  9.12 us
    all_to_all x1, starting transfers between devices, body(): grad_mine = lax.all_to_all(grad, ('x', 'z'), 0, 0, tiled=True)  7.94 us
  transfers between devices with their start and end apart: 21, of which 13 were waited for; matrix products, arithmetic and copies ran while one was open for 0% of the time, Pallas kernels for 0%

profile of v3, /device:TPU:1, one launch (start us, length us, event | category | flops | bytes accessed | tf_op | source)
XLA Modules:
  0.0 206.0 jit_solution(92770843077932564)
XLA Ops:
  0.6 0.0 copy-start.2
  0.6 0.9 copy-done.2
  1.5 1.1 spread.1
  2.7 10.6 %all-to-all-start = ((bf16[32,128,128]{2,1,0:T(8,128)(2,1)}), bf16[32,128,128]{2,1,0:T(8,128)(2,1)S(1)}, u32[]{:S(2)}, u32[]{:S(2)}) async-start(bf16[32,128,128]{2,1,0:T(8,128)(2,1)} %spread.1), calls=%async_computation | async-start | bytes 2097152 | tf_op jit(solution)/shard_map/all_to_all | solution.py:157
  13.3 0.0 copy-done.1
  13.3 3.1 %collective-permute-start.3 = (bf16[1024,128]{1,0:T(8,128)(2,1)S(1)}, bf16[1024,128]{1,0:T(8,128)(2,1)S(1)}, u32[]{:S(2)}, u32[]{:S(2)}) collective-permute-start(bf16[1024,128]{1,0:T(8,128)(2,1)S(1)} %bitcast.23), channel_id=1, source_target_pairs={{0,16},{16,0},{32,48},{48,32},{1,17},{17,1},{33,49},{49,33},{2,18}... | collective-permute-start | bytes 786440 | tf_op jit(solution)/shard_map/ppermute | solution.py:135
  16.5 4.3 %collective-permute-start.4 = (bf16[1024,128]{1,0:T(8,128)(2,1)S(1)}, bf16[1024,128]{1,0:T(8,128)(2,1)S(1)}, u32[]{:S(2)}, u32[]{:S(2)}) collective-permute-start(bf16[1024,128]{1,0:T(8,128)(2,1)S(1)} %bitcast.24), channel_id=1, source_target_pairs={{0,32},{16,48},{32,0},{48,16},{1,33},{17,49},{33,1},{49,17},{2,34}... | collective-permute-start | bytes 786440 | tf_op jit(solution)/shard_map/ppermute | solution.py:135
  20.8 2.1 %collective-permute-start.5 = (bf16[1024,128]{1,0:T(8,128)(2,1)S(1)}, bf16[1024,128]{1,0:T(8,128)(2,1)S(1)}, u32[]{:S(2)}, u32[]{:S(2)}) collective-permute-start(bf16[1024,128]{1,0:T(8,128)(2,1)S(1)} %bitcast.25), channel_id=1, source_target_pairs={{0,48},{16,32},{32,16},{48,0},{1,49},{17,33},{33,17},{49,1},{2,50}... | collective-permute-start | bytes 786440 | tf_op jit(solution)/shard_map/ppermute | solution.py:135
  22.9 0.0 copy-done.4
  22.9 0.0 copy-done.5
  22.9 0.0 copy-done.6
  23.0 0.1 add_bitcast_fusion
  23.0 4.3 %collective-permute-start.2 = (s32[1,24]{1,0:T(1,128)S(1)}, s32[1,24]{1,0:T(1,128)S(1)}, u32[]{:S(2)}, u32[]{:S(2)}) collective-permute-start(s32[1,24]{1,0:T(1,128)S(1)} %add_bitcast_fusion), channel_id=1, source_target_pairs={{0,48},{16,32},{32,16},{48,0},{1,49},{17,33},{33,17},{49,1},{2,50}... | collective-permute-start | bytes 296 | tf_op jit(solution)/shard_map/ppermute | solution.py:135
  27.4 1.9 collective-permute-start.1
  29.3 0.1 pad_add_fusion.1.place_ref.core_ref
  29.4 14.1 %collective-permute-done.2 = s32[1,24]{1,0:T(1,128)S(1)} collective-permute-done((s32[1,24]{1,0:T(1,128)S(1)}, s32[1,24]{1,0:T(1,128)S(1)}, u32[]{:S(2)}, u32[]{:S(2)}) %collective-permute-start.2) | collective-permute-done | bytes 128 | tf_op jit(solution)/shard_map/ppermute | solution.py:135
  43.5 1.9 collective-permute-start
  45.4 0.0 collective-permute-done.1
  45.4 2.3 %collective-permute-done = s32[1,24]{1,0:T(1,128)S(1)} collective-permute-done((s32[1,24]{1,0:T(1,128)S(1)}, s32[1,24]{1,0:T(1,128)S(1)}, u32[]{:S(2)}, u32[]{:S(2)}) %collective-permute-start) | collective-permute-done | bytes 128 | tf_op jit(solution)/shard_map/ppermute | solution.py:135
  47.7 0.0 collective-permute-done.3.refs_1_
  47.8 0.0 collective-permute-done.4.refs_2_
  47.8 0.0 collective-permute-done.5.refs_3_
  47.8 0.0 all-to-all-done.panel_ref
  47.8 1.5 forward_tiles.1
  49.3 4.6 %collective-permute-start.6 = (bf16[32,128,128]{2,1,0:T(8,128)(2,1)S(1)}, bf16[32,128,128]{2,1,0:T(8,128)(2,1)S(1)}, u32[]{:S(2)}, u32[]{:S(2)}) collective-permute-start(bf16[32,128,128]{2,1,0:T(8,128)(2,1)S(1)} %get-tuple-element.16), channel_id=1, source_target_pairs={{0,1},{1,0},{2,3},{3,2},{4,5},{5,4},{6,7},{7,6},{8,9},{9,8},{10,11... | collective-permute-start | bytes 3145736 | tf_op jit(solution)/shard_map/ppermute | solution.py:135
  53.9 2.3 %collective-permute-done.6 = bf16[32,128,128]{2,1,0:T(8,128)(2,1)S(1)} collective-permute-done((bf16[32,128,128]{2,1,0:T(8,128)(2,1)S(1)}, bf16[32,128,128]{2,1,0:T(8,128)(2,1)S(1)}, u32[]{:S(2)}, u32[]{:S(2)}) %collective-permute-start.6) | collective-permute-done | bytes 1048608 | tf_op jit(solution)/shard_map/ppermute | solution.py:135
  56.1 0.4 add_convert_fusion
  56.5 0.0 copy-start
  56.5 0.0 copy-start.3
  56.5 35.6 %all_to_all.25.parts_ref = bf16[32,128,128]{2,1,0:T(8,128)(2,1)S(1)} all-to-all(bf16[32,128,128]{2,1,0:T(8,128)(2,1)S(1)} %add_convert_fusion), channel_id=1, replica_groups=mesh['y'=8,'x'=4,'z'=8,'core'=2] {'x','z'}, dimensions={0} | all-to-all | bytes 2097152 | tf_op jit(solution)/shard_map/all_to_all | solution.py:174
  92.1 0.0 copy-done
  92.1 0.0 copy-done.3
  92.1 2.1 %middle.1 = (bf16[128,512]{1,0:T(8,128)(2,1)}, bf16[32,128,128]{2,1,0:T(8,128)(2,1)}, bf16[256,512]{1,0:T(8,128)(2,1)S(1)}, bf16[256,512]{1,0:T(8,128)(2,1)S(1)}) custom-call(s32[2]{0:T(128)S(1)} %pad_add_fusion.1.place_ref.core_ref, bf16[32,128,128]{2,1,0:T(8,128)(2,1)S(1)} %all_to_all.25.parts_ref, bf16[512,512]{1,0:T(8,128)(2,1)S(1)} %copy-done, ...), custom_call_target="tpu_custom_call" | custom-call | tf_op jit(solution)/shard_map/middle/pallas_call | solution.py:177
  94.2 7.9 %all-to-all-start.2 = ((bf16[32,128,128]{2,1,0:T(8,128)(2,1)}), bf16[32,128,128]{2,1,0:T(8,128)(2,1)S(1)}, u32[]{:S(2)}, u32[]{:S(2)}) async-start(bf16[32,128,128]{2,1,0:T(8,128)(2,1)} %get-tuple-element.18), calls=%async_computation.2 | async-start | bytes 2097152 | tf_op jit(solution)/shard_map/all_to_all | solution.py:191
  102.1 3.4 %collective-permute-start.7 = (bf16[256,512]{1,0:T(8,128)(2,1)S(1)}, bf16[256,512]{1,0:T(8,128)(2,1)S(1)}, u32[]{:S(2)}, u32[]{:S(2)}) collective-permute-start(bf16[256,512]{1,0:T(8,128)(2,1)S(1)} %get-tuple-element.20), channel_id=1, source_target_pairs={{0,1},{1,0},{2,3},{3,2},{4,5},{5,4},{6,7},{7,6},{8,9},{9,8},{10,11... | collective-permute-start | bytes 786440 | tf_op jit(solution)/shard_map/ppermute | solution.py:135
  105.5 1.1 collective-permute-done.7
  106.7 0.1 add_convert_fusion.1
  106.8 3.1 %collective-permute-start.8 = (bf16[128,512]{1,0:T(8,128)(2,1)S(1)}, bf16[128,512]{1,0:T(8,128)(2,1)S(1)}, u32[]{:S(2)}, u32[]{:S(2)}) collective-permute-start(bf16[128,512]{1,0:T(8,128)(2,1)S(1)} %dynamic-slice_bitcast_fusion), channel_id=1, source_target_pairs={{0,64},{64,0},{128,192},{192,128},{256,320},{320,256},{384,448},{4... | collective-permute-start | bytes 393224 | tf_op jit(solution)/shard_map/ppermute | solution.py:135
  109.9 3.5 %collective-permute-done.8 = bf16[128,512]{1,0:T(8,128)(2,1)S(1)} collective-permute-done((bf16[128,512]{1,0:T(8,128)(2,1)S(1)}, bf16[128,512]{1,0:T(8,128)(2,1)S(1)}, u32[]{:S(2)}, u32[]{:S(2)}) %collective-permute-start.8) | collective-permute-done | bytes 131104 | tf_op jit(solution)/shard_map/ppermute | solution.py:135
  113.4 3.8 %collective-permute-start.9 = (bf16[64,512]{1,0:T(8,128)(2,1)S(1)}, bf16[64,512]{1,0:T(8,128)(2,1)S(1)}, u32[]{:S(2)}, u32[]{:S(2)}) collective-permute-start(bf16[64,512]{1,0:T(8,128)(2,1)S(1)} %dynamic-slice_bitcast_fusion.1), channel_id=1, source_target_pairs={{0,128},{64,192},{128,0},{192,64},{256,384},{320,448},{384,256},{4... | collective-permute-start | bytes 196616 | tf_op jit(solution)/shard_map/ppermute | solution.py:135
  117.2 2.4 %collective-permute-done.9 = bf16[64,512]{1,0:T(8,128)(2,1)S(1)} collective-permute-done((bf16[64,512]{1,0:T(8,128)(2,1)S(1)}, bf16[64,512]{1,0:T(8,128)(2,1)S(1)}, u32[]{:S(2)}, u32[]{:S(2)}) %collective-permute-start.9) | collective-permute-done | bytes 65568 | tf_op jit(solution)/shard_map/ppermute | solution.py:135
  119.7 6.7 %collective-permute-start.10 = (bf16[32,512]{1,0:T(8,128)(2,1)S(1)}, bf16[32,512]{1,0:T(8,128)(2,1)S(1)}, u32[]{:S(2)}, u32[]{:S(2)}) collective-permute-start(bf16[32,512]{1,0:T(8,128)(2,1)S(1)} %dynamic-slice_bitcast_fusion.2), channel_id=1, source_target_pairs={{0,256},{64,320},{128,384},{192,448},{256,0},{320,64},{384,128},{4... | collective-permute-start | bytes 98312 | tf_op jit(solution)/shard_map/ppermute | solution.py:135
  126.4 2.1 %collective-permute-done.10 = bf16[32,512]{1,0:T(8,128)(2,1)S(1)} collective-permute-done((bf16[32,512]{1,0:T(8,128)(2,1)S(1)}, bf16[32,512]{1,0:T(8,128)(2,1)S(1)}, u32[]{:S(2)}, u32[]{:S(2)}) %collective-permute-start.10) | collective-permute-done | bytes 32800 | tf_op jit(solution)/shard_map/ppermute | solution.py:135
  128.6 0.0 all-to-all-done.2.mine_ref
  128.6 5.2 %collective-permute-start.11 = (bf16[32,128,128]{2,1,0:T(8,128)(2,1)S(1)}, bf16[32,128,128]{2,1,0:T(8,128)(2,1)S(1)}, u32[]{:S(2)}, u32[]{:S(2)}) collective-permute-start(bf16[32,128,128]{2,1,0:T(8,128)(2,1)S(1)} %all-to-all-done.2.mine_ref), channel_id=1, source_target_pairs={{0,1},{1,0},{2,3},{3,2},{4,5},{5,4},{6,7},{7,6},{8,9},{9,8},{10,11... | collective-permute-start | bytes 3145736 | tf_op jit(solution)/shard_map/ppermute | solution.py:135
  133.8 3.2 %collective-permute-start.12 = (f32[32,512]{1,0:T(8,128)S(1)}, f32[32,512]{1,0:T(8,128)S(1)}, u32[]{:S(2)}, u32[]{:S(2)}) collective-permute-start(f32[32,512]{1,0:T(8,128)S(1)} %convert_element_type.78), channel_id=1, source_target_pairs={{0,2},{2,0},{4,6},{6,4},{8,10},{10,8},{12,14},{14,12},{1,3},{3,1},... | collective-permute-start | bytes 196616 | tf_op jit(solution)/shard_map/ppermute | solution.py:135
  137.0 2.4 %collective-permute-done.12 = f32[32,512]{1,0:T(8,128)S(1)} collective-permute-done((f32[32,512]{1,0:T(8,128)S(1)}, f32[32,512]{1,0:T(8,128)S(1)}, u32[]{:S(2)}, u32[]{:S(2)}) %collective-permute-start.12) | collective-permute-done | bytes 65568 | tf_op jit(solution)/shard_map/ppermute | solution.py:135
  139.4 0.0 collective-permute-done.11.other_ref
  139.4 2.4 %backward_tiles.1 = bf16[32,128,128]{2,1,0:T(8,128)(2,1)} custom-call(s32[2]{0:T(128)S(1)} %pad_add_fusion.1.place_ref.core_ref, s32[4,24]{1,0:T(4,128)S(1)} %pad_add_fusion.index_ref, bf16[32,128,128]{2,1,0:T(8,128)(2,1)S(1)} %all-to-all-done.2.mine_ref, bf16[32,128,128]{2,1,0:T(8,128)(2,1)S(1)} %collective-permute-done.11.other_ref, ...), custom_call_target="tpu_custom_call" | custom-call | tf_op jit(solution)/shard_map/backward_tiles/pallas_call | solution.py:201
  141.8 9.1 %all-to-all-start.3 = ((bf16[32,128,128]{2,1,0:T(8,128)(2,1)}), bf16[32,128,128]{2,1,0:T(8,128)(2,1)S(1)}, u32[]{:S(2)}, u32[]{:S(2)}) async-start(bf16[32,128,128]{2,1,0:T(8,128)(2,1)} %backward_tiles.1), calls=%async_computation.3 | async-start | bytes 2097152 | tf_op jit(solution)/shard_map/all_to_all | solution.py:211
  150.9 4.0 %collective-permute-start.13 = (f32[32,512]{1,0:T(8,128)S(1)}, f32[32,512]{1,0:T(8,128)S(1)}, u32[]{:S(2)}, u32[]{:S(2)}) collective-permute-start(f32[32,512]{1,0:T(8,128)S(1)} %convert_add_fusion.3), channel_id=1, source_target_pairs={{0,4},{2,6},{4,0},{6,2},{8,12},{10,14},{12,8},{14,10},{1,5},{3,7},... | collective-permute-start | bytes 196616 | tf_op jit(solution)/shard_map/ppermute | solution.py:135
  154.9 2.2 %collective-permute-done.13 = f32[32,512]{1,0:T(8,128)S(1)} collective-permute-done((f32[32,512]{1,0:T(8,128)S(1)}, f32[32,512]{1,0:T(8,128)S(1)}, u32[]{:S(2)}, u32[]{:S(2)}) %collective-permute-start.13) | collective-permute-done | bytes 65568 | tf_op jit(solution)/shard_map/ppermute | solution.py:135
  157.1 7.4 %collective-permute-start.14 = (f32[32,512]{1,0:T(8,128)S(1)}, f32[32,512]{1,0:T(8,128)S(1)}, u32[]{:S(2)}, u32[]{:S(2)}) collective-permute-start(f32[32,512]{1,0:T(8,128)S(1)} %add.66), channel_id=1, source_target_pairs={{0,8},{2,10},{4,12},{6,14},{8,0},{10,2},{12,4},{14,6},{1,9},{3,11}... | collective-permute-start | bytes 196616 | tf_op jit(solution)/shard_map/ppermute | solution.py:135
  164.5 1.9 collective-permute-done.14
  166.5 2.9 %collective-permute-start.15 = (f32[32,512]{1,0:T(8,128)S(1)}, f32[32,512]{1,0:T(8,128)S(1)}, u32[]{:S(2)}, u32[]{:S(2)}) collective-permute-start(f32[32,512]{1,0:T(8,128)S(1)} %add.67), channel_id=1, source_target_pairs={{0,16},{16,0},{32,48},{48,32},{1,17},{17,1},{33,49},{49,33},{2,18}... | collective-permute-start | bytes 196616 | tf_op jit(solution)/shard_map/ppermute | solution.py:135
  169.4 3.7 %collective-permute-done.15 = f32[32,512]{1,0:T(8,128)S(1)} collective-permute-done((f32[32,512]{1,0:T(8,128)S(1)}, f32[32,512]{1,0:T(8,128)S(1)}, u32[]{:S(2)}, u32[]{:S(2)}) %collective-permute-start.15) | collective-permute-done | bytes 65568 | tf_op jit(solution)/shard_map/ppermute | solution.py:135
  173.2 3.8 %collective-permute-start.16 = (f32[32,512]{1,0:T(8,128)S(1)}, f32[32,512]{1,0:T(8,128)S(1)}, u32[]{:S(2)}, u32[]{:S(2)}) collective-permute-start(f32[32,512]{1,0:T(8,128)S(1)} %add.68), channel_id=1, source_target_pairs={{0,32},{16,48},{32,0},{48,16},{1,33},{17,49},{33,1},{49,17},{2,34}... | collective-permute-start | bytes 196616 | tf_op jit(solution)/shard_map/ppermute | solution.py:135
  177.0 2.8 %collective-permute-done.16 = f32[32,512]{1,0:T(8,128)S(1)} collective-permute-done((f32[32,512]{1,0:T(8,128)S(1)}, f32[32,512]{1,0:T(8,128)S(1)}, u32[]{:S(2)}, u32[]{:S(2)}) %collective-permute-start.16) | collective-permute-done | bytes 65568 | tf_op jit(solution)/shard_map/ppermute | solution.py:135
  179.8 0.0 all-to-all-done.3.parts_ref
  179.8 15.3 %all_to_all.26.mine_ref = bf16[8,32,512]{2,1,0:T(8,128)(2,1)S(1)} all-to-all(bf16[8,32,512]{2,1,0:T(8,128)(2,1)S(1)} %broadcast_in_dim.2), channel_id=1, replica_groups=mesh['y'=8,'x'=4,'z'=8,'core'=2] {'y'}, dimensions={0} | all-to-all | bytes 524288 | tf_op jit(solution)/shard_map/all_to_all | solution.py:227
  195.1 8.1 %collective-permute-start.17 = (bf16[8,32,512]{2,1,0:T(8,128)(2,1)S(1)}, bf16[8,32,512]{2,1,0:T(8,128)(2,1)S(1)}, u32[]{:S(2)}, u32[]{:S(2)}) collective-permute-start(bf16[8,32,512]{2,1,0:T(8,128)(2,1)S(1)} %all_to_all.26.mine_ref), channel_id=1, source_target_pairs={{0,1},{1,0},{2,3},{3,2},{4,5},{5,4},{6,7},{7,6},{8,9},{9,8},{10,11... | collective-permute-start | bytes 786440 | tf_op jit(solution)/shard_map/ppermute | solution.py:135
  203.3 1.0 last.1
  204.2 0.2 collective-permute-done.17.other_ref
  204.4 1.6 place_rows.1
  (18 shorter events, 0.2 us)
Async XLA Ops:
  0.6 0.9 copy-start.2
  2.6 10.7 %copy-start.1 = (bf16[1,1,8,128,128]{4,3,2,1,0:T(8,128)(2,1)S(1)}, bf16[1,1,8,128,128]{4,3,2,1,0:T(8,128)(2,1)}, u32[]{:S(2)}) copy-start(bf16[1,1,8,128,128]{4,3,2,1,0:T(8,128)(2,1)} %param.10) | copy-start | bytes 786436
  2.6 20.3 %copy-start.4 = (s32[1,1,8]{2,1,0:T(1,128)S(1)}, s32[1,1,8]{2,1,0:T(1,128)}, u32[]{:S(2)}) copy-start(s32[1,1,8]{2,1,0:T(1,128)} %param.13) | copy-start | bytes 100
  2.6 20.3 %copy-start.5 = (s32[1,1,8]{2,1,0:T(1,128)S(1)}, s32[1,1,8]{2,1,0:T(1,128)}, u32[]{:S(2)}) copy-start(s32[1,1,8]{2,1,0:T(1,128)} %param.12) | copy-start | bytes 100
  2.6 20.3 %copy-start.6 = (s32[1,1,8]{2,1,0:T(1,128)S(1)}, s32[1,1,8]{2,1,0:T(1,128)}, u32[]{:S(2)}) copy-start(s32[1,1,8]{2,1,0:T(1,128)} %param.11) | copy-start | bytes 100
  2.7 45.1 %all-to-all-start = ((bf16[32,128,128]{2,1,0:T(8,128)(2,1)}), bf16[32,128,128]{2,1,0:T(8,128)(2,1)S(1)}, u32[]{:S(2)}, u32[]{:S(2)}) async-start(bf16[32,128,128]{2,1,0:T(8,128)(2,1)} %spread.1), calls=%async_computation | async-start | bytes 2097152 | tf_op jit(solution)/shard_map/all_to_all | solution.py:157
  13.3 34.4 %collective-permute-start.3 = (bf16[1024,128]{1,0:T(8,128)(2,1)S(1)}, bf16[1024,128]{1,0:T(8,128)(2,1)S(1)}, u32[]{:S(2)}, u32[]{:S(2)}) collective-permute-start(bf16[1024,128]{1,0:T(8,128)(2,1)S(1)} %bitcast.23), channel_id=1, source_target_pairs={{0,16},{16,0},{32,48},{48,32},{1,17},{17,1},{33,49},{49,33},{2,18}... | collective-permute-start | bytes 786440 | tf_op jit(solution)/shard_map/ppermute | solution.py:135
  16.5 31.3 %collective-permute-start.4 = (bf16[1024,128]{1,0:T(8,128)(2,1)S(1)}, bf16[1024,128]{1,0:T(8,128)(2,1)S(1)}, u32[]{:S(2)}, u32[]{:S(2)}) collective-permute-start(bf16[1024,128]{1,0:T(8,128)(2,1)S(1)} %bitcast.24), channel_id=1, source_target_pairs={{0,32},{16,48},{32,0},{48,16},{1,33},{17,49},{33,1},{49,17},{2,34}... | collective-permute-start | bytes 786440 | tf_op jit(solution)/shard_map/ppermute | solution.py:135
  20.8 27.0 %collective-permute-start.5 = (bf16[1024,128]{1,0:T(8,128)(2,1)S(1)}, bf16[1024,128]{1,0:T(8,128)(2,1)S(1)}, u32[]{:S(2)}, u32[]{:S(2)}) collective-permute-start(bf16[1024,128]{1,0:T(8,128)(2,1)S(1)} %bitcast.25), channel_id=1, source_target_pairs={{0,48},{16,32},{32,16},{48,0},{1,49},{17,33},{33,17},{49,1},{2,50}... | collective-permute-start | bytes 786440 | tf_op jit(solution)/shard_map/ppermute | solution.py:135
  23.0 20.4 %collective-permute-start.2 = (s32[1,24]{1,0:T(1,128)S(1)}, s32[1,24]{1,0:T(1,128)S(1)}, u32[]{:S(2)}, u32[]{:S(2)}) collective-permute-start(s32[1,24]{1,0:T(1,128)S(1)} %add_bitcast_fusion), channel_id=1, source_target_pairs={{0,48},{16,32},{32,16},{48,0},{1,49},{17,33},{33,17},{49,1},{2,50}... | collective-permute-start | bytes 296 | tf_op jit(solution)/shard_map/ppermute | solution.py:135
  27.4 18.0 %collective-permute-start.1 = (s32[1,24]{1,0:T(1,128)S(1)}, s32[1,24]{1,0:T(1,128)S(1)}, u32[]{:S(2)}, u32[]{:S(2)}) collective-permute-start(s32[1,24]{1,0:T(1,128)S(1)} %add_bitcast_fusion), channel_id=1, source_target_pairs={{0,32},{16,48},{32,0},{48,16},{1,33},{17,49},{33,1},{49,17},{2,34}... | collective-permute-start | bytes 296 | tf_op jit(solution)/shard_map/ppermute | solution.py:135
  43.5 4.3 %collective-permute-start = (s32[1,24]{1,0:T(1,128)S(1)}, s32[1,24]{1,0:T(1,128)S(1)}, u32[]{:S(2)}, u32[]{:S(2)}) collective-permute-start(s32[1,24]{1,0:T(1,128)S(1)} %add_bitcast_fusion), channel_id=1, source_target_pairs={{0,16},{16,0},{32,48},{48,32},{1,17},{17,1},{33,49},{49,33},{2,18}... | collective-permute-start | bytes 296 | tf_op jit(solution)/shard_map/ppermute | solution.py:135
  49.3 6.8 %collective-permute-start.6 = (bf16[32,128,128]{2,1,0:T(8,128)(2,1)S(1)}, bf16[32,128,128]{2,1,0:T(8,128)(2,1)S(1)}, u32[]{:S(2)}, u32[]{:S(2)}) collective-permute-start(bf16[32,128,128]{2,1,0:T(8,128)(2,1)S(1)} %get-tuple-element.16), channel_id=1, source_target_pairs={{0,1},{1,0},{2,3},{3,2},{4,5},{5,4},{6,7},{7,6},{8,9},{9,8},{10,11... | collective-permute-start | bytes 3145736 | tf_op jit(solution)/shard_map/ppermute | solution.py:135
  56.5 35.6 %copy-start = (bf16[512,512]{1,0:T(8,128)(2,1)S(1)}, bf16[512,512]{1,0:T(8,128)(2,1)}, u32[]{:S(2)}) copy-start(bf16[512,512]{1,0:T(8,128)(2,1)} %weight_ref.3) | copy-start | bytes 1572868
  56.5 35.6 %copy-start.3 = (bf16[128,512]{1,0:T(8,128)(2,1)S(1)}, bf16[128,512]{1,0:T(8,128)(2,1)}, u32[]{:S(2)}) copy-start(bf16[128,512]{1,0:T(8,128)(2,1)} %cotangent_ref.1) | copy-start | bytes 393220
  94.2 34.4 %all-to-all-start.2 = ((bf16[32,128,128]{2,1,0:T(8,128)(2,1)}), bf16[32,128,128]{2,1,0:T(8,128)(2,1)S(1)}, u32[]{:S(2)}, u32[]{:S(2)}) async-start(bf16[32,128,128]{2,1,0:T(8,128)(2,1)} %get-tuple-element.18), calls=%async_computation.2 | async-start | bytes 2097152 | tf_op jit(solution)/shard_map/all_to_all | solution.py:191
  102.1 4.6 %collective-permute-start.7 = (bf16[256,512]{1,0:T(8,128)(2,1)S(1)}, bf16[256,512]{1,0:T(8,128)(2,1)S(1)}, u32[]{:S(2)}, u32[]{:S(2)}) collective-permute-start(bf16[256,512]{1,0:T(8,128)(2,1)S(1)} %get-tuple-element.20), channel_id=1, source_target_pairs={{0,1},{1,0},{2,3},{3,2},{4,5},{5,4},{6,7},{7,6},{8,9},{9,8},{10,11... | collective-permute-start | bytes 786440 | tf_op jit(solution)/shard_map/ppermute | solution.py:135
  106.8 6.6 %collective-permute-start.8 = (bf16[128,512]{1,0:T(8,128)(2,1)S(1)}, bf16[128,512]{1,0:T(8,128)(2,1)S(1)}, u32[]{:S(2)}, u32[]{:S(2)}) collective-permute-start(bf16[128,512]{1,0:T(8,128)(2,1)S(1)} %dynamic-slice_bitcast_fusion), channel_id=1, source_target_pairs={{0,64},{64,0},{128,192},{192,128},{256,320},{320,256},{384,448},{4... | collective-permute-start | bytes 393224 | tf_op jit(solution)/shard_map/ppermute | solution.py:135
  113.4 6.2 %collective-permute-start.9 = (bf16[64,512]{1,0:T(8,128)(2,1)S(1)}, bf16[64,512]{1,0:T(8,128)(2,1)S(1)}, u32[]{:S(2)}, u32[]{:S(2)}) collective-permute-start(bf16[64,512]{1,0:T(8,128)(2,1)S(1)} %dynamic-slice_bitcast_fusion.1), channel_id=1, source_target_pairs={{0,128},{64,192},{128,0},{192,64},{256,384},{320,448},{384,256},{4... | collective-permute-start | bytes 196616 | tf_op jit(solution)/shard_map/ppermute | solution.py:135
  119.7 8.9 %collective-permute-start.10 = (bf16[32,512]{1,0:T(8,128)(2,1)S(1)}, bf16[32,512]{1,0:T(8,128)(2,1)S(1)}, u32[]{:S(2)}, u32[]{:S(2)}) collective-permute-start(bf16[32,512]{1,0:T(8,128)(2,1)S(1)} %dynamic-slice_bitcast_fusion.2), channel_id=1, source_target_pairs={{0,256},{64,320},{128,384},{192,448},{256,0},{320,64},{384,128},{4... | collective-permute-start | bytes 98312 | tf_op jit(solution)/shard_map/ppermute | solution.py:135
  128.6 10.8 %collective-permute-start.11 = (bf16[32,128,128]{2,1,0:T(8,128)(2,1)S(1)}, bf16[32,128,128]{2,1,0:T(8,128)(2,1)S(1)}, u32[]{:S(2)}, u32[]{:S(2)}) collective-permute-start(bf16[32,128,128]{2,1,0:T(8,128)(2,1)S(1)} %all-to-all-done.2.mine_ref), channel_id=1, source_target_pairs={{0,1},{1,0},{2,3},{3,2},{4,5},{5,4},{6,7},{7,6},{8,9},{9,8},{10,11... | collective-permute-start | bytes 3145736 | tf_op jit(solution)/shard_map/ppermute | solution.py:135
  133.8 5.6 %collective-permute-start.12 = (f32[32,512]{1,0:T(8,128)S(1)}, f32[32,512]{1,0:T(8,128)S(1)}, u32[]{:S(2)}, u32[]{:S(2)}) collective-permute-start(f32[32,512]{1,0:T(8,128)S(1)} %convert_element_type.78), channel_id=1, source_target_pairs={{0,2},{2,0},{4,6},{6,4},{8,10},{10,8},{12,14},{14,12},{1,3},{3,1},... | collective-permute-start | bytes 196616 | tf_op jit(solution)/shard_map/ppermute | solution.py:135
  141.8 38.0 %all-to-all-start.3 = ((bf16[32,128,128]{2,1,0:T(8,128)(2,1)}), bf16[32,128,128]{2,1,0:T(8,128)(2,1)S(1)}, u32[]{:S(2)}, u32[]{:S(2)}) async-start(bf16[32,128,128]{2,1,0:T(8,128)(2,1)} %backward_tiles.1), calls=%async_computation.3 | async-start | bytes 2097152 | tf_op jit(solution)/shard_map/all_to_all | solution.py:211
  150.9 6.2 %collective-permute-start.13 = (f32[32,512]{1,0:T(8,128)S(1)}, f32[32,512]{1,0:T(8,128)S(1)}, u32[]{:S(2)}, u32[]{:S(2)}) collective-permute-start(f32[32,512]{1,0:T(8,128)S(1)} %convert_add_fusion.3), channel_id=1, source_target_pairs={{0,4},{2,6},{4,0},{6,2},{8,12},{10,14},{12,8},{14,10},{1,5},{3,7},... | collective-permute-start | bytes 196616 | tf_op jit(solution)/shard_map/ppermute | solution.py:135
  157.1 9.4 %collective-permute-start.14 = (f32[32,512]{1,0:T(8,128)S(1)}, f32[32,512]{1,0:T(8,128)S(1)}, u32[]{:S(2)}, u32[]{:S(2)}) collective-permute-start(f32[32,512]{1,0:T(8,128)S(1)} %add.66), channel_id=1, source_target_pairs={{0,8},{2,10},{4,12},{6,14},{8,0},{10,2},{12,4},{14,6},{1,9},{3,11}... | collective-permute-start | bytes 196616 | tf_op jit(solution)/shard_map/ppermute | solution.py:135
  166.5 6.7 %collective-permute-start.15 = (f32[32,512]{1,0:T(8,128)S(1)}, f32[32,512]{1,0:T(8,128)S(1)}, u32[]{:S(2)}, u32[]{:S(2)}) collective-permute-start(f32[32,512]{1,0:T(8,128)S(1)} %add.67), channel_id=1, source_target_pairs={{0,16},{16,0},{32,48},{48,32},{1,17},{17,1},{33,49},{49,33},{2,18}... | collective-permute-start | bytes 196616 | tf_op jit(solution)/shard_map/ppermute | solution.py:135
  173.2 6.6 %collective-permute-start.16 = (f32[32,512]{1,0:T(8,128)S(1)}, f32[32,512]{1,0:T(8,128)S(1)}, u32[]{:S(2)}, u32[]{:S(2)}) collective-permute-start(f32[32,512]{1,0:T(8,128)S(1)} %add.68), channel_id=1, source_target_pairs={{0,32},{16,48},{32,0},{48,16},{1,33},{17,49},{33,1},{49,17},{2,34}... | collective-permute-start | bytes 196616 | tf_op jit(solution)/shard_map/ppermute | solution.py:135
  195.1 9.3 %collective-permute-start.17 = (bf16[8,32,512]{2,1,0:T(8,128)(2,1)S(1)}, bf16[8,32,512]{2,1,0:T(8,128)(2,1)S(1)}, u32[]{:S(2)}, u32[]{:S(2)}) collective-permute-start(bf16[8,32,512]{2,1,0:T(8,128)(2,1)S(1)} %all_to_all.26.mine_ref), channel_id=1, source_target_pairs={{0,1},{1,0},{2,3},{3,2},{4,5},{5,4},{6,7},{7,6},{8,9},{9,8},{10,11... | collective-permute-start | bytes 786440 | tf_op jit(solution)/shard_map/ppermute | solution.py:135

commit v4 on v3

--- a/solution.py
+++ b/solution.py
@@ -143,6 +143,10 @@
     return (keep.astype(F32) + exchange(send, axis, distance).astype(F32)).astype(BF16)
 
 
+def double(array, axis, distance):
+    return (array.astype(F32) + exchange(array, axis, distance).astype(F32)).astype(BF16)
+
+
 def body(features, weight, cotangent, tile_values, tile_rows, tile_cols, tile_valid):
     place = jnp.stack([lax.axis_index("core"), lax.axis_index("x")]).astype(jnp.int32)
 
@@ -159,7 +163,8 @@
     tiles = tile_values.reshape(SLOTS * TILE, TILE)
     tiles = [tiles] + [exchange(tiles, "x", distance) for distance in range(1, X)]
     index = jnp.concatenate([tile_rows, tile_cols, tile_valid], axis=2).reshape(1, 3 * SLOTS)
-    index = jnp.concatenate([index] + [exchange(index, "x", distance) for distance in range(1, X)])
+    for distance in (1, 2):
+        index = jnp.concatenate([index, exchange(index, "x", distance)])
 
     mine, other = pl.pallas_call(
         forward_tiles,
@@ -196,8 +201,9 @@
     grad_mine, piece = lax.optimization_barrier((grad_mine, piece))
 
     grad_other = exchange(grad_mine, "core", 1)
-    piece = piece.astype(F32)
-    piece = piece + exchange(piece, "z", 1)
+    piece = double(piece, "z", 1)
+    grad_mine, grad_other, piece = lax.optimization_barrier((grad_mine, grad_other, piece))
+    piece = double(piece, "z", 2)
     back = pl.pallas_call(
         backward_tiles,
         in_specs=[smem(), smem()] + [vmem()] * (2 + X),
@@ -209,8 +215,8 @@
     )(place, index, grad_mine, grad_other, *tiles)
     back, piece = lax.optimization_barrier((back, piece))
     back = lax.all_to_all(back, ("y", "x"), 0, 0, tiled=True)
-    for axis, distance in (("z", 2), ("z", 4), ("x", 1), ("x", 2)):
-        piece = piece + exchange(piece, axis, distance)
+    for axis, distance in (("z", 4), ("x", 1), ("x", 2)):
+        piece = double(piece, axis, distance)
     back, piece = lax.optimization_barrier((back, piece))
 
     input_grad = pl.pallas_call(
@@ -223,7 +229,7 @@
     )(back, weight)
 
     share = WIDTH // (Y * CORES)
-    piece = jnp.broadcast_to(piece.astype(BF16)[None], (Y, share, WIDTH))
+    piece = jnp.broadcast_to(piece[None], (Y, share, WIDTH))
     whole = lax.all_to_all(piece, "y", 0, 0, tiled=True)
     weight_grad = pl.pallas_call(
         place_rows,

time: 207 us -> 202 us (0.976)
  starting transfers between devices: 102 us -> 92.8 us
  waiting for transfers between devices: 41.1 us -> 45.5 us
    ppermute x18 -> x17, starting transfers between devices: 74 us -> 67 us  [exchange(): return lax.ppermute(array, axis, [(i, i ^ distance) for i in range(size)])]
    all_to_all x1, waiting for transfers between devices: 0.01 us -> 3.87 us  [body(): back = lax.all_to_all(back, ('y', 'x'), 0, 0, tiled=True)]
    all_to_all x1, blocking collectives: 15.3 us -> 12.9 us  [body(): whole = lax.all_to_all(piece, 'y', 0, 0, tiled=True)]
    all_to_all x1, blocking collectives: 35.6 us -> 37.9 us  [body(): parts = lax.all_to_all(term, ('x', 'z'), 0, 0, tiled=True)]
    ppermute x18 -> x17, waiting for transfers between devices: 41.1 us -> 41.6 us  [exchange(): return lax.ppermute(array, axis, [(i, i ^ distance) for i in range(size)])]
  transfers between devices with their start and end apart: 21 -> 20, of which waited for: 13 -> 13; matrix products, arithmetic and copies ran while one was open for 0% -> 0% of each run, Pallas kernels for 0% -> 2%
where the time goes in v4:
time: 202 us; the launch traced here: 201 us
  starting transfers between devices  92.8 us (46%)
  blocking collectives  50.8 us (25%)
  waiting for transfers between devices  45.5 us (23%)
  Pallas kernels  9.59 us (5%)
    ppermute x17, starting transfers between devices, exchange(): return lax.ppermute(array, axis, [(i, i ^ distance) for i in range(size)])  67 us
    ppermute x17, waiting for transfers between devices, exchange(): return lax.ppermute(array, axis, [(i, i ^ distance) for i in range(size)])  41.6 us
    all_to_all x1, blocking collectives, body(): parts = lax.all_to_all(term, ('x', 'z'), 0, 0, tiled=True)  37.9 us
    all_to_all x1, blocking collectives, body(): whole = lax.all_to_all(piece, 'y', 0, 0, tiled=True)  12.9 us
    all_to_all x1, starting transfers between devices, body(): panel = lax.all_to_all(chunks, ('y', 'x'), 0, 0, tiled=True)  10.6 us
    all_to_all x1, starting transfers between devices, body(): grad_mine = lax.all_to_all(grad, ('x', 'z'), 0, 0, tiled=True)  7.94 us
    all_to_all x1, starting transfers between devices, body(): back = lax.all_to_all(back, ('y', 'x'), 0, 0, tiled=True)  7.12 us
  transfers between devices with their start and end apart: 20, of which 13 were waited for; matrix products, arithmetic and copies ran while one was open for 0% of the time, Pallas kernels for 2%

profile of v4, /device:TPU:1, one launch (start us, length us, event | category | flops | bytes accessed | tf_op | source)
XLA Modules:
  0.0 201.3 jit_solution(259300789591846093)
XLA Ops:
  0.6 0.0 copy-start.2
  0.6 0.9 copy-done.2
  1.5 1.1 spread.1
  2.6 0.0 copy-start.1
  2.6 0.0 copy-start.4
  2.7 10.6 %all-to-all-start = ((bf16[32,128,128]{2,1,0:T(8,128)(2,1)}), bf16[32,128,128]{2,1,0:T(8,128)(2,1)S(1)}, u32[]{:S(2)}, u32[]{:S(2)}) async-start(bf16[32,128,128]{2,1,0:T(8,128)(2,1)} %spread.1), calls=%async_computation | async-start | bytes 2097152 | tf_op jit(solution)/shard_map/all_to_all | solution.py:161
  13.3 0.0 copy-done.1
  13.3 4.3 %collective-permute-start.4 = (bf16[1024,128]{1,0:T(8,128)(2,1)S(1)}, bf16[1024,128]{1,0:T(8,128)(2,1)S(1)}, u32[]{:S(2)}, u32[]{:S(2)}) collective-permute-start(bf16[1024,128]{1,0:T(8,128)(2,1)S(1)} %bitcast.23), channel_id=1, source_target_pairs={{0,48},{16,32},{32,16},{48,0},{1,49},{17,33},{33,17},{49,1},{2,50}... | collective-permute-start | bytes 786440 | tf_op jit(solution)/shard_map/ppermute | solution.py:135
  17.7 2.5 %collective-permute-start.3 = (bf16[1024,128]{1,0:T(8,128)(2,1)S(1)}, bf16[1024,128]{1,0:T(8,128)(2,1)S(1)}, u32[]{:S(2)}, u32[]{:S(2)}) collective-permute-start(bf16[1024,128]{1,0:T(8,128)(2,1)S(1)} %bitcast.24), channel_id=1, source_target_pairs={{0,32},{16,48},{32,0},{48,16},{1,33},{17,49},{33,1},{49,17},{2,34}... | collective-permute-start | bytes 786440 | tf_op jit(solution)/shard_map/ppermute | solution.py:135
  20.2 2.1 %collective-permute-start.2 = (bf16[1024,128]{1,0:T(8,128)(2,1)S(1)}, bf16[1024,128]{1,0:T(8,128)(2,1)S(1)}, u32[]{:S(2)}, u32[]{:S(2)}) collective-permute-start(bf16[1024,128]{1,0:T(8,128)(2,1)S(1)} %bitcast.25), channel_id=1, source_target_pairs={{0,16},{16,0},{32,48},{48,32},{1,17},{17,1},{33,49},{49,33},{2,18}... | collective-permute-start | bytes 786440 | tf_op jit(solution)/shard_map/ppermute | solution.py:135
  22.3 0.0 copy-done.4
  22.3 0.0 copy-done.5
  22.3 0.0 copy-done.6
  22.3 0.1 add_bitcast_fusion
  22.4 3.1 %collective-permute-start = (s32[1,24]{1,0:T(1,128)S(1)}, s32[1,24]{1,0:T(1,128)S(1)}, u32[]{:S(2)}, u32[]{:S(2)}) collective-permute-start(s32[1,24]{1,0:T(1,128)S(1)} %add_bitcast_fusion), channel_id=1, source_target_pairs={{0,16},{16,0},{32,48},{48,32},{1,17},{17,1},{33,49},{49,33},{2,18}... | collective-permute-start | bytes 296 | tf_op jit(solution)/shard_map/ppermute | solution.py:135
  25.6 15.3 %collective-permute-done = s32[1,24]{1,0:T(1,128)S(1)} collective-permute-done((s32[1,24]{1,0:T(1,128)S(1)}, s32[1,24]{1,0:T(1,128)S(1)}, u32[]{:S(2)}, u32[]{:S(2)}) %collective-permute-start) | collective-permute-done | bytes 128 | tf_op jit(solution)/shard_map/ppermute | solution.py:135
  40.9 3.6 %collective-permute-start.1 = (s32[2,24]{1,0:T(2,128)S(1)}, s32[2,24]{1,0:T(2,128)S(1)}, u32[]{:S(2)}, u32[]{:S(2)}) collective-permute-start(s32[2,24]{1,0:T(2,128)S(1)} %pad_add_fusion.1), channel_id=1, source_target_pairs={{0,32},{16,48},{32,0},{48,16},{1,33},{17,49},{33,1},{49,17},{2,34}... | collective-permute-start | bytes 584 | tf_op jit(solution)/shard_map/ppermute | solution.py:135
  44.4 0.1 pad_add_fusion.2.place_ref.core_ref
  44.5 2.2 %collective-permute-done.1 = s32[2,24]{1,0:T(2,128)S(1)} collective-permute-done((s32[2,24]{1,0:T(2,128)S(1)}, s32[2,24]{1,0:T(2,128)S(1)}, u32[]{:S(2)}, u32[]{:S(2)}) %collective-permute-start.1) | collective-permute-done | bytes 224 | tf_op jit(solution)/shard_map/ppermute | solution.py:135
  46.7 0.0 collective-permute-done.4.refs_3_
  46.7 0.0 collective-permute-done.3.refs_2_
  46.7 0.0 collective-permute-done.2.refs_1_
  46.7 0.0 all-to-all-done.panel_ref
  46.7 1.5 forward_tiles.1
  48.2 3.9 %collective-permute-start.5 = (bf16[32,128,128]{2,1,0:T(8,128)(2,1)S(1)}, bf16[32,128,128]{2,1,0:T(8,128)(2,1)S(1)}, u32[]{:S(2)}, u32[]{:S(2)}) collective-permute-start(bf16[32,128,128]{2,1,0:T(8,128)(2,1)S(1)} %get-tuple-element.19), channel_id=1, source_target_pairs={{0,1},{1,0},{2,3},{3,2},{4,5},{5,4},{6,7},{7,6},{8,9},{9,8},{10,11... | collective-permute-start | bytes 3145736 | tf_op jit(solution)/shard_map/ppermute | solution.py:135
  52.2 2.3 %collective-permute-done.5 = bf16[32,128,128]{2,1,0:T(8,128)(2,1)S(1)} collective-permute-done((bf16[32,128,128]{2,1,0:T(8,128)(2,1)S(1)}, bf16[32,128,128]{2,1,0:T(8,128)(2,1)S(1)}, u32[]{:S(2)}, u32[]{:S(2)}) %collective-permute-start.5) | collective-permute-done | bytes 1048608 | tf_op jit(solution)/shard_map/ppermute | solution.py:135
  54.5 0.4 add_convert_fusion
  54.8 0.0 copy-start
  54.8 0.0 copy-start.3
  54.9 37.9 %all_to_all.25.parts_ref = bf16[32,128,128]{2,1,0:T(8,128)(2,1)S(1)} all-to-all(bf16[32,128,128]{2,1,0:T(8,128)(2,1)S(1)} %add_convert_fusion), channel_id=1, replica_groups=mesh['y'=8,'x'=4,'z'=8,'core'=2] {'x','z'}, dimensions={0} | all-to-all | bytes 2097152 | tf_op jit(solution)/shard_map/all_to_all | solution.py:179
  92.8 0.0 copy-done
  92.8 0.0 copy-done.3
  92.8 2.1 %middle.1 = (bf16[128,512]{1,0:T(8,128)(2,1)}, bf16[32,128,128]{2,1,0:T(8,128)(2,1)}, bf16[256,512]{1,0:T(8,128)(2,1)S(1)}, bf16[256,512]{1,0:T(8,128)(2,1)S(1)}) custom-call(s32[2]{0:T(128)S(1)} %pad_add_fusion.2.place_ref.core_ref, bf16[32,128,128]{2,1,0:T(8,128)(2,1)S(1)} %all_to_all.25.parts_ref, bf16[512,512]{1,0:T(8,128)(2,1)S(1)} %copy-done, ...), custom_call_target="tpu_custom_call" | custom-call | tf_op jit(solution)/shard_map/middle/pallas_call | solution.py:182
  94.8 7.9 %all-to-all-start.2 = ((bf16[32,128,128]{2,1,0:T(8,128)(2,1)}), bf16[32,128,128]{2,1,0:T(8,128)(2,1)S(1)}, u32[]{:S(2)}, u32[]{:S(2)}) async-start(bf16[32,128,128]{2,1,0:T(8,128)(2,1)} %get-tuple-element.21), calls=%async_computation.2 | async-start | bytes 2097152 | tf_op jit(solution)/shard_map/all_to_all | solution.py:196
  102.8 3.4 %collective-permute-start.6 = (bf16[256,512]{1,0:T(8,128)(2,1)S(1)}, bf16[256,512]{1,0:T(8,128)(2,1)S(1)}, u32[]{:S(2)}, u32[]{:S(2)}) collective-permute-start(bf16[256,512]{1,0:T(8,128)(2,1)S(1)} %get-tuple-element.23), channel_id=1, source_target_pairs={{0,1},{1,0},{2,3},{3,2},{4,5},{5,4},{6,7},{7,6},{8,9},{9,8},{10,11... | collective-permute-start | bytes 786440 | tf_op jit(solution)/shard_map/ppermute | solution.py:135
  106.2 1.1 collective-permute-done.6
  107.4 0.1 add_convert_fusion.1
  107.5 2.4 %collective-permute-start.7 = (bf16[128,512]{1,0:T(8,128)(2,1)S(1)}, bf16[128,512]{1,0:T(8,128)(2,1)S(1)}, u32[]{:S(2)}, u32[]{:S(2)}) collective-permute-start(bf16[128,512]{1,0:T(8,128)(2,1)S(1)} %dynamic-slice_bitcast_fusion), channel_id=1, source_target_pairs={{0,64},{64,0},{128,192},{192,128},{256,320},{320,256},{384,448},{4... | collective-permute-start | bytes 393224 | tf_op jit(solution)/shard_map/ppermute | solution.py:135
  109.8 4.2 %collective-permute-done.7 = bf16[128,512]{1,0:T(8,128)(2,1)S(1)} collective-permute-done((bf16[128,512]{1,0:T(8,128)(2,1)S(1)}, bf16[128,512]{1,0:T(8,128)(2,1)S(1)}, u32[]{:S(2)}, u32[]{:S(2)}) %collective-permute-start.7) | collective-permute-done | bytes 131104 | tf_op jit(solution)/shard_map/ppermute | solution.py:135
  114.1 3.6 %collective-permute-start.8 = (bf16[64,512]{1,0:T(8,128)(2,1)S(1)}, bf16[64,512]{1,0:T(8,128)(2,1)S(1)}, u32[]{:S(2)}, u32[]{:S(2)}) collective-permute-start(bf16[64,512]{1,0:T(8,128)(2,1)S(1)} %dynamic-slice_bitcast_fusion.1), channel_id=1, source_target_pairs={{0,128},{64,192},{128,0},{192,64},{256,384},{320,448},{384,256},{4... | collective-permute-start | bytes 196616 | tf_op jit(solution)/shard_map/ppermute | solution.py:135
  117.8 3.3 %collective-permute-done.8 = bf16[64,512]{1,0:T(8,128)(2,1)S(1)} collective-permute-done((bf16[64,512]{1,0:T(8,128)(2,1)S(1)}, bf16[64,512]{1,0:T(8,128)(2,1)S(1)}, u32[]{:S(2)}, u32[]{:S(2)}) %collective-permute-start.8) | collective-permute-done | bytes 65568 | tf_op jit(solution)/shard_map/ppermute | solution.py:135
  121.1 4.9 %collective-permute-start.9 = (bf16[32,512]{1,0:T(8,128)(2,1)S(1)}, bf16[32,512]{1,0:T(8,128)(2,1)S(1)}, u32[]{:S(2)}, u32[]{:S(2)}) collective-permute-start(bf16[32,512]{1,0:T(8,128)(2,1)S(1)} %dynamic-slice_bitcast_fusion.2), channel_id=1, source_target_pairs={{0,256},{64,320},{128,384},{192,448},{256,0},{320,64},{384,128},{4... | collective-permute-start | bytes 98312 | tf_op jit(solution)/shard_map/ppermute | solution.py:135
  126.0 3.7 %collective-permute-done.9 = bf16[32,512]{1,0:T(8,128)(2,1)S(1)} collective-permute-done((bf16[32,512]{1,0:T(8,128)(2,1)S(1)}, bf16[32,512]{1,0:T(8,128)(2,1)S(1)}, u32[]{:S(2)}, u32[]{:S(2)}) %collective-permute-start.9) | collective-permute-done | bytes 32800 | tf_op jit(solution)/shard_map/ppermute | solution.py:135
  129.7 0.0 all-to-all-done.2.mine_ref
  129.7 5.1 %collective-permute-start.10 = (bf16[32,128,128]{2,1,0:T(8,128)(2,1)S(1)}, bf16[32,128,128]{2,1,0:T(8,128)(2,1)S(1)}, u32[]{:S(2)}, u32[]{:S(2)}) collective-permute-start(bf16[32,128,128]{2,1,0:T(8,128)(2,1)S(1)} %all-to-all-done.2.mine_ref), channel_id=1, source_target_pairs={{0,1},{1,0},{2,3},{3,2},{4,5},{5,4},{6,7},{7,6},{8,9},{9,8},{10,11... | collective-permute-start | bytes 3145736 | tf_op jit(solution)/shard_map/ppermute | solution.py:135
  134.8 3.4 %collective-permute-start.11 = (bf16[32,512]{1,0:T(8,128)(2,1)S(1)}, bf16[32,512]{1,0:T(8,128)(2,1)S(1)}, u32[]{:S(2)}, u32[]{:S(2)}) collective-permute-start(bf16[32,512]{1,0:T(8,128)(2,1)S(1)} %fusion.2), channel_id=1, source_target_pairs={{0,2},{2,0},{4,6},{6,4},{8,10},{10,8},{12,14},{14,12},{1,3},{3,1},... | collective-permute-start | bytes 98312 | tf_op jit(solution)/shard_map/ppermute | solution.py:135
  138.2 1.3 collective-permute-done.11
  139.5 0.0 collective-permute-done.10.other_ref
  139.5 4.3 %collective-permute-start.12 = (bf16[32,512]{1,0:T(8,128)(2,1)S(1)}, bf16[32,512]{1,0:T(8,128)(2,1)S(1)}, u32[]{:S(2)}, u32[]{:S(2)}) collective-permute-start(bf16[32,512]{1,0:T(8,128)(2,1)S(1)} %add_convert_fusion.6), channel_id=1, source_target_pairs={{0,4},{2,6},{4,0},{6,2},{8,12},{10,14},{12,8},{14,10},{1,5},{3,7},... | collective-permute-start | bytes 98312 | tf_op jit(solution)/shard_map/ppermute | solution.py:135
  143.8 2.4 %backward_tiles.1 = bf16[32,128,128]{2,1,0:T(8,128)(2,1)} custom-call(s32[2]{0:T(128)S(1)} %pad_add_fusion.2.place_ref.core_ref, s32[4,24]{1,0:T(4,128)S(1)} %pad_add_fusion.index_ref, bf16[32,128,128]{2,1,0:T(8,128)(2,1)S(1)} %all-to-all-done.2.mine_ref, bf16[32,128,128]{2,1,0:T(8,128)(2,1)S(1)} %collective-permute-done.10.other_ref, ...), custom_call_target="tpu_custom_call" | custom-call | tf_op jit(solution)/shard_map/backward_tiles/pallas_call | solution.py:207
  146.1 0.0 collective-permute-done.12
  146.2 7.1 %all-to-all-start.3 = ((bf16[32,128,128]{2,1,0:T(8,128)(2,1)}), bf16[32,128,128]{2,1,0:T(8,128)(2,1)S(1)}, u32[]{:S(2)}, u32[]{:S(2)}) async-start(bf16[32,128,128]{2,1,0:T(8,128)(2,1)} %backward_tiles.1), calls=%async_computation.3 | async-start | bytes 2097152 | tf_op jit(solution)/shard_map/all_to_all | solution.py:217
  153.3 6.6 %collective-permute-start.13 = (bf16[32,512]{1,0:T(8,128)(2,1)S(1)}, bf16[32,512]{1,0:T(8,128)(2,1)S(1)}, u32[]{:S(2)}, u32[]{:S(2)}) collective-permute-start(bf16[32,512]{1,0:T(8,128)(2,1)S(1)} %add_convert_fusion.5), channel_id=1, source_target_pairs={{0,8},{2,10},{4,12},{6,14},{8,0},{10,2},{12,4},{14,6},{1,9},{3,11}... | collective-permute-start | bytes 98312 | tf_op jit(solution)/shard_map/ppermute | solution.py:135
  159.9 2.3 %collective-permute-done.13 = bf16[32,512]{1,0:T(8,128)(2,1)S(1)} collective-permute-done((bf16[32,512]{1,0:T(8,128)(2,1)S(1)}, bf16[32,512]{1,0:T(8,128)(2,1)S(1)}, u32[]{:S(2)}, u32[]{:S(2)}) %collective-permute-start.13) | collective-permute-done | bytes 32800 | tf_op jit(solution)/shard_map/ppermute | solution.py:135
  162.2 2.8 %collective-permute-start.14 = (bf16[32,512]{1,0:T(8,128)(2,1)S(1)}, bf16[32,512]{1,0:T(8,128)(2,1)S(1)}, u32[]{:S(2)}, u32[]{:S(2)}) collective-permute-start(bf16[32,512]{1,0:T(8,128)(2,1)S(1)} %add_convert_fusion.4), channel_id=1, source_target_pairs={{0,16},{16,0},{32,48},{48,32},{1,17},{17,1},{33,49},{49,33},{2,18}... | collective-permute-start | bytes 98312 | tf_op jit(solution)/shard_map/ppermute | solution.py:135
  165.0 2.8 %collective-permute-done.14 = bf16[32,512]{1,0:T(8,128)(2,1)S(1)} collective-permute-done((bf16[32,512]{1,0:T(8,128)(2,1)S(1)}, bf16[32,512]{1,0:T(8,128)(2,1)S(1)}, u32[]{:S(2)}, u32[]{:S(2)}) %collective-permute-start.14) | collective-permute-done | bytes 32800 | tf_op jit(solution)/shard_map/ppermute | solution.py:135
  167.8 4.1 %collective-permute-start.15 = (bf16[32,512]{1,0:T(8,128)(2,1)S(1)}, bf16[32,512]{1,0:T(8,128)(2,1)S(1)}, u32[]{:S(2)}, u32[]{:S(2)}) collective-permute-start(bf16[32,512]{1,0:T(8,128)(2,1)S(1)} %add_convert_fusion.3), channel_id=1, source_target_pairs={{0,32},{16,48},{32,0},{48,16},{1,33},{17,49},{33,1},{49,17},{2,34}... | collective-permute-start | bytes 98312 | tf_op jit(solution)/shard_map/ppermute | solution.py:135
  171.9 3.1 %collective-permute-done.15 = bf16[32,512]{1,0:T(8,128)(2,1)S(1)} collective-permute-done((bf16[32,512]{1,0:T(8,128)(2,1)S(1)}, bf16[32,512]{1,0:T(8,128)(2,1)S(1)}, u32[]{:S(2)}, u32[]{:S(2)}) %collective-permute-start.15) | collective-permute-done | bytes 32800 | tf_op jit(solution)/shard_map/ppermute | solution.py:135
  175.1 3.9 %all-to-all-done.3.parts_ref = bf16[32,128,128]{2,1,0:T(8,128)(2,1)S(1)} async-done(((bf16[32,128,128]{2,1,0:T(8,128)(2,1)}), bf16[32,128,128]{2,1,0:T(8,128)(2,1)S(1)}, u32[]{:S(2)}, u32[]{:S(2)}) %all-to-all-start.3) | async-done | bytes 1048608 | tf_op jit(solution)/shard_map/all_to_all | solution.py:217
  178.9 12.9 %all_to_all.26.mine_ref = bf16[8,32,512]{2,1,0:T(8,128)(2,1)S(1)} all-to-all(bf16[8,32,512]{2,1,0:T(8,128)(2,1)S(1)} %broadcast_in_dim.2), channel_id=1, replica_groups=mesh['y'=8,'x'=4,'z'=8,'core'=2] {'y'}, dimensions={0} | all-to-all | bytes 524288 | tf_op jit(solution)/shard_map/all_to_all | solution.py:233
  191.8 6.8 %collective-permute-start.16 = (bf16[8,32,512]{2,1,0:T(8,128)(2,1)S(1)}, bf16[8,32,512]{2,1,0:T(8,128)(2,1)S(1)}, u32[]{:S(2)}, u32[]{:S(2)}) collective-permute-start(bf16[8,32,512]{2,1,0:T(8,128)(2,1)S(1)} %all_to_all.26.mine_ref), channel_id=1, source_target_pairs={{0,1},{1,0},{2,3},{3,2},{4,5},{5,4},{6,7},{7,6},{8,9},{9,8},{10,11... | collective-permute-start | bytes 786440 | tf_op jit(solution)/shard_map/ppermute | solution.py:135
  198.6 1.0 last.1
  199.6 0.2 collective-permute-done.16.other_ref
  199.7 1.6 place_rows.1
  (16 shorter events, 0.2 us)
Async XLA Ops:
  0.6 0.9 copy-start.2
  2.6 10.7 %copy-start.1 = (bf16[1,1,8,128,128]{4,3,2,1,0:T(8,128)(2,1)S(1)}, bf16[1,1,8,128,128]{4,3,2,1,0:T(8,128)(2,1)}, u32[]{:S(2)}) copy-start(bf16[1,1,8,128,128]{4,3,2,1,0:T(8,128)(2,1)} %param.10) | copy-start | bytes 786436
  2.6 19.7 %copy-start.4 = (s32[1,1,8]{2,1,0:T(1,128)S(1)}, s32[1,1,8]{2,1,0:T(1,128)}, u32[]{:S(2)}) copy-start(s32[1,1,8]{2,1,0:T(1,128)} %param.13) | copy-start | bytes 100
  2.6 19.7 %copy-start.5 = (s32[1,1,8]{2,1,0:T(1,128)S(1)}, s32[1,1,8]{2,1,0:T(1,128)}, u32[]{:S(2)}) copy-start(s32[1,1,8]{2,1,0:T(1,128)} %param.12) | copy-start | bytes 100
  2.6 19.7 %copy-start.6 = (s32[1,1,8]{2,1,0:T(1,128)S(1)}, s32[1,1,8]{2,1,0:T(1,128)}, u32[]{:S(2)}) copy-start(s32[1,1,8]{2,1,0:T(1,128)} %param.11) | copy-start | bytes 100
  2.7 44.1 %all-to-all-start = ((bf16[32,128,128]{2,1,0:T(8,128)(2,1)}), bf16[32,128,128]{2,1,0:T(8,128)(2,1)S(1)}, u32[]{:S(2)}, u32[]{:S(2)}) async-start(bf16[32,128,128]{2,1,0:T(8,128)(2,1)} %spread.1), calls=%async_computation | async-start | bytes 2097152 | tf_op jit(solution)/shard_map/all_to_all | solution.py:161
  13.3 33.4 %collective-permute-start.4 = (bf16[1024,128]{1,0:T(8,128)(2,1)S(1)}, bf16[1024,128]{1,0:T(8,128)(2,1)S(1)}, u32[]{:S(2)}, u32[]{:S(2)}) collective-permute-start(bf16[1024,128]{1,0:T(8,128)(2,1)S(1)} %bitcast.23), channel_id=1, source_target_pairs={{0,48},{16,32},{32,16},{48,0},{1,49},{17,33},{33,17},{49,1},{2,50}... | collective-permute-start | bytes 786440 | tf_op jit(solution)/shard_map/ppermute | solution.py:135
  17.7 29.0 %collective-permute-start.3 = (bf16[1024,128]{1,0:T(8,128)(2,1)S(1)}, bf16[1024,128]{1,0:T(8,128)(2,1)S(1)}, u32[]{:S(2)}, u32[]{:S(2)}) collective-permute-start(bf16[1024,128]{1,0:T(8,128)(2,1)S(1)} %bitcast.24), channel_id=1, source_target_pairs={{0,32},{16,48},{32,0},{48,16},{1,33},{17,49},{33,1},{49,17},{2,34}... | collective-permute-start | bytes 786440 | tf_op jit(solution)/shard_map/ppermute | solution.py:135
  20.2 26.5 %collective-permute-start.2 = (bf16[1024,128]{1,0:T(8,128)(2,1)S(1)}, bf16[1024,128]{1,0:T(8,128)(2,1)S(1)}, u32[]{:S(2)}, u32[]{:S(2)}) collective-permute-start(bf16[1024,128]{1,0:T(8,128)(2,1)S(1)} %bitcast.25), channel_id=1, source_target_pairs={{0,16},{16,0},{32,48},{48,32},{1,17},{17,1},{33,49},{49,33},{2,18}... | collective-permute-start | bytes 786440 | tf_op jit(solution)/shard_map/ppermute | solution.py:135
  22.4 18.4 %collective-permute-start = (s32[1,24]{1,0:T(1,128)S(1)}, s32[1,24]{1,0:T(1,128)S(1)}, u32[]{:S(2)}, u32[]{:S(2)}) collective-permute-start(s32[1,24]{1,0:T(1,128)S(1)} %add_bitcast_fusion), channel_id=1, source_target_pairs={{0,16},{16,0},{32,48},{48,32},{1,17},{17,1},{33,49},{49,33},{2,18}... | collective-permute-start | bytes 296 | tf_op jit(solution)/shard_map/ppermute | solution.py:135
  40.9 5.8 %collective-permute-start.1 = (s32[2,24]{1,0:T(2,128)S(1)}, s32[2,24]{1,0:T(2,128)S(1)}, u32[]{:S(2)}, u32[]{:S(2)}) collective-permute-start(s32[2,24]{1,0:T(2,128)S(1)} %pad_add_fusion.1), channel_id=1, source_target_pairs={{0,32},{16,48},{32,0},{48,16},{1,33},{17,49},{33,1},{49,17},{2,34}... | collective-permute-start | bytes 584 | tf_op jit(solution)/shard_map/ppermute | solution.py:135
  48.2 6.2 %collective-permute-start.5 = (bf16[32,128,128]{2,1,0:T(8,128)(2,1)S(1)}, bf16[32,128,128]{2,1,0:T(8,128)(2,1)S(1)}, u32[]{:S(2)}, u32[]{:S(2)}) collective-permute-start(bf16[32,128,128]{2,1,0:T(8,128)(2,1)S(1)} %get-tuple-element.19), channel_id=1, source_target_pairs={{0,1},{1,0},{2,3},{3,2},{4,5},{5,4},{6,7},{7,6},{8,9},{9,8},{10,11... | collective-permute-start | bytes 3145736 | tf_op jit(solution)/shard_map/ppermute | solution.py:135
  54.8 37.9 %copy-start = (bf16[512,512]{1,0:T(8,128)(2,1)S(1)}, bf16[512,512]{1,0:T(8,128)(2,1)}, u32[]{:S(2)}) copy-start(bf16[512,512]{1,0:T(8,128)(2,1)} %weight_ref.3) | copy-start | bytes 1572868
  54.8 37.9 %copy-start.3 = (bf16[128,512]{1,0:T(8,128)(2,1)S(1)}, bf16[128,512]{1,0:T(8,128)(2,1)}, u32[]{:S(2)}) copy-start(bf16[128,512]{1,0:T(8,128)(2,1)} %cotangent_ref.1) | copy-start | bytes 393220
  94.8 34.8 %all-to-all-start.2 = ((bf16[32,128,128]{2,1,0:T(8,128)(2,1)}), bf16[32,128,128]{2,1,0:T(8,128)(2,1)S(1)}, u32[]{:S(2)}, u32[]{:S(2)}) async-start(bf16[32,128,128]{2,1,0:T(8,128)(2,1)} %get-tuple-element.21), calls=%async_computation.2 | async-start | bytes 2097152 | tf_op jit(solution)/shard_map/all_to_all | solution.py:196
  102.8 4.6 %collective-permute-start.6 = (bf16[256,512]{1,0:T(8,128)(2,1)S(1)}, bf16[256,512]{1,0:T(8,128)(2,1)S(1)}, u32[]{:S(2)}, u32[]{:S(2)}) collective-permute-start(bf16[256,512]{1,0:T(8,128)(2,1)S(1)} %get-tuple-element.23), channel_id=1, source_target_pairs={{0,1},{1,0},{2,3},{3,2},{4,5},{5,4},{6,7},{7,6},{8,9},{9,8},{10,11... | collective-permute-start | bytes 786440 | tf_op jit(solution)/shard_map/ppermute | solution.py:135
  107.5 6.6 %collective-permute-start.7 = (bf16[128,512]{1,0:T(8,128)(2,1)S(1)}, bf16[128,512]{1,0:T(8,128)(2,1)S(1)}, u32[]{:S(2)}, u32[]{:S(2)}) collective-permute-start(bf16[128,512]{1,0:T(8,128)(2,1)S(1)} %dynamic-slice_bitcast_fusion), channel_id=1, source_target_pairs={{0,64},{64,0},{128,192},{192,128},{256,320},{320,256},{384,448},{4... | collective-permute-start | bytes 393224 | tf_op jit(solution)/shard_map/ppermute | solution.py:135
  114.1 6.9 %collective-permute-start.8 = (bf16[64,512]{1,0:T(8,128)(2,1)S(1)}, bf16[64,512]{1,0:T(8,128)(2,1)S(1)}, u32[]{:S(2)}, u32[]{:S(2)}) collective-permute-start(bf16[64,512]{1,0:T(8,128)(2,1)S(1)} %dynamic-slice_bitcast_fusion.1), channel_id=1, source_target_pairs={{0,128},{64,192},{128,0},{192,64},{256,384},{320,448},{384,256},{4... | collective-permute-start | bytes 196616 | tf_op jit(solution)/shard_map/ppermute | solution.py:135
  121.1 8.6 %collective-permute-start.9 = (bf16[32,512]{1,0:T(8,128)(2,1)S(1)}, bf16[32,512]{1,0:T(8,128)(2,1)S(1)}, u32[]{:S(2)}, u32[]{:S(2)}) collective-permute-start(bf16[32,512]{1,0:T(8,128)(2,1)S(1)} %dynamic-slice_bitcast_fusion.2), channel_id=1, source_target_pairs={{0,256},{64,320},{128,384},{192,448},{256,0},{320,64},{384,128},{4... | collective-permute-start | bytes 98312 | tf_op jit(solution)/shard_map/ppermute | solution.py:135
  129.7 9.9 %collective-permute-start.10 = (bf16[32,128,128]{2,1,0:T(8,128)(2,1)S(1)}, bf16[32,128,128]{2,1,0:T(8,128)(2,1)S(1)}, u32[]{:S(2)}, u32[]{:S(2)}) collective-permute-start(bf16[32,128,128]{2,1,0:T(8,128)(2,1)S(1)} %all-to-all-done.2.mine_ref), channel_id=1, source_target_pairs={{0,1},{1,0},{2,3},{3,2},{4,5},{5,4},{6,7},{7,6},{8,9},{9,8},{10,11... | collective-permute-start | bytes 3145736 | tf_op jit(solution)/shard_map/ppermute | solution.py:135
  134.8 4.7 %collective-permute-start.11 = (bf16[32,512]{1,0:T(8,128)(2,1)S(1)}, bf16[32,512]{1,0:T(8,128)(2,1)S(1)}, u32[]{:S(2)}, u32[]{:S(2)}) collective-permute-start(bf16[32,512]{1,0:T(8,128)(2,1)S(1)} %fusion.2), channel_id=1, source_target_pairs={{0,2},{2,0},{4,6},{6,4},{8,10},{10,8},{12,14},{14,12},{1,3},{3,1},... | collective-permute-start | bytes 98312 | tf_op jit(solution)/shard_map/ppermute | solution.py:135
  139.5 6.6 %collective-permute-start.12 = (bf16[32,512]{1,0:T(8,128)(2,1)S(1)}, bf16[32,512]{1,0:T(8,128)(2,1)S(1)}, u32[]{:S(2)}, u32[]{:S(2)}) collective-permute-start(bf16[32,512]{1,0:T(8,128)(2,1)S(1)} %add_convert_fusion.6), channel_id=1, source_target_pairs={{0,4},{2,6},{4,0},{6,2},{8,12},{10,14},{12,8},{14,10},{1,5},{3,7},... | collective-permute-start | bytes 98312 | tf_op jit(solution)/shard_map/ppermute | solution.py:135
  146.2 32.8 %all-to-all-start.3 = ((bf16[32,128,128]{2,1,0:T(8,128)(2,1)}), bf16[32,128,128]{2,1,0:T(8,128)(2,1)S(1)}, u32[]{:S(2)}, u32[]{:S(2)}) async-start(bf16[32,128,128]{2,1,0:T(8,128)(2,1)} %backward_tiles.1), calls=%async_computation.3 | async-start | bytes 2097152 | tf_op jit(solution)/shard_map/all_to_all | solution.py:217
  153.3 8.9 %collective-permute-start.13 = (bf16[32,512]{1,0:T(8,128)(2,1)S(1)}, bf16[32,512]{1,0:T(8,128)(2,1)S(1)}, u32[]{:S(2)}, u32[]{:S(2)}) collective-permute-start(bf16[32,512]{1,0:T(8,128)(2,1)S(1)} %add_convert_fusion.5), channel_id=1, source_target_pairs={{0,8},{2,10},{4,12},{6,14},{8,0},{10,2},{12,4},{14,6},{1,9},{3,11}... | collective-permute-start | bytes 98312 | tf_op jit(solution)/shard_map/ppermute | solution.py:135
  162.2 5.6 %collective-permute-start.14 = (bf16[32,512]{1,0:T(8,128)(2,1)S(1)}, bf16[32,512]{1,0:T(8,128)(2,1)S(1)}, u32[]{:S(2)}, u32[]{:S(2)}) collective-permute-start(bf16[32,512]{1,0:T(8,128)(2,1)S(1)} %add_convert_fusion.4), channel_id=1, source_target_pairs={{0,16},{16,0},{32,48},{48,32},{1,17},{17,1},{33,49},{49,33},{2,18}... | collective-permute-start | bytes 98312 | tf_op jit(solution)/shard_map/ppermute | solution.py:135
  167.8 7.2 %collective-permute-start.15 = (bf16[32,512]{1,0:T(8,128)(2,1)S(1)}, bf16[32,512]{1,0:T(8,128)(2,1)S(1)}, u32[]{:S(2)}, u32[]{:S(2)}) collective-permute-start(bf16[32,512]{1,0:T(8,128)(2,1)S(1)} %add_convert_fusion.3), channel_id=1, source_target_pairs={{0,32},{16,48},{32,0},{48,16},{1,33},{17,49},{33,1},{49,17},{2,34}... | collective-permute-start | bytes 98312 | tf_op jit(solution)/shard_map/ppermute | solution.py:135
  191.8 7.9 %collective-permute-start.16 = (bf16[8,32,512]{2,1,0:T(8,128)(2,1)S(1)}, bf16[8,32,512]{2,1,0:T(8,128)(2,1)S(1)}, u32[]{:S(2)}, u32[]{:S(2)}) collective-permute-start(bf16[8,32,512]{2,1,0:T(8,128)(2,1)S(1)} %all_to_all.26.mine_ref), channel_id=1, source_target_pairs={{0,1},{1,0},{2,3},{3,2},{4,5},{5,4},{6,7},{7,6},{8,9},{9,8},{10,11... | collective-permute-start | bytes 786440 | tf_op jit(solution)/shard_map/ppermute | solution.py:135

commit v5 on v2

--- a/solution.py
+++ b/solution.py
@@ -56,7 +56,7 @@
             other_ref[block * Z + pair] = total[2 * pair + 1 - core].astype(BF16)
 
 
-def middle(core_ref, parts_ref, weight_ref, cotangent_ref, act_ref, grad_ref, keep_ref, send_ref):
+def middle(parts_ref, weight_ref, cotangent_ref, act_ref, grad_ref, weight_part_ref):
     chunks = []
     for chunk in range(X):
         total = parts_ref[chunk * Z].astype(F32)
@@ -77,13 +77,9 @@
         piece = grad[:, chunk * CHUNK : (chunk + 1) * CHUNK]
         for z in range(Z):
             grad_ref[chunk * Z + z] = piece
-    weight_part = lax.dot_general(
+    weight_part_ref[...] = lax.dot_general(
         high, grad, (((0,), (0,)), ((), ())), preferred_element_type=F32
     ).astype(BF16)
-    low_half, high_half = weight_part[: WIDTH // 2], weight_part[WIDTH // 2 :]
-    upper = core_ref[0] == 1
-    keep_ref[...] = jnp.where(upper, high_half, low_half)
-    send_ref[...] = jnp.where(upper, low_half, high_half)
 
 
 def backward_tiles(place_ref, index_ref, mine_ref, other_ref, *refs):
@@ -120,6 +116,14 @@
     ).astype(BF16)
 
 
+def place_rows(pieces_ref, out_ref):
+    share = WIDTH // Y
+    scale = 1.0 / math.sqrt(TILE * Y * X * Z * CORES)
+    for y in range(Y):
+        at = ((y & 1) * 4 + (y >> 1 & 1) * 2 + (y >> 2)) * share
+        out_ref[at : at + share, :] = pieces_ref[y].astype(F32) * scale
+
+
 def exchange(array, axis, distance):
     size = lax.axis_size(axis)
     return lax.ppermute(array, axis, [(i, i ^ distance) for i in range(size)])
@@ -131,6 +135,10 @@
     send = lax.dynamic_index_in_dim(halves, 1 - upper, 0, keepdims=False)
     keep = lax.dynamic_index_in_dim(halves, upper, 0, keepdims=False)
     return (keep.astype(F32) + exchange(send, axis, distance).astype(F32)).astype(BF16)
+
+
+def double(array, axis, distance):
+    return (array.astype(F32) + exchange(array, axis, distance).astype(F32)).astype(BF16)
 
 
 def body(features, weight, cotangent, tile_values, tile_rows, tile_cols, tile_valid):
@@ -168,29 +176,27 @@
     term = (mine.astype(F32) + exchange(other, "core", 1).astype(F32)).astype(BF16)
     parts = lax.all_to_all(term, ("x", "z"), 0, 0, tiled=True)
 
-    half = WIDTH // CORES
-    activations, grad, weight_keep, weight_send = pl.pallas_call(
+    activations, grad, piece = pl.pallas_call(
         middle,
-        in_specs=[smem()] + [vmem()] * 3,
-        out_specs=[vmem()] * 4,
+        in_specs=[vmem()] * 3,
+        out_specs=[vmem()] * 3,
         out_shape=[
             jax.ShapeDtypeStruct((TILE, WIDTH), BF16),
             jax.ShapeDtypeStruct((X * Z, TILE, CHUNK), BF16),
-            jax.ShapeDtypeStruct((half, WIDTH), BF16),
-            jax.ShapeDtypeStruct((half, WIDTH), BF16),
+            jax.ShapeDtypeStruct((WIDTH, WIDTH), BF16),
         ],
         compiler_params=params(),
         name="middle",
-    )(place, parts, weight, cotangent)
+    )(parts, weight, cotangent)
 
     grad_mine = lax.all_to_all(grad, ("x", "z"), 0, 0, tiled=True)
-    piece = weight_keep.astype(F32) + exchange(weight_send, "core", 1).astype(F32)
-    piece = piece.astype(BF16)
     for distance in (1, 2, 4):
         piece = halve(piece, "y", distance)
+    piece = double(piece, "z", 1)
     grad_mine, piece = lax.optimization_barrier((grad_mine, piece))
 
     grad_other = exchange(grad_mine, "core", 1)
+    piece = double(piece, "z", 2)
     back = pl.pallas_call(
         backward_tiles,
         in_specs=[smem(), smem()] + [vmem()] * (2 + X),
@@ -200,10 +206,10 @@
         compiler_params=params(),
         name="backward_tiles",
     )(place, index, grad_mine, grad_other, *tiles)
-    back, piece = lax.optimization_barrier((back, piece.astype(F32)))
+    back, piece = lax.optimization_barrier((back, piece))
     back = lax.all_to_all(back, ("y", "x"), 0, 0, tiled=True)
-    for axis, distance in (("z", 1), ("z", 2), ("z", 4), ("x", 1), ("x", 2)):
-        piece = piece + exchange(piece, axis, distance)
+    piece = double(piece, "z", 4)
+    piece = lax.all_gather(piece, ("x", "core"), axis=0).astype(F32).sum(0).astype(BF16)
     back, piece = lax.optimization_barrier((back, piece))
 
     input_grad = pl.pallas_call(
@@ -215,12 +221,16 @@
         name="last",
     )(back, weight)
 
-    share = WIDTH // (Y * CORES)
-    piece = jnp.broadcast_to(piece.astype(BF16)[None], (Y * CORES, share, WIDTH))
-    whole = lax.all_to_all(piece, ("y", "core"), 0, 0, tiled=True)
-    whole = whole.reshape(2, 2, 2, CORES, share, WIDTH).transpose(3, 2, 1, 0, 4, 5)
-    nodes = TILE * Y * X * Z * CORES
-    weight_grad = whole.reshape(WIDTH, WIDTH).astype(F32) * (1.0 / math.sqrt(nodes))
+    piece = jnp.broadcast_to(piece[None], (Y, WIDTH // Y, WIDTH))
+    whole = lax.all_to_all(piece, "y", 0, 0, tiled=True)
+    weight_grad = pl.pallas_call(
+        place_rows,
+        in_specs=[vmem()],
+        out_specs=vmem(),
+        out_shape=jax.ShapeDtypeStruct((WIDTH, WIDTH), F32),
+        compiler_params=params(),
+        name="place_rows",
+    )(whole)
     return (activations, input_grad, weight_grad)
 
 

time: 207 us -> 207 us (level)
  blocking collectives: 38.3 us -> 55.4 us
  starting transfers between devices: 89.4 us -> 77.1 us
  waiting for transfers between devices: 64.4 us -> 60.1 us
    all_gather x0 -> x1, blocking collectives: none -> 17.1 us  [body(): lax.all_gather(piece, ('x', 'core'), axis=0).astype(F32).sum(0).astype(BF16)]
    ppermute x14 -> x11, starting transfers between devices: 51.8 us -> 44 us  [exchange(): return lax.ppermute(array, axis, [(i, i ^ distance) for i in range(size)])]
    all_to_all x1, starting transfers between devices: 12.2 us -> 6.25 us  [body(): whole = lax.all_to_all(piece, 'y', 0, 0, tiled=True)]
    ppermute x14 -> x11, waiting for transfers between devices: 48.1 us -> 43.1 us  [exchange(): return lax.ppermute(array, axis, [(i, i ^ distance) for i in range(size)])]
  transfers between devices with their start and end apart: 18 -> 15, of which waited for: 14 -> 10; matrix products, arithmetic and copies ran while one was open for 0% -> 1% of each run, Pallas kernels for 0% -> 0%
where the time goes in v5:
time: 207 us
  starting transfers between devices  77.1 us (37%)
  waiting for transfers between devices  60.1 us (29%)
  blocking collectives  55.4 us (27%)
  Pallas kernels  8.15 us (4%)
  local copies, waits for them, and re-layouts  2.95 us (1%)
    ppermute x11, starting transfers between devices, exchange(): return lax.ppermute(array, axis, [(i, i ^ distance) for i in range(size)])  44 us
    ppermute x11, waiting for transfers between devices, exchange(): return lax.ppermute(array, axis, [(i, i ^ distance) for i in range(size)])  43.1 us
    all_to_all x1, blocking collectives, body(): parts = lax.all_to_all(term, ('x', 'z'), 0, 0, tiled=True)  38.3 us
    all_gather x1, blocking collectives, body(): lax.all_gather(piece, ('x', 'core'), axis=0).astype(F32).sum(0).astype(BF16)  17.1 us
    all_to_all x1, waiting for transfers between devices, body(): whole = lax.all_to_all(piece, 'y', 0, 0, tiled=True)  17 us
    all_to_all x1, starting transfers between devices, body(): panel = lax.all_to_all(chunks, ('y', 'x'), 0, 0, tiled=True)  10.6 us
    all_to_all x1, starting transfers between devices, body(): back = lax.all_to_all(back, ('y', 'x'), 0, 0, tiled=True)  8.28 us
    all_to_all x1, starting transfers between devices, body(): grad_mine = lax.all_to_all(grad, ('x', 'z'), 0, 0, tiled=True)  7.95 us
  transfers between devices with their start and end apart: 15, of which 10 were waited for; matrix products, arithmetic and copies ran while one was open for 1% of the time, Pallas kernels for 0%

profile of v5, /device:TPU:1, one launch (start us, length us, event | category | flops | bytes accessed | tf_op | source)
XLA Modules:
  0.0 206.5 jit_solution(6161745279808126813)
XLA Ops:
  0.6 0.0 copy-start.2
  0.6 0.9 copy-done.2
  1.5 1.1 spread.1
  2.6 0.0 copy-start.8
  2.6 0.0 copy-start.6
  2.6 0.0 copy-start.7
  2.6 0.0 copy-start.4
  2.7 0.0 copy-start.5
  2.7 10.6 %all-to-all-start = ((bf16[32,128,128]{2,1,0:T(8,128)(2,1)}), bf16[32,128,128]{2,1,0:T(8,128)(2,1)S(1)}, u32[]{:S(2)}, u32[]{:S(2)}) async-start(bf16[32,128,128]{2,1,0:T(8,128)(2,1)} %spread.1), calls=%async_computation | async-start | bytes 2097152 | tf_op jit(solution)/shard_map/all_to_all | solution.py:155
  13.3 0.0 copy-done.8
  13.3 0.0 copy-done.6
  13.3 0.0 copy-done.7
  13.4 0.1 fusion.11
  13.5 0.0 copy-done.4
  13.5 4.3 %collective-permute-start.2 = (bf16[1040,128]{1,0:T(8,128)(2,1)S(1)}, bf16[1040,128]{1,0:T(8,128)(2,1)S(1)}, u32[]{:S(2)}, u32[]{:S(2)}) collective-permute-start(bf16[1040,128]{1,0:T(8,128)(2,1)S(1)} %pad_maximum_fusion.refs_0_), channel_id=1, source_target_pairs={{0,48},{16,32},{32,16},{48,0},{1,49},{17,33},{33,17},{49,1},{2,50}... | collective-permute-start | bytes 798728 | tf_op jit(solution)/shard_map/ppermute | solution.py:129
  17.8 2.5 %collective-permute-start.1 = (bf16[1040,128]{1,0:T(8,128)(2,1)S(1)}, bf16[1040,128]{1,0:T(8,128)(2,1)S(1)}, u32[]{:S(2)}, u32[]{:S(2)}) collective-permute-start(bf16[1040,128]{1,0:T(8,128)(2,1)S(1)} %pad_maximum_fusion.refs_0_), channel_id=1, source_target_pairs={{0,32},{16,48},{32,0},{48,16},{1,33},{17,49},{33,1},{49,17},{2,34}... | collective-permute-start | bytes 798728 | tf_op jit(solution)/shard_map/ppermute | solution.py:129
  20.3 2.1 %collective-permute-start = (bf16[1040,128]{1,0:T(8,128)(2,1)S(1)}, bf16[1040,128]{1,0:T(8,128)(2,1)S(1)}, u32[]{:S(2)}, u32[]{:S(2)}) collective-permute-start(bf16[1040,128]{1,0:T(8,128)(2,1)S(1)} %pad_maximum_fusion.refs_0_), channel_id=1, source_target_pairs={{0,16},{16,0},{32,48},{48,32},{1,17},{17,1},{33,49},{49,33},{2,18}... | collective-permute-start | bytes 798728 | tf_op jit(solution)/shard_map/ppermute | solution.py:129
  22.5 0.0 copy-done.5
  22.5 0.1 broadcast_in_dim.4
  22.6 0.1 min.23
  22.7 0.1 pad_add_fusion.place_ref
  22.7 14.6 %collective-permute-done.2.refs_3_ = bf16[1040,128]{1,0:T(8,128)(2,1)S(1)} collective-permute-done((bf16[1040,128]{1,0:T(8,128)(2,1)S(1)}, bf16[1040,128]{1,0:T(8,128)(2,1)S(1)}, u32[]{:S(2)}, u32[]{:S(2)}) %collective-permute-start.2) | collective-permute-done | bytes 266272 | tf_op jit(solution)/shard_map/ppermute | solution.py:129
  37.4 0.0 collective-permute-done.1.refs_2_
  37.4 3.7 %collective-permute-done.refs_1_ = bf16[1040,128]{1,0:T(8,128)(2,1)S(1)} collective-permute-done((bf16[1040,128]{1,0:T(8,128)(2,1)S(1)}, bf16[1040,128]{1,0:T(8,128)(2,1)S(1)}, u32[]{:S(2)}, u32[]{:S(2)}) %collective-permute-start) | collective-permute-done | bytes 266272 | tf_op jit(solution)/shard_map/ppermute | solution.py:129
  41.1 0.1 maximum_minimum_fusion.index_ref
  41.2 0.0 all-to-all-done.panel_ref
  41.2 1.5 forward_tiles.1
  42.7 3.1 %collective-permute-start.3 = (bf16[32,128,128]{2,1,0:T(8,128)(2,1)S(1)}, bf16[32,128,128]{2,1,0:T(8,128)(2,1)S(1)}, u32[]{:S(2)}, u32[]{:S(2)}) collective-permute-start(bf16[32,128,128]{2,1,0:T(8,128)(2,1)S(1)} %get-tuple-element.15), channel_id=1, source_target_pairs={{0,1},{1,0},{2,3},{3,2},{4,5},{5,4},{6,7},{7,6},{8,9},{9,8},{10,11... | collective-permute-start | bytes 3145736 | tf_op jit(solution)/shard_map/ppermute | solution.py:129
  45.8 2.3 %collective-permute-done.3 = bf16[32,128,128]{2,1,0:T(8,128)(2,1)S(1)} collective-permute-done((bf16[32,128,128]{2,1,0:T(8,128)(2,1)S(1)}, bf16[32,128,128]{2,1,0:T(8,128)(2,1)S(1)}, u32[]{:S(2)}, u32[]{:S(2)}) %collective-permute-start.3) | collective-permute-done | bytes 1048608 | tf_op jit(solution)/shard_map/ppermute | solution.py:129
  48.1 0.4 add_convert_fusion
  48.4 0.0 copy-start
  48.4 0.0 copy-start.3
  48.5 38.3 %all_to_all.25.parts_ref = bf16[32,128,128]{2,1,0:T(8,128)(2,1)S(1)} all-to-all(bf16[32,128,128]{2,1,0:T(8,128)(2,1)S(1)} %add_convert_fusion), channel_id=1, replica_groups=mesh['y'=8,'x'=4,'z'=8,'core'=2] {'x','z'}, dimensions={0} | all-to-all | bytes 2097152 | tf_op jit(solution)/shard_map/all_to_all | solution.py:177
  86.7 0.0 copy-done
  86.7 0.0 copy-done.3
  86.7 1.2 middle.1
  87.9 1.0 copy-done.1
  88.9 7.9 %all-to-all-start.2 = ((bf16[32,128,128]{2,1,0:T(8,128)(2,1)}), bf16[32,128,128]{2,1,0:T(8,128)(2,1)S(1)}, u32[]{:S(2)}, u32[]{:S(2)}) async-start(bf16[32,128,128]{2,1,0:T(8,128)(2,1)} %copy-done.1), calls=%async_computation.2 | async-start | bytes 2097152 | tf_op jit(solution)/shard_map/all_to_all | solution.py:192
  96.9 2.2 %collective-permute-start.4 = (bf16[256,512]{1,0:T(8,128)(2,1)S(1)}, bf16[256,512]{1,0:T(8,128)(2,1)}, u32[]{:S(2)}, u32[]{:S(2)}) collective-permute-start(bf16[256,512]{1,0:T(8,128)(2,1)S(1)} %dynamic-slice_bitcast_fusion), channel_id=1, source_target_pairs={{0,64},{64,0},{128,192},{192,128},{256,320},{320,256},{384,448},{4... | collective-permute-start | bytes 786440 | tf_op jit(solution)/shard_map/ppermute | solution.py:129
  99.1 6.0 %collective-permute-done.4 = bf16[256,512]{1,0:T(8,128)(2,1)} collective-permute-done((bf16[256,512]{1,0:T(8,128)(2,1)S(1)}, bf16[256,512]{1,0:T(8,128)(2,1)}, u32[]{:S(2)}, u32[]{:S(2)}) %collective-permute-start.4) | collective-permute-done | bytes 262176 | tf_op jit(solution)/shard_map/ppermute | solution.py:129
  105.1 1.0 fusion
  106.2 3.0 %collective-permute-start.5 = (bf16[128,512]{1,0:T(8,128)(2,1)S(1)}, bf16[128,512]{1,0:T(8,128)(2,1)S(1)}, u32[]{:S(2)}, u32[]{:S(2)}) collective-permute-start(bf16[128,512]{1,0:T(8,128)(2,1)S(1)} %dynamic-slice_bitcast_fusion.1), channel_id=1, source_target_pairs={{0,128},{64,192},{128,0},{192,64},{256,384},{320,448},{384,256},{4... | collective-permute-start | bytes 393224 | tf_op jit(solution)/shard_map/ppermute | solution.py:129
  109.2 5.3 %collective-permute-done.5 = bf16[128,512]{1,0:T(8,128)(2,1)S(1)} collective-permute-done((bf16[128,512]{1,0:T(8,128)(2,1)S(1)}, bf16[128,512]{1,0:T(8,128)(2,1)S(1)}, u32[]{:S(2)}, u32[]{:S(2)}) %collective-permute-start.5) | collective-permute-done | bytes 131104 | tf_op jit(solution)/shard_map/ppermute | solution.py:129
  114.6 5.0 %collective-permute-start.6 = (bf16[64,512]{1,0:T(8,128)(2,1)S(1)}, bf16[64,512]{1,0:T(8,128)(2,1)S(1)}, u32[]{:S(2)}, u32[]{:S(2)}) collective-permute-start(bf16[64,512]{1,0:T(8,128)(2,1)S(1)} %dynamic-slice_bitcast_fusion.2), channel_id=1, source_target_pairs={{0,256},{64,320},{128,384},{192,448},{256,0},{320,64},{384,128},{4... | collective-permute-start | bytes 196616 | tf_op jit(solution)/shard_map/ppermute | solution.py:129
  119.5 4.6 %collective-permute-done.6 = bf16[64,512]{1,0:T(8,128)(2,1)S(1)} collective-permute-done((bf16[64,512]{1,0:T(8,128)(2,1)S(1)}, bf16[64,512]{1,0:T(8,128)(2,1)S(1)}, u32[]{:S(2)}, u32[]{:S(2)}) %collective-permute-start.6) | collective-permute-done | bytes 65568 | tf_op jit(solution)/shard_map/ppermute | solution.py:129
  124.2 2.9 %collective-permute-start.7 = (bf16[64,512]{1,0:T(8,128)(2,1)S(1)}, bf16[64,512]{1,0:T(8,128)(2,1)S(1)}, u32[]{:S(2)}, u32[]{:S(2)}) collective-permute-start(bf16[64,512]{1,0:T(8,128)(2,1)S(1)} %fusion.2), channel_id=1, source_target_pairs={{0,2},{2,0},{4,6},{6,4},{8,10},{10,8},{12,14},{14,12},{1,3},{3,1},... | collective-permute-start | bytes 196616 | tf_op jit(solution)/shard_map/ppermute | solution.py:129
  127.0 2.1 %collective-permute-done.7 = bf16[64,512]{1,0:T(8,128)(2,1)S(1)} collective-permute-done((bf16[64,512]{1,0:T(8,128)(2,1)S(1)}, bf16[64,512]{1,0:T(8,128)(2,1)S(1)}, u32[]{:S(2)}, u32[]{:S(2)}) %collective-permute-start.7) | collective-permute-done | bytes 65568 | tf_op jit(solution)/shard_map/ppermute | solution.py:129
  129.2 0.0 all-to-all-done.2.mine_ref
  129.2 7.5 %collective-permute-start.8 = (bf16[32,128,128]{2,1,0:T(8,128)(2,1)S(1)}, bf16[32,128,128]{2,1,0:T(8,128)(2,1)S(1)}, u32[]{:S(2)}, u32[]{:S(2)}) collective-permute-start(bf16[32,128,128]{2,1,0:T(8,128)(2,1)S(1)} %all-to-all-done.2.mine_ref), channel_id=1, source_target_pairs={{0,1},{1,0},{2,3},{3,2},{4,5},{5,4},{6,7},{7,6},{8,9},{9,8},{10,11... | collective-permute-start | bytes 3145736 | tf_op jit(solution)/shard_map/ppermute | solution.py:129
  136.7 4.0 %collective-permute-start.9 = (bf16[64,512]{1,0:T(8,128)(2,1)S(1)}, bf16[64,512]{1,0:T(8,128)(2,1)S(1)}, u32[]{:S(2)}, u32[]{:S(2)}) collective-permute-start(bf16[64,512]{1,0:T(8,128)(2,1)S(1)} %add_convert_fusion.3), channel_id=1, source_target_pairs={{0,4},{2,6},{4,0},{6,2},{8,12},{10,14},{12,8},{14,10},{1,5},{3,7},... | collective-permute-start | bytes 196616 | tf_op jit(solution)/shard_map/ppermute | solution.py:129
  140.8 2.5 %collective-permute-done.9 = bf16[64,512]{1,0:T(8,128)(2,1)S(1)} collective-permute-done((bf16[64,512]{1,0:T(8,128)(2,1)S(1)}, bf16[64,512]{1,0:T(8,128)(2,1)S(1)}, u32[]{:S(2)}, u32[]{:S(2)}) %collective-permute-start.9) | collective-permute-done | bytes 65568 | tf_op jit(solution)/shard_map/ppermute | solution.py:129
  143.3 0.0 collective-permute-done.8.other_ref
  143.3 2.4 %backward_tiles.1 = bf16[32,128,128]{2,1,0:T(8,128)(2,1)} custom-call(s32[2]{0:T(128)S(1)} %pad_add_fusion.place_ref, s32[4,24]{1,0:T(4,128)S(1)} %maximum_minimum_fusion.index_ref, bf16[32,128,128]{2,1,0:T(8,128)(2,1)S(1)} %all-to-all-done.2.mine_ref, bf16[32,128,128]{2,1,0:T(8,128)(2,1)S(1)} %collective-permute-done.8.other_ref, ...), custom_call_target="tpu_custom_call" | custom-call | tf_op jit(solution)/shard_map/backward_tiles/pallas_call | solution.py:200
  145.7 8.3 %all-to-all-start.3 = ((bf16[32,128,128]{2,1,0:T(8,128)(2,1)}), bf16[32,128,128]{2,1,0:T(8,128)(2,1)S(1)}, u32[]{:S(2)}, u32[]{:S(2)}) async-start(bf16[32,128,128]{2,1,0:T(8,128)(2,1)} %backward_tiles.1), calls=%async_computation.3 | async-start | bytes 2097152 | tf_op jit(solution)/shard_map/all_to_all | solution.py:210
  154.0 7.3 %collective-permute-start.10 = (bf16[64,512]{1,0:T(8,128)(2,1)S(1)}, bf16[64,512]{1,0:T(8,128)(2,1)S(1)}, u32[]{:S(2)}, u32[]{:S(2)}) collective-permute-start(bf16[64,512]{1,0:T(8,128)(2,1)S(1)} %add_convert_fusion.2), channel_id=1, source_target_pairs={{0,8},{2,10},{4,12},{6,14},{8,0},{10,2},{12,4},{14,6},{1,9},{3,11}... | collective-permute-start | bytes 196616 | tf_op jit(solution)/shard_map/ppermute | solution.py:129
  161.3 1.9 collective-permute-done.10
  163.2 17.1 %all-gather = bf16[512,512]{1,0:T(8,128)(2,1)S(1)} all-gather(bf16[64,512]{1,0:T(8,128)(2,1)S(1)} %add_convert_fusion.1), channel_id=2, replica_groups=mesh['y'=8,'x'=4,'z'=8,'core'=2] {'x','core'}, dimensions={0}, use_global_device_ids=true | all-gather | bytes 589824 | tf_op jit(solution)/shard_map/all_gather | solution.py:212
  180.3 0.1 reduce_sum.12
  180.4 0.0 all-to-all-done.3.parts_ref
  180.4 0.8 broadcast_in_dim.5
  181.2 6.3 %all-to-all-start.4 = ((bf16[8,64,512]{2,1,0:T(8,128)(2,1)}), bf16[8,64,512]{2,1,0:T(8,128)(2,1)S(1)}, u32[]{:S(2)}, u32[]{:S(2)}) async-start(bf16[8,64,512]{2,1,0:T(8,128)(2,1)} %broadcast_in_dim.5), calls=%async_computation.4 | async-start | bytes 1048576 | tf_op jit(solution)/shard_map/all_to_all | solution.py:225
  187.5 1.0 last.1
  188.5 17.0 %all-to-all-done.4.pieces_ref = bf16[8,64,512]{2,1,0:T(8,128)(2,1)S(1)} async-done(((bf16[8,64,512]{2,1,0:T(8,128)(2,1)}), bf16[8,64,512]{2,1,0:T(8,128)(2,1)S(1)}, u32[]{:S(2)}, u32[]{:S(2)}) %all-to-all-start.4) | async-done | bytes 524320 | tf_op jit(solution)/shard_map/all_to_all | solution.py:225
  205.5 1.0 place_rows.1
  (15 shorter events, 0.2 us)
Async XLA Ops:
  0.6 0.9 copy-start.2
  2.6 10.7 %copy-start.8 = (s32[1,1,8]{2,1,0:T(1,128)S(1)}, s32[1,1,8]{2,1,0:T(1,128)}, u32[]{:S(2)}) copy-start(s32[1,1,8]{2,1,0:T(1,128)} %param.12) | copy-start | bytes 100
  2.6 10.7 %copy-start.6 = (s32[1,1,8]{2,1,0:T(1,128)S(1)}, s32[1,1,8]{2,1,0:T(1,128)}, u32[]{:S(2)}) copy-start(s32[1,1,8]{2,1,0:T(1,128)} %param.14) | copy-start | bytes 100
  2.6 10.7 %copy-start.7 = (s32[1,1,8]{2,1,0:T(1,128)S(1)}, s32[1,1,8]{2,1,0:T(1,128)}, u32[]{:S(2)}) copy-start(s32[1,1,8]{2,1,0:T(1,128)} %param.13) | copy-start | bytes 100
  2.6 10.8 %copy-start.4 = (bf16[1,1,8,128,128]{4,3,2,1,0:T(8,128)(2,1)S(1)}, bf16[1,1,8,128,128]{4,3,2,1,0:T(8,128)(2,1)}, u32[]{:S(2)}) copy-start(bf16[1,1,8,128,128]{4,3,2,1,0:T(8,128)(2,1)} %param.11) | copy-start | bytes 786436
  2.7 19.8 %copy-start.5 = (s32[3]{0:T(128)S(1)}, s32[3]{0:T(128)}, u32[]{:S(2)}) copy-start(s32[3]{0:T(128)} %constant.52.clone) | copy-start | bytes 40
  2.7 38.5 %all-to-all-start = ((bf16[32,128,128]{2,1,0:T(8,128)(2,1)}), bf16[32,128,128]{2,1,0:T(8,128)(2,1)S(1)}, u32[]{:S(2)}, u32[]{:S(2)}) async-start(bf16[32,128,128]{2,1,0:T(8,128)(2,1)} %spread.1), calls=%async_computation | async-start | bytes 2097152 | tf_op jit(solution)/shard_map/all_to_all | solution.py:155
  13.5 23.9 %collective-permute-start.2 = (bf16[1040,128]{1,0:T(8,128)(2,1)S(1)}, bf16[1040,128]{1,0:T(8,128)(2,1)S(1)}, u32[]{:S(2)}, u32[]{:S(2)}) collective-permute-start(bf16[1040,128]{1,0:T(8,128)(2,1)S(1)} %pad_maximum_fusion.refs_0_), channel_id=1, source_target_pairs={{0,48},{16,32},{32,16},{48,0},{1,49},{17,33},{33,17},{49,1},{2,50}... | collective-permute-start | bytes 798728 | tf_op jit(solution)/shard_map/ppermute | solution.py:129
  17.8 19.5 %collective-permute-start.1 = (bf16[1040,128]{1,0:T(8,128)(2,1)S(1)}, bf16[1040,128]{1,0:T(8,128)(2,1)S(1)}, u32[]{:S(2)}, u32[]{:S(2)}) collective-permute-start(bf16[1040,128]{1,0:T(8,128)(2,1)S(1)} %pad_maximum_fusion.refs_0_), channel_id=1, source_target_pairs={{0,32},{16,48},{32,0},{48,16},{1,33},{17,49},{33,1},{49,17},{2,34}... | collective-permute-start | bytes 798728 | tf_op jit(solution)/shard_map/ppermute | solution.py:129
  20.3 20.7 %collective-permute-start = (bf16[1040,128]{1,0:T(8,128)(2,1)S(1)}, bf16[1040,128]{1,0:T(8,128)(2,1)S(1)}, u32[]{:S(2)}, u32[]{:S(2)}) collective-permute-start(bf16[1040,128]{1,0:T(8,128)(2,1)S(1)} %pad_maximum_fusion.refs_0_), channel_id=1, source_target_pairs={{0,16},{16,0},{32,48},{48,32},{1,17},{17,1},{33,49},{49,33},{2,18}... | collective-permute-start | bytes 798728 | tf_op jit(solution)/shard_map/ppermute | solution.py:129
  42.7 5.4 %collective-permute-start.3 = (bf16[32,128,128]{2,1,0:T(8,128)(2,1)S(1)}, bf16[32,128,128]{2,1,0:T(8,128)(2,1)S(1)}, u32[]{:S(2)}, u32[]{:S(2)}) collective-permute-start(bf16[32,128,128]{2,1,0:T(8,128)(2,1)S(1)} %get-tuple-element.15), channel_id=1, source_target_pairs={{0,1},{1,0},{2,3},{3,2},{4,5},{5,4},{6,7},{7,6},{8,9},{9,8},{10,11... | collective-permute-start | bytes 3145736 | tf_op jit(solution)/shard_map/ppermute | solution.py:129
  48.4 38.3 %copy-start = (bf16[512,512]{1,0:T(8,128)(2,1)S(1)}, bf16[512,512]{1,0:T(8,128)(2,1)}, u32[]{:S(2)}) copy-start(bf16[512,512]{1,0:T(8,128)(2,1)} %weight_ref.3) | copy-start | bytes 1572868
  48.4 38.3 %copy-start.3 = (bf16[128,512]{1,0:T(8,128)(2,1)S(1)}, bf16[128,512]{1,0:T(8,128)(2,1)}, u32[]{:S(2)}) copy-start(bf16[128,512]{1,0:T(8,128)(2,1)} %cotangent_ref.1) | copy-start | bytes 393220
  87.9 1.0 copy-start.1
  88.9 40.3 %all-to-all-start.2 = ((bf16[32,128,128]{2,1,0:T(8,128)(2,1)}), bf16[32,128,128]{2,1,0:T(8,128)(2,1)S(1)}, u32[]{:S(2)}, u32[]{:S(2)}) async-start(bf16[32,128,128]{2,1,0:T(8,128)(2,1)} %copy-done.1), calls=%async_computation.2 | async-start | bytes 2097152 | tf_op jit(solution)/shard_map/all_to_all | solution.py:192
  96.9 8.3 %collective-permute-start.4 = (bf16[256,512]{1,0:T(8,128)(2,1)S(1)}, bf16[256,512]{1,0:T(8,128)(2,1)}, u32[]{:S(2)}, u32[]{:S(2)}) collective-permute-start(bf16[256,512]{1,0:T(8,128)(2,1)S(1)} %dynamic-slice_bitcast_fusion), channel_id=1, source_target_pairs={{0,64},{64,0},{128,192},{192,128},{256,320},{320,256},{384,448},{4... | collective-permute-start | bytes 786440 | tf_op jit(solution)/shard_map/ppermute | solution.py:129
  106.2 8.3 %collective-permute-start.5 = (bf16[128,512]{1,0:T(8,128)(2,1)S(1)}, bf16[128,512]{1,0:T(8,128)(2,1)S(1)}, u32[]{:S(2)}, u32[]{:S(2)}) collective-permute-start(bf16[128,512]{1,0:T(8,128)(2,1)S(1)} %dynamic-slice_bitcast_fusion.1), channel_id=1, source_target_pairs={{0,128},{64,192},{128,0},{192,64},{256,384},{320,448},{384,256},{4... | collective-permute-start | bytes 393224 | tf_op jit(solution)/shard_map/ppermute | solution.py:129
  114.6 9.6 %collective-permute-start.6 = (bf16[64,512]{1,0:T(8,128)(2,1)S(1)}, bf16[64,512]{1,0:T(8,128)(2,1)S(1)}, u32[]{:S(2)}, u32[]{:S(2)}) collective-permute-start(bf16[64,512]{1,0:T(8,128)(2,1)S(1)} %dynamic-slice_bitcast_fusion.2), channel_id=1, source_target_pairs={{0,256},{64,320},{128,384},{192,448},{256,0},{320,64},{384,128},{4... | collective-permute-start | bytes 196616 | tf_op jit(solution)/shard_map/ppermute | solution.py:129
  124.2 5.0 %collective-permute-start.7 = (bf16[64,512]{1,0:T(8,128)(2,1)S(1)}, bf16[64,512]{1,0:T(8,128)(2,1)S(1)}, u32[]{:S(2)}, u32[]{:S(2)}) collective-permute-start(bf16[64,512]{1,0:T(8,128)(2,1)S(1)} %fusion.2), channel_id=1, source_target_pairs={{0,2},{2,0},{4,6},{6,4},{8,10},{10,8},{12,14},{14,12},{1,3},{3,1},... | collective-permute-start | bytes 196616 | tf_op jit(solution)/shard_map/ppermute | solution.py:129
  129.2 14.1 %collective-permute-start.8 = (bf16[32,128,128]{2,1,0:T(8,128)(2,1)S(1)}, bf16[32,128,128]{2,1,0:T(8,128)(2,1)S(1)}, u32[]{:S(2)}, u32[]{:S(2)}) collective-permute-start(bf16[32,128,128]{2,1,0:T(8,128)(2,1)S(1)} %all-to-all-done.2.mine_ref), channel_id=1, source_target_pairs={{0,1},{1,0},{2,3},{3,2},{4,5},{5,4},{6,7},{7,6},{8,9},{9,8},{10,11... | collective-permute-start | bytes 3145736 | tf_op jit(solution)/shard_map/ppermute | solution.py:129
  136.7 6.5 %collective-permute-start.9 = (bf16[64,512]{1,0:T(8,128)(2,1)S(1)}, bf16[64,512]{1,0:T(8,128)(2,1)S(1)}, u32[]{:S(2)}, u32[]{:S(2)}) collective-permute-start(bf16[64,512]{1,0:T(8,128)(2,1)S(1)} %add_convert_fusion.3), channel_id=1, source_target_pairs={{0,4},{2,6},{4,0},{6,2},{8,12},{10,14},{12,8},{14,10},{1,5},{3,7},... | collective-permute-start | bytes 196616 | tf_op jit(solution)/shard_map/ppermute | solution.py:129
  145.7 34.7 %all-to-all-start.3 = ((bf16[32,128,128]{2,1,0:T(8,128)(2,1)}), bf16[32,128,128]{2,1,0:T(8,128)(2,1)S(1)}, u32[]{:S(2)}, u32[]{:S(2)}) async-start(bf16[32,128,128]{2,1,0:T(8,128)(2,1)} %backward_tiles.1), calls=%async_computation.3 | async-start | bytes 2097152 | tf_op jit(solution)/shard_map/all_to_all | solution.py:210
  154.0 9.2 %collective-permute-start.10 = (bf16[64,512]{1,0:T(8,128)(2,1)S(1)}, bf16[64,512]{1,0:T(8,128)(2,1)S(1)}, u32[]{:S(2)}, u32[]{:S(2)}) collective-permute-start(bf16[64,512]{1,0:T(8,128)(2,1)S(1)} %add_convert_fusion.2), channel_id=1, source_target_pairs={{0,8},{2,10},{4,12},{6,14},{8,0},{10,2},{12,4},{14,6},{1,9},{3,11}... | collective-permute-start | bytes 196616 | tf_op jit(solution)/shard_map/ppermute | solution.py:129
  181.2 24.2 %all-to-all-start.4 = ((bf16[8,64,512]{2,1,0:T(8,128)(2,1)}), bf16[8,64,512]{2,1,0:T(8,128)(2,1)S(1)}, u32[]{:S(2)}, u32[]{:S(2)}) async-start(bf16[8,64,512]{2,1,0:T(8,128)(2,1)} %broadcast_in_dim.5), calls=%async_computation.4 | async-start | bytes 1048576 | tf_op jit(solution)/shard_map/all_to_all | solution.py:225

commit v6 on v4

--- a/solution.py
+++ b/solution.py
@@ -14,6 +14,7 @@
 CHUNK = WIDTH // X
 ROW_TILES = Z * CORES
 COL_TILES = Y * X
+INDEX_ROWS = 16
 BF16 = jnp.bfloat16
 F32 = jnp.float32
 
@@ -160,11 +161,15 @@
     )(features)
     panel = lax.all_to_all(chunks, ("y", "x"), 0, 0, tiled=True)
 
-    tiles = tile_values.reshape(SLOTS * TILE, TILE)
+    index = jnp.concatenate(
+        [tile_rows.reshape(-1), tile_cols.reshape(-1), tile_valid.reshape(-1)]
+    ).astype(BF16)
+    index = jnp.pad(index[None, :], ((0, INDEX_ROWS - 1), (0, TILE - 3 * SLOTS)))
+    tiles = jnp.concatenate([tile_values.reshape(SLOTS * TILE, TILE), index], axis=0)
     tiles = [tiles] + [exchange(tiles, "x", distance) for distance in range(1, X)]
-    index = jnp.concatenate([tile_rows, tile_cols, tile_valid], axis=2).reshape(1, 3 * SLOTS)
-    for distance in (1, 2):
-        index = jnp.concatenate([index, exchange(index, "x", distance)])
+    index = jnp.stack([t[SLOTS * TILE, : 3 * SLOTS] for t in tiles]).astype(jnp.int32)
+    limit = jnp.repeat(jnp.array([ROW_TILES - 1, COL_TILES - 1, 1], jnp.int32), SLOTS)
+    index = jnp.clip(index, 0, limit[None, :])
 
     mine, other = pl.pallas_call(
         forward_tiles,
@@ -202,8 +207,6 @@
 
     grad_other = exchange(grad_mine, "core", 1)
     piece = double(piece, "z", 1)
-    grad_mine, grad_other, piece = lax.optimization_barrier((grad_mine, grad_other, piece))
-    piece = double(piece, "z", 2)
     back = pl.pallas_call(
         backward_tiles,
         in_specs=[smem(), smem()] + [vmem()] * (2 + X),
@@ -215,8 +218,9 @@
     )(place, index, grad_mine, grad_other, *tiles)
     back, piece = lax.optimization_barrier((back, piece))
     back = lax.all_to_all(back, ("y", "x"), 0, 0, tiled=True)
-    for axis, distance in (("z", 4), ("x", 1), ("x", 2)):
-        piece = double(piece, axis, distance)
+    for distance in (2, 4):
+        piece = double(piece, "z", distance)
+    piece = lax.all_gather(piece, "x", axis=0).astype(F32).sum(0).astype(BF16)
     back, piece = lax.optimization_barrier((back, piece))
 
     input_grad = pl.pallas_call(

time: 202 us -> 197 us (0.975)
  blocking collectives: 50.8 us -> 64.5 us
  starting transfers between devices: 92.8 us -> 79.3 us
  waiting for transfers between devices: 45.5 us -> 39.4 us
    ppermute x17 -> x13, starting transfers between devices: 67 us -> 54 us  [exchange(): return lax.ppermute(array, axis, [(i, i ^ distance) for i in range(size)])]
    all_gather x0 -> x1, blocking collectives: none -> 10.7 us  [body(): piece = lax.all_gather(piece, 'x', axis=0).astype(F32).sum(0).astype(BF16)]
    all_to_all x1, waiting for transfers between devices: 3.87 us -> 0.2 us  [body(): back = lax.all_to_all(back, ('y', 'x'), 0, 0, tiled=True)]
    all_to_all x1, blocking collectives: 12.9 us -> 15.6 us  [body(): whole = lax.all_to_all(piece, 'y', 0, 0, tiled=True)]
    ppermute x17 -> x13, waiting for transfers between devices: 41.6 us -> 39.2 us  [exchange(): return lax.ppermute(array, axis, [(i, i ^ distance) for i in range(size)])]
  transfers between devices with their start and end apart: 20 -> 16, of which waited for: 13 -> 12; matrix products, arithmetic and copies ran while one was open for 0% -> 0% of each run, Pallas kernels for 2% -> 0%
where the time goes in v6:
time: 197 us; the launch traced here: 196 us
  starting transfers between devices  79.3 us (40%)
  blocking collectives  64.5 us (33%)
  waiting for transfers between devices  39.4 us (20%)
  Pallas kernels  9.24 us (5%)
  local copies, waits for them, and re-layouts  2.12 us (1%)
    ppermute x13, starting transfers between devices, exchange(): return lax.ppermute(array, axis, [(i, i ^ distance) for i in range(size)])  54 us
    ppermute x13, waiting for transfers between devices, exchange(): return lax.ppermute(array, axis, [(i, i ^ distance) for i in range(size)])  39.2 us
    all_to_all x1, blocking collectives, body(): parts = lax.all_to_all(term, ('x', 'z'), 0, 0, tiled=True)  38.3 us
    all_to_all x1, blocking collectives, body(): whole = lax.all_to_all(piece, 'y', 0, 0, tiled=True)  15.6 us
    all_gather x1, blocking collectives, body(): piece = lax.all_gather(piece, 'x', axis=0).astype(F32).sum(0).astype(BF16)  10.7 us
    all_to_all x1, starting transfers between devices, body(): panel = lax.all_to_all(chunks, ('y', 'x'), 0, 0, tiled=True)  10.6 us
    all_to_all x1, starting transfers between devices, body(): grad_mine = lax.all_to_all(grad, ('x', 'z'), 0, 0, tiled=True)  7.95 us
    all_to_all x1, starting transfers between devices, body(): back = lax.all_to_all(back, ('y', 'x'), 0, 0, tiled=True)  6.72 us
  transfers between devices with their start and end apart: 16, of which 12 were waited for; matrix products, arithmetic and copies ran while one was open for 0% of the time, Pallas kernels for 0%

profile of v6, /device:TPU:1, one launch (start us, length us, event | category | flops | bytes accessed | tf_op | source)
XLA Modules:
  0.0 196.4 jit_solution(3338274990206525186)
XLA Ops:
  0.6 0.0 copy-start.2
  0.6 0.9 copy-done.2
  1.5 1.1 spread.1
  2.6 0.0 copy-start.8
  2.6 0.0 copy-start.6
  2.6 0.0 copy-start.7
  2.7 0.0 copy-start.5
  2.7 10.6 %all-to-all-start = ((bf16[32,128,128]{2,1,0:T(8,128)(2,1)}), bf16[32,128,128]{2,1,0:T(8,128)(2,1)S(1)}, u32[]{:S(2)}, u32[]{:S(2)}) async-start(bf16[32,128,128]{2,1,0:T(8,128)(2,1)} %spread.1), calls=%async_computation | async-start | bytes 2097152 | tf_op jit(solution)/shard_map/all_to_all | solution.py:162
  13.3 0.0 copy-done.8
  13.3 0.0 copy-done.6
  13.3 0.0 copy-done.7
  13.4 0.1 fusion.11
  13.5 0.0 copy-done.4
  13.5 4.3 %collective-permute-start.2 = (bf16[1040,128]{1,0:T(8,128)(2,1)S(1)}, bf16[1040,128]{1,0:T(8,128)(2,1)S(1)}, u32[]{:S(2)}, u32[]{:S(2)}) collective-permute-start(bf16[1040,128]{1,0:T(8,128)(2,1)S(1)} %pad_maximum_fusion.refs_0_), channel_id=1, source_target_pairs={{0,48},{16,32},{32,16},{48,0},{1,49},{17,33},{33,17},{49,1},{2,50}... | collective-permute-start | bytes 798728 | tf_op jit(solution)/shard_map/ppermute | solution.py:136
  17.8 2.5 %collective-permute-start.1 = (bf16[1040,128]{1,0:T(8,128)(2,1)S(1)}, bf16[1040,128]{1,0:T(8,128)(2,1)S(1)}, u32[]{:S(2)}, u32[]{:S(2)}) collective-permute-start(bf16[1040,128]{1,0:T(8,128)(2,1)S(1)} %pad_maximum_fusion.refs_0_), channel_id=1, source_target_pairs={{0,32},{16,48},{32,0},{48,16},{1,33},{17,49},{33,1},{49,17},{2,34}... | collective-permute-start | bytes 798728 | tf_op jit(solution)/shard_map/ppermute | solution.py:136
  20.3 2.1 %collective-permute-start = (bf16[1040,128]{1,0:T(8,128)(2,1)S(1)}, bf16[1040,128]{1,0:T(8,128)(2,1)S(1)}, u32[]{:S(2)}, u32[]{:S(2)}) collective-permute-start(bf16[1040,128]{1,0:T(8,128)(2,1)S(1)} %pad_maximum_fusion.refs_0_), channel_id=1, source_target_pairs={{0,16},{16,0},{32,48},{48,32},{1,17},{17,1},{33,49},{49,33},{2,18}... | collective-permute-start | bytes 798728 | tf_op jit(solution)/shard_map/ppermute | solution.py:136
  22.5 0.0 copy-done.5
  22.5 0.1 broadcast_in_dim.4
  22.6 0.1 min.23
  22.7 0.1 pad_add_fusion.place_ref.core_ref
  22.7 14.6 %collective-permute-done.2.refs_3_ = bf16[1040,128]{1,0:T(8,128)(2,1)S(1)} collective-permute-done((bf16[1040,128]{1,0:T(8,128)(2,1)S(1)}, bf16[1040,128]{1,0:T(8,128)(2,1)S(1)}, u32[]{:S(2)}, u32[]{:S(2)}) %collective-permute-start.2) | collective-permute-done | bytes 266272 | tf_op jit(solution)/shard_map/ppermute | solution.py:136
  37.4 0.0 collective-permute-done.1.refs_2_
  37.4 3.7 %collective-permute-done.refs_1_ = bf16[1040,128]{1,0:T(8,128)(2,1)S(1)} collective-permute-done((bf16[1040,128]{1,0:T(8,128)(2,1)S(1)}, bf16[1040,128]{1,0:T(8,128)(2,1)S(1)}, u32[]{:S(2)}, u32[]{:S(2)}) %collective-permute-start) | collective-permute-done | bytes 266272 | tf_op jit(solution)/shard_map/ppermute | solution.py:136
  41.1 0.1 maximum_minimum_fusion.index_ref
  41.2 0.0 all-to-all-done.panel_ref
  41.2 1.5 forward_tiles.1
  42.7 3.1 %collective-permute-start.3 = (bf16[32,128,128]{2,1,0:T(8,128)(2,1)S(1)}, bf16[32,128,128]{2,1,0:T(8,128)(2,1)S(1)}, u32[]{:S(2)}, u32[]{:S(2)}) collective-permute-start(bf16[32,128,128]{2,1,0:T(8,128)(2,1)S(1)} %get-tuple-element.16), channel_id=1, source_target_pairs={{0,1},{1,0},{2,3},{3,2},{4,5},{5,4},{6,7},{7,6},{8,9},{9,8},{10,11... | collective-permute-start | bytes 3145736 | tf_op jit(solution)/shard_map/ppermute | solution.py:136
  45.8 2.3 %collective-permute-done.3 = bf16[32,128,128]{2,1,0:T(8,128)(2,1)S(1)} collective-permute-done((bf16[32,128,128]{2,1,0:T(8,128)(2,1)S(1)}, bf16[32,128,128]{2,1,0:T(8,128)(2,1)S(1)}, u32[]{:S(2)}, u32[]{:S(2)}) %collective-permute-start.3) | collective-permute-done | bytes 1048608 | tf_op jit(solution)/shard_map/ppermute | solution.py:136
  48.1 0.4 add_convert_fusion
  48.4 0.0 copy-start
  48.4 0.0 copy-start.3
  48.5 38.3 %all_to_all.25.parts_ref = bf16[32,128,128]{2,1,0:T(8,128)(2,1)S(1)} all-to-all(bf16[32,128,128]{2,1,0:T(8,128)(2,1)S(1)} %add_convert_fusion), channel_id=1, replica_groups=mesh['y'=8,'x'=4,'z'=8,'core'=2] {'x','z'}, dimensions={0} | all-to-all | bytes 2097152 | tf_op jit(solution)/shard_map/all_to_all | solution.py:184
  86.7 0.0 copy-done
  86.7 0.0 copy-done.3
  86.7 1.7 middle.1
  88.4 1.0 copy-done.1
  89.4 7.9 %all-to-all-start.2 = ((bf16[32,128,128]{2,1,0:T(8,128)(2,1)}), bf16[32,128,128]{2,1,0:T(8,128)(2,1)S(1)}, u32[]{:S(2)}, u32[]{:S(2)}) async-start(bf16[32,128,128]{2,1,0:T(8,128)(2,1)} %copy-done.1), calls=%async_computation.2 | async-start | bytes 2097152 | tf_op jit(solution)/shard_map/all_to_all | solution.py:201
  97.4 3.4 %collective-permute-start.4 = (bf16[256,512]{1,0:T(8,128)(2,1)S(1)}, bf16[256,512]{1,0:T(8,128)(2,1)S(1)}, u32[]{:S(2)}, u32[]{:S(2)}) collective-permute-start(bf16[256,512]{1,0:T(8,128)(2,1)S(1)} %get-tuple-element.20), channel_id=1, source_target_pairs={{0,1},{1,0},{2,3},{3,2},{4,5},{5,4},{6,7},{7,6},{8,9},{9,8},{10,11... | collective-permute-start | bytes 786440 | tf_op jit(solution)/shard_map/ppermute | solution.py:136
  100.8 1.1 collective-permute-done.4
  101.9 0.1 add_convert_fusion.1
  102.0 2.2 %collective-permute-start.5 = (bf16[128,512]{1,0:T(8,128)(2,1)S(1)}, bf16[128,512]{1,0:T(8,128)(2,1)S(1)}, u32[]{:S(2)}, u32[]{:S(2)}) collective-permute-start(bf16[128,512]{1,0:T(8,128)(2,1)S(1)} %dynamic-slice_bitcast_fusion), channel_id=1, source_target_pairs={{0,64},{64,0},{128,192},{192,128},{256,320},{320,256},{384,448},{4... | collective-permute-start | bytes 393224 | tf_op jit(solution)/shard_map/ppermute | solution.py:136
  104.3 4.4 %collective-permute-done.5 = bf16[128,512]{1,0:T(8,128)(2,1)S(1)} collective-permute-done((bf16[128,512]{1,0:T(8,128)(2,1)S(1)}, bf16[128,512]{1,0:T(8,128)(2,1)S(1)}, u32[]{:S(2)}, u32[]{:S(2)}) %collective-permute-start.5) | collective-permute-done | bytes 131104 | tf_op jit(solution)/shard_map/ppermute | solution.py:136
  108.7 3.0 %collective-permute-start.6 = (bf16[64,512]{1,0:T(8,128)(2,1)S(1)}, bf16[64,512]{1,0:T(8,128)(2,1)S(1)}, u32[]{:S(2)}, u32[]{:S(2)}) collective-permute-start(bf16[64,512]{1,0:T(8,128)(2,1)S(1)} %dynamic-slice_bitcast_fusion.1), channel_id=1, source_target_pairs={{0,128},{64,192},{128,0},{192,64},{256,384},{320,448},{384,256},{4... | collective-permute-start | bytes 196616 | tf_op jit(solution)/shard_map/ppermute | solution.py:136
  111.7 3.9 %collective-permute-done.6 = bf16[64,512]{1,0:T(8,128)(2,1)S(1)} collective-permute-done((bf16[64,512]{1,0:T(8,128)(2,1)S(1)}, bf16[64,512]{1,0:T(8,128)(2,1)S(1)}, u32[]{:S(2)}, u32[]{:S(2)}) %collective-permute-start.6) | collective-permute-done | bytes 65568 | tf_op jit(solution)/shard_map/ppermute | solution.py:136
  115.6 4.3 %collective-permute-start.7 = (bf16[32,512]{1,0:T(8,128)(2,1)S(1)}, bf16[32,512]{1,0:T(8,128)(2,1)S(1)}, u32[]{:S(2)}, u32[]{:S(2)}) collective-permute-start(bf16[32,512]{1,0:T(8,128)(2,1)S(1)} %dynamic-slice_bitcast_fusion.2), channel_id=1, source_target_pairs={{0,256},{64,320},{128,384},{192,448},{256,0},{320,64},{384,128},{4... | collective-permute-start | bytes 98312 | tf_op jit(solution)/shard_map/ppermute | solution.py:136
  119.9 4.3 %collective-permute-done.7 = bf16[32,512]{1,0:T(8,128)(2,1)S(1)} collective-permute-done((bf16[32,512]{1,0:T(8,128)(2,1)S(1)}, bf16[32,512]{1,0:T(8,128)(2,1)S(1)}, u32[]{:S(2)}, u32[]{:S(2)}) %collective-permute-start.7) | collective-permute-done | bytes 32800 | tf_op jit(solution)/shard_map/ppermute | solution.py:136
  124.2 0.0 all-to-all-done.2.mine_ref
  124.2 5.1 %collective-permute-start.8 = (bf16[32,128,128]{2,1,0:T(8,128)(2,1)S(1)}, bf16[32,128,128]{2,1,0:T(8,128)(2,1)S(1)}, u32[]{:S(2)}, u32[]{:S(2)}) collective-permute-start(bf16[32,128,128]{2,1,0:T(8,128)(2,1)S(1)} %all-to-all-done.2.mine_ref), channel_id=1, source_target_pairs={{0,1},{1,0},{2,3},{3,2},{4,5},{5,4},{6,7},{7,6},{8,9},{9,8},{10,11... | collective-permute-start | bytes 3145736 | tf_op jit(solution)/shard_map/ppermute | solution.py:136
  129.4 3.4 %collective-permute-start.9 = (bf16[32,512]{1,0:T(8,128)(2,1)S(1)}, bf16[32,512]{1,0:T(8,128)(2,1)S(1)}, u32[]{:S(2)}, u32[]{:S(2)}) collective-permute-start(bf16[32,512]{1,0:T(8,128)(2,1)S(1)} %fusion.2), channel_id=1, source_target_pairs={{0,2},{2,0},{4,6},{6,4},{8,10},{10,8},{12,14},{14,12},{1,3},{3,1},... | collective-permute-start | bytes 98312 | tf_op jit(solution)/shard_map/ppermute | solution.py:136
  132.8 1.3 collective-permute-done.9
  134.1 0.0 collective-permute-done.8.other_ref
  134.1 2.4 %backward_tiles.1 = bf16[32,128,128]{2,1,0:T(8,128)(2,1)} custom-call(s32[2]{0:T(128)S(1)} %pad_add_fusion.place_ref.core_ref, s32[4,24]{1,0:T(4,128)S(1)} %maximum_minimum_fusion.index_ref, bf16[32,128,128]{2,1,0:T(8,128)(2,1)S(1)} %all-to-all-done.2.mine_ref, bf16[32,128,128]{2,1,0:T(8,128)(2,1)S(1)} %collective-permute-done.8.other_ref, ...), custom_call_target="tpu_custom_call" | custom-call | tf_op jit(solution)/shard_map/backward_tiles/pallas_call | solution.py:210
  136.5 6.7 %all-to-all-start.3 = ((bf16[32,128,128]{2,1,0:T(8,128)(2,1)}), bf16[32,128,128]{2,1,0:T(8,128)(2,1)S(1)}, u32[]{:S(2)}, u32[]{:S(2)}) async-start(bf16[32,128,128]{2,1,0:T(8,128)(2,1)} %backward_tiles.1), calls=%async_computation.3 | async-start | bytes 2097152 | tf_op jit(solution)/shard_map/all_to_all | solution.py:220
  143.2 4.0 %collective-permute-start.10 = (bf16[32,512]{1,0:T(8,128)(2,1)S(1)}, bf16[32,512]{1,0:T(8,128)(2,1)S(1)}, u32[]{:S(2)}, u32[]{:S(2)}) collective-permute-start(bf16[32,512]{1,0:T(8,128)(2,1)S(1)} %add_convert_fusion.4), channel_id=1, source_target_pairs={{0,4},{2,6},{4,0},{6,2},{8,12},{10,14},{12,8},{14,10},{1,5},{3,7},... | collective-permute-start | bytes 98312 | tf_op jit(solution)/shard_map/ppermute | solution.py:136
  147.2 1.9 collective-permute-done.10
  149.1 7.4 %collective-permute-start.11 = (bf16[32,512]{1,0:T(8,128)(2,1)S(1)}, bf16[32,512]{1,0:T(8,128)(2,1)S(1)}, u32[]{:S(2)}, u32[]{:S(2)}) collective-permute-start(bf16[32,512]{1,0:T(8,128)(2,1)S(1)} %add_convert_fusion.3), channel_id=1, source_target_pairs={{0,8},{2,10},{4,12},{6,14},{8,0},{10,2},{12,4},{14,6},{1,9},{3,11}... | collective-permute-start | bytes 98312 | tf_op jit(solution)/shard_map/ppermute | solution.py:136
  156.4 1.6 collective-permute-done.11
  158.0 10.7 %all-gather = bf16[128,512]{1,0:T(8,128)(2,1)S(1)} all-gather(bf16[32,512]{1,0:T(8,128)(2,1)S(1)} %add_convert_fusion.2), channel_id=2, replica_groups=mesh['y'=8,'x'=4,'z'=8,'core'=2] {'x'}, dimensions={0}, use_global_device_ids=true | all-gather | bytes 163840 | tf_op jit(solution)/shard_map/all_gather | solution.py:223
  168.7 0.2 all-to-all-done.3.parts_ref
  168.9 15.6 %all_to_all.26.mine_ref = bf16[8,32,512]{2,1,0:T(8,128)(2,1)S(1)} all-to-all(bf16[8,32,512]{2,1,0:T(8,128)(2,1)S(1)} %broadcast_in_dim.5), channel_id=1, replica_groups=mesh['y'=8,'x'=4,'z'=8,'core'=2] {'y'}, dimensions={0} | all-to-all | bytes 524288 | tf_op jit(solution)/shard_map/all_to_all | solution.py:237
  184.6 9.1 %collective-permute-start.12 = (bf16[8,32,512]{2,1,0:T(8,128)(2,1)S(1)}, bf16[8,32,512]{2,1,0:T(8,128)(2,1)S(1)}, u32[]{:S(2)}, u32[]{:S(2)}) collective-permute-start(bf16[8,32,512]{2,1,0:T(8,128)(2,1)S(1)} %all_to_all.26.mine_ref), channel_id=1, source_target_pairs={{0,1},{1,0},{2,3},{3,2},{4,5},{5,4},{6,7},{7,6},{8,9},{9,8},{10,11... | collective-permute-start | bytes 786440 | tf_op jit(solution)/shard_map/ppermute | solution.py:136
  193.7 1.0 last.1
  194.7 0.2 collective-permute-done.12.other_ref
  194.8 1.6 place_rows.1
  (19 shorter events, 0.2 us)
Async XLA Ops:
  0.6 0.9 copy-start.2
  2.6 10.7 %copy-start.8 = (s32[1,1,8]{2,1,0:T(1,128)S(1)}, s32[1,1,8]{2,1,0:T(1,128)}, u32[]{:S(2)}) copy-start(s32[1,1,8]{2,1,0:T(1,128)} %param.12) | copy-start | bytes 100
  2.6 10.7 %copy-start.6 = (s32[1,1,8]{2,1,0:T(1,128)S(1)}, s32[1,1,8]{2,1,0:T(1,128)}, u32[]{:S(2)}) copy-start(s32[1,1,8]{2,1,0:T(1,128)} %param.14) | copy-start | bytes 100
  2.6 10.7 %copy-start.7 = (s32[1,1,8]{2,1,0:T(1,128)S(1)}, s32[1,1,8]{2,1,0:T(1,128)}, u32[]{:S(2)}) copy-start(s32[1,1,8]{2,1,0:T(1,128)} %param.13) | copy-start | bytes 100
  2.6 10.8 %copy-start.4 = (bf16[1,1,8,128,128]{4,3,2,1,0:T(8,128)(2,1)S(1)}, bf16[1,1,8,128,128]{4,3,2,1,0:T(8,128)(2,1)}, u32[]{:S(2)}) copy-start(bf16[1,1,8,128,128]{4,3,2,1,0:T(8,128)(2,1)} %param.11) | copy-start | bytes 786436
  2.7 19.8 %copy-start.5 = (s32[3]{0:T(128)S(1)}, s32[3]{0:T(128)}, u32[]{:S(2)}) copy-start(s32[3]{0:T(128)} %constant.52.clone) | copy-start | bytes 40
  2.7 38.5 %all-to-all-start = ((bf16[32,128,128]{2,1,0:T(8,128)(2,1)}), bf16[32,128,128]{2,1,0:T(8,128)(2,1)S(1)}, u32[]{:S(2)}, u32[]{:S(2)}) async-start(bf16[32,128,128]{2,1,0:T(8,128)(2,1)} %spread.1), calls=%async_computation | async-start | bytes 2097152 | tf_op jit(solution)/shard_map/all_to_all | solution.py:162
  13.5 23.9 %collective-permute-start.2 = (bf16[1040,128]{1,0:T(8,128)(2,1)S(1)}, bf16[1040,128]{1,0:T(8,128)(2,1)S(1)}, u32[]{:S(2)}, u32[]{:S(2)}) collective-permute-start(bf16[1040,128]{1,0:T(8,128)(2,1)S(1)} %pad_maximum_fusion.refs_0_), channel_id=1, source_target_pairs={{0,48},{16,32},{32,16},{48,0},{1,49},{17,33},{33,17},{49,1},{2,50}... | collective-permute-start | bytes 798728 | tf_op jit(solution)/shard_map/ppermute | solution.py:136
  17.8 19.5 %collective-permute-start.1 = (bf16[1040,128]{1,0:T(8,128)(2,1)S(1)}, bf16[1040,128]{1,0:T(8,128)(2,1)S(1)}, u32[]{:S(2)}, u32[]{:S(2)}) collective-permute-start(bf16[1040,128]{1,0:T(8,128)(2,1)S(1)} %pad_maximum_fusion.refs_0_), channel_id=1, source_target_pairs={{0,32},{16,48},{32,0},{48,16},{1,33},{17,49},{33,1},{49,17},{2,34}... | collective-permute-start | bytes 798728 | tf_op jit(solution)/shard_map/ppermute | solution.py:136
  20.3 20.7 %collective-permute-start = (bf16[1040,128]{1,0:T(8,128)(2,1)S(1)}, bf16[1040,128]{1,0:T(8,128)(2,1)S(1)}, u32[]{:S(2)}, u32[]{:S(2)}) collective-permute-start(bf16[1040,128]{1,0:T(8,128)(2,1)S(1)} %pad_maximum_fusion.refs_0_), channel_id=1, source_target_pairs={{0,16},{16,0},{32,48},{48,32},{1,17},{17,1},{33,49},{49,33},{2,18}... | collective-permute-start | bytes 798728 | tf_op jit(solution)/shard_map/ppermute | solution.py:136
  42.7 5.4 %collective-permute-start.3 = (bf16[32,128,128]{2,1,0:T(8,128)(2,1)S(1)}, bf16[32,128,128]{2,1,0:T(8,128)(2,1)S(1)}, u32[]{:S(2)}, u32[]{:S(2)}) collective-permute-start(bf16[32,128,128]{2,1,0:T(8,128)(2,1)S(1)} %get-tuple-element.16), channel_id=1, source_target_pairs={{0,1},{1,0},{2,3},{3,2},{4,5},{5,4},{6,7},{7,6},{8,9},{9,8},{10,11... | collective-permute-start | bytes 3145736 | tf_op jit(solution)/shard_map/ppermute | solution.py:136
  48.4 38.3 %copy-start = (bf16[512,512]{1,0:T(8,128)(2,1)S(1)}, bf16[512,512]{1,0:T(8,128)(2,1)}, u32[]{:S(2)}) copy-start(bf16[512,512]{1,0:T(8,128)(2,1)} %weight_ref.3) | copy-start | bytes 1572868
  48.4 38.3 %copy-start.3 = (bf16[128,512]{1,0:T(8,128)(2,1)S(1)}, bf16[128,512]{1,0:T(8,128)(2,1)}, u32[]{:S(2)}) copy-start(bf16[128,512]{1,0:T(8,128)(2,1)} %cotangent_ref.1) | copy-start | bytes 393220
  88.4 1.0 copy-start.1
  89.4 34.8 %all-to-all-start.2 = ((bf16[32,128,128]{2,1,0:T(8,128)(2,1)}), bf16[32,128,128]{2,1,0:T(8,128)(2,1)S(1)}, u32[]{:S(2)}, u32[]{:S(2)}) async-start(bf16[32,128,128]{2,1,0:T(8,128)(2,1)} %copy-done.1), calls=%async_computation.2 | async-start | bytes 2097152 | tf_op jit(solution)/shard_map/all_to_all | solution.py:201
  97.4 4.6 %collective-permute-start.4 = (bf16[256,512]{1,0:T(8,128)(2,1)S(1)}, bf16[256,512]{1,0:T(8,128)(2,1)S(1)}, u32[]{:S(2)}, u32[]{:S(2)}) collective-permute-start(bf16[256,512]{1,0:T(8,128)(2,1)S(1)} %get-tuple-element.20), channel_id=1, source_target_pairs={{0,1},{1,0},{2,3},{3,2},{4,5},{5,4},{6,7},{7,6},{8,9},{9,8},{10,11... | collective-permute-start | bytes 786440 | tf_op jit(solution)/shard_map/ppermute | solution.py:136
  102.0 6.6 %collective-permute-start.5 = (bf16[128,512]{1,0:T(8,128)(2,1)S(1)}, bf16[128,512]{1,0:T(8,128)(2,1)S(1)}, u32[]{:S(2)}, u32[]{:S(2)}) collective-permute-start(bf16[128,512]{1,0:T(8,128)(2,1)S(1)} %dynamic-slice_bitcast_fusion), channel_id=1, source_target_pairs={{0,64},{64,0},{128,192},{192,128},{256,320},{320,256},{384,448},{4... | collective-permute-start | bytes 393224 | tf_op jit(solution)/shard_map/ppermute | solution.py:136
  108.7 6.9 %collective-permute-start.6 = (bf16[64,512]{1,0:T(8,128)(2,1)S(1)}, bf16[64,512]{1,0:T(8,128)(2,1)S(1)}, u32[]{:S(2)}, u32[]{:S(2)}) collective-permute-start(bf16[64,512]{1,0:T(8,128)(2,1)S(1)} %dynamic-slice_bitcast_fusion.1), channel_id=1, source_target_pairs={{0,128},{64,192},{128,0},{192,64},{256,384},{320,448},{384,256},{4... | collective-permute-start | bytes 196616 | tf_op jit(solution)/shard_map/ppermute | solution.py:136
  115.6 8.6 %collective-permute-start.7 = (bf16[32,512]{1,0:T(8,128)(2,1)S(1)}, bf16[32,512]{1,0:T(8,128)(2,1)S(1)}, u32[]{:S(2)}, u32[]{:S(2)}) collective-permute-start(bf16[32,512]{1,0:T(8,128)(2,1)S(1)} %dynamic-slice_bitcast_fusion.2), channel_id=1, source_target_pairs={{0,256},{64,320},{128,384},{192,448},{256,0},{320,64},{384,128},{4... | collective-permute-start | bytes 98312 | tf_op jit(solution)/shard_map/ppermute | solution.py:136
  124.2 9.9 %collective-permute-start.8 = (bf16[32,128,128]{2,1,0:T(8,128)(2,1)S(1)}, bf16[32,128,128]{2,1,0:T(8,128)(2,1)S(1)}, u32[]{:S(2)}, u32[]{:S(2)}) collective-permute-start(bf16[32,128,128]{2,1,0:T(8,128)(2,1)S(1)} %all-to-all-done.2.mine_ref), channel_id=1, source_target_pairs={{0,1},{1,0},{2,3},{3,2},{4,5},{5,4},{6,7},{7,6},{8,9},{9,8},{10,11... | collective-permute-start | bytes 3145736 | tf_op jit(solution)/shard_map/ppermute | solution.py:136
  129.4 4.7 %collective-permute-start.9 = (bf16[32,512]{1,0:T(8,128)(2,1)S(1)}, bf16[32,512]{1,0:T(8,128)(2,1)S(1)}, u32[]{:S(2)}, u32[]{:S(2)}) collective-permute-start(bf16[32,512]{1,0:T(8,128)(2,1)S(1)} %fusion.2), channel_id=1, source_target_pairs={{0,2},{2,0},{4,6},{6,4},{8,10},{10,8},{12,14},{14,12},{1,3},{3,1},... | collective-permute-start | bytes 98312 | tf_op jit(solution)/shard_map/ppermute | solution.py:136
  136.5 32.4 %all-to-all-start.3 = ((bf16[32,128,128]{2,1,0:T(8,128)(2,1)}), bf16[32,128,128]{2,1,0:T(8,128)(2,1)S(1)}, u32[]{:S(2)}, u32[]{:S(2)}) async-start(bf16[32,128,128]{2,1,0:T(8,128)(2,1)} %backward_tiles.1), calls=%async_computation.3 | async-start | bytes 2097152 | tf_op jit(solution)/shard_map/all_to_all | solution.py:220
  143.2 5.9 %collective-permute-start.10 = (bf16[32,512]{1,0:T(8,128)(2,1)S(1)}, bf16[32,512]{1,0:T(8,128)(2,1)S(1)}, u32[]{:S(2)}, u32[]{:S(2)}) collective-permute-start(bf16[32,512]{1,0:T(8,128)(2,1)S(1)} %add_convert_fusion.4), channel_id=1, source_target_pairs={{0,4},{2,6},{4,0},{6,2},{8,12},{10,14},{12,8},{14,10},{1,5},{3,7},... | collective-permute-start | bytes 98312 | tf_op jit(solution)/shard_map/ppermute | solution.py:136
  149.1 9.0 %collective-permute-start.11 = (bf16[32,512]{1,0:T(8,128)(2,1)S(1)}, bf16[32,512]{1,0:T(8,128)(2,1)S(1)}, u32[]{:S(2)}, u32[]{:S(2)}) collective-permute-start(bf16[32,512]{1,0:T(8,128)(2,1)S(1)} %add_convert_fusion.3), channel_id=1, source_target_pairs={{0,8},{2,10},{4,12},{6,14},{8,0},{10,2},{12,4},{14,6},{1,9},{3,11}... | collective-permute-start | bytes 98312 | tf_op jit(solution)/shard_map/ppermute | solution.py:136
  184.6 10.3 %collective-permute-start.12 = (bf16[8,32,512]{2,1,0:T(8,128)(2,1)S(1)}, bf16[8,32,512]{2,1,0:T(8,128)(2,1)S(1)}, u32[]{:S(2)}, u32[]{:S(2)}) collective-permute-start(bf16[8,32,512]{2,1,0:T(8,128)(2,1)S(1)} %all_to_all.26.mine_ref), channel_id=1, source_target_pairs={{0,1},{1,0},{2,3},{3,2},{4,5},{5,4},{6,7},{7,6},{8,9},{9,8},{10,11... | collective-permute-start | bytes 786440 | tf_op jit(solution)/shard_map/ppermute | solution.py:136

commit v7 on v6

--- a/solution.py
+++ b/solution.py
@@ -12,6 +12,7 @@
 SLOTS = 8
 WIDTH = 512
 CHUNK = WIDTH // X
+HALF = CHUNK // CORES
 ROW_TILES = Z * CORES
 COL_TILES = Y * X
 INDEX_ROWS = 16
@@ -54,6 +55,20 @@
         for pair in range(Z):
             mine_ref[block * Z + pair] = total[2 * pair + core].astype(BF16)
             other_ref[block * Z + pair] = total[2 * pair + 1 - core].astype(BF16)
+
+
+def split_lanes(tile):
+    rows = TILE // 2
+    top, bottom = tile[:rows], tile[rows:]
+    left = jnp.concatenate([top[:, :HALF], bottom[:, :HALF]], axis=1)
+    right = jnp.concatenate([top[:, HALF:], bottom[:, HALF:]], axis=1)
+    return left, right
+
+
+def join_lanes(left, right):
+    top = jnp.concatenate([left[:, :HALF], right[:, :HALF]], axis=1)
+    bottom = jnp.concatenate([left[:, HALF:], right[:, HALF:]], axis=1)
+    return jnp.concatenate([top, bottom], axis=0)
 
 
 def middle(core_ref, parts_ref, weight_ref, cotangent_ref, act_ref, grad_ref, keep_ref, send_ref):
@@ -74,9 +89,10 @@
     act_ref[...] = (aggregated * sig).astype(BF16)
     grad = (cotangent_ref[...].astype(F32) * sig * (1.0 + aggregated * (1.0 - sig))).astype(BF16)
     for chunk in range(X):
-        piece = grad[:, chunk * CHUNK : (chunk + 1) * CHUNK]
-        for z in range(Z):
-            grad_ref[chunk * Z + z] = piece
+        both = grad[:, chunk * CHUNK : (chunk + 1) * CHUNK]
+        for core, piece in enumerate(split_lanes(both)):
+            for z in range(Z):
+                grad_ref[(chunk * Z + z) * CORES + core] = piece
     weight_part = lax.dot_general(
         high, grad, (((0,), (0,)), ((), ())), preferred_element_type=F32
     ).astype(BF16)
@@ -86,34 +102,41 @@
     send_ref[...] = jnp.where(upper, low_half, high_half)
 
 
-def backward_tiles(place_ref, index_ref, mine_ref, other_ref, *refs):
-    tiles_refs, (out_ref, total) = refs[:X], refs[X:]
-    core = place_ref[0]
+def backward_tiles(place_ref, index_ref, grad_ref, *refs):
+    tiles_refs, (out_ref, panel, total) = refs[: CORES * X], refs[CORES * X :]
+    for tile in range(X * ROW_TILES):
+        piece = grad_ref[tile]
+        panel[tile] = join_lanes(piece, piece)
     total[...] = jnp.zeros_like(total)
-    for step in range(X):
-        block = place_ref[1] ^ step
+    right = lax.broadcasted_iota(jnp.int32, (TILE, CHUNK), 1) // HALF
+    for step in range(CORES * X):
+        core = place_ref[0] ^ (step // X)
+        block = place_ref[1] ^ (step % X)
+        mine = right == core
         for slot in range(SLOTS):
             row = index_ref[step, slot]
             col = index_ref[step, SLOTS + slot]
             valid = index_ref[step, 2 * SLOTS + slot]
-            at = block * Z + row // 2
-            panel = jnp.where(row % 2 == core, mine_ref[at], other_ref[at])
             tile = tiles_refs[step][slot * TILE : (slot + 1) * TILE, :]
             product = lax.dot_general(
-                tile, panel, (((0,), (0,)), ((), ())), preferred_element_type=F32
+                tile, panel[block * ROW_TILES + row], (((0,), (0,)), ((), ())), preferred_element_type=F32
             )
-            total[col] += jnp.where(valid > 0, product, 0.0)
+            total[col] += jnp.where(mine & (valid > 0), product, 0.0)
     for tile in range(COL_TILES):
-        out_ref[tile] = total[tile].astype(BF16)
+        for core, piece in enumerate(split_lanes(total[tile].astype(BF16))):
+            out_ref[tile * CORES + core] = piece
 
 
 def last(parts_ref, weight_ref, out_ref):
     chunks = []
     for chunk in range(X):
-        total = parts_ref[chunk].astype(F32)
-        for y in range(1, Y):
-            total += parts_ref[y * X + chunk].astype(F32)
-        chunks.append(total)
+        halves = []
+        for core in range(CORES):
+            total = parts_ref[chunk * CORES + core].astype(F32)
+            for y in range(1, Y):
+                total += parts_ref[(y * X + chunk) * CORES + core].astype(F32)
+            halves.append(total)
+        chunks.append(join_lanes(*halves))
     summed = jnp.concatenate(chunks, axis=1).astype(BF16)
     out_ref[...] = lax.dot_general(
         summed, weight_ref[...], (((1,), (1,)), ((), ())), preferred_element_type=F32
@@ -148,6 +171,12 @@
     return (array.astype(F32) + exchange(array, axis, distance).astype(F32)).astype(BF16)
 
 
+def slots_of(tiles):
+    index = jnp.stack([t[SLOTS * TILE, : 3 * SLOTS] for t in tiles]).astype(jnp.int32)
+    limit = jnp.repeat(jnp.array([ROW_TILES - 1, COL_TILES - 1, 1], jnp.int32), SLOTS)
+    return jnp.clip(index, 0, limit[None, :])
+
+
 def body(features, weight, cotangent, tile_values, tile_rows, tile_cols, tile_valid):
     place = jnp.stack([lax.axis_index("core"), lax.axis_index("x")]).astype(jnp.int32)
 
@@ -167,9 +196,7 @@
     index = jnp.pad(index[None, :], ((0, INDEX_ROWS - 1), (0, TILE - 3 * SLOTS)))
     tiles = jnp.concatenate([tile_values.reshape(SLOTS * TILE, TILE), index], axis=0)
     tiles = [tiles] + [exchange(tiles, "x", distance) for distance in range(1, X)]
-    index = jnp.stack([t[SLOTS * TILE, : 3 * SLOTS] for t in tiles]).astype(jnp.int32)
-    limit = jnp.repeat(jnp.array([ROW_TILES - 1, COL_TILES - 1, 1], jnp.int32), SLOTS)
-    index = jnp.clip(index, 0, limit[None, :])
+    index = slots_of(tiles)
 
     mine, other = pl.pallas_call(
         forward_tiles,
@@ -181,7 +208,11 @@
         name="forward_tiles",
     )(place, index, panel, *tiles)
     term = (mine.astype(F32) + exchange(other, "core", 1).astype(F32)).astype(BF16)
+    term, *theirs = lax.optimization_barrier((term, *tiles))
     parts = lax.all_to_all(term, ("x", "z"), 0, 0, tiled=True)
+    theirs = [exchange(t, "core", 1) for t in theirs]
+    all_index = jnp.concatenate([index, slots_of(theirs)])
+    parts, all_index, *theirs = lax.optimization_barrier((parts, all_index, *theirs))
 
     half = WIDTH // CORES
     activations, grad, weight_keep, weight_send = pl.pallas_call(
@@ -190,7 +221,7 @@
         out_specs=[vmem()] * 4,
         out_shape=[
             jax.ShapeDtypeStruct((TILE, WIDTH), BF16),
-            jax.ShapeDtypeStruct((X * Z, TILE, CHUNK), BF16),
+            jax.ShapeDtypeStruct((X * ROW_TILES, TILE // 2, CHUNK), BF16),
             jax.ShapeDtypeStruct((half, WIDTH), BF16),
             jax.ShapeDtypeStruct((half, WIDTH), BF16),
         ],
@@ -198,26 +229,28 @@
         name="middle",
     )(place, parts, weight, cotangent)
 
-    grad_mine = lax.all_to_all(grad, ("x", "z"), 0, 0, tiled=True)
+    panel = lax.all_to_all(grad, ("x", "z", "core"), 0, 0, tiled=True)
     piece = weight_keep.astype(F32) + exchange(weight_send, "core", 1).astype(F32)
     piece = piece.astype(BF16)
     for distance in (1, 2, 4):
         piece = halve(piece, "y", distance)
-    grad_mine, piece = lax.optimization_barrier((grad_mine, piece))
-
-    grad_other = exchange(grad_mine, "core", 1)
+    panel, piece = lax.optimization_barrier((panel, piece))
+
     piece = double(piece, "z", 1)
     back = pl.pallas_call(
         backward_tiles,
-        in_specs=[smem(), smem()] + [vmem()] * (2 + X),
+        in_specs=[smem(), smem()] + [vmem()] * (1 + CORES * X),
         out_specs=vmem(),
-        out_shape=jax.ShapeDtypeStruct((COL_TILES, TILE, CHUNK), BF16),
-        scratch_shapes=[pltpu.VMEM((COL_TILES, TILE, CHUNK), F32)],
+        out_shape=jax.ShapeDtypeStruct((COL_TILES * CORES, TILE // 2, CHUNK), BF16),
+        scratch_shapes=[
+            pltpu.VMEM((X * ROW_TILES, TILE, CHUNK), BF16),
+            pltpu.VMEM((COL_TILES, TILE, CHUNK), F32),
+        ],
         compiler_params=params(),
         name="backward_tiles",
-    )(place, index, grad_mine, grad_other, *tiles)
+    )(place, all_index, panel, *tiles, *theirs)
     back, piece = lax.optimization_barrier((back, piece))
-    back = lax.all_to_all(back, ("y", "x"), 0, 0, tiled=True)
+    back = lax.all_to_all(back, ("y", "x", "core"), 0, 0, tiled=True)
     for distance in (2, 4):
         piece = double(piece, "z", distance)
     piece = lax.all_gather(piece, "x", axis=0).astype(F32).sum(0).astype(BF16)

time: 197 us -> 208 us (1.056)
  blocking collectives: 64.5 us -> 24.3 us
  starting transfers between devices: 79.3 us -> 102 us
  waiting for transfers between devices: 39.4 us -> 55.7 us
  local copies, waits for them, and re-layouts: 2.12 us -> 8.06 us
  other arithmetic: 0.82 us -> 5.44 us
    all_to_all x1 -> x0, blocking collectives: 38.3 us -> none  [body(): parts = lax.all_to_all(term, ('x', 'z'), 0, 0, tiled=True)]
    all_to_all x2 -> x3, starting transfers between devices: 14.7 us -> 33.4 us  [the longest x1 13.2 us: body(): back = lax.all_to_all(back, ('y', 'x', 'core'), 0, 0, tiled=True)]
    all_to_all x2 -> x3, waiting for transfers between devices: 0.2 us -> 16.6 us  [the longest x1 14.1 us: body(): parts = lax.all_to_all(term, ('x', 'z'), 0, 0, tiled=True)]
    unnamed x18 -> x30, local copies, waits for them, and re-layouts: 1.9 us -> 7.19 us
    ppermute x13 -> x16, starting transfers between devices: 54 us -> 58 us  [exchange(): return lax.ppermute(array, axis, [(i, i ^ distance) for i in range(size)])]
    convert_element_type x3, other arithmetic: 0.07 us -> 2.66 us  [halve(): (keep.astype(F32) + exchange(send, axis, distance).astype(F32)).astype(BF16)]
    ppermute x13 -> x16, waiting for transfers between devices: 39.2 us -> 39.1 us  [exchange(): return lax.ppermute(array, axis, [(i, i ^ distance) for i in range(size)])]
  transfers between devices with their start and end apart: 16 -> 20, of which waited for: 12 -> 14; matrix products, arithmetic and copies ran while one was open for 0% -> 2% of each run, Pallas kernels for 0% -> 2%
where the time goes in v7:
time: 208 us; the launch traced here: 207 us
  starting transfers between devices  102 us (49%)
  waiting for transfers between devices  55.7 us (27%)
  blocking collectives  24.3 us (12%)
  Pallas kernels  10 us (5%)
  local copies, waits for them, and re-layouts  8.06 us (4%)
  other arithmetic  5.44 us (3%)
    ppermute x16, starting transfers between devices, exchange(): return lax.ppermute(array, axis, [(i, i ^ distance) for i in range(size)])  58 us
    ppermute x16, waiting for transfers between devices, exchange(): return lax.ppermute(array, axis, [(i, i ^ distance) for i in range(size)])  39.1 us
    all_to_all x1, waiting for transfers between devices, body(): parts = lax.all_to_all(term, ('x', 'z'), 0, 0, tiled=True)  14.1 us
    all_to_all x1, blocking collectives, body(): whole = lax.all_to_all(piece, 'y', 0, 0, tiled=True)  13.6 us
    all_to_all x1, starting transfers between devices, body(): back = lax.all_to_all(back, ('y', 'x', 'core'), 0, 0, tiled=True)  13.2 us
    all_gather x1, blocking collectives, body(): piece = lax.all_gather(piece, 'x', axis=0).astype(F32).sum(0).astype(BF16)  10.7 us
    all_to_all x1, starting transfers between devices, body(): panel = lax.all_to_all(chunks, ('y', 'x'), 0, 0, tiled=True)  10.6 us
    all_to_all x1, starting transfers between devices, body(): parts = lax.all_to_all(term, ('x', 'z'), 0, 0, tiled=True)  10.6 us
  transfers between devices with their start and end apart: 20, of which 14 were waited for; matrix products, arithmetic and copies ran while one was open for 2% of the time, Pallas kernels for 2%

profile of v7, /device:TPU:1, one launch (start us, length us, event | category | flops | bytes accessed | tf_op | source)
XLA Modules:
  0.0 206.6 jit_solution(530766535517600455)
XLA Ops:
  0.6 0.9 copy-done.5
  1.5 1.1 spread.1
  2.7 0.0 copy-start.11
  2.7 10.6 %all-to-all-start = ((bf16[32,128,128]{2,1,0:T(8,128)(2,1)}), bf16[32,128,128]{2,1,0:T(8,128)(2,1)S(1)}, u32[]{:S(2)}, u32[]{:S(2)}) async-start(bf16[32,128,128]{2,1,0:T(8,128)(2,1)} %spread.1), calls=%async_computation | async-start | bytes 2097152 | tf_op jit(solution)/shard_map/all_to_all | solution.py:191
  13.4 0.1 fusion.11
  13.5 3.1 %collective-permute-start = (bf16[1040,128]{1,0:T(8,128)(2,1)S(1)}, bf16[1040,128]{1,0:T(8,128)(2,1)S(1)}, u32[]{:S(2)}, u32[]{:S(2)}) collective-permute-start(bf16[1040,128]{1,0:T(8,128)(2,1)S(1)} %pad_maximum_fusion.refs_0_), channel_id=1, source_target_pairs={{0,16},{16,0},{32,48},{48,32},{1,17},{17,1},{33,49},{49,33},{2,18}... | collective-permute-start | bytes 798728 | tf_op jit(solution)/shard_map/ppermute | solution.py:159
  16.6 4.3 %collective-permute-start.1 = (bf16[1040,128]{1,0:T(8,128)(2,1)S(1)}, bf16[1040,128]{1,0:T(8,128)(2,1)S(1)}, u32[]{:S(2)}, u32[]{:S(2)}) collective-permute-start(bf16[1040,128]{1,0:T(8,128)(2,1)S(1)} %pad_maximum_fusion.refs_0_), channel_id=1, source_target_pairs={{0,32},{16,48},{32,0},{48,16},{1,33},{17,49},{33,1},{49,17},{2,34}... | collective-permute-start | bytes 798728 | tf_op jit(solution)/shard_map/ppermute | solution.py:159
  20.9 2.1 %collective-permute-start.2 = (bf16[1040,128]{1,0:T(8,128)(2,1)S(1)}, bf16[1040,128]{1,0:T(8,128)(2,1)S(1)}, u32[]{:S(2)}, u32[]{:S(2)}) collective-permute-start(bf16[1040,128]{1,0:T(8,128)(2,1)S(1)} %pad_maximum_fusion.refs_0_), channel_id=1, source_target_pairs={{0,48},{16,32},{32,16},{48,0},{1,49},{17,33},{33,17},{49,1},{2,50}... | collective-permute-start | bytes 798728 | tf_op jit(solution)/shard_map/ppermute | solution.py:159
  23.1 0.1 broadcast_in_dim.6
  23.2 0.1 min.33
  23.3 0.1 pad_add_fusion.1.place_ref.core_ref
  23.3 4.3 %collective-permute-done.refs_1_ = bf16[1040,128]{1,0:T(8,128)(2,1)S(1)} collective-permute-done((bf16[1040,128]{1,0:T(8,128)(2,1)S(1)}, bf16[1040,128]{1,0:T(8,128)(2,1)S(1)}, u32[]{:S(2)}, u32[]{:S(2)}) %collective-permute-start) | collective-permute-done | bytes 266272 | tf_op jit(solution)/shard_map/ppermute | solution.py:159
  27.6 12.2 %collective-permute-done.1.refs_2_ = bf16[1040,128]{1,0:T(8,128)(2,1)S(1)} collective-permute-done((bf16[1040,128]{1,0:T(8,128)(2,1)S(1)}, bf16[1040,128]{1,0:T(8,128)(2,1)S(1)}, u32[]{:S(2)}, u32[]{:S(2)}) %collective-permute-start.1) | collective-permute-done | bytes 266272 | tf_op jit(solution)/shard_map/ppermute | solution.py:159
  39.9 3.8 %collective-permute-done.2.refs_3_ = bf16[1040,128]{1,0:T(8,128)(2,1)S(1)} collective-permute-done((bf16[1040,128]{1,0:T(8,128)(2,1)S(1)}, bf16[1040,128]{1,0:T(8,128)(2,1)S(1)}, u32[]{:S(2)}, u32[]{:S(2)}) %collective-permute-start.2) | collective-permute-done | bytes 266272 | tf_op jit(solution)/shard_map/ppermute | solution.py:159
  43.7 0.1 maximum_minimum_fusion.1.index_ref
  43.8 1.5 forward_tiles.1
  45.4 3.4 %collective-permute-start.3 = (bf16[32,128,128]{2,1,0:T(8,128)(2,1)S(1)}, bf16[32,128,128]{2,1,0:T(8,128)(2,1)S(1)}, u32[]{:S(2)}, u32[]{:S(2)}) collective-permute-start(bf16[32,128,128]{2,1,0:T(8,128)(2,1)S(1)} %get-tuple-element.27), channel_id=1, source_target_pairs={{0,1},{1,0},{2,3},{3,2},{4,5},{5,4},{6,7},{7,6},{8,9},{9,8},{10,11... | collective-permute-start | bytes 3145736 | tf_op jit(solution)/shard_map/ppermute | solution.py:159
  48.7 2.3 %collective-permute-done.3 = bf16[32,128,128]{2,1,0:T(8,128)(2,1)S(1)} collective-permute-done((bf16[32,128,128]{2,1,0:T(8,128)(2,1)S(1)}, bf16[32,128,128]{2,1,0:T(8,128)(2,1)S(1)}, u32[]{:S(2)}, u32[]{:S(2)}) %collective-permute-start.3) | collective-permute-done | bytes 1048608 | tf_op jit(solution)/shard_map/ppermute | solution.py:159
  51.0 1.3 add_convert_fusion
  52.4 10.6 %all-to-all-start.1 = ((bf16[32,128,128]{2,1,0:T(8,128)(2,1)}), bf16[32,128,128]{2,1,0:T(8,128)(2,1)S(1)}, u32[]{:S(2)}, u32[]{:S(2)}) async-start(bf16[32,128,128]{2,1,0:T(8,128)(2,1)} %add_convert_fusion), calls=%async_computation.1 | async-start | bytes 2097152 | tf_op jit(solution)/shard_map/all_to_all | solution.py:212
  62.9 2.6 %collective-permute-start.4 = (bf16[1040,128]{1,0:T(8,128)(2,1)S(1)}, bf16[1040,128]{1,0:T(8,128)(2,1)S(1)}, u32[]{:S(2)}, u32[]{:S(2)}) collective-permute-start(bf16[1040,128]{1,0:T(8,128)(2,1)S(1)} %pad_maximum_fusion.refs_0_), channel_id=1, source_target_pairs={{0,1},{1,0},{2,3},{3,2},{4,5},{5,4},{6,7},{7,6},{8,9},{9,8},{10,11... | collective-permute-start | bytes 798728 | tf_op jit(solution)/shard_map/ppermute | solution.py:159
  65.5 1.9 collective-permute-start.5
  67.4 2.4 %collective-permute-start.6 = (bf16[1040,128]{1,0:T(8,128)(2,1)S(1)}, bf16[1040,128]{1,0:T(8,128)(2,1)S(1)}, u32[]{:S(2)}, u32[]{:S(2)}) collective-permute-start(bf16[1040,128]{1,0:T(8,128)(2,1)S(1)} %collective-permute-done.1.refs_2_), channel_id=1, source_target_pairs={{0,1},{1,0},{2,3},{3,2},{4,5},{5,4},{6,7},{7,6},{8,9},{9,8},{10,11... | collective-permute-start | bytes 798728 | tf_op jit(solution)/shard_map/ppermute | solution.py:159
  69.8 1.9 collective-permute-start.7
  71.8 1.4 collective-permute-done.7.refs_7_
  73.3 0.7 copy-done.2
  74.0 14.1 %all-to-all-done.1.parts_ref = bf16[32,128,128]{2,1,0:T(8,128)(2,1)S(1)} async-done(((bf16[32,128,128]{2,1,0:T(8,128)(2,1)}), bf16[32,128,128]{2,1,0:T(8,128)(2,1)S(1)}, u32[]{:S(2)}, u32[]{:S(2)}) %all-to-all-start.1) | async-done | bytes 1048608 | tf_op jit(solution)/shard_map/all_to_all | solution.py:212
  88.1 0.9 copy-done.6
  89.0 1.7 middle.1
  90.7 1.0 copy-done.1
  91.7 0.7 copy-done.4
  92.4 0.7 copy-done.7
  93.1 9.6 %all-to-all-start.2 = ((bf16[64,64,128]{2,1,0:T(8,128)(2,1)}), bf16[64,64,128]{2,1,0:T(8,128)(2,1)S(1)}, u32[]{:S(2)}, u32[]{:S(2)}) async-start(bf16[64,64,128]{2,1,0:T(8,128)(2,1)} %copy-done.1), calls=%async_computation.2 | async-start | bytes 2097152 | tf_op jit(solution)/shard_map/all_to_all | solution.py:232
  102.7 2.4 %collective-permute-start.8 = (bf16[256,512]{1,0:T(8,128)(2,1)}, bf16[256,512]{1,0:T(8,128)(2,1)}, u32[]{:S(2)}, u32[]{:S(2)}) collective-permute-start(bf16[256,512]{1,0:T(8,128)(2,1)} %copy-done.7), channel_id=1, source_target_pairs={{0,1},{1,0},{2,3},{3,2},{4,5},{5,4},{6,7},{7,6},{8,9},{9,8},{10,11... | collective-permute-start | bytes 786440 | tf_op jit(solution)/shard_map/ppermute | solution.py:159
  105.1 1.5 collective-permute-done.8
  106.6 1.1 add_convert_fusion.1
  107.7 0.7 copy-done.8
  108.4 0.7 dynamic-slice_bitcast_fusion
  109.0 3.1 %collective-permute-start.9 = (bf16[128,512]{1,0:T(8,128)(2,1)}, bf16[128,512]{1,0:T(8,128)(2,1)}, u32[]{:S(2)}, u32[]{:S(2)}) collective-permute-start(bf16[128,512]{1,0:T(8,128)(2,1)} %dynamic-slice_bitcast_fusion), channel_id=1, source_target_pairs={{0,64},{64,0},{128,192},{192,128},{256,320},{320,256},{384,448},{4... | collective-permute-start | bytes 393224 | tf_op jit(solution)/shard_map/ppermute | solution.py:159
  112.1 3.8 %collective-permute-done.9 = bf16[128,512]{1,0:T(8,128)(2,1)} collective-permute-done((bf16[128,512]{1,0:T(8,128)(2,1)}, bf16[128,512]{1,0:T(8,128)(2,1)}, u32[]{:S(2)}, u32[]{:S(2)}) %collective-permute-start.9) | collective-permute-done | bytes 131104 | tf_op jit(solution)/shard_map/ppermute | solution.py:159
  115.9 1.0 fusion
  117.0 0.0 copy-start.9
  117.0 0.6 copy-done.9
  117.6 3.5 %collective-permute-start.10 = (bf16[64,512]{1,0:T(8,128)(2,1)S(1)}, bf16[64,512]{1,0:T(8,128)(2,1)}, u32[]{:S(2)}, u32[]{:S(2)}) collective-permute-start(bf16[64,512]{1,0:T(8,128)(2,1)S(1)} %dynamic-slice_bitcast_fusion.1), channel_id=1, source_target_pairs={{0,128},{64,192},{128,0},{192,64},{256,384},{320,448},{384,256},{4... | collective-permute-start | bytes 196616 | tf_op jit(solution)/shard_map/ppermute | solution.py:159
  121.2 2.6 %collective-permute-done.10 = bf16[64,512]{1,0:T(8,128)(2,1)} collective-permute-done((bf16[64,512]{1,0:T(8,128)(2,1)S(1)}, bf16[64,512]{1,0:T(8,128)(2,1)}, u32[]{:S(2)}, u32[]{:S(2)}) %collective-permute-start.10) | collective-permute-done | bytes 65568 | tf_op jit(solution)/shard_map/ppermute | solution.py:159
  123.8 0.9 fusion.1
  124.7 6.7 %collective-permute-start.11 = (bf16[32,512]{1,0:T(8,128)(2,1)S(1)}, bf16[32,512]{1,0:T(8,128)(2,1)}, u32[]{:S(2)}, u32[]{:S(2)}) collective-permute-start(bf16[32,512]{1,0:T(8,128)(2,1)S(1)} %dynamic-slice_bitcast_fusion.2), channel_id=1, source_target_pairs={{0,256},{64,320},{128,384},{192,448},{256,0},{320,64},{384,128},{4... | collective-permute-start | bytes 98312 | tf_op jit(solution)/shard_map/ppermute | solution.py:159
  131.4 2.0 collective-permute-done.11
  133.4 0.8 fusion.2
  134.2 3.2 %collective-permute-start.12 = (bf16[32,512]{1,0:T(8,128)(2,1)S(1)}, bf16[32,512]{1,0:T(8,128)(2,1)S(1)}, u32[]{:S(2)}, u32[]{:S(2)}) collective-permute-start(bf16[32,512]{1,0:T(8,128)(2,1)S(1)} %fusion.2), channel_id=1, source_target_pairs={{0,2},{2,0},{4,6},{6,4},{8,10},{10,8},{12,14},{14,12},{1,3},{3,1},... | collective-permute-start | bytes 98312 | tf_op jit(solution)/shard_map/ppermute | solution.py:159
  137.4 0.9 copy-done.3
  138.4 3.1 %backward_tiles.1 = bf16[64,64,128]{2,1,0:T(8,128)(2,1)} custom-call(s32[2]{0:T(128)S(1)} %pad_add_fusion.1.place_ref.core_ref, s32[8,24]{1,0:T(8,128)S(1)} %pad_add_fusion.index_ref, bf16[64,64,128]{2,1,0:T(8,128)(2,1)S(1)} %all-to-all-done.2.grad_ref, bf16[1040,128]{1,0:T(8,128)(2,1)S(1)} %pad_maximum_fusion.refs_0_, ...), custom_call_target="tpu_custom_call" | custom-call | tf_op jit(solution)/shard_map/backward_tiles/pallas_call | solution.py:240
  141.5 13.2 %all-to-all-start.3 = ((bf16[64,64,128]{2,1,0:T(8,128)(2,1)}), bf16[64,64,128]{2,1,0:T(8,128)(2,1)S(1)}, u32[]{:S(2)}, u32[]{:S(2)}) async-start(bf16[64,64,128]{2,1,0:T(8,128)(2,1)} %backward_tiles.1), calls=%async_computation.3 | async-start | bytes 2097152 | tf_op jit(solution)/shard_map/all_to_all | solution.py:253
  154.8 4.0 %collective-permute-start.13 = (bf16[32,512]{1,0:T(8,128)(2,1)S(1)}, bf16[32,512]{1,0:T(8,128)(2,1)S(1)}, u32[]{:S(2)}, u32[]{:S(2)}) collective-permute-start(bf16[32,512]{1,0:T(8,128)(2,1)S(1)} %add_convert_fusion.4), channel_id=1, source_target_pairs={{0,4},{2,6},{4,0},{6,2},{8,12},{10,14},{12,8},{14,10},{1,5},{3,7},... | collective-permute-start | bytes 98312 | tf_op jit(solution)/shard_map/ppermute | solution.py:159
  158.8 2.2 %collective-permute-done.13 = bf16[32,512]{1,0:T(8,128)(2,1)S(1)} collective-permute-done((bf16[32,512]{1,0:T(8,128)(2,1)S(1)}, bf16[32,512]{1,0:T(8,128)(2,1)S(1)}, u32[]{:S(2)}, u32[]{:S(2)}) %collective-permute-start.13) | collective-permute-done | bytes 32800 | tf_op jit(solution)/shard_map/ppermute | solution.py:159
  161.0 5.8 %collective-permute-start.14 = (bf16[32,512]{1,0:T(8,128)(2,1)S(1)}, bf16[32,512]{1,0:T(8,128)(2,1)S(1)}, u32[]{:S(2)}, u32[]{:S(2)}) collective-permute-start(bf16[32,512]{1,0:T(8,128)(2,1)S(1)} %add_convert_fusion.3), channel_id=1, source_target_pairs={{0,8},{2,10},{4,12},{6,14},{8,0},{10,2},{12,4},{14,6},{1,9},{3,11}... | collective-permute-start | bytes 98312 | tf_op jit(solution)/shard_map/ppermute | solution.py:159
  166.8 2.8 %collective-permute-done.14 = bf16[32,512]{1,0:T(8,128)(2,1)S(1)} collective-permute-done((bf16[32,512]{1,0:T(8,128)(2,1)S(1)}, bf16[32,512]{1,0:T(8,128)(2,1)S(1)}, u32[]{:S(2)}, u32[]{:S(2)}) %collective-permute-start.14) | collective-permute-done | bytes 32800 | tf_op jit(solution)/shard_map/ppermute | solution.py:159
  169.6 10.7 %all-gather = bf16[128,512]{1,0:T(8,128)(2,1)S(1)} all-gather(bf16[32,512]{1,0:T(8,128)(2,1)S(1)} %add_convert_fusion.2), channel_id=2, replica_groups=mesh['y'=8,'x'=4,'z'=8,'core'=2] {'x'}, dimensions={0}, use_global_device_ids=true | all-gather | bytes 163840 | tf_op jit(solution)/shard_map/all_gather | solution.py:256
  180.3 2.4 %all-to-all-done.3.parts_ref = bf16[64,64,128]{2,1,0:T(8,128)(2,1)S(1)} async-done(((bf16[64,64,128]{2,1,0:T(8,128)(2,1)}), bf16[64,64,128]{2,1,0:T(8,128)(2,1)S(1)}, u32[]{:S(2)}, u32[]{:S(2)}) %all-to-all-start.3) | async-done | bytes 1048608 | tf_op jit(solution)/shard_map/all_to_all | solution.py:253
  182.8 13.6 %all_to_all.25.mine_ref = bf16[8,32,512]{2,1,0:T(8,128)(2,1)S(1)} all-to-all(bf16[8,32,512]{2,1,0:T(8,128)(2,1)S(1)} %broadcast_in_dim.15), channel_id=1, replica_groups=mesh['y'=8,'x'=4,'z'=8,'core'=2] {'y'}, dimensions={0} | all-to-all | bytes 524288 | tf_op jit(solution)/shard_map/all_to_all | solution.py:270
  196.3 7.5 %collective-permute-start.15 = (bf16[8,32,512]{2,1,0:T(8,128)(2,1)S(1)}, bf16[8,32,512]{2,1,0:T(8,128)(2,1)S(1)}, u32[]{:S(2)}, u32[]{:S(2)}) collective-permute-start(bf16[8,32,512]{2,1,0:T(8,128)(2,1)S(1)} %all_to_all.25.mine_ref), channel_id=1, source_target_pairs={{0,1},{1,0},{2,3},{3,2},{4,5},{5,4},{6,7},{7,6},{8,9},{9,8},{10,11... | collective-permute-start | bytes 786440 | tf_op jit(solution)/shard_map/ppermute | solution.py:159
  203.9 1.0 last.1
  204.9 0.1 collective-permute-done.15.other_ref
  205.0 1.6 place_rows.1
  (44 shorter events, 0.2 us)
Async XLA Ops:
  0.6 0.9 copy-start.5
  2.6 10.7 %copy-start.14 = (s32[1,1,8]{2,1,0:T(1,128)S(1)}, s32[1,1,8]{2,1,0:T(1,128)}, u32[]{:S(2)}) copy-start(s32[1,1,8]{2,1,0:T(1,128)} %param.13) | copy-start | bytes 100
  2.6 10.7 %copy-start.12 = (s32[1,1,8]{2,1,0:T(1,128)S(1)}, s32[1,1,8]{2,1,0:T(1,128)}, u32[]{:S(2)}) copy-start(s32[1,1,8]{2,1,0:T(1,128)} %param.15) | copy-start | bytes 100
  2.6 10.7 %copy-start.13 = (s32[1,1,8]{2,1,0:T(1,128)S(1)}, s32[1,1,8]{2,1,0:T(1,128)}, u32[]{:S(2)}) copy-start(s32[1,1,8]{2,1,0:T(1,128)} %param.14) | copy-start | bytes 100
  2.6 10.8 %copy-start.10 = (bf16[1,1,8,128,128]{4,3,2,1,0:T(8,128)(2,1)S(1)}, bf16[1,1,8,128,128]{4,3,2,1,0:T(8,128)(2,1)}, u32[]{:S(2)}) copy-start(bf16[1,1,8,128,128]{4,3,2,1,0:T(8,128)(2,1)} %param.12) | copy-start | bytes 786436
  2.7 20.4 %copy-start.11 = (s32[3]{0:T(128)S(1)}, s32[3]{0:T(128)}, u32[]{:S(2)}) copy-start(s32[3]{0:T(128)} %constant.52.clone) | copy-start | bytes 40
  2.7 41.2 %all-to-all-start = ((bf16[32,128,128]{2,1,0:T(8,128)(2,1)}), bf16[32,128,128]{2,1,0:T(8,128)(2,1)S(1)}, u32[]{:S(2)}, u32[]{:S(2)}) async-start(bf16[32,128,128]{2,1,0:T(8,128)(2,1)} %spread.1), calls=%async_computation | async-start | bytes 2097152 | tf_op jit(solution)/shard_map/all_to_all | solution.py:191
  13.5 14.2 %collective-permute-start = (bf16[1040,128]{1,0:T(8,128)(2,1)S(1)}, bf16[1040,128]{1,0:T(8,128)(2,1)S(1)}, u32[]{:S(2)}, u32[]{:S(2)}) collective-permute-start(bf16[1040,128]{1,0:T(8,128)(2,1)S(1)} %pad_maximum_fusion.refs_0_), channel_id=1, source_target_pairs={{0,16},{16,0},{32,48},{48,32},{1,17},{17,1},{33,49},{49,33},{2,18}... | collective-permute-start | bytes 798728 | tf_op jit(solution)/shard_map/ppermute | solution.py:159
  16.6 23.3 %collective-permute-start.1 = (bf16[1040,128]{1,0:T(8,128)(2,1)S(1)}, bf16[1040,128]{1,0:T(8,128)(2,1)S(1)}, u32[]{:S(2)}, u32[]{:S(2)}) collective-permute-start(bf16[1040,128]{1,0:T(8,128)(2,1)S(1)} %pad_maximum_fusion.refs_0_), channel_id=1, source_target_pairs={{0,32},{16,48},{32,0},{48,16},{1,33},{17,49},{33,1},{49,17},{2,34}... | collective-permute-start | bytes 798728 | tf_op jit(solution)/shard_map/ppermute | solution.py:159
  20.9 22.8 %collective-permute-start.2 = (bf16[1040,128]{1,0:T(8,128)(2,1)S(1)}, bf16[1040,128]{1,0:T(8,128)(2,1)S(1)}, u32[]{:S(2)}, u32[]{:S(2)}) collective-permute-start(bf16[1040,128]{1,0:T(8,128)(2,1)S(1)} %pad_maximum_fusion.refs_0_), channel_id=1, source_target_pairs={{0,48},{16,32},{32,16},{48,0},{1,49},{17,33},{33,17},{49,1},{2,50}... | collective-permute-start | bytes 798728 | tf_op jit(solution)/shard_map/ppermute | solution.py:159
  45.4 5.7 %collective-permute-start.3 = (bf16[32,128,128]{2,1,0:T(8,128)(2,1)S(1)}, bf16[32,128,128]{2,1,0:T(8,128)(2,1)S(1)}, u32[]{:S(2)}, u32[]{:S(2)}) collective-permute-start(bf16[32,128,128]{2,1,0:T(8,128)(2,1)S(1)} %get-tuple-element.27), channel_id=1, source_target_pairs={{0,1},{1,0},{2,3},{3,2},{4,5},{5,4},{6,7},{7,6},{8,9},{9,8},{10,11... | collective-permute-start | bytes 3145736 | tf_op jit(solution)/shard_map/ppermute | solution.py:159
  52.3 35.8 %copy-start = (bf16[512,512]{1,0:T(8,128)(2,1)S(1)}, bf16[512,512]{1,0:T(8,128)(2,1)}, u32[]{:S(2)}) copy-start(bf16[512,512]{1,0:T(8,128)(2,1)} %weight_ref.3) | copy-start | bytes 1572868
  52.4 35.8 %all-to-all-start.1 = ((bf16[32,128,128]{2,1,0:T(8,128)(2,1)}), bf16[32,128,128]{2,1,0:T(8,128)(2,1)S(1)}, u32[]{:S(2)}, u32[]{:S(2)}) async-start(bf16[32,128,128]{2,1,0:T(8,128)(2,1)} %add_convert_fusion), calls=%async_computation.1 | async-start | bytes 2097152 | tf_op jit(solution)/shard_map/all_to_all | solution.py:212
  62.9 8.8 %collective-permute-start.4 = (bf16[1040,128]{1,0:T(8,128)(2,1)S(1)}, bf16[1040,128]{1,0:T(8,128)(2,1)S(1)}, u32[]{:S(2)}, u32[]{:S(2)}) collective-permute-start(bf16[1040,128]{1,0:T(8,128)(2,1)S(1)} %pad_maximum_fusion.refs_0_), channel_id=1, source_target_pairs={{0,1},{1,0},{2,3},{3,2},{4,5},{5,4},{6,7},{7,6},{8,9},{9,8},{10,11... | collective-permute-start | bytes 798728 | tf_op jit(solution)/shard_map/ppermute | solution.py:159
  65.5 6.3 %collective-permute-start.5 = (bf16[1040,128]{1,0:T(8,128)(2,1)S(1)}, bf16[1040,128]{1,0:T(8,128)(2,1)S(1)}, u32[]{:S(2)}, u32[]{:S(2)}) collective-permute-start(bf16[1040,128]{1,0:T(8,128)(2,1)S(1)} %collective-permute-done.refs_1_), channel_id=1, source_target_pairs={{0,1},{1,0},{2,3},{3,2},{4,5},{5,4},{6,7},{7,6},{8,9},{9,8},{10,11... | collective-permute-start | bytes 798728 | tf_op jit(solution)/shard_map/ppermute | solution.py:159
  67.4 4.4 %collective-permute-start.6 = (bf16[1040,128]{1,0:T(8,128)(2,1)S(1)}, bf16[1040,128]{1,0:T(8,128)(2,1)S(1)}, u32[]{:S(2)}, u32[]{:S(2)}) collective-permute-start(bf16[1040,128]{1,0:T(8,128)(2,1)S(1)} %collective-permute-done.1.refs_2_), channel_id=1, source_target_pairs={{0,1},{1,0},{2,3},{3,2},{4,5},{5,4},{6,7},{7,6},{8,9},{9,8},{10,11... | collective-permute-start | bytes 798728 | tf_op jit(solution)/shard_map/ppermute | solution.py:159
  69.8 3.4 %collective-permute-start.7 = (bf16[1040,128]{1,0:T(8,128)(2,1)S(1)}, bf16[1040,128]{1,0:T(8,128)(2,1)S(1)}, u32[]{:S(2)}, u32[]{:S(2)}) collective-permute-start(bf16[1040,128]{1,0:T(8,128)(2,1)S(1)} %collective-permute-done.2.refs_3_), channel_id=1, source_target_pairs={{0,1},{1,0},{2,3},{3,2},{4,5},{5,4},{6,7},{7,6},{8,9},{9,8},{10,11... | collective-permute-start | bytes 798728 | tf_op jit(solution)/shard_map/ppermute | solution.py:159
  73.3 0.7 copy-start.2
  88.1 0.9 copy-start.6
  90.7 1.0 copy-start.1
  91.7 0.7 copy-start.4
  92.4 0.7 copy-start.7
  93.1 41.1 %all-to-all-start.2 = ((bf16[64,64,128]{2,1,0:T(8,128)(2,1)}), bf16[64,64,128]{2,1,0:T(8,128)(2,1)S(1)}, u32[]{:S(2)}, u32[]{:S(2)}) async-start(bf16[64,64,128]{2,1,0:T(8,128)(2,1)} %copy-done.1), calls=%async_computation.2 | async-start | bytes 2097152 | tf_op jit(solution)/shard_map/all_to_all | solution.py:232
  102.7 3.9 %collective-permute-start.8 = (bf16[256,512]{1,0:T(8,128)(2,1)}, bf16[256,512]{1,0:T(8,128)(2,1)}, u32[]{:S(2)}, u32[]{:S(2)}) collective-permute-start(bf16[256,512]{1,0:T(8,128)(2,1)} %copy-done.7), channel_id=1, source_target_pairs={{0,1},{1,0},{2,3},{3,2},{4,5},{5,4},{6,7},{7,6},{8,9},{9,8},{10,11... | collective-permute-start | bytes 786440 | tf_op jit(solution)/shard_map/ppermute | solution.py:159
  107.7 0.7 copy-start.8
  109.0 6.9 %collective-permute-start.9 = (bf16[128,512]{1,0:T(8,128)(2,1)}, bf16[128,512]{1,0:T(8,128)(2,1)}, u32[]{:S(2)}, u32[]{:S(2)}) collective-permute-start(bf16[128,512]{1,0:T(8,128)(2,1)} %dynamic-slice_bitcast_fusion), channel_id=1, source_target_pairs={{0,64},{64,0},{128,192},{192,128},{256,320},{320,256},{384,448},{4... | collective-permute-start | bytes 393224 | tf_op jit(solution)/shard_map/ppermute | solution.py:159
  117.0 0.7 copy-start.9
  117.6 6.2 %collective-permute-start.10 = (bf16[64,512]{1,0:T(8,128)(2,1)S(1)}, bf16[64,512]{1,0:T(8,128)(2,1)}, u32[]{:S(2)}, u32[]{:S(2)}) collective-permute-start(bf16[64,512]{1,0:T(8,128)(2,1)S(1)} %dynamic-slice_bitcast_fusion.1), channel_id=1, source_target_pairs={{0,128},{64,192},{128,0},{192,64},{256,384},{320,448},{384,256},{4... | collective-permute-start | bytes 196616 | tf_op jit(solution)/shard_map/ppermute | solution.py:159
  124.7 8.7 %collective-permute-start.11 = (bf16[32,512]{1,0:T(8,128)(2,1)S(1)}, bf16[32,512]{1,0:T(8,128)(2,1)}, u32[]{:S(2)}, u32[]{:S(2)}) collective-permute-start(bf16[32,512]{1,0:T(8,128)(2,1)S(1)} %dynamic-slice_bitcast_fusion.2), channel_id=1, source_target_pairs={{0,256},{64,320},{128,384},{192,448},{256,0},{320,64},{384,128},{4... | collective-permute-start | bytes 98312 | tf_op jit(solution)/shard_map/ppermute | solution.py:159
  134.2 7.3 %collective-permute-start.12 = (bf16[32,512]{1,0:T(8,128)(2,1)S(1)}, bf16[32,512]{1,0:T(8,128)(2,1)S(1)}, u32[]{:S(2)}, u32[]{:S(2)}) collective-permute-start(bf16[32,512]{1,0:T(8,128)(2,1)S(1)} %fusion.2), channel_id=1, source_target_pairs={{0,2},{2,0},{4,6},{6,4},{8,10},{10,8},{12,14},{14,12},{1,3},{3,1},... | collective-permute-start | bytes 98312 | tf_op jit(solution)/shard_map/ppermute | solution.py:159
  137.4 1.0 copy-start.3
  141.5 41.2 %all-to-all-start.3 = ((bf16[64,64,128]{2,1,0:T(8,128)(2,1)}), bf16[64,64,128]{2,1,0:T(8,128)(2,1)S(1)}, u32[]{:S(2)}, u32[]{:S(2)}) async-start(bf16[64,64,128]{2,1,0:T(8,128)(2,1)} %backward_tiles.1), calls=%async_computation.3 | async-start | bytes 2097152 | tf_op jit(solution)/shard_map/all_to_all | solution.py:253
  154.8 6.2 %collective-permute-start.13 = (bf16[32,512]{1,0:T(8,128)(2,1)S(1)}, bf16[32,512]{1,0:T(8,128)(2,1)S(1)}, u32[]{:S(2)}, u32[]{:S(2)}) collective-permute-start(bf16[32,512]{1,0:T(8,128)(2,1)S(1)} %add_convert_fusion.4), channel_id=1, source_target_pairs={{0,4},{2,6},{4,0},{6,2},{8,12},{10,14},{12,8},{14,10},{1,5},{3,7},... | collective-permute-start | bytes 98312 | tf_op jit(solution)/shard_map/ppermute | solution.py:159
  161.0 8.6 %collective-permute-start.14 = (bf16[32,512]{1,0:T(8,128)(2,1)S(1)}, bf16[32,512]{1,0:T(8,128)(2,1)S(1)}, u32[]{:S(2)}, u32[]{:S(2)}) collective-permute-start(bf16[32,512]{1,0:T(8,128)(2,1)S(1)} %add_convert_fusion.3), channel_id=1, source_target_pairs={{0,8},{2,10},{4,12},{6,14},{8,0},{10,2},{12,4},{14,6},{1,9},{3,11}... | collective-permute-start | bytes 98312 | tf_op jit(solution)/shard_map/ppermute | solution.py:159
  196.3 8.7 %collective-permute-start.15 = (bf16[8,32,512]{2,1,0:T(8,128)(2,1)S(1)}, bf16[8,32,512]{2,1,0:T(8,128)(2,1)S(1)}, u32[]{:S(2)}, u32[]{:S(2)}) collective-permute-start(bf16[8,32,512]{2,1,0:T(8,128)(2,1)S(1)} %all_to_all.25.mine_ref), channel_id=1, source_target_pairs={{0,1},{1,0},{2,3},{3,2},{4,5},{5,4},{6,7},{7,6},{8,9},{9,8},{10,11... | collective-permute-start | bytes 786440 | tf_op jit(solution)/shard_map/ppermute | solution.py:159

commit v8 on v6

--- a/solution.py
+++ b/solution.py
@@ -122,13 +122,13 @@
 
 def place_rows(place_ref, mine_ref, other_ref, out_ref):
     core = place_ref[0]
-    half, share = WIDTH // CORES, WIDTH // (Y * CORES)
+    half, share = WIDTH // CORES, WIDTH // (X * CORES)
     scale = 1.0 / math.sqrt(TILE * Y * X * Z * CORES)
-    for y in range(Y):
-        at = (y & 1) * 4 * share + (y >> 1 & 1) * 2 * share + (y >> 2) * share
+    for x in range(X):
+        at = ((x & 1) * 2 + (x >> 1)) * share
         for side, ref in ((core, mine_ref), (1 - core, other_ref)):
             start = pl.multiple_of(side * half + at, share)
-            out_ref[pl.ds(start, share), :] = ref[y].astype(F32) * scale
+            out_ref[pl.ds(start, share), :] = ref[x].astype(F32) * scale
 
 
 def exchange(array, axis, distance):
@@ -201,8 +201,9 @@
     grad_mine = lax.all_to_all(grad, ("x", "z"), 0, 0, tiled=True)
     piece = weight_keep.astype(F32) + exchange(weight_send, "core", 1).astype(F32)
     piece = piece.astype(BF16)
-    for distance in (1, 2, 4):
-        piece = halve(piece, "y", distance)
+    for distance in (1, 2):
+        piece = halve(piece, "x", distance)
+    piece = double(piece, "y", 1)
     grad_mine, piece = lax.optimization_barrier((grad_mine, piece))
 
     grad_other = exchange(grad_mine, "core", 1)
@@ -218,9 +219,8 @@
     )(place, index, grad_mine, grad_other, *tiles)
     back, piece = lax.optimization_barrier((back, piece))
     back = lax.all_to_all(back, ("y", "x"), 0, 0, tiled=True)
-    for distance in (2, 4):
-        piece = double(piece, "z", distance)
-    piece = lax.all_gather(piece, "x", axis=0).astype(F32).sum(0).astype(BF16)
+    for axis, distance in (("y", 2), ("y", 4), ("z", 2), ("z", 4)):
+        piece = double(piece, axis, distance)
     back, piece = lax.optimization_barrier((back, piece))
 
     input_grad = pl.pallas_call(
@@ -232,9 +232,9 @@
         name="last",
     )(back, weight)
 
-    share = WIDTH // (Y * CORES)
-    piece = jnp.broadcast_to(piece[None], (Y, share, WIDTH))
-    whole = lax.all_to_all(piece, "y", 0, 0, tiled=True)
+    share = WIDTH // (X * CORES)
+    piece = jnp.broadcast_to(piece[None], (X, share, WIDTH))
+    whole = lax.all_to_all(piece, "x", 0, 0, tiled=True)
     weight_grad = pl.pallas_call(
         place_rows,
         in_specs=[smem()] + [vmem()] * 2,

time: 197 us -> 219 us (1.11)
  waiting for transfers between devices: 39.4 us -> 61.3 us
  blocking collectives: 64.5 us -> 48 us
  starting transfers between devices: 79.3 us -> 95.8 us
    ppermute x13 -> x15, waiting for transfers between devices: 39.2 us -> 61.3 us  [exchange(): return lax.ppermute(array, axis, [(i, i ^ distance) for i in range(size)])]
    ppermute x13 -> x15, starting transfers between devices: 54 us -> 69.3 us  [exchange(): return lax.ppermute(array, axis, [(i, i ^ distance) for i in range(size)])]
    all_gather x1 -> x0, blocking collectives: 10.7 us -> none  [body(): piece = lax.all_gather(piece, 'x', axis=0).astype(F32).sum(0).astype(BF16)]
    all_to_all x1, blocking collectives: 15.6 us -> 9.75 us  [body(): whole = lax.all_to_all(piece, 'x', 0, 0, tiled=True)]
  transfers between devices with their start and end apart: 16 -> 18, of which waited for: 12 -> 13; matrix products, arithmetic and copies ran while one was open for 0% -> 0% of each run, Pallas kernels for 0% -> 0%
where the time goes in v8:
time: 219 us; the launch traced here: 218 us
  starting transfers between devices  95.8 us (44%)
  waiting for transfers between devices  61.3 us (28%)
  blocking collectives  48 us (22%)
  Pallas kernels  9.23 us (4%)
    ppermute x15, starting transfers between devices, exchange(): return lax.ppermute(array, axis, [(i, i ^ distance) for i in range(size)])  69.3 us
    ppermute x15, waiting for transfers between devices, exchange(): return lax.ppermute(array, axis, [(i, i ^ distance) for i in range(size)])  61.3 us
    all_to_all x1, blocking collectives, body(): parts = lax.all_to_all(term, ('x', 'z'), 0, 0, tiled=True)  38.3 us
    all_to_all x1, starting transfers between devices, body(): panel = lax.all_to_all(chunks, ('y', 'x'), 0, 0, tiled=True)  10.6 us
    all_to_all x1, blocking collectives, body(): whole = lax.all_to_all(piece, 'x', 0, 0, tiled=True)  9.75 us
    all_to_all x1, starting transfers between devices, body(): grad_mine = lax.all_to_all(grad, ('x', 'z'), 0, 0, tiled=True)  7.94 us
    all_to_all x1, starting transfers between devices, body(): back = lax.all_to_all(back, ('y', 'x'), 0, 0, tiled=True)  7.82 us
  transfers between devices with their start and end apart: 18, of which 13 were waited for; matrix products, arithmetic and copies ran while one was open for 0% of the time, Pallas kernels for 0%

profile of v8, /device:TPU:1, one launch (start us, length us, event | category | flops | bytes accessed | tf_op | source)
XLA Modules:
  0.0 218.3 jit_solution(17841184952486619765)
XLA Ops:
  0.6 0.0 copy-start.2
  0.6 0.9 copy-done.2
  1.5 1.1 spread.1
  2.7 0.0 copy-start.5
  2.7 10.6 %all-to-all-start = ((bf16[32,128,128]{2,1,0:T(8,128)(2,1)}), bf16[32,128,128]{2,1,0:T(8,128)(2,1)S(1)}, u32[]{:S(2)}, u32[]{:S(2)}) async-start(bf16[32,128,128]{2,1,0:T(8,128)(2,1)} %spread.1), calls=%async_computation | async-start | bytes 2097152 | tf_op jit(solution)/shard_map/all_to_all | solution.py:162
  13.3 0.0 copy-done.8
  13.3 0.0 copy-done.6
  13.3 0.0 copy-done.7
  13.4 0.1 fusion.10
  13.5 0.0 copy-done.4
  13.5 4.3 %collective-permute-start.2 = (bf16[1040,128]{1,0:T(8,128)(2,1)S(1)}, bf16[1040,128]{1,0:T(8,128)(2,1)S(1)}, u32[]{:S(2)}, u32[]{:S(2)}) collective-permute-start(bf16[1040,128]{1,0:T(8,128)(2,1)S(1)} %pad_maximum_fusion.refs_0_), channel_id=1, source_target_pairs={{0,48},{16,32},{32,16},{48,0},{1,49},{17,33},{33,17},{49,1},{2,50}... | collective-permute-start | bytes 798728 | tf_op jit(solution)/shard_map/ppermute | solution.py:136
  17.8 2.5 %collective-permute-start.1 = (bf16[1040,128]{1,0:T(8,128)(2,1)S(1)}, bf16[1040,128]{1,0:T(8,128)(2,1)S(1)}, u32[]{:S(2)}, u32[]{:S(2)}) collective-permute-start(bf16[1040,128]{1,0:T(8,128)(2,1)S(1)} %pad_maximum_fusion.refs_0_), channel_id=1, source_target_pairs={{0,32},{16,48},{32,0},{48,16},{1,33},{17,49},{33,1},{49,17},{2,34}... | collective-permute-start | bytes 798728 | tf_op jit(solution)/shard_map/ppermute | solution.py:136
  20.3 2.1 collective-permute-start
  22.5 0.0 copy-done.5
  22.5 0.1 broadcast_in_dim.4
  22.6 0.1 min.20
  22.7 0.1 pad_add_fusion.place_ref.core_ref
  22.7 14.6 %collective-permute-done.2.refs_3_ = bf16[1040,128]{1,0:T(8,128)(2,1)S(1)} collective-permute-done((bf16[1040,128]{1,0:T(8,128)(2,1)S(1)}, bf16[1040,128]{1,0:T(8,128)(2,1)S(1)}, u32[]{:S(2)}, u32[]{:S(2)}) %collective-permute-start.2) | collective-permute-done | bytes 266272 | tf_op jit(solution)/shard_map/ppermute | solution.py:136
  37.4 0.0 collective-permute-done.1.refs_2_
  37.4 3.7 %collective-permute-done.refs_1_ = bf16[1040,128]{1,0:T(8,128)(2,1)S(1)} collective-permute-done((bf16[1040,128]{1,0:T(8,128)(2,1)S(1)}, bf16[1040,128]{1,0:T(8,128)(2,1)S(1)}, u32[]{:S(2)}, u32[]{:S(2)}) %collective-permute-start) | collective-permute-done | bytes 266272 | tf_op jit(solution)/shard_map/ppermute | solution.py:136
  41.1 0.1 maximum_minimum_fusion.index_ref
  41.2 0.0 all-to-all-done.panel_ref
  41.2 1.5 forward_tiles.1
  42.7 3.1 %collective-permute-start.3 = (bf16[32,128,128]{2,1,0:T(8,128)(2,1)S(1)}, bf16[32,128,128]{2,1,0:T(8,128)(2,1)S(1)}, u32[]{:S(2)}, u32[]{:S(2)}) collective-permute-start(bf16[32,128,128]{2,1,0:T(8,128)(2,1)S(1)} %get-tuple-element.16), channel_id=1, source_target_pairs={{0,1},{1,0},{2,3},{3,2},{4,5},{5,4},{6,7},{7,6},{8,9},{9,8},{10,11... | collective-permute-start | bytes 3145736 | tf_op jit(solution)/shard_map/ppermute | solution.py:136
  45.8 2.3 %collective-permute-done.3 = bf16[32,128,128]{2,1,0:T(8,128)(2,1)S(1)} collective-permute-done((bf16[32,128,128]{2,1,0:T(8,128)(2,1)S(1)}, bf16[32,128,128]{2,1,0:T(8,128)(2,1)S(1)}, u32[]{:S(2)}, u32[]{:S(2)}) %collective-permute-start.3) | collective-permute-done | bytes 1048608 | tf_op jit(solution)/shard_map/ppermute | solution.py:136
  48.1 0.4 add_convert_fusion
  48.4 0.0 copy-start
  48.4 0.0 copy-start.3
  48.5 38.3 %all_to_all.25.parts_ref = bf16[32,128,128]{2,1,0:T(8,128)(2,1)S(1)} all-to-all(bf16[32,128,128]{2,1,0:T(8,128)(2,1)S(1)} %add_convert_fusion), channel_id=1, replica_groups=mesh['y'=8,'x'=4,'z'=8,'core'=2] {'x','z'}, dimensions={0} | all-to-all | bytes 2097152 | tf_op jit(solution)/shard_map/all_to_all | solution.py:184
  86.7 0.0 copy-done
  86.7 0.0 copy-done.3
  86.7 1.7 middle.1
  88.4 1.0 copy-done.1
  89.4 7.9 %all-to-all-start.2 = ((bf16[32,128,128]{2,1,0:T(8,128)(2,1)}), bf16[32,128,128]{2,1,0:T(8,128)(2,1)S(1)}, u32[]{:S(2)}, u32[]{:S(2)}) async-start(bf16[32,128,128]{2,1,0:T(8,128)(2,1)} %copy-done.1), calls=%async_computation.2 | async-start | bytes 2097152 | tf_op jit(solution)/shard_map/all_to_all | solution.py:201
  97.3 3.4 %collective-permute-start.4 = (bf16[256,512]{1,0:T(8,128)(2,1)S(1)}, bf16[256,512]{1,0:T(8,128)(2,1)S(1)}, u32[]{:S(2)}, u32[]{:S(2)}) collective-permute-start(bf16[256,512]{1,0:T(8,128)(2,1)S(1)} %get-tuple-element.20), channel_id=1, source_target_pairs={{0,1},{1,0},{2,3},{3,2},{4,5},{5,4},{6,7},{7,6},{8,9},{9,8},{10,11... | collective-permute-start | bytes 786440 | tf_op jit(solution)/shard_map/ppermute | solution.py:136
  100.8 1.1 collective-permute-done.4
  101.9 0.1 add_convert_fusion.1
  102.0 3.4 %collective-permute-start.5 = (bf16[128,512]{1,0:T(8,128)(2,1)S(1)}, bf16[128,512]{1,0:T(8,128)(2,1)S(1)}, u32[]{:S(2)}, u32[]{:S(2)}) collective-permute-start(bf16[128,512]{1,0:T(8,128)(2,1)S(1)} %dynamic-slice_bitcast_fusion), channel_id=1, source_target_pairs={{0,16},{16,0},{32,48},{48,32},{1,17},{17,1},{33,49},{49,33},{2,18}... | collective-permute-start | bytes 393224 | tf_op jit(solution)/shard_map/ppermute | solution.py:136
  105.5 5.2 %collective-permute-done.5 = bf16[128,512]{1,0:T(8,128)(2,1)S(1)} collective-permute-done((bf16[128,512]{1,0:T(8,128)(2,1)S(1)}, bf16[128,512]{1,0:T(8,128)(2,1)S(1)}, u32[]{:S(2)}, u32[]{:S(2)}) %collective-permute-start.5) | collective-permute-done | bytes 131104 | tf_op jit(solution)/shard_map/ppermute | solution.py:136
  110.7 4.7 %collective-permute-start.6 = (bf16[64,512]{1,0:T(8,128)(2,1)S(1)}, bf16[64,512]{1,0:T(8,128)(2,1)S(1)}, u32[]{:S(2)}, u32[]{:S(2)}) collective-permute-start(bf16[64,512]{1,0:T(8,128)(2,1)S(1)} %dynamic-slice_bitcast_fusion.1), channel_id=1, source_target_pairs={{0,32},{16,48},{32,0},{48,16},{1,33},{17,49},{33,1},{49,17},{2,34}... | collective-permute-start | bytes 196616 | tf_op jit(solution)/shard_map/ppermute | solution.py:136
  115.5 2.5 %collective-permute-done.6 = bf16[64,512]{1,0:T(8,128)(2,1)S(1)} collective-permute-done((bf16[64,512]{1,0:T(8,128)(2,1)S(1)}, bf16[64,512]{1,0:T(8,128)(2,1)S(1)}, u32[]{:S(2)}, u32[]{:S(2)}) %collective-permute-start.6) | collective-permute-done | bytes 65568 | tf_op jit(solution)/shard_map/ppermute | solution.py:136
  118.1 2.2 %collective-permute-start.7 = (bf16[64,512]{1,0:T(8,128)(2,1)S(1)}, bf16[64,512]{1,0:T(8,128)(2,1)S(1)}, u32[]{:S(2)}, u32[]{:S(2)}) collective-permute-start(bf16[64,512]{1,0:T(8,128)(2,1)S(1)} %fusion.1), channel_id=1, source_target_pairs={{0,64},{64,0},{128,192},{192,128},{256,320},{320,256},{384,448},{4... | collective-permute-start | bytes 196616 | tf_op jit(solution)/shard_map/ppermute | solution.py:136
  120.3 3.1 %collective-permute-done.7 = bf16[64,512]{1,0:T(8,128)(2,1)S(1)} collective-permute-done((bf16[64,512]{1,0:T(8,128)(2,1)S(1)}, bf16[64,512]{1,0:T(8,128)(2,1)S(1)}, u32[]{:S(2)}, u32[]{:S(2)}) %collective-permute-start.7) | collective-permute-done | bytes 65568 | tf_op jit(solution)/shard_map/ppermute | solution.py:136
  123.4 0.0 all-to-all-done.2.mine_ref
  123.4 5.6 %collective-permute-start.8 = (bf16[32,128,128]{2,1,0:T(8,128)(2,1)S(1)}, bf16[32,128,128]{2,1,0:T(8,128)(2,1)S(1)}, u32[]{:S(2)}, u32[]{:S(2)}) collective-permute-start(bf16[32,128,128]{2,1,0:T(8,128)(2,1)S(1)} %all-to-all-done.2.mine_ref), channel_id=1, source_target_pairs={{0,1},{1,0},{2,3},{3,2},{4,5},{5,4},{6,7},{7,6},{8,9},{9,8},{10,11... | collective-permute-start | bytes 3145736 | tf_op jit(solution)/shard_map/ppermute | solution.py:136
  129.0 3.4 %collective-permute-start.9 = (bf16[64,512]{1,0:T(8,128)(2,1)S(1)}, bf16[64,512]{1,0:T(8,128)(2,1)S(1)}, u32[]{:S(2)}, u32[]{:S(2)}) collective-permute-start(bf16[64,512]{1,0:T(8,128)(2,1)S(1)} %add_convert_fusion.7), channel_id=1, source_target_pairs={{0,2},{2,0},{4,6},{6,4},{8,10},{10,8},{12,14},{14,12},{1,3},{3,1},... | collective-permute-start | bytes 196616 | tf_op jit(solution)/shard_map/ppermute | solution.py:136
  132.4 2.3 %collective-permute-done.9 = bf16[64,512]{1,0:T(8,128)(2,1)S(1)} collective-permute-done((bf16[64,512]{1,0:T(8,128)(2,1)S(1)}, bf16[64,512]{1,0:T(8,128)(2,1)S(1)}, u32[]{:S(2)}, u32[]{:S(2)}) %collective-permute-start.9) | collective-permute-done | bytes 65568 | tf_op jit(solution)/shard_map/ppermute | solution.py:136
  134.8 0.0 collective-permute-done.8.other_ref
  134.8 2.4 %backward_tiles.1 = bf16[32,128,128]{2,1,0:T(8,128)(2,1)} custom-call(s32[2]{0:T(128)S(1)} %pad_add_fusion.place_ref.core_ref, s32[4,24]{1,0:T(4,128)S(1)} %maximum_minimum_fusion.index_ref, bf16[32,128,128]{2,1,0:T(8,128)(2,1)S(1)} %all-to-all-done.2.mine_ref, bf16[32,128,128]{2,1,0:T(8,128)(2,1)S(1)} %collective-permute-done.8.other_ref, ...), custom_call_target="tpu_custom_call" | custom-call | tf_op jit(solution)/shard_map/backward_tiles/pallas_call | solution.py:211
  137.1 7.8 %all-to-all-start.3 = ((bf16[32,128,128]{2,1,0:T(8,128)(2,1)}), bf16[32,128,128]{2,1,0:T(8,128)(2,1)S(1)}, u32[]{:S(2)}, u32[]{:S(2)}) async-start(bf16[32,128,128]{2,1,0:T(8,128)(2,1)} %backward_tiles.1), calls=%async_computation.3 | async-start | bytes 2097152 | tf_op jit(solution)/shard_map/all_to_all | solution.py:221
  145.0 4.0 %collective-permute-start.10 = (bf16[64,512]{1,0:T(8,128)(2,1)S(1)}, bf16[64,512]{1,0:T(8,128)(2,1)S(1)}, u32[]{:S(2)}, u32[]{:S(2)}) collective-permute-start(bf16[64,512]{1,0:T(8,128)(2,1)S(1)} %add_convert_fusion.6), channel_id=1, source_target_pairs={{0,128},{64,192},{128,0},{192,64},{256,384},{320,448},{384,256},{4... | collective-permute-start | bytes 196616 | tf_op jit(solution)/shard_map/ppermute | solution.py:136
  149.0 21.2 %collective-permute-done.10 = bf16[64,512]{1,0:T(8,128)(2,1)S(1)} collective-permute-done((bf16[64,512]{1,0:T(8,128)(2,1)S(1)}, bf16[64,512]{1,0:T(8,128)(2,1)S(1)}, u32[]{:S(2)}, u32[]{:S(2)}) %collective-permute-start.10) | collective-permute-done | bytes 65568 | tf_op jit(solution)/shard_map/ppermute | solution.py:136
  170.3 7.6 %collective-permute-start.11 = (bf16[64,512]{1,0:T(8,128)(2,1)S(1)}, bf16[64,512]{1,0:T(8,128)(2,1)S(1)}, u32[]{:S(2)}, u32[]{:S(2)}) collective-permute-start(bf16[64,512]{1,0:T(8,128)(2,1)S(1)} %add_convert_fusion.5), channel_id=1, source_target_pairs={{0,256},{64,320},{128,384},{192,448},{256,0},{320,64},{384,128},{4... | collective-permute-start | bytes 196616 | tf_op jit(solution)/shard_map/ppermute | solution.py:136
  177.9 1.6 collective-permute-done.11
  179.5 4.4 %collective-permute-start.12 = (bf16[64,512]{1,0:T(8,128)(2,1)S(1)}, bf16[64,512]{1,0:T(8,128)(2,1)S(1)}, u32[]{:S(2)}, u32[]{:S(2)}) collective-permute-start(bf16[64,512]{1,0:T(8,128)(2,1)S(1)} %add_convert_fusion.4), channel_id=1, source_target_pairs={{0,4},{2,6},{4,0},{6,2},{8,12},{10,14},{12,8},{14,10},{1,5},{3,7},... | collective-permute-start | bytes 196616 | tf_op jit(solution)/shard_map/ppermute | solution.py:136
  183.9 1.6 collective-permute-done.12
  185.6 7.8 %collective-permute-start.13 = (bf16[64,512]{1,0:T(8,128)(2,1)S(1)}, bf16[64,512]{1,0:T(8,128)(2,1)S(1)}, u32[]{:S(2)}, u32[]{:S(2)}) collective-permute-start(bf16[64,512]{1,0:T(8,128)(2,1)S(1)} %add_convert_fusion.3), channel_id=1, source_target_pairs={{0,8},{2,10},{4,12},{6,14},{8,0},{10,2},{12,4},{14,6},{1,9},{3,11}... | collective-permute-start | bytes 196616 | tf_op jit(solution)/shard_map/ppermute | solution.py:136
  193.4 1.7 collective-permute-done.13
  195.2 0.0 all-to-all-done.3.parts_ref
  195.2 9.7 %all_to_all.26.mine_ref = bf16[4,64,512]{2,1,0:T(8,128)(2,1)S(1)} all-to-all(bf16[4,64,512]{2,1,0:T(8,128)(2,1)S(1)} %broadcast_in_dim.5), channel_id=1, replica_groups=mesh['y'=8,'x'=4,'z'=8,'core'=2] {'x'}, dimensions={0} | all-to-all | bytes 524288 | tf_op jit(solution)/shard_map/all_to_all | solution.py:237
  204.9 10.6 %collective-permute-start.14 = (bf16[4,64,512]{2,1,0:T(8,128)(2,1)S(1)}, bf16[4,64,512]{2,1,0:T(8,128)(2,1)S(1)}, u32[]{:S(2)}, u32[]{:S(2)}) collective-permute-start(bf16[4,64,512]{2,1,0:T(8,128)(2,1)S(1)} %all_to_all.26.mine_ref), channel_id=1, source_target_pairs={{0,1},{1,0},{2,3},{3,2},{4,5},{5,4},{6,7},{7,6},{8,9},{9,8},{10,11... | collective-permute-start | bytes 786440 | tf_op jit(solution)/shard_map/ppermute | solution.py:136
  215.5 1.0 last.1
  216.5 0.2 collective-permute-done.14.other_ref
  216.7 1.6 place_rows.1
  (22 shorter events, 0.3 us)
Async XLA Ops:
  0.6 0.9 copy-start.2
  2.6 10.7 %copy-start.8 = (s32[1,1,8]{2,1,0:T(1,128)S(1)}, s32[1,1,8]{2,1,0:T(1,128)}, u32[]{:S(2)}) copy-start(s32[1,1,8]{2,1,0:T(1,128)} %param.12) | copy-start | bytes 100
  2.6 10.7 %copy-start.6 = (s32[1,1,8]{2,1,0:T(1,128)S(1)}, s32[1,1,8]{2,1,0:T(1,128)}, u32[]{:S(2)}) copy-start(s32[1,1,8]{2,1,0:T(1,128)} %param.14) | copy-start | bytes 100
  2.6 10.7 %copy-start.7 = (s32[1,1,8]{2,1,0:T(1,128)S(1)}, s32[1,1,8]{2,1,0:T(1,128)}, u32[]{:S(2)}) copy-start(s32[1,1,8]{2,1,0:T(1,128)} %param.13) | copy-start | bytes 100
  2.6 10.8 %copy-start.4 = (bf16[1,1,8,128,128]{4,3,2,1,0:T(8,128)(2,1)S(1)}, bf16[1,1,8,128,128]{4,3,2,1,0:T(8,128)(2,1)}, u32[]{:S(2)}) copy-start(bf16[1,1,8,128,128]{4,3,2,1,0:T(8,128)(2,1)} %param.11) | copy-start | bytes 786436
  2.7 19.8 %copy-start.5 = (s32[3]{0:T(128)S(1)}, s32[3]{0:T(128)}, u32[]{:S(2)}) copy-start(s32[3]{0:T(128)} %constant.35.clone) | copy-start | bytes 40
  2.7 38.5 %all-to-all-start = ((bf16[32,128,128]{2,1,0:T(8,128)(2,1)}), bf16[32,128,128]{2,1,0:T(8,128)(2,1)S(1)}, u32[]{:S(2)}, u32[]{:S(2)}) async-start(bf16[32,128,128]{2,1,0:T(8,128)(2,1)} %spread.1), calls=%async_computation | async-start | bytes 2097152 | tf_op jit(solution)/shard_map/all_to_all | solution.py:162
  13.5 23.9 %collective-permute-start.2 = (bf16[1040,128]{1,0:T(8,128)(2,1)S(1)}, bf16[1040,128]{1,0:T(8,128)(2,1)S(1)}, u32[]{:S(2)}, u32[]{:S(2)}) collective-permute-start(bf16[1040,128]{1,0:T(8,128)(2,1)S(1)} %pad_maximum_fusion.refs_0_), channel_id=1, source_target_pairs={{0,48},{16,32},{32,16},{48,0},{1,49},{17,33},{33,17},{49,1},{2,50}... | collective-permute-start | bytes 798728 | tf_op jit(solution)/shard_map/ppermute | solution.py:136
  17.8 19.5 %collective-permute-start.1 = (bf16[1040,128]{1,0:T(8,128)(2,1)S(1)}, bf16[1040,128]{1,0:T(8,128)(2,1)S(1)}, u32[]{:S(2)}, u32[]{:S(2)}) collective-permute-start(bf16[1040,128]{1,0:T(8,128)(2,1)S(1)} %pad_maximum_fusion.refs_0_), channel_id=1, source_target_pairs={{0,32},{16,48},{32,0},{48,16},{1,33},{17,49},{33,1},{49,17},{2,34}... | collective-permute-start | bytes 798728 | tf_op jit(solution)/shard_map/ppermute | solution.py:136
  20.3 20.7 %collective-permute-start = (bf16[1040,128]{1,0:T(8,128)(2,1)S(1)}, bf16[1040,128]{1,0:T(8,128)(2,1)S(1)}, u32[]{:S(2)}, u32[]{:S(2)}) collective-permute-start(bf16[1040,128]{1,0:T(8,128)(2,1)S(1)} %pad_maximum_fusion.refs_0_), channel_id=1, source_target_pairs={{0,16},{16,0},{32,48},{48,32},{1,17},{17,1},{33,49},{49,33},{2,18}... | collective-permute-start | bytes 798728 | tf_op jit(solution)/shard_map/ppermute | solution.py:136
  42.7 5.4 %collective-permute-start.3 = (bf16[32,128,128]{2,1,0:T(8,128)(2,1)S(1)}, bf16[32,128,128]{2,1,0:T(8,128)(2,1)S(1)}, u32[]{:S(2)}, u32[]{:S(2)}) collective-permute-start(bf16[32,128,128]{2,1,0:T(8,128)(2,1)S(1)} %get-tuple-element.16), channel_id=1, source_target_pairs={{0,1},{1,0},{2,3},{3,2},{4,5},{5,4},{6,7},{7,6},{8,9},{9,8},{10,11... | collective-permute-start | bytes 3145736 | tf_op jit(solution)/shard_map/ppermute | solution.py:136
  48.4 38.3 %copy-start = (bf16[512,512]{1,0:T(8,128)(2,1)S(1)}, bf16[512,512]{1,0:T(8,128)(2,1)}, u32[]{:S(2)}) copy-start(bf16[512,512]{1,0:T(8,128)(2,1)} %weight_ref.3) | copy-start | bytes 1572868
  48.4 38.3 %copy-start.3 = (bf16[128,512]{1,0:T(8,128)(2,1)S(1)}, bf16[128,512]{1,0:T(8,128)(2,1)}, u32[]{:S(2)}) copy-start(bf16[128,512]{1,0:T(8,128)(2,1)} %cotangent_ref.1) | copy-start | bytes 393220
  88.4 1.0 copy-start.1
  89.4 34.0 %all-to-all-start.2 = ((bf16[32,128,128]{2,1,0:T(8,128)(2,1)}), bf16[32,128,128]{2,1,0:T(8,128)(2,1)S(1)}, u32[]{:S(2)}, u32[]{:S(2)}) async-start(bf16[32,128,128]{2,1,0:T(8,128)(2,1)} %copy-done.1), calls=%async_computation.2 | async-start | bytes 2097152 | tf_op jit(solution)/shard_map/all_to_all | solution.py:201
  97.3 4.6 %collective-permute-start.4 = (bf16[256,512]{1,0:T(8,128)(2,1)S(1)}, bf16[256,512]{1,0:T(8,128)(2,1)S(1)}, u32[]{:S(2)}, u32[]{:S(2)}) collective-permute-start(bf16[256,512]{1,0:T(8,128)(2,1)S(1)} %get-tuple-element.20), channel_id=1, source_target_pairs={{0,1},{1,0},{2,3},{3,2},{4,5},{5,4},{6,7},{7,6},{8,9},{9,8},{10,11... | collective-permute-start | bytes 786440 | tf_op jit(solution)/shard_map/ppermute | solution.py:136
  102.0 8.7 %collective-permute-start.5 = (bf16[128,512]{1,0:T(8,128)(2,1)S(1)}, bf16[128,512]{1,0:T(8,128)(2,1)S(1)}, u32[]{:S(2)}, u32[]{:S(2)}) collective-permute-start(bf16[128,512]{1,0:T(8,128)(2,1)S(1)} %dynamic-slice_bitcast_fusion), channel_id=1, source_target_pairs={{0,16},{16,0},{32,48},{48,32},{1,17},{17,1},{33,49},{49,33},{2,18}... | collective-permute-start | bytes 393224 | tf_op jit(solution)/shard_map/ppermute | solution.py:136
  110.7 7.3 %collective-permute-start.6 = (bf16[64,512]{1,0:T(8,128)(2,1)S(1)}, bf16[64,512]{1,0:T(8,128)(2,1)S(1)}, u32[]{:S(2)}, u32[]{:S(2)}) collective-permute-start(bf16[64,512]{1,0:T(8,128)(2,1)S(1)} %dynamic-slice_bitcast_fusion.1), channel_id=1, source_target_pairs={{0,32},{16,48},{32,0},{48,16},{1,33},{17,49},{33,1},{49,17},{2,34}... | collective-permute-start | bytes 196616 | tf_op jit(solution)/shard_map/ppermute | solution.py:136
  118.1 5.3 %collective-permute-start.7 = (bf16[64,512]{1,0:T(8,128)(2,1)S(1)}, bf16[64,512]{1,0:T(8,128)(2,1)S(1)}, u32[]{:S(2)}, u32[]{:S(2)}) collective-permute-start(bf16[64,512]{1,0:T(8,128)(2,1)S(1)} %fusion.1), channel_id=1, source_target_pairs={{0,64},{64,0},{128,192},{192,128},{256,320},{320,256},{384,448},{4... | collective-permute-start | bytes 196616 | tf_op jit(solution)/shard_map/ppermute | solution.py:136
  123.4 11.4 %collective-permute-start.8 = (bf16[32,128,128]{2,1,0:T(8,128)(2,1)S(1)}, bf16[32,128,128]{2,1,0:T(8,128)(2,1)S(1)}, u32[]{:S(2)}, u32[]{:S(2)}) collective-permute-start(bf16[32,128,128]{2,1,0:T(8,128)(2,1)S(1)} %all-to-all-done.2.mine_ref), channel_id=1, source_target_pairs={{0,1},{1,0},{2,3},{3,2},{4,5},{5,4},{6,7},{7,6},{8,9},{9,8},{10,11... | collective-permute-start | bytes 3145736 | tf_op jit(solution)/shard_map/ppermute | solution.py:136
  129.0 5.7 %collective-permute-start.9 = (bf16[64,512]{1,0:T(8,128)(2,1)S(1)}, bf16[64,512]{1,0:T(8,128)(2,1)S(1)}, u32[]{:S(2)}, u32[]{:S(2)}) collective-permute-start(bf16[64,512]{1,0:T(8,128)(2,1)S(1)} %add_convert_fusion.7), channel_id=1, source_target_pairs={{0,2},{2,0},{4,6},{6,4},{8,10},{10,8},{12,14},{14,12},{1,3},{3,1},... | collective-permute-start | bytes 196616 | tf_op jit(solution)/shard_map/ppermute | solution.py:136
  137.1 58.0 %all-to-all-start.3 = ((bf16[32,128,128]{2,1,0:T(8,128)(2,1)}), bf16[32,128,128]{2,1,0:T(8,128)(2,1)S(1)}, u32[]{:S(2)}, u32[]{:S(2)}) async-start(bf16[32,128,128]{2,1,0:T(8,128)(2,1)} %backward_tiles.1), calls=%async_computation.3 | async-start | bytes 2097152 | tf_op jit(solution)/shard_map/all_to_all | solution.py:221
  145.0 25.3 %collective-permute-start.10 = (bf16[64,512]{1,0:T(8,128)(2,1)S(1)}, bf16[64,512]{1,0:T(8,128)(2,1)S(1)}, u32[]{:S(2)}, u32[]{:S(2)}) collective-permute-start(bf16[64,512]{1,0:T(8,128)(2,1)S(1)} %add_convert_fusion.6), channel_id=1, source_target_pairs={{0,128},{64,192},{128,0},{192,64},{256,384},{320,448},{384,256},{4... | collective-permute-start | bytes 196616 | tf_op jit(solution)/shard_map/ppermute | solution.py:136
  170.3 9.2 %collective-permute-start.11 = (bf16[64,512]{1,0:T(8,128)(2,1)S(1)}, bf16[64,512]{1,0:T(8,128)(2,1)S(1)}, u32[]{:S(2)}, u32[]{:S(2)}) collective-permute-start(bf16[64,512]{1,0:T(8,128)(2,1)S(1)} %add_convert_fusion.5), channel_id=1, source_target_pairs={{0,256},{64,320},{128,384},{192,448},{256,0},{320,64},{384,128},{4... | collective-permute-start | bytes 196616 | tf_op jit(solution)/shard_map/ppermute | solution.py:136
  179.5 6.1 %collective-permute-start.12 = (bf16[64,512]{1,0:T(8,128)(2,1)S(1)}, bf16[64,512]{1,0:T(8,128)(2,1)S(1)}, u32[]{:S(2)}, u32[]{:S(2)}) collective-permute-start(bf16[64,512]{1,0:T(8,128)(2,1)S(1)} %add_convert_fusion.4), channel_id=1, source_target_pairs={{0,4},{2,6},{4,0},{6,2},{8,12},{10,14},{12,8},{14,10},{1,5},{3,7},... | collective-permute-start | bytes 196616 | tf_op jit(solution)/shard_map/ppermute | solution.py:136
  185.6 9.5 %collective-permute-start.13 = (bf16[64,512]{1,0:T(8,128)(2,1)S(1)}, bf16[64,512]{1,0:T(8,128)(2,1)S(1)}, u32[]{:S(2)}, u32[]{:S(2)}) collective-permute-start(bf16[64,512]{1,0:T(8,128)(2,1)S(1)} %add_convert_fusion.3), channel_id=1, source_target_pairs={{0,8},{2,10},{4,12},{6,14},{8,0},{10,2},{12,4},{14,6},{1,9},{3,11}... | collective-permute-start | bytes 196616 | tf_op jit(solution)/shard_map/ppermute | solution.py:136
  204.9 11.7 %collective-permute-start.14 = (bf16[4,64,512]{2,1,0:T(8,128)(2,1)S(1)}, bf16[4,64,512]{2,1,0:T(8,128)(2,1)S(1)}, u32[]{:S(2)}, u32[]{:S(2)}) collective-permute-start(bf16[4,64,512]{2,1,0:T(8,128)(2,1)S(1)} %all_to_all.26.mine_ref), channel_id=1, source_target_pairs={{0,1},{1,0},{2,3},{3,2},{4,5},{5,4},{6,7},{7,6},{8,9},{9,8},{10,11... | collective-permute-start | bytes 786440 | tf_op jit(solution)/shard_map/ppermute | solution.py:136

commit v9 on v8

--- a/solution.py
+++ b/solution.py
@@ -125,9 +125,8 @@
     half, share = WIDTH // CORES, WIDTH // (X * CORES)
     scale = 1.0 / math.sqrt(TILE * Y * X * Z * CORES)
     for x in range(X):
-        at = ((x & 1) * 2 + (x >> 1)) * share
         for side, ref in ((core, mine_ref), (1 - core, other_ref)):
-            start = pl.multiple_of(side * half + at, share)
+            start = pl.multiple_of(side * half + x * share, share)
             out_ref[pl.ds(start, share), :] = ref[x].astype(F32) * scale
 
 
@@ -136,12 +135,17 @@
     return lax.ppermute(array, axis, [(i, i ^ distance) for i in range(size)])
 
 
-def halve(array, axis, distance):
-    upper = jnp.minimum(lax.axis_index(axis) & distance, 1)
-    halves = array.reshape(2, array.shape[0] // 2, array.shape[1])
-    send = lax.dynamic_index_in_dim(halves, 1 - upper, 0, keepdims=False)
-    keep = lax.dynamic_index_in_dim(halves, upper, 0, keepdims=False)
-    return (keep.astype(F32) + exchange(send, axis, distance).astype(F32)).astype(BF16)
+def scatter(array, axis):
+    size, place = lax.axis_size(axis), lax.axis_index(axis)
+    shares = array.reshape(size, array.shape[0] // size, array.shape[1])
+
+    def share(distance):
+        return lax.dynamic_index_in_dim(shares, place ^ distance, 0, keepdims=False)
+
+    total = share(0).astype(F32)
+    for distance in range(1, size):
+        total = total + exchange(share(distance), axis, distance).astype(F32)
+    return total.astype(BF16)
 
 
 def double(array, axis, distance):
@@ -201,13 +205,13 @@
     grad_mine = lax.all_to_all(grad, ("x", "z"), 0, 0, tiled=True)
     piece = weight_keep.astype(F32) + exchange(weight_send, "core", 1).astype(F32)
     piece = piece.astype(BF16)
+    piece = scatter(piece, "x")
     for distance in (1, 2):
-        piece = halve(piece, "x", distance)
-    piece = double(piece, "y", 1)
+        piece = double(piece, "y", distance)
     grad_mine, piece = lax.optimization_barrier((grad_mine, piece))
 
     grad_other = exchange(grad_mine, "core", 1)
-    piece = double(piece, "z", 1)
+    piece = double(piece, "y", 4)
     back = pl.pallas_call(
         backward_tiles,
         in_specs=[smem(), smem()] + [vmem()] * (2 + X),
@@ -219,8 +223,8 @@
     )(place, index, grad_mine, grad_other, *tiles)
     back, piece = lax.optimization_barrier((back, piece))
     back = lax.all_to_all(back, ("y", "x"), 0, 0, tiled=True)
-    for axis, distance in (("y", 2), ("y", 4), ("z", 2), ("z", 4)):
-        piece = double(piece, axis, distance)
+    for distance in (1, 2, 4):
+        piece = double(piece, "z", distance)
     back, piece = lax.optimization_barrier((back, piece))
 
     input_grad = pl.pallas_call(

time: 219 us -> 198 us (0.904)
  starting transfers between devices: 95.8 us -> 83.5 us
  waiting for transfers between devices: 61.3 us -> 52.2 us
    ppermute x15 -> x16, waiting for transfers between devices: 61.3 us -> 47.4 us  [exchange(): return lax.ppermute(array, axis, [(i, i ^ distance) for i in range(size)])]
    ppermute x15 -> x16, starting transfers between devices: 69.3 us -> 60.9 us  [exchange(): return lax.ppermute(array, axis, [(i, i ^ distance) for i in range(size)])]
    all_to_all x1, waiting for transfers between devices: 0.01 us -> 4.83 us  [body(): back = lax.all_to_all(back, ('y', 'x'), 0, 0, tiled=True)]
    all_to_all x1, starting transfers between devices: 7.82 us -> 4.03 us  [body(): back = lax.all_to_all(back, ('y', 'x'), 0, 0, tiled=True)]
  transfers between devices with their start and end apart: 18 -> 19, of which waited for: 13 -> 14; matrix products, arithmetic and copies ran while one was open for 0% -> 0% of each run, Pallas kernels for 0% -> 0%
where the time goes in v9:
time: 198 us; the launch traced here: 197 us
  starting transfers between devices  83.5 us (42%)
  waiting for transfers between devices  52.2 us (26%)
  blocking collectives  47.7 us (24%)
  Pallas kernels  9.23 us (5%)
  local copies, waits for them, and re-layouts  2.1 us (1%)
    ppermute x16, starting transfers between devices, exchange(): return lax.ppermute(array, axis, [(i, i ^ distance) for i in range(size)])  60.9 us
    ppermute x16, waiting for transfers between devices, exchange(): return lax.ppermute(array, axis, [(i, i ^ distance) for i in range(size)])  47.4 us
    all_to_all x1, blocking collectives, body(): parts = lax.all_to_all(term, ('x', 'z'), 0, 0, tiled=True)  38.3 us
    all_to_all x1, starting transfers between devices, body(): panel = lax.all_to_all(chunks, ('y', 'x'), 0, 0, tiled=True)  10.6 us
    all_to_all x1, blocking collectives, body(): whole = lax.all_to_all(piece, 'x', 0, 0, tiled=True)  9.47 us
    all_to_all x1, starting transfers between devices, body(): grad_mine = lax.all_to_all(grad, ('x', 'z'), 0, 0, tiled=True)  7.94 us
    all_to_all x1, waiting for transfers between devices, body(): back = lax.all_to_all(back, ('y', 'x'), 0, 0, tiled=True)  4.83 us
    all_to_all x1, starting transfers between devices, body(): back = lax.all_to_all(back, ('y', 'x'), 0, 0, tiled=True)  4.03 us
  transfers between devices with their start and end apart: 19, of which 14 were waited for; matrix products, arithmetic and copies ran while one was open for 0% of the time, Pallas kernels for 0%

profile of v9, /device:TPU:1, one launch (start us, length us, event | category | flops | bytes accessed | tf_op | source)
XLA Modules:
  0.0 196.7 jit_solution(15188347593785398741)
XLA Ops:
  0.6 0.0 copy-start.2
  0.6 0.9 copy-done.2
  1.5 1.1 spread.1
  2.7 0.0 copy-start.5
  2.7 10.6 %all-to-all-start = ((bf16[32,128,128]{2,1,0:T(8,128)(2,1)}), bf16[32,128,128]{2,1,0:T(8,128)(2,1)S(1)}, u32[]{:S(2)}, u32[]{:S(2)}) async-start(bf16[32,128,128]{2,1,0:T(8,128)(2,1)} %spread.1), calls=%async_computation | async-start | bytes 2097152 | tf_op jit(solution)/shard_map/all_to_all | solution.py:166
  13.3 0.0 copy-done.8
  13.3 0.0 copy-done.6
  13.3 0.0 copy-done.7
  13.4 0.1 fusion.11
  13.5 4.3 %collective-permute-start.2 = (bf16[1040,128]{1,0:T(8,128)(2,1)S(1)}, bf16[1040,128]{1,0:T(8,128)(2,1)S(1)}, u32[]{:S(2)}, u32[]{:S(2)}) collective-permute-start(bf16[1040,128]{1,0:T(8,128)(2,1)S(1)} %pad_maximum_fusion.refs_0_), channel_id=1, source_target_pairs={{0,48},{16,32},{32,16},{48,0},{1,49},{17,33},{33,17},{49,1},{2,50}... | collective-permute-start | bytes 798728 | tf_op jit(solution)/shard_map/ppermute | solution.py:135
  17.8 2.5 %collective-permute-start.1 = (bf16[1040,128]{1,0:T(8,128)(2,1)S(1)}, bf16[1040,128]{1,0:T(8,128)(2,1)S(1)}, u32[]{:S(2)}, u32[]{:S(2)}) collective-permute-start(bf16[1040,128]{1,0:T(8,128)(2,1)S(1)} %pad_maximum_fusion.refs_0_), channel_id=1, source_target_pairs={{0,32},{16,48},{32,0},{48,16},{1,33},{17,49},{33,1},{49,17},{2,34}... | collective-permute-start | bytes 798728 | tf_op jit(solution)/shard_map/ppermute | solution.py:135
  20.3 2.1 %collective-permute-start = (bf16[1040,128]{1,0:T(8,128)(2,1)S(1)}, bf16[1040,128]{1,0:T(8,128)(2,1)S(1)}, u32[]{:S(2)}, u32[]{:S(2)}) collective-permute-start(bf16[1040,128]{1,0:T(8,128)(2,1)S(1)} %pad_maximum_fusion.refs_0_), channel_id=1, source_target_pairs={{0,16},{16,0},{32,48},{48,32},{1,17},{17,1},{33,49},{49,33},{2,18}... | collective-permute-start | bytes 798728 | tf_op jit(solution)/shard_map/ppermute | solution.py:135
  22.5 0.0 copy-done.5
  22.5 0.1 broadcast_in_dim.4
  22.6 0.1 min.14
  22.7 0.1 pad_add_fusion.place_ref.core_ref
  22.7 14.6 %collective-permute-done.2.refs_3_ = bf16[1040,128]{1,0:T(8,128)(2,1)S(1)} collective-permute-done((bf16[1040,128]{1,0:T(8,128)(2,1)S(1)}, bf16[1040,128]{1,0:T(8,128)(2,1)S(1)}, u32[]{:S(2)}, u32[]{:S(2)}) %collective-permute-start.2) | collective-permute-done | bytes 266272 | tf_op jit(solution)/shard_map/ppermute | solution.py:135
  37.4 0.0 collective-permute-done.1.refs_2_
  37.4 3.7 %collective-permute-done.refs_1_ = bf16[1040,128]{1,0:T(8,128)(2,1)S(1)} collective-permute-done((bf16[1040,128]{1,0:T(8,128)(2,1)S(1)}, bf16[1040,128]{1,0:T(8,128)(2,1)S(1)}, u32[]{:S(2)}, u32[]{:S(2)}) %collective-permute-start) | collective-permute-done | bytes 266272 | tf_op jit(solution)/shard_map/ppermute | solution.py:135
  41.1 0.1 maximum_minimum_fusion.index_ref
  41.2 0.0 all-to-all-done.panel_ref
  41.2 1.5 forward_tiles.1
  42.7 3.1 %collective-permute-start.3 = (bf16[32,128,128]{2,1,0:T(8,128)(2,1)S(1)}, bf16[32,128,128]{2,1,0:T(8,128)(2,1)S(1)}, u32[]{:S(2)}, u32[]{:S(2)}) collective-permute-start(bf16[32,128,128]{2,1,0:T(8,128)(2,1)S(1)} %get-tuple-element.16), channel_id=1, source_target_pairs={{0,1},{1,0},{2,3},{3,2},{4,5},{5,4},{6,7},{7,6},{8,9},{9,8},{10,11... | collective-permute-start | bytes 3145736 | tf_op jit(solution)/shard_map/ppermute | solution.py:135
  45.8 2.3 %collective-permute-done.3 = bf16[32,128,128]{2,1,0:T(8,128)(2,1)S(1)} collective-permute-done((bf16[32,128,128]{2,1,0:T(8,128)(2,1)S(1)}, bf16[32,128,128]{2,1,0:T(8,128)(2,1)S(1)}, u32[]{:S(2)}, u32[]{:S(2)}) %collective-permute-start.3) | collective-permute-done | bytes 1048608 | tf_op jit(solution)/shard_map/ppermute | solution.py:135
  48.1 0.4 add_convert_fusion
  48.4 0.0 copy-start
  48.4 0.0 copy-start.3
  48.5 38.3 %all_to_all.25.parts_ref = bf16[32,128,128]{2,1,0:T(8,128)(2,1)S(1)} all-to-all(bf16[32,128,128]{2,1,0:T(8,128)(2,1)S(1)} %add_convert_fusion), channel_id=1, replica_groups=mesh['y'=8,'x'=4,'z'=8,'core'=2] {'x','z'}, dimensions={0} | all-to-all | bytes 2097152 | tf_op jit(solution)/shard_map/all_to_all | solution.py:188
  86.7 0.0 copy-done
  86.7 1.7 middle.1
  88.4 1.0 copy-done.1
  89.4 7.9 %all-to-all-start.2 = ((bf16[32,128,128]{2,1,0:T(8,128)(2,1)}), bf16[32,128,128]{2,1,0:T(8,128)(2,1)S(1)}, u32[]{:S(2)}, u32[]{:S(2)}) async-start(bf16[32,128,128]{2,1,0:T(8,128)(2,1)} %copy-done.1), calls=%async_computation.2 | async-start | bytes 2097152 | tf_op jit(solution)/shard_map/all_to_all | solution.py:205
  97.3 3.4 %collective-permute-start.4 = (bf16[256,512]{1,0:T(8,128)(2,1)S(1)}, bf16[256,512]{1,0:T(8,128)(2,1)S(1)}, u32[]{:S(2)}, u32[]{:S(2)}) collective-permute-start(bf16[256,512]{1,0:T(8,128)(2,1)S(1)} %get-tuple-element.20), channel_id=1, source_target_pairs={{0,1},{1,0},{2,3},{3,2},{4,5},{5,4},{6,7},{7,6},{8,9},{9,8},{10,11... | collective-permute-start | bytes 786440 | tf_op jit(solution)/shard_map/ppermute | solution.py:135
  100.8 1.1 collective-permute-done.4
  101.9 0.1 add_convert_fusion.1
  102.0 3.4 %collective-permute-start.5 = (bf16[64,512]{1,0:T(8,128)(2,1)S(1)}, bf16[64,512]{1,0:T(8,128)(2,1)S(1)}, u32[]{:S(2)}, u32[]{:S(2)}) collective-permute-start(bf16[64,512]{1,0:T(8,128)(2,1)S(1)} %get-tuple-element.27), channel_id=1, source_target_pairs={{0,16},{16,0},{32,48},{48,32},{1,17},{17,1},{33,49},{49,33},{2,18}... | collective-permute-start | bytes 196616 | tf_op jit(solution)/shard_map/ppermute | solution.py:135
  105.5 3.7 %collective-permute-start.7 = (bf16[64,512]{1,0:T(8,128)(2,1)S(1)}, bf16[64,512]{1,0:T(8,128)(2,1)S(1)}, u32[]{:S(2)}, u32[]{:S(2)}) collective-permute-start(bf16[64,512]{1,0:T(8,128)(2,1)S(1)} %get-tuple-element.28), channel_id=1, source_target_pairs={{0,48},{16,32},{32,16},{48,0},{1,49},{17,33},{33,17},{49,1},{2,50}... | collective-permute-start | bytes 196616 | tf_op jit(solution)/shard_map/ppermute | solution.py:135
  109.2 2.6 %collective-permute-start.6 = (bf16[64,512]{1,0:T(8,128)(2,1)S(1)}, bf16[64,512]{1,0:T(8,128)(2,1)S(1)}, u32[]{:S(2)}, u32[]{:S(2)}) collective-permute-start(bf16[64,512]{1,0:T(8,128)(2,1)S(1)} %get-tuple-element.29), channel_id=1, source_target_pairs={{0,32},{16,48},{32,0},{48,16},{1,33},{17,49},{33,1},{49,17},{2,34}... | collective-permute-start | bytes 196616 | tf_op jit(solution)/shard_map/ppermute | solution.py:135
  111.7 0.0 collective-permute-done.5
  111.7 0.4 collective-permute-done.7
  112.1 5.3 %collective-permute-done.6 = bf16[64,512]{1,0:T(8,128)(2,1)S(1)} collective-permute-done((bf16[64,512]{1,0:T(8,128)(2,1)S(1)}, bf16[64,512]{1,0:T(8,128)(2,1)S(1)}, u32[]{:S(2)}, u32[]{:S(2)}) %collective-permute-start.6) | collective-permute-done | bytes 65568 | tf_op jit(solution)/shard_map/ppermute | solution.py:135
  117.5 2.2 %collective-permute-start.8 = (bf16[64,512]{1,0:T(8,128)(2,1)S(1)}, bf16[64,512]{1,0:T(8,128)(2,1)S(1)}, u32[]{:S(2)}, u32[]{:S(2)}) collective-permute-start(bf16[64,512]{1,0:T(8,128)(2,1)S(1)} %fusion.2), channel_id=1, source_target_pairs={{0,64},{64,0},{128,192},{192,128},{256,320},{320,256},{384,448},{4... | collective-permute-start | bytes 196616 | tf_op jit(solution)/shard_map/ppermute | solution.py:135
  119.7 3.1 %collective-permute-done.8 = bf16[64,512]{1,0:T(8,128)(2,1)S(1)} collective-permute-done((bf16[64,512]{1,0:T(8,128)(2,1)S(1)}, bf16[64,512]{1,0:T(8,128)(2,1)S(1)}, u32[]{:S(2)}, u32[]{:S(2)}) %collective-permute-start.8) | collective-permute-done | bytes 65568 | tf_op jit(solution)/shard_map/ppermute | solution.py:135
  122.8 3.0 %collective-permute-start.9 = (bf16[64,512]{1,0:T(8,128)(2,1)S(1)}, bf16[64,512]{1,0:T(8,128)(2,1)S(1)}, u32[]{:S(2)}, u32[]{:S(2)}) collective-permute-start(bf16[64,512]{1,0:T(8,128)(2,1)S(1)} %add_convert_fusion.7), channel_id=1, source_target_pairs={{0,128},{64,192},{128,0},{192,64},{256,384},{320,448},{384,256},{4... | collective-permute-start | bytes 196616 | tf_op jit(solution)/shard_map/ppermute | solution.py:135
  125.8 3.6 %collective-permute-done.9 = bf16[64,512]{1,0:T(8,128)(2,1)S(1)} collective-permute-done((bf16[64,512]{1,0:T(8,128)(2,1)S(1)}, bf16[64,512]{1,0:T(8,128)(2,1)S(1)}, u32[]{:S(2)}, u32[]{:S(2)}) %collective-permute-start.9) | collective-permute-done | bytes 65568 | tf_op jit(solution)/shard_map/ppermute | solution.py:135
  129.4 0.0 all-to-all-done.2.mine_ref
  129.4 5.1 %collective-permute-start.10 = (bf16[32,128,128]{2,1,0:T(8,128)(2,1)S(1)}, bf16[32,128,128]{2,1,0:T(8,128)(2,1)S(1)}, u32[]{:S(2)}, u32[]{:S(2)}) collective-permute-start(bf16[32,128,128]{2,1,0:T(8,128)(2,1)S(1)} %all-to-all-done.2.mine_ref), channel_id=1, source_target_pairs={{0,1},{1,0},{2,3},{3,2},{4,5},{5,4},{6,7},{7,6},{8,9},{9,8},{10,11... | collective-permute-start | bytes 3145736 | tf_op jit(solution)/shard_map/ppermute | solution.py:135
  134.6 4.3 %collective-permute-start.11 = (bf16[64,512]{1,0:T(8,128)(2,1)S(1)}, bf16[64,512]{1,0:T(8,128)(2,1)S(1)}, u32[]{:S(2)}, u32[]{:S(2)}) collective-permute-start(bf16[64,512]{1,0:T(8,128)(2,1)S(1)} %add_convert_fusion.6), channel_id=1, source_target_pairs={{0,256},{64,320},{128,384},{192,448},{256,0},{320,64},{384,128},{4... | collective-permute-start | bytes 196616 | tf_op jit(solution)/shard_map/ppermute | solution.py:135
  138.9 6.6 %collective-permute-done.11 = bf16[64,512]{1,0:T(8,128)(2,1)S(1)} collective-permute-done((bf16[64,512]{1,0:T(8,128)(2,1)S(1)}, bf16[64,512]{1,0:T(8,128)(2,1)S(1)}, u32[]{:S(2)}, u32[]{:S(2)}) %collective-permute-start.11) | collective-permute-done | bytes 65568 | tf_op jit(solution)/shard_map/ppermute | solution.py:135
  145.5 0.0 collective-permute-done.10.other_ref
  145.5 2.4 %backward_tiles.1 = bf16[32,128,128]{2,1,0:T(8,128)(2,1)} custom-call(s32[2]{0:T(128)S(1)} %pad_add_fusion.place_ref.core_ref, s32[4,24]{1,0:T(4,128)S(1)} %maximum_minimum_fusion.index_ref, bf16[32,128,128]{2,1,0:T(8,128)(2,1)S(1)} %all-to-all-done.2.mine_ref, bf16[32,128,128]{2,1,0:T(8,128)(2,1)S(1)} %collective-permute-done.10.other_ref, ...), custom_call_target="tpu_custom_call" | custom-call | tf_op jit(solution)/shard_map/backward_tiles/pallas_call | solution.py:215
  147.9 4.0 %all-to-all-start.3 = ((bf16[32,128,128]{2,1,0:T(8,128)(2,1)}), bf16[32,128,128]{2,1,0:T(8,128)(2,1)S(1)}, u32[]{:S(2)}, u32[]{:S(2)}) async-start(bf16[32,128,128]{2,1,0:T(8,128)(2,1)} %backward_tiles.1), calls=%async_computation.3 | async-start | bytes 2097152 | tf_op jit(solution)/shard_map/all_to_all | solution.py:225
  152.0 3.3 %collective-permute-start.12 = (bf16[64,512]{1,0:T(8,128)(2,1)S(1)}, bf16[64,512]{1,0:T(8,128)(2,1)S(1)}, u32[]{:S(2)}, u32[]{:S(2)}) collective-permute-start(bf16[64,512]{1,0:T(8,128)(2,1)S(1)} %add_convert_fusion.5), channel_id=1, source_target_pairs={{0,2},{2,0},{4,6},{6,4},{8,10},{10,8},{12,14},{14,12},{1,3},{3,1},... | collective-permute-start | bytes 196616 | tf_op jit(solution)/shard_map/ppermute | solution.py:135
  155.3 2.0 %collective-permute-done.12 = bf16[64,512]{1,0:T(8,128)(2,1)S(1)} collective-permute-done((bf16[64,512]{1,0:T(8,128)(2,1)S(1)}, bf16[64,512]{1,0:T(8,128)(2,1)S(1)}, u32[]{:S(2)}, u32[]{:S(2)}) %collective-permute-start.12) | collective-permute-done | bytes 65568 | tf_op jit(solution)/shard_map/ppermute | solution.py:135
  157.3 4.2 %collective-permute-start.13 = (bf16[64,512]{1,0:T(8,128)(2,1)S(1)}, bf16[64,512]{1,0:T(8,128)(2,1)S(1)}, u32[]{:S(2)}, u32[]{:S(2)}) collective-permute-start(bf16[64,512]{1,0:T(8,128)(2,1)S(1)} %add_convert_fusion.4), channel_id=1, source_target_pairs={{0,4},{2,6},{4,0},{6,2},{8,12},{10,14},{12,8},{14,10},{1,5},{3,7},... | collective-permute-start | bytes 196616 | tf_op jit(solution)/shard_map/ppermute | solution.py:135
  161.5 2.0 collective-permute-done.13
  163.5 6.7 %collective-permute-start.14 = (bf16[64,512]{1,0:T(8,128)(2,1)S(1)}, bf16[64,512]{1,0:T(8,128)(2,1)S(1)}, u32[]{:S(2)}, u32[]{:S(2)}) collective-permute-start(bf16[64,512]{1,0:T(8,128)(2,1)S(1)} %add_convert_fusion.3), channel_id=1, source_target_pairs={{0,8},{2,10},{4,12},{6,14},{8,0},{10,2},{12,4},{14,6},{1,9},{3,11}... | collective-permute-start | bytes 196616 | tf_op jit(solution)/shard_map/ppermute | solution.py:135
  170.2 2.5 %collective-permute-done.14 = bf16[64,512]{1,0:T(8,128)(2,1)S(1)} collective-permute-done((bf16[64,512]{1,0:T(8,128)(2,1)S(1)}, bf16[64,512]{1,0:T(8,128)(2,1)S(1)}, u32[]{:S(2)}, u32[]{:S(2)}) %collective-permute-start.14) | collective-permute-done | bytes 65568 | tf_op jit(solution)/shard_map/ppermute | solution.py:135
  172.7 4.8 %all-to-all-done.3.parts_ref = bf16[32,128,128]{2,1,0:T(8,128)(2,1)S(1)} async-done(((bf16[32,128,128]{2,1,0:T(8,128)(2,1)}), bf16[32,128,128]{2,1,0:T(8,128)(2,1)S(1)}, u32[]{:S(2)}, u32[]{:S(2)}) %all-to-all-start.3) | async-done | bytes 1048608 | tf_op jit(solution)/shard_map/all_to_all | solution.py:225
  177.6 9.5 %all_to_all.26.mine_ref = bf16[4,64,512]{2,1,0:T(8,128)(2,1)S(1)} all-to-all(bf16[4,64,512]{2,1,0:T(8,128)(2,1)S(1)} %broadcast_in_dim.5), channel_id=1, replica_groups=mesh['y'=8,'x'=4,'z'=8,'core'=2] {'x'}, dimensions={0} | all-to-all | bytes 524288 | tf_op jit(solution)/shard_map/all_to_all | solution.py:241
  187.1 6.9 %collective-permute-start.15 = (bf16[4,64,512]{2,1,0:T(8,128)(2,1)S(1)}, bf16[4,64,512]{2,1,0:T(8,128)(2,1)S(1)}, u32[]{:S(2)}, u32[]{:S(2)}) collective-permute-start(bf16[4,64,512]{2,1,0:T(8,128)(2,1)S(1)} %all_to_all.26.mine_ref), channel_id=1, source_target_pairs={{0,1},{1,0},{2,3},{3,2},{4,5},{5,4},{6,7},{7,6},{8,9},{9,8},{10,11... | collective-permute-start | bytes 786440 | tf_op jit(solution)/shard_map/ppermute | solution.py:135
  193.9 1.0 last.1
  194.9 0.2 collective-permute-done.15.other_ref
  195.1 1.6 place_rows.1
  (22 shorter events, 0.2 us)
Async XLA Ops:
  0.6 0.9 copy-start.2
  2.6 10.7 %copy-start.8 = (s32[1,1,8]{2,1,0:T(1,128)S(1)}, s32[1,1,8]{2,1,0:T(1,128)}, u32[]{:S(2)}) copy-start(s32[1,1,8]{2,1,0:T(1,128)} %param.12) | copy-start | bytes 100
  2.6 10.7 %copy-start.6 = (s32[1,1,8]{2,1,0:T(1,128)S(1)}, s32[1,1,8]{2,1,0:T(1,128)}, u32[]{:S(2)}) copy-start(s32[1,1,8]{2,1,0:T(1,128)} %param.14) | copy-start | bytes 100
  2.6 10.7 %copy-start.7 = (s32[1,1,8]{2,1,0:T(1,128)S(1)}, s32[1,1,8]{2,1,0:T(1,128)}, u32[]{:S(2)}) copy-start(s32[1,1,8]{2,1,0:T(1,128)} %param.13) | copy-start | bytes 100
  2.6 10.8 %copy-start.4 = (bf16[1,1,8,128,128]{4,3,2,1,0:T(8,128)(2,1)S(1)}, bf16[1,1,8,128,128]{4,3,2,1,0:T(8,128)(2,1)}, u32[]{:S(2)}) copy-start(bf16[1,1,8,128,128]{4,3,2,1,0:T(8,128)(2,1)} %param.11) | copy-start | bytes 786436
  2.7 19.8 %copy-start.5 = (s32[3]{0:T(128)S(1)}, s32[3]{0:T(128)}, u32[]{:S(2)}) copy-start(s32[3]{0:T(128)} %constant.33.clone) | copy-start | bytes 40
  2.7 38.5 %all-to-all-start = ((bf16[32,128,128]{2,1,0:T(8,128)(2,1)}), bf16[32,128,128]{2,1,0:T(8,128)(2,1)S(1)}, u32[]{:S(2)}, u32[]{:S(2)}) async-start(bf16[32,128,128]{2,1,0:T(8,128)(2,1)} %spread.1), calls=%async_computation | async-start | bytes 2097152 | tf_op jit(solution)/shard_map/all_to_all | solution.py:166
  13.5 23.9 %collective-permute-start.2 = (bf16[1040,128]{1,0:T(8,128)(2,1)S(1)}, bf16[1040,128]{1,0:T(8,128)(2,1)S(1)}, u32[]{:S(2)}, u32[]{:S(2)}) collective-permute-start(bf16[1040,128]{1,0:T(8,128)(2,1)S(1)} %pad_maximum_fusion.refs_0_), channel_id=1, source_target_pairs={{0,48},{16,32},{32,16},{48,0},{1,49},{17,33},{33,17},{49,1},{2,50}... | collective-permute-start | bytes 798728 | tf_op jit(solution)/shard_map/ppermute | solution.py:135
  17.8 19.5 %collective-permute-start.1 = (bf16[1040,128]{1,0:T(8,128)(2,1)S(1)}, bf16[1040,128]{1,0:T(8,128)(2,1)S(1)}, u32[]{:S(2)}, u32[]{:S(2)}) collective-permute-start(bf16[1040,128]{1,0:T(8,128)(2,1)S(1)} %pad_maximum_fusion.refs_0_), channel_id=1, source_target_pairs={{0,32},{16,48},{32,0},{48,16},{1,33},{17,49},{33,1},{49,17},{2,34}... | collective-permute-start | bytes 798728 | tf_op jit(solution)/shard_map/ppermute | solution.py:135
  20.3 20.7 %collective-permute-start = (bf16[1040,128]{1,0:T(8,128)(2,1)S(1)}, bf16[1040,128]{1,0:T(8,128)(2,1)S(1)}, u32[]{:S(2)}, u32[]{:S(2)}) collective-permute-start(bf16[1040,128]{1,0:T(8,128)(2,1)S(1)} %pad_maximum_fusion.refs_0_), channel_id=1, source_target_pairs={{0,16},{16,0},{32,48},{48,32},{1,17},{17,1},{33,49},{49,33},{2,18}... | collective-permute-start | bytes 798728 | tf_op jit(solution)/shard_map/ppermute | solution.py:135
  42.7 5.4 %collective-permute-start.3 = (bf16[32,128,128]{2,1,0:T(8,128)(2,1)S(1)}, bf16[32,128,128]{2,1,0:T(8,128)(2,1)S(1)}, u32[]{:S(2)}, u32[]{:S(2)}) collective-permute-start(bf16[32,128,128]{2,1,0:T(8,128)(2,1)S(1)} %get-tuple-element.16), channel_id=1, source_target_pairs={{0,1},{1,0},{2,3},{3,2},{4,5},{5,4},{6,7},{7,6},{8,9},{9,8},{10,11... | collective-permute-start | bytes 3145736 | tf_op jit(solution)/shard_map/ppermute | solution.py:135
  48.4 38.3 %copy-start = (bf16[512,512]{1,0:T(8,128)(2,1)S(1)}, bf16[512,512]{1,0:T(8,128)(2,1)}, u32[]{:S(2)}) copy-start(bf16[512,512]{1,0:T(8,128)(2,1)} %weight_ref.3) | copy-start | bytes 1572868
  48.4 38.3 %copy-start.3 = (bf16[128,512]{1,0:T(8,128)(2,1)S(1)}, bf16[128,512]{1,0:T(8,128)(2,1)}, u32[]{:S(2)}) copy-start(bf16[128,512]{1,0:T(8,128)(2,1)} %cotangent_ref.1) | copy-start | bytes 393220
  88.4 1.0 copy-start.1
  89.4 40.0 %all-to-all-start.2 = ((bf16[32,128,128]{2,1,0:T(8,128)(2,1)}), bf16[32,128,128]{2,1,0:T(8,128)(2,1)S(1)}, u32[]{:S(2)}, u32[]{:S(2)}) async-start(bf16[32,128,128]{2,1,0:T(8,128)(2,1)} %copy-done.1), calls=%async_computation.2 | async-start | bytes 2097152 | tf_op jit(solution)/shard_map/all_to_all | solution.py:205
  97.3 4.6 %collective-permute-start.4 = (bf16[256,512]{1,0:T(8,128)(2,1)S(1)}, bf16[256,512]{1,0:T(8,128)(2,1)S(1)}, u32[]{:S(2)}, u32[]{:S(2)}) collective-permute-start(bf16[256,512]{1,0:T(8,128)(2,1)S(1)} %get-tuple-element.20), channel_id=1, source_target_pairs={{0,1},{1,0},{2,3},{3,2},{4,5},{5,4},{6,7},{7,6},{8,9},{9,8},{10,11... | collective-permute-start | bytes 786440 | tf_op jit(solution)/shard_map/ppermute | solution.py:135
  102.0 9.7 %collective-permute-start.5 = (bf16[64,512]{1,0:T(8,128)(2,1)S(1)}, bf16[64,512]{1,0:T(8,128)(2,1)S(1)}, u32[]{:S(2)}, u32[]{:S(2)}) collective-permute-start(bf16[64,512]{1,0:T(8,128)(2,1)S(1)} %get-tuple-element.27), channel_id=1, source_target_pairs={{0,16},{16,0},{32,48},{48,32},{1,17},{17,1},{33,49},{49,33},{2,18}... | collective-permute-start | bytes 196616 | tf_op jit(solution)/shard_map/ppermute | solution.py:135
  105.5 6.7 %collective-permute-start.7 = (bf16[64,512]{1,0:T(8,128)(2,1)S(1)}, bf16[64,512]{1,0:T(8,128)(2,1)S(1)}, u32[]{:S(2)}, u32[]{:S(2)}) collective-permute-start(bf16[64,512]{1,0:T(8,128)(2,1)S(1)} %get-tuple-element.28), channel_id=1, source_target_pairs={{0,48},{16,32},{32,16},{48,0},{1,49},{17,33},{33,17},{49,1},{2,50}... | collective-permute-start | bytes 196616 | tf_op jit(solution)/shard_map/ppermute | solution.py:135
  109.2 8.3 %collective-permute-start.6 = (bf16[64,512]{1,0:T(8,128)(2,1)S(1)}, bf16[64,512]{1,0:T(8,128)(2,1)S(1)}, u32[]{:S(2)}, u32[]{:S(2)}) collective-permute-start(bf16[64,512]{1,0:T(8,128)(2,1)S(1)} %get-tuple-element.29), channel_id=1, source_target_pairs={{0,32},{16,48},{32,0},{48,16},{1,33},{17,49},{33,1},{49,17},{2,34}... | collective-permute-start | bytes 196616 | tf_op jit(solution)/shard_map/ppermute | solution.py:135
  117.5 5.3 %collective-permute-start.8 = (bf16[64,512]{1,0:T(8,128)(2,1)S(1)}, bf16[64,512]{1,0:T(8,128)(2,1)S(1)}, u32[]{:S(2)}, u32[]{:S(2)}) collective-permute-start(bf16[64,512]{1,0:T(8,128)(2,1)S(1)} %fusion.2), channel_id=1, source_target_pairs={{0,64},{64,0},{128,192},{192,128},{256,320},{320,256},{384,448},{4... | collective-permute-start | bytes 196616 | tf_op jit(solution)/shard_map/ppermute | solution.py:135
  122.8 6.6 %collective-permute-start.9 = (bf16[64,512]{1,0:T(8,128)(2,1)S(1)}, bf16[64,512]{1,0:T(8,128)(2,1)S(1)}, u32[]{:S(2)}, u32[]{:S(2)}) collective-permute-start(bf16[64,512]{1,0:T(8,128)(2,1)S(1)} %add_convert_fusion.7), channel_id=1, source_target_pairs={{0,128},{64,192},{128,0},{192,64},{256,384},{320,448},{384,256},{4... | collective-permute-start | bytes 196616 | tf_op jit(solution)/shard_map/ppermute | solution.py:135
  129.4 16.1 %collective-permute-start.10 = (bf16[32,128,128]{2,1,0:T(8,128)(2,1)S(1)}, bf16[32,128,128]{2,1,0:T(8,128)(2,1)S(1)}, u32[]{:S(2)}, u32[]{:S(2)}) collective-permute-start(bf16[32,128,128]{2,1,0:T(8,128)(2,1)S(1)} %all-to-all-done.2.mine_ref), channel_id=1, source_target_pairs={{0,1},{1,0},{2,3},{3,2},{4,5},{5,4},{6,7},{7,6},{8,9},{9,8},{10,11... | collective-permute-start | bytes 3145736 | tf_op jit(solution)/shard_map/ppermute | solution.py:135
  134.6 10.9 %collective-permute-start.11 = (bf16[64,512]{1,0:T(8,128)(2,1)S(1)}, bf16[64,512]{1,0:T(8,128)(2,1)S(1)}, u32[]{:S(2)}, u32[]{:S(2)}) collective-permute-start(bf16[64,512]{1,0:T(8,128)(2,1)S(1)} %add_convert_fusion.6), channel_id=1, source_target_pairs={{0,256},{64,320},{128,384},{192,448},{256,0},{320,64},{384,128},{4... | collective-permute-start | bytes 196616 | tf_op jit(solution)/shard_map/ppermute | solution.py:135
  147.9 29.7 %all-to-all-start.3 = ((bf16[32,128,128]{2,1,0:T(8,128)(2,1)}), bf16[32,128,128]{2,1,0:T(8,128)(2,1)S(1)}, u32[]{:S(2)}, u32[]{:S(2)}) async-start(bf16[32,128,128]{2,1,0:T(8,128)(2,1)} %backward_tiles.1), calls=%async_computation.3 | async-start | bytes 2097152 | tf_op jit(solution)/shard_map/all_to_all | solution.py:225
  152.0 5.3 %collective-permute-start.12 = (bf16[64,512]{1,0:T(8,128)(2,1)S(1)}, bf16[64,512]{1,0:T(8,128)(2,1)S(1)}, u32[]{:S(2)}, u32[]{:S(2)}) collective-permute-start(bf16[64,512]{1,0:T(8,128)(2,1)S(1)} %add_convert_fusion.5), channel_id=1, source_target_pairs={{0,2},{2,0},{4,6},{6,4},{8,10},{10,8},{12,14},{14,12},{1,3},{3,1},... | collective-permute-start | bytes 196616 | tf_op jit(solution)/shard_map/ppermute | solution.py:135
  157.3 6.2 %collective-permute-start.13 = (bf16[64,512]{1,0:T(8,128)(2,1)S(1)}, bf16[64,512]{1,0:T(8,128)(2,1)S(1)}, u32[]{:S(2)}, u32[]{:S(2)}) collective-permute-start(bf16[64,512]{1,0:T(8,128)(2,1)S(1)} %add_convert_fusion.4), channel_id=1, source_target_pairs={{0,4},{2,6},{4,0},{6,2},{8,12},{10,14},{12,8},{14,10},{1,5},{3,7},... | collective-permute-start | bytes 196616 | tf_op jit(solution)/shard_map/ppermute | solution.py:135
  163.5 9.2 %collective-permute-start.14 = (bf16[64,512]{1,0:T(8,128)(2,1)S(1)}, bf16[64,512]{1,0:T(8,128)(2,1)S(1)}, u32[]{:S(2)}, u32[]{:S(2)}) collective-permute-start(bf16[64,512]{1,0:T(8,128)(2,1)S(1)} %add_convert_fusion.3), channel_id=1, source_target_pairs={{0,8},{2,10},{4,12},{6,14},{8,0},{10,2},{12,4},{14,6},{1,9},{3,11}... | collective-permute-start | bytes 196616 | tf_op jit(solution)/shard_map/ppermute | solution.py:135
  187.1 8.0 %collective-permute-start.15 = (bf16[4,64,512]{2,1,0:T(8,128)(2,1)S(1)}, bf16[4,64,512]{2,1,0:T(8,128)(2,1)S(1)}, u32[]{:S(2)}, u32[]{:S(2)}) collective-permute-start(bf16[4,64,512]{2,1,0:T(8,128)(2,1)S(1)} %all_to_all.26.mine_ref), channel_id=1, source_target_pairs={{0,1},{1,0},{2,3},{3,2},{4,5},{5,4},{6,7},{7,6},{8,9},{9,8},{10,11... | collective-permute-start | bytes 786440 | tf_op jit(solution)/shard_map/ppermute | solution.py:135

commit v10 on v9

--- a/solution.py
+++ b/solution.py
@@ -152,6 +152,11 @@
     return (array.astype(F32) + exchange(array, axis, distance).astype(F32)).astype(BF16)
 
 
+def double4(array, axis):
+    one, two, three = (exchange(array, axis, distance).astype(F32) for distance in (1, 2, 3))
+    return ((array.astype(F32) + one) + (two + three)).astype(BF16)
+
+
 def body(features, weight, cotangent, tile_values, tile_rows, tile_cols, tile_valid):
     place = jnp.stack([lax.axis_index("core"), lax.axis_index("x")]).astype(jnp.int32)
 
@@ -206,12 +211,11 @@
     piece = weight_keep.astype(F32) + exchange(weight_send, "core", 1).astype(F32)
     piece = piece.astype(BF16)
     piece = scatter(piece, "x")
-    for distance in (1, 2):
-        piece = double(piece, "y", distance)
+    piece = double4(piece, "y")
     grad_mine, piece = lax.optimization_barrier((grad_mine, piece))
 
     grad_other = exchange(grad_mine, "core", 1)
-    piece = double(piece, "y", 4)
+    piece = double(piece, "y", Y - 1)
     back = pl.pallas_call(
         backward_tiles,
         in_specs=[smem(), smem()] + [vmem()] * (2 + X),
@@ -223,7 +227,7 @@
     )(place, index, grad_mine, grad_other, *tiles)
     back, piece = lax.optimization_barrier((back, piece))
     back = lax.all_to_all(back, ("y", "x"), 0, 0, tiled=True)
-    for distance in (1, 2, 4):
+    for distance in (1, 2, Z - 1):
         piece = double(piece, "z", distance)
     back, piece = lax.optimization_barrier((back, piece))
 

time: 198 us -> 196 us (0.990)
  waiting for transfers between devices: 52.2 us -> 45.6 us
  starting transfers between devices: 83.5 us -> 87.7 us
    ppermute x16 -> x17, waiting for transfers between devices: 47.4 us -> 38.7 us  [exchange(): return lax.ppermute(array, axis, [(i, i ^ distance) for i in range(size)])]
    all_to_all x1, starting transfers between devices: 4.03 us -> 7.81 us  [body(): back = lax.all_to_all(back, ('y', 'x'), 0, 0, tiled=True)]
    all_to_all x1, waiting for transfers between devices: 4.83 us -> 6.87 us  [body(): back = lax.all_to_all(back, ('y', 'x'), 0, 0, tiled=True)]
    ppermute x16 -> x17, starting transfers between devices: 60.9 us -> 61.3 us  [exchange(): return lax.ppermute(array, axis, [(i, i ^ distance) for i in range(size)])]
  transfers between devices with their start and end apart: 19 -> 20, of which waited for: 14 -> 14; matrix products, arithmetic and copies ran while one was open for 0% -> 0% of each run, Pallas kernels for 0% -> 0%
where the time goes in v10:
time: 196 us; the launch traced here: 195 us
  starting transfers between devices  87.7 us (45%)
  blocking collectives  48.3 us (25%)
  waiting for transfers between devices  45.6 us (23%)
  Pallas kernels  9.23 us (5%)
  local copies, waits for them, and re-layouts  2.1 us (1%)
    ppermute x17, starting transfers between devices, exchange(): return lax.ppermute(array, axis, [(i, i ^ distance) for i in range(size)])  61.3 us
    ppermute x17, waiting for transfers between devices, exchange(): return lax.ppermute(array, axis, [(i, i ^ distance) for i in range(size)])  38.7 us
    all_to_all x1, blocking collectives, body(): parts = lax.all_to_all(term, ('x', 'z'), 0, 0, tiled=True)  38.3 us
    all_to_all x1, starting transfers between devices, body(): panel = lax.all_to_all(chunks, ('y', 'x'), 0, 0, tiled=True)  10.6 us
    all_to_all x1, blocking collectives, body(): whole = lax.all_to_all(piece, 'x', 0, 0, tiled=True)  10 us
    all_to_all x1, starting transfers between devices, body(): grad_mine = lax.all_to_all(grad, ('x', 'z'), 0, 0, tiled=True)  7.94 us
    all_to_all x1, starting transfers between devices, body(): back = lax.all_to_all(back, ('y', 'x'), 0, 0, tiled=True)  7.81 us
    all_to_all x1, waiting for transfers between devices, body(): back = lax.all_to_all(back, ('y', 'x'), 0, 0, tiled=True)  6.87 us
  transfers between devices with their start and end apart: 20, of which 14 were waited for; matrix products, arithmetic and copies ran while one was open for 0% of the time, Pallas kernels for 0%

profile of v10, /device:TPU:1, one launch (start us, length us, event | category | flops | bytes accessed | tf_op | source)
XLA Modules:
  0.0 194.8 jit_solution(871429871477581745)
XLA Ops:
  0.6 0.0 copy-start.2
  0.6 0.9 copy-done.2
  1.5 1.1 spread.1
  2.7 0.0 copy-start.5
  2.7 10.6 %all-to-all-start = ((bf16[32,128,128]{2,1,0:T(8,128)(2,1)}), bf16[32,128,128]{2,1,0:T(8,128)(2,1)S(1)}, u32[]{:S(2)}, u32[]{:S(2)}) async-start(bf16[32,128,128]{2,1,0:T(8,128)(2,1)} %spread.1), calls=%async_computation | async-start | bytes 2097152 | tf_op jit(solution)/shard_map/all_to_all | solution.py:171
  13.3 0.0 copy-done.8
  13.4 0.1 fusion.11
  13.5 4.3 %collective-permute-start.2 = (bf16[1040,128]{1,0:T(8,128)(2,1)S(1)}, bf16[1040,128]{1,0:T(8,128)(2,1)S(1)}, u32[]{:S(2)}, u32[]{:S(2)}) collective-permute-start(bf16[1040,128]{1,0:T(8,128)(2,1)S(1)} %pad_maximum_fusion.refs_0_), channel_id=1, source_target_pairs={{0,48},{16,32},{32,16},{48,0},{1,49},{17,33},{33,17},{49,1},{2,50}... | collective-permute-start | bytes 798728 | tf_op jit(solution)/shard_map/ppermute | solution.py:135
  17.8 2.5 %collective-permute-start.1 = (bf16[1040,128]{1,0:T(8,128)(2,1)S(1)}, bf16[1040,128]{1,0:T(8,128)(2,1)S(1)}, u32[]{:S(2)}, u32[]{:S(2)}) collective-permute-start(bf16[1040,128]{1,0:T(8,128)(2,1)S(1)} %pad_maximum_fusion.refs_0_), channel_id=1, source_target_pairs={{0,32},{16,48},{32,0},{48,16},{1,33},{17,49},{33,1},{49,17},{2,34}... | collective-permute-start | bytes 798728 | tf_op jit(solution)/shard_map/ppermute | solution.py:135
  20.3 2.1 %collective-permute-start = (bf16[1040,128]{1,0:T(8,128)(2,1)S(1)}, bf16[1040,128]{1,0:T(8,128)(2,1)S(1)}, u32[]{:S(2)}, u32[]{:S(2)}) collective-permute-start(bf16[1040,128]{1,0:T(8,128)(2,1)S(1)} %pad_maximum_fusion.refs_0_), channel_id=1, source_target_pairs={{0,16},{16,0},{32,48},{48,32},{1,17},{17,1},{33,49},{49,33},{2,18}... | collective-permute-start | bytes 798728 | tf_op jit(solution)/shard_map/ppermute | solution.py:135
  22.5 0.0 copy-done.5
  22.5 0.1 broadcast_in_dim.4
  22.6 0.1 min.14
  22.7 0.1 pad_add_fusion.place_ref.core_ref
  22.7 14.6 %collective-permute-done.2.refs_3_ = bf16[1040,128]{1,0:T(8,128)(2,1)S(1)} collective-permute-done((bf16[1040,128]{1,0:T(8,128)(2,1)S(1)}, bf16[1040,128]{1,0:T(8,128)(2,1)S(1)}, u32[]{:S(2)}, u32[]{:S(2)}) %collective-permute-start.2) | collective-permute-done | bytes 266272 | tf_op jit(solution)/shard_map/ppermute | solution.py:135
  37.4 0.0 collective-permute-done.1.refs_2_
  37.4 3.7 %collective-permute-done.refs_1_ = bf16[1040,128]{1,0:T(8,128)(2,1)S(1)} collective-permute-done((bf16[1040,128]{1,0:T(8,128)(2,1)S(1)}, bf16[1040,128]{1,0:T(8,128)(2,1)S(1)}, u32[]{:S(2)}, u32[]{:S(2)}) %collective-permute-start) | collective-permute-done | bytes 266272 | tf_op jit(solution)/shard_map/ppermute | solution.py:135
  41.1 0.1 maximum_minimum_fusion.index_ref
  41.2 0.0 all-to-all-done.panel_ref
  41.2 1.5 forward_tiles.1
  42.7 3.1 %collective-permute-start.3 = (bf16[32,128,128]{2,1,0:T(8,128)(2,1)S(1)}, bf16[32,128,128]{2,1,0:T(8,128)(2,1)S(1)}, u32[]{:S(2)}, u32[]{:S(2)}) collective-permute-start(bf16[32,128,128]{2,1,0:T(8,128)(2,1)S(1)} %get-tuple-element.16), channel_id=1, source_target_pairs={{0,1},{1,0},{2,3},{3,2},{4,5},{5,4},{6,7},{7,6},{8,9},{9,8},{10,11... | collective-permute-start | bytes 3145736 | tf_op jit(solution)/shard_map/ppermute | solution.py:135
  45.8 2.3 %collective-permute-done.3 = bf16[32,128,128]{2,1,0:T(8,128)(2,1)S(1)} collective-permute-done((bf16[32,128,128]{2,1,0:T(8,128)(2,1)S(1)}, bf16[32,128,128]{2,1,0:T(8,128)(2,1)S(1)}, u32[]{:S(2)}, u32[]{:S(2)}) %collective-permute-start.3) | collective-permute-done | bytes 1048608 | tf_op jit(solution)/shard_map/ppermute | solution.py:135
  48.1 0.4 add_convert_fusion
  48.4 0.0 copy-start
  48.4 0.0 copy-start.3
  48.5 38.3 %all_to_all.25.parts_ref = bf16[32,128,128]{2,1,0:T(8,128)(2,1)S(1)} all-to-all(bf16[32,128,128]{2,1,0:T(8,128)(2,1)S(1)} %add_convert_fusion), channel_id=1, replica_groups=mesh['y'=8,'x'=4,'z'=8,'core'=2] {'x','z'}, dimensions={0} | all-to-all | bytes 2097152 | tf_op jit(solution)/shard_map/all_to_all | solution.py:193
  86.7 0.0 copy-done
  86.7 1.7 middle.1
  88.4 1.0 copy-done.1
  89.4 7.9 %all-to-all-start.2 = ((bf16[32,128,128]{2,1,0:T(8,128)(2,1)}), bf16[32,128,128]{2,1,0:T(8,128)(2,1)S(1)}, u32[]{:S(2)}, u32[]{:S(2)}) async-start(bf16[32,128,128]{2,1,0:T(8,128)(2,1)} %copy-done.1), calls=%async_computation.2 | async-start | bytes 2097152 | tf_op jit(solution)/shard_map/all_to_all | solution.py:210
  97.3 3.4 %collective-permute-start.4 = (bf16[256,512]{1,0:T(8,128)(2,1)S(1)}, bf16[256,512]{1,0:T(8,128)(2,1)S(1)}, u32[]{:S(2)}, u32[]{:S(2)}) collective-permute-start(bf16[256,512]{1,0:T(8,128)(2,1)S(1)} %get-tuple-element.20), channel_id=1, source_target_pairs={{0,1},{1,0},{2,3},{3,2},{4,5},{5,4},{6,7},{7,6},{8,9},{9,8},{10,11... | collective-permute-start | bytes 786440 | tf_op jit(solution)/shard_map/ppermute | solution.py:135
  100.8 1.1 collective-permute-done.4
  101.9 0.1 add_convert_fusion.1
  102.0 3.4 %collective-permute-start.5 = (bf16[64,512]{1,0:T(8,128)(2,1)S(1)}, bf16[64,512]{1,0:T(8,128)(2,1)S(1)}, u32[]{:S(2)}, u32[]{:S(2)}) collective-permute-start(bf16[64,512]{1,0:T(8,128)(2,1)S(1)} %get-tuple-element.27), channel_id=1, source_target_pairs={{0,16},{16,0},{32,48},{48,32},{1,17},{17,1},{33,49},{49,33},{2,18}... | collective-permute-start | bytes 196616 | tf_op jit(solution)/shard_map/ppermute | solution.py:135
  105.5 3.7 %collective-permute-start.7 = (bf16[64,512]{1,0:T(8,128)(2,1)S(1)}, bf16[64,512]{1,0:T(8,128)(2,1)S(1)}, u32[]{:S(2)}, u32[]{:S(2)}) collective-permute-start(bf16[64,512]{1,0:T(8,128)(2,1)S(1)} %get-tuple-element.28), channel_id=1, source_target_pairs={{0,48},{16,32},{32,16},{48,0},{1,49},{17,33},{33,17},{49,1},{2,50}... | collective-permute-start | bytes 196616 | tf_op jit(solution)/shard_map/ppermute | solution.py:135
  109.2 2.6 %collective-permute-start.6 = (bf16[64,512]{1,0:T(8,128)(2,1)S(1)}, bf16[64,512]{1,0:T(8,128)(2,1)S(1)}, u32[]{:S(2)}, u32[]{:S(2)}) collective-permute-start(bf16[64,512]{1,0:T(8,128)(2,1)S(1)} %get-tuple-element.29), channel_id=1, source_target_pairs={{0,32},{16,48},{32,0},{48,16},{1,33},{17,49},{33,1},{49,17},{2,34}... | collective-permute-start | bytes 196616 | tf_op jit(solution)/shard_map/ppermute | solution.py:135
  111.7 0.0 collective-permute-done.5
  111.7 0.4 collective-permute-done.7
  112.1 5.3 %collective-permute-done.6 = bf16[64,512]{1,0:T(8,128)(2,1)S(1)} collective-permute-done((bf16[64,512]{1,0:T(8,128)(2,1)S(1)}, bf16[64,512]{1,0:T(8,128)(2,1)S(1)}, u32[]{:S(2)}, u32[]{:S(2)}) %collective-permute-start.6) | collective-permute-done | bytes 65568 | tf_op jit(solution)/shard_map/ppermute | solution.py:135
  117.5 3.4 %collective-permute-start.10 = (bf16[64,512]{1,0:T(8,128)(2,1)S(1)}, bf16[64,512]{1,0:T(8,128)(2,1)S(1)}, u32[]{:S(2)}, u32[]{:S(2)}) collective-permute-start(bf16[64,512]{1,0:T(8,128)(2,1)S(1)} %fusion.2), channel_id=1, source_target_pairs={{0,192},{64,128},{128,64},{192,0},{256,448},{320,384},{384,320},{4... | collective-permute-start | bytes 196616 | tf_op jit(solution)/shard_map/ppermute | solution.py:135
  120.9 1.9 collective-permute-start.9
  122.8 3.9 %collective-permute-start.8 = (bf16[64,512]{1,0:T(8,128)(2,1)S(1)}, bf16[64,512]{1,0:T(8,128)(2,1)S(1)}, u32[]{:S(2)}, u32[]{:S(2)}) collective-permute-start(bf16[64,512]{1,0:T(8,128)(2,1)S(1)} %fusion.2), channel_id=1, source_target_pairs={{0,64},{64,0},{128,192},{192,128},{256,320},{320,256},{384,448},{4... | collective-permute-start | bytes 196616 | tf_op jit(solution)/shard_map/ppermute | solution.py:135
  126.8 0.0 collective-permute-done.10
  126.8 0.6 collective-permute-done.9
  127.4 1.4 collective-permute-done.8
  128.8 0.0 all-to-all-done.2.mine_ref
  128.8 4.2 %collective-permute-start.11 = (bf16[32,128,128]{2,1,0:T(8,128)(2,1)S(1)}, bf16[32,128,128]{2,1,0:T(8,128)(2,1)S(1)}, u32[]{:S(2)}, u32[]{:S(2)}) collective-permute-start(bf16[32,128,128]{2,1,0:T(8,128)(2,1)S(1)} %all-to-all-done.2.mine_ref), channel_id=1, source_target_pairs={{0,1},{1,0},{2,3},{3,2},{4,5},{5,4},{6,7},{7,6},{8,9},{9,8},{10,11... | collective-permute-start | bytes 3145736 | tf_op jit(solution)/shard_map/ppermute | solution.py:135
  133.0 3.5 %collective-permute-start.12 = (bf16[64,512]{1,0:T(8,128)(2,1)S(1)}, bf16[64,512]{1,0:T(8,128)(2,1)S(1)}, u32[]{:S(2)}, u32[]{:S(2)}) collective-permute-start(bf16[64,512]{1,0:T(8,128)(2,1)S(1)} %add_convert_fusion.6), channel_id=1, source_target_pairs={{0,448},{64,384},{128,320},{192,256},{256,192},{320,128},{384,64},... | collective-permute-start | bytes 196616 | tf_op jit(solution)/shard_map/ppermute | solution.py:135
  136.5 3.3 %collective-permute-done.12 = bf16[64,512]{1,0:T(8,128)(2,1)S(1)} collective-permute-done((bf16[64,512]{1,0:T(8,128)(2,1)S(1)}, bf16[64,512]{1,0:T(8,128)(2,1)S(1)}, u32[]{:S(2)}, u32[]{:S(2)}) %collective-permute-start.12) | collective-permute-done | bytes 65568 | tf_op jit(solution)/shard_map/ppermute | solution.py:135
  139.9 0.0 collective-permute-done.11.other_ref
  139.9 2.4 %backward_tiles.1 = bf16[32,128,128]{2,1,0:T(8,128)(2,1)} custom-call(s32[2]{0:T(128)S(1)} %pad_add_fusion.place_ref.core_ref, s32[4,24]{1,0:T(4,128)S(1)} %maximum_minimum_fusion.index_ref, bf16[32,128,128]{2,1,0:T(8,128)(2,1)S(1)} %all-to-all-done.2.mine_ref, bf16[32,128,128]{2,1,0:T(8,128)(2,1)S(1)} %collective-permute-done.11.other_ref, ...), custom_call_target="tpu_custom_call" | custom-call | tf_op jit(solution)/shard_map/backward_tiles/pallas_call | solution.py:219
  142.3 7.8 %all-to-all-start.3 = ((bf16[32,128,128]{2,1,0:T(8,128)(2,1)}), bf16[32,128,128]{2,1,0:T(8,128)(2,1)S(1)}, u32[]{:S(2)}, u32[]{:S(2)}) async-start(bf16[32,128,128]{2,1,0:T(8,128)(2,1)} %backward_tiles.1), calls=%async_computation.3 | async-start | bytes 2097152 | tf_op jit(solution)/shard_map/all_to_all | solution.py:229
  150.1 3.3 %collective-permute-start.13 = (bf16[64,512]{1,0:T(8,128)(2,1)S(1)}, bf16[64,512]{1,0:T(8,128)(2,1)S(1)}, u32[]{:S(2)}, u32[]{:S(2)}) collective-permute-start(bf16[64,512]{1,0:T(8,128)(2,1)S(1)} %add_convert_fusion.5), channel_id=1, source_target_pairs={{0,2},{2,0},{4,6},{6,4},{8,10},{10,8},{12,14},{14,12},{1,3},{3,1},... | collective-permute-start | bytes 196616 | tf_op jit(solution)/shard_map/ppermute | solution.py:135
  153.4 2.0 %collective-permute-done.13 = bf16[64,512]{1,0:T(8,128)(2,1)S(1)} collective-permute-done((bf16[64,512]{1,0:T(8,128)(2,1)S(1)}, bf16[64,512]{1,0:T(8,128)(2,1)S(1)}, u32[]{:S(2)}, u32[]{:S(2)}) %collective-permute-start.13) | collective-permute-done | bytes 65568 | tf_op jit(solution)/shard_map/ppermute | solution.py:135
  155.4 4.3 %collective-permute-start.14 = (bf16[64,512]{1,0:T(8,128)(2,1)S(1)}, bf16[64,512]{1,0:T(8,128)(2,1)S(1)}, u32[]{:S(2)}, u32[]{:S(2)}) collective-permute-start(bf16[64,512]{1,0:T(8,128)(2,1)S(1)} %add_convert_fusion.4), channel_id=1, source_target_pairs={{0,4},{2,6},{4,0},{6,2},{8,12},{10,14},{12,8},{14,10},{1,5},{3,7},... | collective-permute-start | bytes 196616 | tf_op jit(solution)/shard_map/ppermute | solution.py:135
  159.7 1.9 collective-permute-done.14
  161.6 5.6 %collective-permute-start.15 = (bf16[64,512]{1,0:T(8,128)(2,1)S(1)}, bf16[64,512]{1,0:T(8,128)(2,1)S(1)}, u32[]{:S(2)}, u32[]{:S(2)}) collective-permute-start(bf16[64,512]{1,0:T(8,128)(2,1)S(1)} %add_convert_fusion.3), channel_id=1, source_target_pairs={{0,14},{2,12},{4,10},{6,8},{8,6},{10,4},{12,2},{14,0},{1,15},{3,13... | collective-permute-start | bytes 196616 | tf_op jit(solution)/shard_map/ppermute | solution.py:135
  167.3 1.9 collective-permute-done.15
  169.2 6.9 %all-to-all-done.3.parts_ref = bf16[32,128,128]{2,1,0:T(8,128)(2,1)S(1)} async-done(((bf16[32,128,128]{2,1,0:T(8,128)(2,1)}), bf16[32,128,128]{2,1,0:T(8,128)(2,1)S(1)}, u32[]{:S(2)}, u32[]{:S(2)}) %all-to-all-start.3) | async-done | bytes 1048608 | tf_op jit(solution)/shard_map/all_to_all | solution.py:229
  176.1 10.0 %all_to_all.26.mine_ref = bf16[4,64,512]{2,1,0:T(8,128)(2,1)S(1)} all-to-all(bf16[4,64,512]{2,1,0:T(8,128)(2,1)S(1)} %broadcast_in_dim.5), channel_id=1, replica_groups=mesh['y'=8,'x'=4,'z'=8,'core'=2] {'x'}, dimensions={0} | all-to-all | bytes 524288 | tf_op jit(solution)/shard_map/all_to_all | solution.py:245
  186.1 5.9 %collective-permute-start.16 = (bf16[4,64,512]{2,1,0:T(8,128)(2,1)S(1)}, bf16[4,64,512]{2,1,0:T(8,128)(2,1)S(1)}, u32[]{:S(2)}, u32[]{:S(2)}) collective-permute-start(bf16[4,64,512]{2,1,0:T(8,128)(2,1)S(1)} %all_to_all.26.mine_ref), channel_id=1, source_target_pairs={{0,1},{1,0},{2,3},{3,2},{4,5},{5,4},{6,7},{7,6},{8,9},{9,8},{10,11... | collective-permute-start | bytes 786440 | tf_op jit(solution)/shard_map/ppermute | solution.py:135
  192.1 1.0 last.1
  193.0 0.2 collective-permute-done.16.other_ref
  193.2 1.6 place_rows.1
  (23 shorter events, 0.2 us)
Async XLA Ops:
  0.6 0.9 copy-start.2
  2.6 10.7 %copy-start.8 = (s32[1,1,8]{2,1,0:T(1,128)S(1)}, s32[1,1,8]{2,1,0:T(1,128)}, u32[]{:S(2)}) copy-start(s32[1,1,8]{2,1,0:T(1,128)} %param.12) | copy-start | bytes 100
  2.6 10.7 %copy-start.6 = (s32[1,1,8]{2,1,0:T(1,128)S(1)}, s32[1,1,8]{2,1,0:T(1,128)}, u32[]{:S(2)}) copy-start(s32[1,1,8]{2,1,0:T(1,128)} %param.14) | copy-start | bytes 100
  2.6 10.7 %copy-start.7 = (s32[1,1,8]{2,1,0:T(1,128)S(1)}, s32[1,1,8]{2,1,0:T(1,128)}, u32[]{:S(2)}) copy-start(s32[1,1,8]{2,1,0:T(1,128)} %param.13) | copy-start | bytes 100
  2.6 10.8 %copy-start.4 = (bf16[1,1,8,128,128]{4,3,2,1,0:T(8,128)(2,1)S(1)}, bf16[1,1,8,128,128]{4,3,2,1,0:T(8,128)(2,1)}, u32[]{:S(2)}) copy-start(bf16[1,1,8,128,128]{4,3,2,1,0:T(8,128)(2,1)} %param.11) | copy-start | bytes 786436
  2.7 19.8 %copy-start.5 = (s32[3]{0:T(128)S(1)}, s32[3]{0:T(128)}, u32[]{:S(2)}) copy-start(s32[3]{0:T(128)} %constant.33.clone) | copy-start | bytes 40
  2.7 38.5 %all-to-all-start = ((bf16[32,128,128]{2,1,0:T(8,128)(2,1)}), bf16[32,128,128]{2,1,0:T(8,128)(2,1)S(1)}, u32[]{:S(2)}, u32[]{:S(2)}) async-start(bf16[32,128,128]{2,1,0:T(8,128)(2,1)} %spread.1), calls=%async_computation | async-start | bytes 2097152 | tf_op jit(solution)/shard_map/all_to_all | solution.py:171
  13.5 23.9 %collective-permute-start.2 = (bf16[1040,128]{1,0:T(8,128)(2,1)S(1)}, bf16[1040,128]{1,0:T(8,128)(2,1)S(1)}, u32[]{:S(2)}, u32[]{:S(2)}) collective-permute-start(bf16[1040,128]{1,0:T(8,128)(2,1)S(1)} %pad_maximum_fusion.refs_0_), channel_id=1, source_target_pairs={{0,48},{16,32},{32,16},{48,0},{1,49},{17,33},{33,17},{49,1},{2,50}... | collective-permute-start | bytes 798728 | tf_op jit(solution)/shard_map/ppermute | solution.py:135
  17.8 19.5 %collective-permute-start.1 = (bf16[1040,128]{1,0:T(8,128)(2,1)S(1)}, bf16[1040,128]{1,0:T(8,128)(2,1)S(1)}, u32[]{:S(2)}, u32[]{:S(2)}) collective-permute-start(bf16[1040,128]{1,0:T(8,128)(2,1)S(1)} %pad_maximum_fusion.refs_0_), channel_id=1, source_target_pairs={{0,32},{16,48},{32,0},{48,16},{1,33},{17,49},{33,1},{49,17},{2,34}... | collective-permute-start | bytes 798728 | tf_op jit(solution)/shard_map/ppermute | solution.py:135
  20.3 20.7 %collective-permute-start = (bf16[1040,128]{1,0:T(8,128)(2,1)S(1)}, bf16[1040,128]{1,0:T(8,128)(2,1)S(1)}, u32[]{:S(2)}, u32[]{:S(2)}) collective-permute-start(bf16[1040,128]{1,0:T(8,128)(2,1)S(1)} %pad_maximum_fusion.refs_0_), channel_id=1, source_target_pairs={{0,16},{16,0},{32,48},{48,32},{1,17},{17,1},{33,49},{49,33},{2,18}... | collective-permute-start | bytes 798728 | tf_op jit(solution)/shard_map/ppermute | solution.py:135
  42.7 5.4 %collective-permute-start.3 = (bf16[32,128,128]{2,1,0:T(8,128)(2,1)S(1)}, bf16[32,128,128]{2,1,0:T(8,128)(2,1)S(1)}, u32[]{:S(2)}, u32[]{:S(2)}) collective-permute-start(bf16[32,128,128]{2,1,0:T(8,128)(2,1)S(1)} %get-tuple-element.16), channel_id=1, source_target_pairs={{0,1},{1,0},{2,3},{3,2},{4,5},{5,4},{6,7},{7,6},{8,9},{9,8},{10,11... | collective-permute-start | bytes 3145736 | tf_op jit(solution)/shard_map/ppermute | solution.py:135
  48.4 38.3 %copy-start = (bf16[512,512]{1,0:T(8,128)(2,1)S(1)}, bf16[512,512]{1,0:T(8,128)(2,1)}, u32[]{:S(2)}) copy-start(bf16[512,512]{1,0:T(8,128)(2,1)} %weight_ref.3) | copy-start | bytes 1572868
  48.4 38.3 %copy-start.3 = (bf16[128,512]{1,0:T(8,128)(2,1)S(1)}, bf16[128,512]{1,0:T(8,128)(2,1)}, u32[]{:S(2)}) copy-start(bf16[128,512]{1,0:T(8,128)(2,1)} %cotangent_ref.1) | copy-start | bytes 393220
  88.4 1.0 copy-start.1
  89.4 39.4 %all-to-all-start.2 = ((bf16[32,128,128]{2,1,0:T(8,128)(2,1)}), bf16[32,128,128]{2,1,0:T(8,128)(2,1)S(1)}, u32[]{:S(2)}, u32[]{:S(2)}) async-start(bf16[32,128,128]{2,1,0:T(8,128)(2,1)} %copy-done.1), calls=%async_computation.2 | async-start | bytes 2097152 | tf_op jit(solution)/shard_map/all_to_all | solution.py:210
  97.3 4.6 %collective-permute-start.4 = (bf16[256,512]{1,0:T(8,128)(2,1)S(1)}, bf16[256,512]{1,0:T(8,128)(2,1)S(1)}, u32[]{:S(2)}, u32[]{:S(2)}) collective-permute-start(bf16[256,512]{1,0:T(8,128)(2,1)S(1)} %get-tuple-element.20), channel_id=1, source_target_pairs={{0,1},{1,0},{2,3},{3,2},{4,5},{5,4},{6,7},{7,6},{8,9},{9,8},{10,11... | collective-permute-start | bytes 786440 | tf_op jit(solution)/shard_map/ppermute | solution.py:135
  102.0 9.7 %collective-permute-start.5 = (bf16[64,512]{1,0:T(8,128)(2,1)S(1)}, bf16[64,512]{1,0:T(8,128)(2,1)S(1)}, u32[]{:S(2)}, u32[]{:S(2)}) collective-permute-start(bf16[64,512]{1,0:T(8,128)(2,1)S(1)} %get-tuple-element.27), channel_id=1, source_target_pairs={{0,16},{16,0},{32,48},{48,32},{1,17},{17,1},{33,49},{49,33},{2,18}... | collective-permute-start | bytes 196616 | tf_op jit(solution)/shard_map/ppermute | solution.py:135
  105.5 6.7 %collective-permute-start.7 = (bf16[64,512]{1,0:T(8,128)(2,1)S(1)}, bf16[64,512]{1,0:T(8,128)(2,1)S(1)}, u32[]{:S(2)}, u32[]{:S(2)}) collective-permute-start(bf16[64,512]{1,0:T(8,128)(2,1)S(1)} %get-tuple-element.28), channel_id=1, source_target_pairs={{0,48},{16,32},{32,16},{48,0},{1,49},{17,33},{33,17},{49,1},{2,50}... | collective-permute-start | bytes 196616 | tf_op jit(solution)/shard_map/ppermute | solution.py:135
  109.2 8.3 %collective-permute-start.6 = (bf16[64,512]{1,0:T(8,128)(2,1)S(1)}, bf16[64,512]{1,0:T(8,128)(2,1)S(1)}, u32[]{:S(2)}, u32[]{:S(2)}) collective-permute-start(bf16[64,512]{1,0:T(8,128)(2,1)S(1)} %get-tuple-element.29), channel_id=1, source_target_pairs={{0,32},{16,48},{32,0},{48,16},{1,33},{17,49},{33,1},{49,17},{2,34}... | collective-permute-start | bytes 196616 | tf_op jit(solution)/shard_map/ppermute | solution.py:135
  117.5 9.3 %collective-permute-start.10 = (bf16[64,512]{1,0:T(8,128)(2,1)S(1)}, bf16[64,512]{1,0:T(8,128)(2,1)S(1)}, u32[]{:S(2)}, u32[]{:S(2)}) collective-permute-start(bf16[64,512]{1,0:T(8,128)(2,1)S(1)} %fusion.2), channel_id=1, source_target_pairs={{0,192},{64,128},{128,64},{192,0},{256,448},{320,384},{384,320},{4... | collective-permute-start | bytes 196616 | tf_op jit(solution)/shard_map/ppermute | solution.py:135
  120.9 6.5 %collective-permute-start.9 = (bf16[64,512]{1,0:T(8,128)(2,1)S(1)}, bf16[64,512]{1,0:T(8,128)(2,1)S(1)}, u32[]{:S(2)}, u32[]{:S(2)}) collective-permute-start(bf16[64,512]{1,0:T(8,128)(2,1)S(1)} %fusion.2), channel_id=1, source_target_pairs={{0,128},{64,192},{128,0},{192,64},{256,384},{320,448},{384,256},{4... | collective-permute-start | bytes 196616 | tf_op jit(solution)/shard_map/ppermute | solution.py:135
  122.8 5.9 %collective-permute-start.8 = (bf16[64,512]{1,0:T(8,128)(2,1)S(1)}, bf16[64,512]{1,0:T(8,128)(2,1)S(1)}, u32[]{:S(2)}, u32[]{:S(2)}) collective-permute-start(bf16[64,512]{1,0:T(8,128)(2,1)S(1)} %fusion.2), channel_id=1, source_target_pairs={{0,64},{64,0},{128,192},{192,128},{256,320},{320,256},{384,448},{4... | collective-permute-start | bytes 196616 | tf_op jit(solution)/shard_map/ppermute | solution.py:135
  128.8 11.1 %collective-permute-start.11 = (bf16[32,128,128]{2,1,0:T(8,128)(2,1)S(1)}, bf16[32,128,128]{2,1,0:T(8,128)(2,1)S(1)}, u32[]{:S(2)}, u32[]{:S(2)}) collective-permute-start(bf16[32,128,128]{2,1,0:T(8,128)(2,1)S(1)} %all-to-all-done.2.mine_ref), channel_id=1, source_target_pairs={{0,1},{1,0},{2,3},{3,2},{4,5},{5,4},{6,7},{7,6},{8,9},{9,8},{10,11... | collective-permute-start | bytes 3145736 | tf_op jit(solution)/shard_map/ppermute | solution.py:135
  133.0 6.8 %collective-permute-start.12 = (bf16[64,512]{1,0:T(8,128)(2,1)S(1)}, bf16[64,512]{1,0:T(8,128)(2,1)S(1)}, u32[]{:S(2)}, u32[]{:S(2)}) collective-permute-start(bf16[64,512]{1,0:T(8,128)(2,1)S(1)} %add_convert_fusion.6), channel_id=1, source_target_pairs={{0,448},{64,384},{128,320},{192,256},{256,192},{320,128},{384,64},... | collective-permute-start | bytes 196616 | tf_op jit(solution)/shard_map/ppermute | solution.py:135
  142.3 33.9 %all-to-all-start.3 = ((bf16[32,128,128]{2,1,0:T(8,128)(2,1)}), bf16[32,128,128]{2,1,0:T(8,128)(2,1)S(1)}, u32[]{:S(2)}, u32[]{:S(2)}) async-start(bf16[32,128,128]{2,1,0:T(8,128)(2,1)} %backward_tiles.1), calls=%async_computation.3 | async-start | bytes 2097152 | tf_op jit(solution)/shard_map/all_to_all | solution.py:229
  150.1 5.3 %collective-permute-start.13 = (bf16[64,512]{1,0:T(8,128)(2,1)S(1)}, bf16[64,512]{1,0:T(8,128)(2,1)S(1)}, u32[]{:S(2)}, u32[]{:S(2)}) collective-permute-start(bf16[64,512]{1,0:T(8,128)(2,1)S(1)} %add_convert_fusion.5), channel_id=1, source_target_pairs={{0,2},{2,0},{4,6},{6,4},{8,10},{10,8},{12,14},{14,12},{1,3},{3,1},... | collective-permute-start | bytes 196616 | tf_op jit(solution)/shard_map/ppermute | solution.py:135
  155.4 6.2 %collective-permute-start.14 = (bf16[64,512]{1,0:T(8,128)(2,1)S(1)}, bf16[64,512]{1,0:T(8,128)(2,1)S(1)}, u32[]{:S(2)}, u32[]{:S(2)}) collective-permute-start(bf16[64,512]{1,0:T(8,128)(2,1)S(1)} %add_convert_fusion.4), channel_id=1, source_target_pairs={{0,4},{2,6},{4,0},{6,2},{8,12},{10,14},{12,8},{14,10},{1,5},{3,7},... | collective-permute-start | bytes 196616 | tf_op jit(solution)/shard_map/ppermute | solution.py:135
  161.6 7.6 %collective-permute-start.15 = (bf16[64,512]{1,0:T(8,128)(2,1)S(1)}, bf16[64,512]{1,0:T(8,128)(2,1)S(1)}, u32[]{:S(2)}, u32[]{:S(2)}) collective-permute-start(bf16[64,512]{1,0:T(8,128)(2,1)S(1)} %add_convert_fusion.3), channel_id=1, source_target_pairs={{0,14},{2,12},{4,10},{6,8},{8,6},{10,4},{12,2},{14,0},{1,15},{3,13... | collective-permute-start | bytes 196616 | tf_op jit(solution)/shard_map/ppermute | solution.py:135
  186.1 7.1 %collective-permute-start.16 = (bf16[4,64,512]{2,1,0:T(8,128)(2,1)S(1)}, bf16[4,64,512]{2,1,0:T(8,128)(2,1)S(1)}, u32[]{:S(2)}, u32[]{:S(2)}) collective-permute-start(bf16[4,64,512]{2,1,0:T(8,128)(2,1)S(1)} %all_to_all.26.mine_ref), channel_id=1, source_target_pairs={{0,1},{1,0},{2,3},{3,2},{4,5},{5,4},{6,7},{7,6},{8,9},{9,8},{10,11... | collective-permute-start | bytes 786440 | tf_op jit(solution)/shard_map/ppermute | solution.py:135

commit v11 on v10

--- a/solution.py
+++ b/solution.py
@@ -56,7 +56,7 @@
             other_ref[block * Z + pair] = total[2 * pair + 1 - core].astype(BF16)
 
 
-def middle(core_ref, parts_ref, weight_ref, cotangent_ref, act_ref, grad_ref, keep_ref, send_ref):
+def middle(parts_ref, weight_ref, cotangent_ref, act_ref, grad_ref, weight_part_ref):
     chunks = []
     for chunk in range(X):
         total = parts_ref[chunk * Z].astype(F32)
@@ -77,13 +77,9 @@
         piece = grad[:, chunk * CHUNK : (chunk + 1) * CHUNK]
         for z in range(Z):
             grad_ref[chunk * Z + z] = piece
-    weight_part = lax.dot_general(
+    weight_part_ref[...] = lax.dot_general(
         high, grad, (((0,), (0,)), ((), ())), preferred_element_type=F32
     ).astype(BF16)
-    low_half, high_half = weight_part[: WIDTH // 2], weight_part[WIDTH // 2 :]
-    upper = core_ref[0] == 1
-    keep_ref[...] = jnp.where(upper, high_half, low_half)
-    send_ref[...] = jnp.where(upper, low_half, high_half)
 
 
 def backward_tiles(place_ref, index_ref, mine_ref, other_ref, *refs):
@@ -120,16 +116,6 @@
     ).astype(BF16)
 
 
-def place_rows(place_ref, mine_ref, other_ref, out_ref):
-    core = place_ref[0]
-    half, share = WIDTH // CORES, WIDTH // (X * CORES)
-    scale = 1.0 / math.sqrt(TILE * Y * X * Z * CORES)
-    for x in range(X):
-        for side, ref in ((core, mine_ref), (1 - core, other_ref)):
-            start = pl.multiple_of(side * half + x * share, share)
-            out_ref[pl.ds(start, share), :] = ref[x].astype(F32) * scale
-
-
 def exchange(array, axis, distance):
     size = lax.axis_size(axis)
     return lax.ppermute(array, axis, [(i, i ^ distance) for i in range(size)])
@@ -192,24 +178,20 @@
     term = (mine.astype(F32) + exchange(other, "core", 1).astype(F32)).astype(BF16)
     parts = lax.all_to_all(term, ("x", "z"), 0, 0, tiled=True)
 
-    half = WIDTH // CORES
-    activations, grad, weight_keep, weight_send = pl.pallas_call(
+    activations, grad, piece = pl.pallas_call(
         middle,
-        in_specs=[smem()] + [vmem()] * 3,
-        out_specs=[vmem()] * 4,
+        in_specs=[vmem()] * 3,
+        out_specs=[vmem()] * 3,
         out_shape=[
             jax.ShapeDtypeStruct((TILE, WIDTH), BF16),
             jax.ShapeDtypeStruct((X * Z, TILE, CHUNK), BF16),
-            jax.ShapeDtypeStruct((half, WIDTH), BF16),
-            jax.ShapeDtypeStruct((half, WIDTH), BF16),
+            jax.ShapeDtypeStruct((WIDTH, WIDTH), BF16),
         ],
         compiler_params=params(),
         name="middle",
-    )(place, parts, weight, cotangent)
+    )(parts, weight, cotangent)
 
     grad_mine = lax.all_to_all(grad, ("x", "z"), 0, 0, tiled=True)
-    piece = weight_keep.astype(F32) + exchange(weight_send, "core", 1).astype(F32)
-    piece = piece.astype(BF16)
     piece = scatter(piece, "x")
     piece = double4(piece, "y")
     grad_mine, piece = lax.optimization_barrier((grad_mine, piece))
@@ -229,6 +211,7 @@
     back = lax.all_to_all(back, ("y", "x"), 0, 0, tiled=True)
     for distance in (1, 2, Z - 1):
         piece = double(piece, "z", distance)
+    piece = double(piece, "core", 1)
     back, piece = lax.optimization_barrier((back, piece))
 
     input_grad = pl.pallas_call(
@@ -240,17 +223,9 @@
         name="last",
     )(back, weight)
 
-    share = WIDTH // (X * CORES)
-    piece = jnp.broadcast_to(piece[None], (X, share, WIDTH))
-    whole = lax.all_to_all(piece, "x", 0, 0, tiled=True)
-    weight_grad = pl.pallas_call(
-        place_rows,
-        in_specs=[smem()] + [vmem()] * 2,
-        out_specs=vmem(),
-        out_shape=jax.ShapeDtypeStruct((WIDTH, WIDTH), F32),
-        compiler_params=params(),
-        name="place_rows",
-    )(place, whole, exchange(whole, "core", 1))
+    whole = lax.all_to_all(jnp.broadcast_to(piece[None], (X, *piece.shape)), "x", 0, 0, tiled=True)
+    nodes = TILE * Y * X * Z * CORES
+    weight_grad = whole.reshape(WIDTH, WIDTH).astype(F32) * (1.0 / math.sqrt(nodes))
     return (activations, input_grad, weight_grad)
 
 

time: 196 us -> 204 us (1.041)
  waiting for transfers between devices: 45.6 us -> 60.8 us
  blocking collectives: 48.3 us -> 38.3 us
  other arithmetic: 0.85 us -> 3.02 us
  Pallas kernels: 9.23 us -> 7.11 us
    ppermute x17 -> x16, waiting for transfers between devices: 38.7 us -> 52.6 us  [exchange(): return lax.ppermute(array, axis, [(i, i ^ distance) for i in range(size)])]
    all_to_all x1 -> x0, blocking collectives: 10 us -> none  [body(): whole = lax.all_to_all(piece, 'x', 0, 0, tiled=True)]
    all_to_all x0 -> x1, waiting for transfers between devices: none -> 8.24 us  [body(): lax.all_to_all(jnp.broadcast_to(piece[None], (X, *piece.shape)), 'x', 0,...]
    all_to_all x1, waiting for transfers between devices: 6.87 us -> 0.01 us  [body(): back = lax.all_to_all(back, ('y', 'x'), 0, 0, tiled=True)]
    all_to_all x0 -> x1, starting transfers between devices: none -> 3.47 us  [body(): lax.all_to_all(jnp.broadcast_to(piece[None], (X, *piece.shape)), 'x', 0,...]
    all_to_all x1, starting transfers between devices: 7.81 us -> 5.43 us  [body(): back = lax.all_to_all(back, ('y', 'x'), 0, 0, tiled=True)]
    pallas_call x2 -> x1, Pallas kernels: 3.28 us -> 1.15 us  [body(): pl.pallas_call(middle, in_specs=[vmem()] * 3, out_specs=[vmem()] * 3, out...]
    ppermute x17 -> x16, starting transfers between devices: 61.3 us -> 61.9 us  [exchange(): return lax.ppermute(array, axis, [(i, i ^ distance) for i in range(size)])]
  transfers between devices with their start and end apart: 20 -> 20, of which waited for: 14 -> 13; matrix products, arithmetic and copies ran while one was open for 0% -> 1% of each run, Pallas kernels for 0% -> 0%
where the time goes in v11:
time: 204 us; the launch traced here: 203 us
  starting transfers between devices  89.4 us (44%)
  waiting for transfers between devices  60.8 us (30%)
  blocking collectives  38.3 us (19%)
  Pallas kernels  7.11 us (3%)
  local copies, waits for them, and re-layouts  3.63 us (2%)
  other arithmetic  3.02 us (1%)
    ppermute x16, starting transfers between devices, exchange(): return lax.ppermute(array, axis, [(i, i ^ distance) for i in range(size)])  61.9 us
    ppermute x16, waiting for transfers between devices, exchange(): return lax.ppermute(array, axis, [(i, i ^ distance) for i in range(size)])  52.6 us
    all_to_all x1, blocking collectives, body(): parts = lax.all_to_all(term, ('x', 'z'), 0, 0, tiled=True)  38.3 us
    all_to_all x1, starting transfers between devices, body(): panel = lax.all_to_all(chunks, ('y', 'x'), 0, 0, tiled=True)  10.6 us
    all_to_all x1, waiting for transfers between devices, body(): lax.all_to_all(jnp.broadcast_to(piece[None], (X, *piece.shape)), 'x', 0,...  8.24 us
    all_to_all x1, starting transfers between devices, body(): grad_mine = lax.all_to_all(grad, ('x', 'z'), 0, 0, tiled=True)  7.94 us
    all_to_all x1, starting transfers between devices, body(): back = lax.all_to_all(back, ('y', 'x'), 0, 0, tiled=True)  5.43 us
  transfers between devices with their start and end apart: 20, of which 13 were waited for; matrix products, arithmetic and copies ran while one was open for 1% of the time, Pallas kernels for 0%

profile of v11, /device:TPU:1, one launch (start us, length us, event | category | flops | bytes accessed | tf_op | source)
XLA Modules:
  0.0 203.3 jit_solution(6590837007026515583)
XLA Ops:
  0.6 0.9 copy-done.2
  1.5 1.1 spread.1
  2.7 0.0 copy-start.5
  2.7 10.6 %all-to-all-start = ((bf16[32,128,128]{2,1,0:T(8,128)(2,1)}), bf16[32,128,128]{2,1,0:T(8,128)(2,1)S(1)}, u32[]{:S(2)}, u32[]{:S(2)}) async-start(bf16[32,128,128]{2,1,0:T(8,128)(2,1)} %spread.1), calls=%async_computation | async-start | bytes 2097152 | tf_op jit(solution)/shard_map/all_to_all | solution.py:157
  13.4 0.1 fusion.11
  13.5 4.3 %collective-permute-start.2 = (bf16[1040,128]{1,0:T(8,128)(2,1)S(1)}, bf16[1040,128]{1,0:T(8,128)(2,1)S(1)}, u32[]{:S(2)}, u32[]{:S(2)}) collective-permute-start(bf16[1040,128]{1,0:T(8,128)(2,1)S(1)} %pad_maximum_fusion.refs_0_), channel_id=1, source_target_pairs={{0,48},{16,32},{32,16},{48,0},{1,49},{17,33},{33,17},{49,1},{2,50}... | collective-permute-start | bytes 798728 | tf_op jit(solution)/shard_map/ppermute | solution.py:121
  17.8 2.5 %collective-permute-start.1 = (bf16[1040,128]{1,0:T(8,128)(2,1)S(1)}, bf16[1040,128]{1,0:T(8,128)(2,1)S(1)}, u32[]{:S(2)}, u32[]{:S(2)}) collective-permute-start(bf16[1040,128]{1,0:T(8,128)(2,1)S(1)} %pad_maximum_fusion.refs_0_), channel_id=1, source_target_pairs={{0,32},{16,48},{32,0},{48,16},{1,33},{17,49},{33,1},{49,17},{2,34}... | collective-permute-start | bytes 798728 | tf_op jit(solution)/shard_map/ppermute | solution.py:121
  20.3 2.1 %collective-permute-start = (bf16[1040,128]{1,0:T(8,128)(2,1)S(1)}, bf16[1040,128]{1,0:T(8,128)(2,1)S(1)}, u32[]{:S(2)}, u32[]{:S(2)}) collective-permute-start(bf16[1040,128]{1,0:T(8,128)(2,1)S(1)} %pad_maximum_fusion.refs_0_), channel_id=1, source_target_pairs={{0,16},{16,0},{32,48},{48,32},{1,17},{17,1},{33,49},{49,33},{2,18}... | collective-permute-start | bytes 798728 | tf_op jit(solution)/shard_map/ppermute | solution.py:121
  22.5 0.0 copy-done.5
  22.5 0.1 broadcast_in_dim.4
  22.6 0.1 min.14
  22.7 0.1 pad_add_fusion.place_ref
  22.7 14.6 %collective-permute-done.2.refs_3_ = bf16[1040,128]{1,0:T(8,128)(2,1)S(1)} collective-permute-done((bf16[1040,128]{1,0:T(8,128)(2,1)S(1)}, bf16[1040,128]{1,0:T(8,128)(2,1)S(1)}, u32[]{:S(2)}, u32[]{:S(2)}) %collective-permute-start.2) | collective-permute-done | bytes 266272 | tf_op jit(solution)/shard_map/ppermute | solution.py:121
  37.4 0.0 collective-permute-done.1.refs_2_
  37.4 3.7 %collective-permute-done.refs_1_ = bf16[1040,128]{1,0:T(8,128)(2,1)S(1)} collective-permute-done((bf16[1040,128]{1,0:T(8,128)(2,1)S(1)}, bf16[1040,128]{1,0:T(8,128)(2,1)S(1)}, u32[]{:S(2)}, u32[]{:S(2)}) %collective-permute-start) | collective-permute-done | bytes 266272 | tf_op jit(solution)/shard_map/ppermute | solution.py:121
  41.1 0.1 maximum_minimum_fusion.index_ref
  41.2 0.0 all-to-all-done.panel_ref
  41.2 1.5 forward_tiles.1
  42.7 3.1 %collective-permute-start.3 = (bf16[32,128,128]{2,1,0:T(8,128)(2,1)S(1)}, bf16[32,128,128]{2,1,0:T(8,128)(2,1)S(1)}, u32[]{:S(2)}, u32[]{:S(2)}) collective-permute-start(bf16[32,128,128]{2,1,0:T(8,128)(2,1)S(1)} %get-tuple-element.15), channel_id=1, source_target_pairs={{0,1},{1,0},{2,3},{3,2},{4,5},{5,4},{6,7},{7,6},{8,9},{9,8},{10,11... | collective-permute-start | bytes 3145736 | tf_op jit(solution)/shard_map/ppermute | solution.py:121
  45.8 2.3 %collective-permute-done.3 = bf16[32,128,128]{2,1,0:T(8,128)(2,1)S(1)} collective-permute-done((bf16[32,128,128]{2,1,0:T(8,128)(2,1)S(1)}, bf16[32,128,128]{2,1,0:T(8,128)(2,1)S(1)}, u32[]{:S(2)}, u32[]{:S(2)}) %collective-permute-start.3) | collective-permute-done | bytes 1048608 | tf_op jit(solution)/shard_map/ppermute | solution.py:121
  48.1 0.4 add_convert_fusion
  48.4 0.0 copy-start
  48.4 0.0 copy-start.3
  48.5 38.3 %all_to_all.25.parts_ref = bf16[32,128,128]{2,1,0:T(8,128)(2,1)S(1)} all-to-all(bf16[32,128,128]{2,1,0:T(8,128)(2,1)S(1)} %add_convert_fusion), channel_id=1, replica_groups=mesh['y'=8,'x'=4,'z'=8,'core'=2] {'x','z'}, dimensions={0} | all-to-all | bytes 2097152 | tf_op jit(solution)/shard_map/all_to_all | solution.py:179
  86.7 0.0 copy-done
  86.7 1.2 middle.1
  87.9 1.0 copy-done.1
  88.9 7.9 %all-to-all-start.2 = ((bf16[32,128,128]{2,1,0:T(8,128)(2,1)}), bf16[32,128,128]{2,1,0:T(8,128)(2,1)S(1)}, u32[]{:S(2)}, u32[]{:S(2)}) async-start(bf16[32,128,128]{2,1,0:T(8,128)(2,1)} %copy-done.1), calls=%async_computation.2 | async-start | bytes 2097152 | tf_op jit(solution)/shard_map/all_to_all | solution.py:194
  96.8 0.7 dynamic-slice_bitcast_fusion.2
  97.6 3.1 %collective-permute-start.4 = (bf16[128,512]{1,0:T(8,128)(2,1)}, bf16[128,512]{1,0:T(8,128)(2,1)S(1)}, u32[]{:S(2)}, u32[]{:S(2)}) collective-permute-start(bf16[128,512]{1,0:T(8,128)(2,1)} %get-tuple-element.25), channel_id=1, source_target_pairs={{0,16},{16,0},{32,48},{48,32},{1,17},{17,1},{33,49},{49,33},{2,18}... | collective-permute-start | bytes 393224 | tf_op jit(solution)/shard_map/ppermute | solution.py:121
  100.7 3.7 %collective-permute-start.6 = (bf16[128,512]{1,0:T(8,128)(2,1)}, bf16[128,512]{1,0:T(8,128)(2,1)}, u32[]{:S(2)}, u32[]{:S(2)}) collective-permute-start(bf16[128,512]{1,0:T(8,128)(2,1)} %get-tuple-element.26), channel_id=1, source_target_pairs={{0,48},{16,32},{32,16},{48,0},{1,49},{17,33},{33,17},{49,1},{2,50}... | collective-permute-start | bytes 393224 | tf_op jit(solution)/shard_map/ppermute | solution.py:121
  104.4 2.6 %collective-permute-start.5 = (bf16[128,512]{1,0:T(8,128)(2,1)S(1)}, bf16[128,512]{1,0:T(8,128)(2,1)}, u32[]{:S(2)}, u32[]{:S(2)}) collective-permute-start(bf16[128,512]{1,0:T(8,128)(2,1)S(1)} %get-tuple-element.27), channel_id=1, source_target_pairs={{0,32},{16,48},{32,0},{48,16},{1,33},{17,49},{33,1},{49,17},{2,34}... | collective-permute-start | bytes 393224 | tf_op jit(solution)/shard_map/ppermute | solution.py:121
  107.0 0.0 collective-permute-done.4
  107.0 2.8 %collective-permute-done.6 = bf16[128,512]{1,0:T(8,128)(2,1)} collective-permute-done((bf16[128,512]{1,0:T(8,128)(2,1)}, bf16[128,512]{1,0:T(8,128)(2,1)}, u32[]{:S(2)}, u32[]{:S(2)}) %collective-permute-start.6) | collective-permute-done | bytes 131104 | tf_op jit(solution)/shard_map/ppermute | solution.py:121
  109.8 2.8 %collective-permute-done.5 = bf16[128,512]{1,0:T(8,128)(2,1)} collective-permute-done((bf16[128,512]{1,0:T(8,128)(2,1)S(1)}, bf16[128,512]{1,0:T(8,128)(2,1)}, u32[]{:S(2)}, u32[]{:S(2)}) %collective-permute-start.5) | collective-permute-done | bytes 131104 | tf_op jit(solution)/shard_map/ppermute | solution.py:121
  112.6 1.0 fusion.2
  113.6 3.5 %collective-permute-start.9 = (bf16[128,512]{1,0:T(8,128)(2,1)S(1)}, bf16[128,512]{1,0:T(8,128)(2,1)S(1)}, u32[]{:S(2)}, u32[]{:S(2)}) collective-permute-start(bf16[128,512]{1,0:T(8,128)(2,1)S(1)} %fusion.2), channel_id=1, source_target_pairs={{0,192},{64,128},{128,64},{192,0},{256,448},{320,384},{384,320},{4... | collective-permute-start | bytes 393224 | tf_op jit(solution)/shard_map/ppermute | solution.py:121
  117.1 1.9 collective-permute-start.8
  119.0 3.9 %collective-permute-start.7 = (bf16[128,512]{1,0:T(8,128)(2,1)S(1)}, bf16[128,512]{1,0:T(8,128)(2,1)S(1)}, u32[]{:S(2)}, u32[]{:S(2)}) collective-permute-start(bf16[128,512]{1,0:T(8,128)(2,1)S(1)} %fusion.2), channel_id=1, source_target_pairs={{0,64},{64,0},{128,192},{192,128},{256,320},{320,256},{384,448},{4... | collective-permute-start | bytes 393224 | tf_op jit(solution)/shard_map/ppermute | solution.py:121
  122.9 0.0 collective-permute-done.9
  122.9 2.4 %collective-permute-done.8 = bf16[128,512]{1,0:T(8,128)(2,1)S(1)} collective-permute-done((bf16[128,512]{1,0:T(8,128)(2,1)S(1)}, bf16[128,512]{1,0:T(8,128)(2,1)S(1)}, u32[]{:S(2)}, u32[]{:S(2)}) %collective-permute-start.8) | collective-permute-done | bytes 131104 | tf_op jit(solution)/shard_map/ppermute | solution.py:121
  125.3 1.2 collective-permute-done.7
  126.5 0.1 add_convert_fusion.6
  126.6 0.0 all-to-all-done.2.mine_ref
  126.6 8.6 %collective-permute-start.10 = (bf16[32,128,128]{2,1,0:T(8,128)(2,1)S(1)}, bf16[32,128,128]{2,1,0:T(8,128)(2,1)S(1)}, u32[]{:S(2)}, u32[]{:S(2)}) collective-permute-start(bf16[32,128,128]{2,1,0:T(8,128)(2,1)S(1)} %all-to-all-done.2.mine_ref), channel_id=1, source_target_pairs={{0,1},{1,0},{2,3},{3,2},{4,5},{5,4},{6,7},{7,6},{8,9},{9,8},{10,11... | collective-permute-start | bytes 3145736 | tf_op jit(solution)/shard_map/ppermute | solution.py:121
  135.1 3.7 %collective-permute-start.11 = (bf16[128,512]{1,0:T(8,128)(2,1)S(1)}, bf16[128,512]{1,0:T(8,128)(2,1)S(1)}, u32[]{:S(2)}, u32[]{:S(2)}) collective-permute-start(bf16[128,512]{1,0:T(8,128)(2,1)S(1)} %add_convert_fusion.6), channel_id=1, source_target_pairs={{0,448},{64,384},{128,320},{192,256},{256,192},{320,128},{384,64},... | collective-permute-start | bytes 393224 | tf_op jit(solution)/shard_map/ppermute | solution.py:121
  138.9 7.3 %collective-permute-done.11 = bf16[128,512]{1,0:T(8,128)(2,1)S(1)} collective-permute-done((bf16[128,512]{1,0:T(8,128)(2,1)S(1)}, bf16[128,512]{1,0:T(8,128)(2,1)S(1)}, u32[]{:S(2)}, u32[]{:S(2)}) %collective-permute-start.11) | collective-permute-done | bytes 131104 | tf_op jit(solution)/shard_map/ppermute | solution.py:121
  146.2 0.0 collective-permute-done.10.other_ref
  146.2 2.4 %backward_tiles.1 = bf16[32,128,128]{2,1,0:T(8,128)(2,1)} custom-call(s32[2]{0:T(128)S(1)} %pad_add_fusion.place_ref, s32[4,24]{1,0:T(4,128)S(1)} %maximum_minimum_fusion.index_ref, bf16[32,128,128]{2,1,0:T(8,128)(2,1)S(1)} %all-to-all-done.2.mine_ref, bf16[32,128,128]{2,1,0:T(8,128)(2,1)S(1)} %collective-permute-done.10.other_ref, ...), custom_call_target="tpu_custom_call" | custom-call | tf_op jit(solution)/shard_map/backward_tiles/pallas_call | solution.py:201
  148.6 5.4 %all-to-all-start.3 = ((bf16[32,128,128]{2,1,0:T(8,128)(2,1)}), bf16[32,128,128]{2,1,0:T(8,128)(2,1)S(1)}, u32[]{:S(2)}, u32[]{:S(2)}) async-start(bf16[32,128,128]{2,1,0:T(8,128)(2,1)} %backward_tiles.1), calls=%async_computation.3 | async-start | bytes 2097152 | tf_op jit(solution)/shard_map/all_to_all | solution.py:211
  154.0 5.6 %collective-permute-start.12 = (bf16[128,512]{1,0:T(8,128)(2,1)S(1)}, bf16[128,512]{1,0:T(8,128)(2,1)S(1)}, u32[]{:S(2)}, u32[]{:S(2)}) collective-permute-start(bf16[128,512]{1,0:T(8,128)(2,1)S(1)} %add_convert_fusion.5), channel_id=1, source_target_pairs={{0,2},{2,0},{4,6},{6,4},{8,10},{10,8},{12,14},{14,12},{1,3},{3,1},... | collective-permute-start | bytes 393224 | tf_op jit(solution)/shard_map/ppermute | solution.py:121
  159.6 3.2 %collective-permute-done.12 = bf16[128,512]{1,0:T(8,128)(2,1)S(1)} collective-permute-done((bf16[128,512]{1,0:T(8,128)(2,1)S(1)}, bf16[128,512]{1,0:T(8,128)(2,1)S(1)}, u32[]{:S(2)}, u32[]{:S(2)}) %collective-permute-start.12) | collective-permute-done | bytes 131104 | tf_op jit(solution)/shard_map/ppermute | solution.py:121
  162.8 4.2 %collective-permute-start.13 = (bf16[128,512]{1,0:T(8,128)(2,1)S(1)}, bf16[128,512]{1,0:T(8,128)(2,1)S(1)}, u32[]{:S(2)}, u32[]{:S(2)}) collective-permute-start(bf16[128,512]{1,0:T(8,128)(2,1)S(1)} %add_convert_fusion.4), channel_id=1, source_target_pairs={{0,4},{2,6},{4,0},{6,2},{8,12},{10,14},{12,8},{14,10},{1,5},{3,7},... | collective-permute-start | bytes 393224 | tf_op jit(solution)/shard_map/ppermute | solution.py:121
  167.0 5.9 %collective-permute-done.13 = bf16[128,512]{1,0:T(8,128)(2,1)S(1)} collective-permute-done((bf16[128,512]{1,0:T(8,128)(2,1)S(1)}, bf16[128,512]{1,0:T(8,128)(2,1)S(1)}, u32[]{:S(2)}, u32[]{:S(2)}) %collective-permute-start.13) | collective-permute-done | bytes 131104 | tf_op jit(solution)/shard_map/ppermute | solution.py:121
  173.0 6.6 %collective-permute-start.14 = (bf16[128,512]{1,0:T(8,128)(2,1)S(1)}, bf16[128,512]{1,0:T(8,128)(2,1)S(1)}, u32[]{:S(2)}, u32[]{:S(2)}) collective-permute-start(bf16[128,512]{1,0:T(8,128)(2,1)S(1)} %add_convert_fusion.3), channel_id=1, source_target_pairs={{0,14},{2,12},{4,10},{6,8},{8,6},{10,4},{12,2},{14,0},{1,15},{3,13... | collective-permute-start | bytes 393224 | tf_op jit(solution)/shard_map/ppermute | solution.py:121
  179.6 5.5 %collective-permute-done.14 = bf16[128,512]{1,0:T(8,128)(2,1)S(1)} collective-permute-done((bf16[128,512]{1,0:T(8,128)(2,1)S(1)}, bf16[128,512]{1,0:T(8,128)(2,1)S(1)}, u32[]{:S(2)}, u32[]{:S(2)}) %collective-permute-start.14) | collective-permute-done | bytes 131104 | tf_op jit(solution)/shard_map/ppermute | solution.py:121
  185.1 2.5 %collective-permute-start.15 = (bf16[128,512]{1,0:T(8,128)(2,1)S(1)}, bf16[128,512]{1,0:T(8,128)(2,1)S(1)}, u32[]{:S(2)}, u32[]{:S(2)}) collective-permute-start(bf16[128,512]{1,0:T(8,128)(2,1)S(1)} %add_convert_fusion.2), channel_id=1, source_target_pairs={{0,1},{1,0},{2,3},{3,2},{4,5},{5,4},{6,7},{7,6},{8,9},{9,8},{10,11... | collective-permute-start | bytes 393224 | tf_op jit(solution)/shard_map/ppermute | solution.py:121
  187.6 1.0 collective-permute-done.15
  188.6 0.0 all-to-all-done.3.parts_ref
  188.6 0.8 broadcast_in_dim.5
  189.5 3.5 %all-to-all-start.4 = ((bf16[4,128,512]{2,1,0:T(8,128)(2,1)}), bf16[4,128,512]{2,1,0:T(8,128)(2,1)S(1)}, u32[]{:S(2)}, u32[]{:S(2)}) async-start(bf16[4,128,512]{2,1,0:T(8,128)(2,1)} %broadcast_in_dim.5), calls=%async_computation.4 | async-start | bytes 1048576 | tf_op jit(solution)/shard_map/all_to_all | solution.py:226
  192.9 1.0 last.1
  193.9 8.2 %all-to-all-done.4 = bf16[4,128,512]{2,1,0:T(8,128)(2,1)S(1)} async-done(((bf16[4,128,512]{2,1,0:T(8,128)(2,1)}), bf16[4,128,512]{2,1,0:T(8,128)(2,1)S(1)}, u32[]{:S(2)}, u32[]{:S(2)}) %all-to-all-start.4) | async-done | bytes 524320 | tf_op jit(solution)/shard_map/all_to_all | solution.py:226
  202.2 1.1 convert_multiply_fusion
  (22 shorter events, 0.2 us)
Async XLA Ops:
  0.6 0.9 copy-start.2
  2.6 10.7 %copy-start.8 = (s32[1,1,8]{2,1,0:T(1,128)S(1)}, s32[1,1,8]{2,1,0:T(1,128)}, u32[]{:S(2)}) copy-start(s32[1,1,8]{2,1,0:T(1,128)} %param.12) | copy-start | bytes 100
  2.6 10.7 %copy-start.6 = (s32[1,1,8]{2,1,0:T(1,128)S(1)}, s32[1,1,8]{2,1,0:T(1,128)}, u32[]{:S(2)}) copy-start(s32[1,1,8]{2,1,0:T(1,128)} %param.14) | copy-start | bytes 100
  2.6 10.7 %copy-start.7 = (s32[1,1,8]{2,1,0:T(1,128)S(1)}, s32[1,1,8]{2,1,0:T(1,128)}, u32[]{:S(2)}) copy-start(s32[1,1,8]{2,1,0:T(1,128)} %param.13) | copy-start | bytes 100
  2.6 10.8 %copy-start.4 = (bf16[1,1,8,128,128]{4,3,2,1,0:T(8,128)(2,1)S(1)}, bf16[1,1,8,128,128]{4,3,2,1,0:T(8,128)(2,1)}, u32[]{:S(2)}) copy-start(bf16[1,1,8,128,128]{4,3,2,1,0:T(8,128)(2,1)} %param.11) | copy-start | bytes 786436
  2.7 19.8 %copy-start.5 = (s32[3]{0:T(128)S(1)}, s32[3]{0:T(128)}, u32[]{:S(2)}) copy-start(s32[3]{0:T(128)} %constant.35.clone) | copy-start | bytes 40
  2.7 38.5 %all-to-all-start = ((bf16[32,128,128]{2,1,0:T(8,128)(2,1)}), bf16[32,128,128]{2,1,0:T(8,128)(2,1)S(1)}, u32[]{:S(2)}, u32[]{:S(2)}) async-start(bf16[32,128,128]{2,1,0:T(8,128)(2,1)} %spread.1), calls=%async_computation | async-start | bytes 2097152 | tf_op jit(solution)/shard_map/all_to_all | solution.py:157
  13.5 23.9 %collective-permute-start.2 = (bf16[1040,128]{1,0:T(8,128)(2,1)S(1)}, bf16[1040,128]{1,0:T(8,128)(2,1)S(1)}, u32[]{:S(2)}, u32[]{:S(2)}) collective-permute-start(bf16[1040,128]{1,0:T(8,128)(2,1)S(1)} %pad_maximum_fusion.refs_0_), channel_id=1, source_target_pairs={{0,48},{16,32},{32,16},{48,0},{1,49},{17,33},{33,17},{49,1},{2,50}... | collective-permute-start | bytes 798728 | tf_op jit(solution)/shard_map/ppermute | solution.py:121
  17.8 19.5 %collective-permute-start.1 = (bf16[1040,128]{1,0:T(8,128)(2,1)S(1)}, bf16[1040,128]{1,0:T(8,128)(2,1)S(1)}, u32[]{:S(2)}, u32[]{:S(2)}) collective-permute-start(bf16[1040,128]{1,0:T(8,128)(2,1)S(1)} %pad_maximum_fusion.refs_0_), channel_id=1, source_target_pairs={{0,32},{16,48},{32,0},{48,16},{1,33},{17,49},{33,1},{49,17},{2,34}... | collective-permute-start | bytes 798728 | tf_op jit(solution)/shard_map/ppermute | solution.py:121
  20.3 20.7 %collective-permute-start = (bf16[1040,128]{1,0:T(8,128)(2,1)S(1)}, bf16[1040,128]{1,0:T(8,128)(2,1)S(1)}, u32[]{:S(2)}, u32[]{:S(2)}) collective-permute-start(bf16[1040,128]{1,0:T(8,128)(2,1)S(1)} %pad_maximum_fusion.refs_0_), channel_id=1, source_target_pairs={{0,16},{16,0},{32,48},{48,32},{1,17},{17,1},{33,49},{49,33},{2,18}... | collective-permute-start | bytes 798728 | tf_op jit(solution)/shard_map/ppermute | solution.py:121
  42.7 5.4 %collective-permute-start.3 = (bf16[32,128,128]{2,1,0:T(8,128)(2,1)S(1)}, bf16[32,128,128]{2,1,0:T(8,128)(2,1)S(1)}, u32[]{:S(2)}, u32[]{:S(2)}) collective-permute-start(bf16[32,128,128]{2,1,0:T(8,128)(2,1)S(1)} %get-tuple-element.15), channel_id=1, source_target_pairs={{0,1},{1,0},{2,3},{3,2},{4,5},{5,4},{6,7},{7,6},{8,9},{9,8},{10,11... | collective-permute-start | bytes 3145736 | tf_op jit(solution)/shard_map/ppermute | solution.py:121
  48.4 38.3 %copy-start = (bf16[512,512]{1,0:T(8,128)(2,1)S(1)}, bf16[512,512]{1,0:T(8,128)(2,1)}, u32[]{:S(2)}) copy-start(bf16[512,512]{1,0:T(8,128)(2,1)} %weight_ref.3) | copy-start | bytes 1572868
  48.4 38.3 %copy-start.3 = (bf16[128,512]{1,0:T(8,128)(2,1)S(1)}, bf16[128,512]{1,0:T(8,128)(2,1)}, u32[]{:S(2)}) copy-start(bf16[128,512]{1,0:T(8,128)(2,1)} %cotangent_ref.1) | copy-start | bytes 393220
  87.9 1.0 copy-start.1
  88.9 37.7 %all-to-all-start.2 = ((bf16[32,128,128]{2,1,0:T(8,128)(2,1)}), bf16[32,128,128]{2,1,0:T(8,128)(2,1)S(1)}, u32[]{:S(2)}, u32[]{:S(2)}) async-start(bf16[32,128,128]{2,1,0:T(8,128)(2,1)} %copy-done.1), calls=%async_computation.2 | async-start | bytes 2097152 | tf_op jit(solution)/shard_map/all_to_all | solution.py:194
  97.6 9.4 %collective-permute-start.4 = (bf16[128,512]{1,0:T(8,128)(2,1)}, bf16[128,512]{1,0:T(8,128)(2,1)S(1)}, u32[]{:S(2)}, u32[]{:S(2)}) collective-permute-start(bf16[128,512]{1,0:T(8,128)(2,1)} %get-tuple-element.25), channel_id=1, source_target_pairs={{0,16},{16,0},{32,48},{48,32},{1,17},{17,1},{33,49},{49,33},{2,18}... | collective-permute-start | bytes 393224 | tf_op jit(solution)/shard_map/ppermute | solution.py:121
  100.7 9.1 %collective-permute-start.6 = (bf16[128,512]{1,0:T(8,128)(2,1)}, bf16[128,512]{1,0:T(8,128)(2,1)}, u32[]{:S(2)}, u32[]{:S(2)}) collective-permute-start(bf16[128,512]{1,0:T(8,128)(2,1)} %get-tuple-element.26), channel_id=1, source_target_pairs={{0,48},{16,32},{32,16},{48,0},{1,49},{17,33},{33,17},{49,1},{2,50}... | collective-permute-start | bytes 393224 | tf_op jit(solution)/shard_map/ppermute | solution.py:121
  104.4 8.2 %collective-permute-start.5 = (bf16[128,512]{1,0:T(8,128)(2,1)S(1)}, bf16[128,512]{1,0:T(8,128)(2,1)}, u32[]{:S(2)}, u32[]{:S(2)}) collective-permute-start(bf16[128,512]{1,0:T(8,128)(2,1)S(1)} %get-tuple-element.27), channel_id=1, source_target_pairs={{0,32},{16,48},{32,0},{48,16},{1,33},{17,49},{33,1},{49,17},{2,34}... | collective-permute-start | bytes 393224 | tf_op jit(solution)/shard_map/ppermute | solution.py:121
  113.6 9.3 %collective-permute-start.9 = (bf16[128,512]{1,0:T(8,128)(2,1)S(1)}, bf16[128,512]{1,0:T(8,128)(2,1)S(1)}, u32[]{:S(2)}, u32[]{:S(2)}) collective-permute-start(bf16[128,512]{1,0:T(8,128)(2,1)S(1)} %fusion.2), channel_id=1, source_target_pairs={{0,192},{64,128},{128,64},{192,0},{256,448},{320,384},{384,320},{4... | collective-permute-start | bytes 393224 | tf_op jit(solution)/shard_map/ppermute | solution.py:121
  117.1 8.3 %collective-permute-start.8 = (bf16[128,512]{1,0:T(8,128)(2,1)S(1)}, bf16[128,512]{1,0:T(8,128)(2,1)S(1)}, u32[]{:S(2)}, u32[]{:S(2)}) collective-permute-start(bf16[128,512]{1,0:T(8,128)(2,1)S(1)} %fusion.2), channel_id=1, source_target_pairs={{0,128},{64,192},{128,0},{192,64},{256,384},{320,448},{384,256},{4... | collective-permute-start | bytes 393224 | tf_op jit(solution)/shard_map/ppermute | solution.py:121
  119.0 7.5 %collective-permute-start.7 = (bf16[128,512]{1,0:T(8,128)(2,1)S(1)}, bf16[128,512]{1,0:T(8,128)(2,1)S(1)}, u32[]{:S(2)}, u32[]{:S(2)}) collective-permute-start(bf16[128,512]{1,0:T(8,128)(2,1)S(1)} %fusion.2), channel_id=1, source_target_pairs={{0,64},{64,0},{128,192},{192,128},{256,320},{320,256},{384,448},{4... | collective-permute-start | bytes 393224 | tf_op jit(solution)/shard_map/ppermute | solution.py:121
  126.6 19.6 %collective-permute-start.10 = (bf16[32,128,128]{2,1,0:T(8,128)(2,1)S(1)}, bf16[32,128,128]{2,1,0:T(8,128)(2,1)S(1)}, u32[]{:S(2)}, u32[]{:S(2)}) collective-permute-start(bf16[32,128,128]{2,1,0:T(8,128)(2,1)S(1)} %all-to-all-done.2.mine_ref), channel_id=1, source_target_pairs={{0,1},{1,0},{2,3},{3,2},{4,5},{5,4},{6,7},{7,6},{8,9},{9,8},{10,11... | collective-permute-start | bytes 3145736 | tf_op jit(solution)/shard_map/ppermute | solution.py:121
  135.1 11.0 %collective-permute-start.11 = (bf16[128,512]{1,0:T(8,128)(2,1)S(1)}, bf16[128,512]{1,0:T(8,128)(2,1)S(1)}, u32[]{:S(2)}, u32[]{:S(2)}) collective-permute-start(bf16[128,512]{1,0:T(8,128)(2,1)S(1)} %add_convert_fusion.6), channel_id=1, source_target_pairs={{0,448},{64,384},{128,320},{192,256},{256,192},{320,128},{384,64},... | collective-permute-start | bytes 393224 | tf_op jit(solution)/shard_map/ppermute | solution.py:121
  148.6 40.0 %all-to-all-start.3 = ((bf16[32,128,128]{2,1,0:T(8,128)(2,1)}), bf16[32,128,128]{2,1,0:T(8,128)(2,1)S(1)}, u32[]{:S(2)}, u32[]{:S(2)}) async-start(bf16[32,128,128]{2,1,0:T(8,128)(2,1)} %backward_tiles.1), calls=%async_computation.3 | async-start | bytes 2097152 | tf_op jit(solution)/shard_map/all_to_all | solution.py:211
  154.0 8.8 %collective-permute-start.12 = (bf16[128,512]{1,0:T(8,128)(2,1)S(1)}, bf16[128,512]{1,0:T(8,128)(2,1)S(1)}, u32[]{:S(2)}, u32[]{:S(2)}) collective-permute-start(bf16[128,512]{1,0:T(8,128)(2,1)S(1)} %add_convert_fusion.5), channel_id=1, source_target_pairs={{0,2},{2,0},{4,6},{6,4},{8,10},{10,8},{12,14},{14,12},{1,3},{3,1},... | collective-permute-start | bytes 393224 | tf_op jit(solution)/shard_map/ppermute | solution.py:121
  162.8 10.1 %collective-permute-start.13 = (bf16[128,512]{1,0:T(8,128)(2,1)S(1)}, bf16[128,512]{1,0:T(8,128)(2,1)S(1)}, u32[]{:S(2)}, u32[]{:S(2)}) collective-permute-start(bf16[128,512]{1,0:T(8,128)(2,1)S(1)} %add_convert_fusion.4), channel_id=1, source_target_pairs={{0,4},{2,6},{4,0},{6,2},{8,12},{10,14},{12,8},{14,10},{1,5},{3,7},... | collective-permute-start | bytes 393224 | tf_op jit(solution)/shard_map/ppermute | solution.py:121
  173.0 12.1 %collective-permute-start.14 = (bf16[128,512]{1,0:T(8,128)(2,1)S(1)}, bf16[128,512]{1,0:T(8,128)(2,1)S(1)}, u32[]{:S(2)}, u32[]{:S(2)}) collective-permute-start(bf16[128,512]{1,0:T(8,128)(2,1)S(1)} %add_convert_fusion.3), channel_id=1, source_target_pairs={{0,14},{2,12},{4,10},{6,8},{8,6},{10,4},{12,2},{14,0},{1,15},{3,13... | collective-permute-start | bytes 393224 | tf_op jit(solution)/shard_map/ppermute | solution.py:121
  185.1 3.5 %collective-permute-start.15 = (bf16[128,512]{1,0:T(8,128)(2,1)S(1)}, bf16[128,512]{1,0:T(8,128)(2,1)S(1)}, u32[]{:S(2)}, u32[]{:S(2)}) collective-permute-start(bf16[128,512]{1,0:T(8,128)(2,1)S(1)} %add_convert_fusion.2), channel_id=1, source_target_pairs={{0,1},{1,0},{2,3},{3,2},{4,5},{5,4},{6,7},{7,6},{8,9},{9,8},{10,11... | collective-permute-start | bytes 393224 | tf_op jit(solution)/shard_map/ppermute | solution.py:121
  189.5 12.7 %all-to-all-start.4 = ((bf16[4,128,512]{2,1,0:T(8,128)(2,1)}), bf16[4,128,512]{2,1,0:T(8,128)(2,1)S(1)}, u32[]{:S(2)}, u32[]{:S(2)}) async-start(bf16[4,128,512]{2,1,0:T(8,128)(2,1)} %broadcast_in_dim.5), calls=%async_computation.4 | async-start | bytes 1048576 | tf_op jit(solution)/shard_map/all_to_all | solution.py:226

commit v12 on v10

--- a/solution.py
+++ b/solution.py
@@ -7,7 +7,10 @@
 from jax.experimental.pallas import tpu as pltpu
 from jax.sharding import Mesh, PartitionSpec as P
 
-Y, X, Z, CORES = 8, 4, 8, 2
+Y_HIGH, Y_LOW, X, Z, CORES = 4, 2, 4, 8, 2
+Y = Y_HIGH * Y_LOW
+ROW = ("y_high", "y_low", "x")
+COL = ("z", "core")
 TILE = 128
 SLOTS = 8
 WIDTH = 512
@@ -122,12 +125,12 @@
 
 def place_rows(place_ref, mine_ref, other_ref, out_ref):
     core = place_ref[0]
-    half, share = WIDTH // CORES, WIDTH // (X * CORES)
+    half, share = WIDTH // CORES, WIDTH // (Y_HIGH * CORES)
     scale = 1.0 / math.sqrt(TILE * Y * X * Z * CORES)
-    for x in range(X):
+    for y in range(Y_HIGH):
         for side, ref in ((core, mine_ref), (1 - core, other_ref)):
-            start = pl.multiple_of(side * half + x * share, share)
-            out_ref[pl.ds(start, share), :] = ref[x].astype(F32) * scale
+            start = pl.multiple_of(side * half + y * share, share)
+            out_ref[pl.ds(start, share), :] = ref[y].astype(F32) * scale
 
 
 def exchange(array, axis, distance):
@@ -168,7 +171,7 @@
         compiler_params=params(),
         name="spread",
     )(features)
-    panel = lax.all_to_all(chunks, ("y", "x"), 0, 0, tiled=True)
+    panel = lax.all_to_all(chunks, ROW, 0, 0, tiled=True)
 
     index = jnp.concatenate(
         [tile_rows.reshape(-1), tile_cols.reshape(-1), tile_valid.reshape(-1)]
@@ -210,12 +213,12 @@
     grad_mine = lax.all_to_all(grad, ("x", "z"), 0, 0, tiled=True)
     piece = weight_keep.astype(F32) + exchange(weight_send, "core", 1).astype(F32)
     piece = piece.astype(BF16)
-    piece = scatter(piece, "x")
-    piece = double4(piece, "y")
+    piece = scatter(piece, "y_high")
+    piece = double(piece, "y_low", 1)
+    piece = double(piece, "x", 1)
     grad_mine, piece = lax.optimization_barrier((grad_mine, piece))
 
     grad_other = exchange(grad_mine, "core", 1)
-    piece = double(piece, "y", Y - 1)
     back = pl.pallas_call(
         backward_tiles,
         in_specs=[smem(), smem()] + [vmem()] * (2 + X),
@@ -226,9 +229,10 @@
         name="backward_tiles",
     )(place, index, grad_mine, grad_other, *tiles)
     back, piece = lax.optimization_barrier((back, piece))
-    back = lax.all_to_all(back, ("y", "x"), 0, 0, tiled=True)
-    for distance in (1, 2, Z - 1):
-        piece = double(piece, "z", distance)
+    back = lax.all_to_all(back, ROW, 0, 0, tiled=True)
+    piece = double4(piece, "z")
+    piece = double(piece, "z", Z - 1)
+    piece = double(piece, "x", X - 1)
     back, piece = lax.optimization_barrier((back, piece))
 
     input_grad = pl.pallas_call(
@@ -240,9 +244,9 @@
         name="last",
     )(back, weight)
 
-    share = WIDTH // (X * CORES)
-    piece = jnp.broadcast_to(piece[None], (X, share, WIDTH))
-    whole = lax.all_to_all(piece, "x", 0, 0, tiled=True)
+    share = WIDTH // (Y_HIGH * CORES)
+    piece = jnp.broadcast_to(piece[None], (Y_HIGH, share, WIDTH))
+    whole = lax.all_to_all(piece, "y_high", 0, 0, tiled=True)
     weight_grad = pl.pallas_call(
         place_rows,
         in_specs=[smem()] + [vmem()] * 2,
@@ -255,21 +259,20 @@
 
 
 def solution(mesh):
-    axes = Mesh(mesh.devices.reshape(Y, X, Z, CORES), ("y", "x", "z", "core"))
-    row, col = ("y", "x"), ("z", "core")
+    axes = Mesh(mesh.devices.reshape(Y_HIGH, Y_LOW, X, Z, CORES), ROW + COL)
     placed = (
-        P(col + row, None),
+        P(COL + ROW, None),
         P(),
-        P(row + col, None),
-        P(row, col, None, None, None),
-        P(row, col, None),
-        P(row, col, None),
-        P(row, col, None),
+        P(ROW + COL, None),
+        P(ROW, COL, None, None, None),
+        P(ROW, COL, None),
+        P(ROW, COL, None),
+        P(ROW, COL, None),
     )
     return jax.shard_map(
         body,
         mesh=axes,
         in_specs=placed,
-        out_specs=(P(row + col, None), P(col + row, None), P()),
+        out_specs=(P(ROW + COL, None), P(COL + ROW, None), P()),
         check_vma=False,
     )

time: 196 us -> 197 us (level)
  blocking collectives: 48.3 us -> 50.9 us
  waiting for transfers between devices: 45.6 us -> 43.4 us
    all_to_all x2, waiting for transfers between devices: 6.87 us -> 0.01 us  [the longest x1 0.01 us: body(): panel = lax.all_to_all(chunks, ROW, 0, 0, tiled=True)]
    ppermute x17, waiting for transfers between devices: 38.7 us -> 43.4 us  [exchange(): return lax.ppermute(array, axis, [(i, i ^ distance) for i in range(size)])]
    all_to_all x1, blocking collectives: 10 us -> 12.6 us  [body(): whole = lax.all_to_all(piece, 'y_high', 0, 0, tiled=True)]
  transfers between devices with their start and end apart: 20 -> 20, of which waited for: 14 -> 13; matrix products, arithmetic and copies ran while one was open for 0% -> 0% of each run, Pallas kernels for 0% -> 0%
where the time goes in v12:
time: 197 us; the launch traced here: 196 us
  starting transfers between devices  88.7 us (45%)
  blocking collectives  50.9 us (26%)
  waiting for transfers between devices  43.4 us (22%)
  Pallas kernels  9.23 us (5%)
  local copies, waits for them, and re-layouts  2.1 us (1%)
    ppermute x17, starting transfers between devices, exchange(): return lax.ppermute(array, axis, [(i, i ^ distance) for i in range(size)])  63.1 us
    ppermute x17, waiting for transfers between devices, exchange(): return lax.ppermute(array, axis, [(i, i ^ distance) for i in range(size)])  43.4 us
    all_to_all x1, blocking collectives, body(): parts = lax.all_to_all(term, ('x', 'z'), 0, 0, tiled=True)  38.3 us
    all_to_all x1, blocking collectives, body(): whole = lax.all_to_all(piece, 'y_high', 0, 0, tiled=True)  12.6 us
    all_to_all x1, starting transfers between devices, body(): panel = lax.all_to_all(chunks, ROW, 0, 0, tiled=True)  10.6 us
    all_to_all x1, starting transfers between devices, body(): grad_mine = lax.all_to_all(grad, ('x', 'z'), 0, 0, tiled=True)  7.95 us
    all_to_all x1, starting transfers between devices, body(): back = lax.all_to_all(back, ROW, 0, 0, tiled=True)  7.05 us
  transfers between devices with their start and end apart: 20, of which 13 were waited for; matrix products, arithmetic and copies ran while one was open for 0% of the time, Pallas kernels for 0%

profile of v12, /device:TPU:1, one launch (start us, length us, event | category | flops | bytes accessed | tf_op | source)
XLA Modules:
  0.0 196.2 jit_solution(13505615893177866062)
XLA Ops:
  0.6 0.0 copy-start.2
  0.6 0.9 copy-done.2
  1.5 1.1 spread.1
  2.7 0.0 copy-start.5
  2.7 10.6 %all-to-all-start = ((bf16[32,128,128]{2,1,0:T(8,128)(2,1)}), bf16[32,128,128]{2,1,0:T(8,128)(2,1)S(1)}, u32[]{:S(2)}, u32[]{:S(2)}) async-start(bf16[32,128,128]{2,1,0:T(8,128)(2,1)} %spread.1), calls=%async_computation | async-start | bytes 2097152 | tf_op jit(solution)/shard_map/all_to_all | solution.py:174
  13.3 0.0 copy-done.8
  13.3 0.0 copy-done.6
  13.4 0.1 fusion.11
  13.5 4.3 %collective-permute-start.2 = (bf16[1040,128]{1,0:T(8,128)(2,1)S(1)}, bf16[1040,128]{1,0:T(8,128)(2,1)S(1)}, u32[]{:S(2)}, u32[]{:S(2)}) collective-permute-start(bf16[1040,128]{1,0:T(8,128)(2,1)S(1)} %pad_maximum_fusion.refs_0_), channel_id=1, source_target_pairs={{0,48},{16,32},{32,16},{48,0},{1,49},{17,33},{33,17},{49,1},{2,50}... | collective-permute-start | bytes 798728 | tf_op jit(solution)/shard_map/ppermute | solution.py:138
  17.8 2.5 %collective-permute-start.1 = (bf16[1040,128]{1,0:T(8,128)(2,1)S(1)}, bf16[1040,128]{1,0:T(8,128)(2,1)S(1)}, u32[]{:S(2)}, u32[]{:S(2)}) collective-permute-start(bf16[1040,128]{1,0:T(8,128)(2,1)S(1)} %pad_maximum_fusion.refs_0_), channel_id=1, source_target_pairs={{0,32},{16,48},{32,0},{48,16},{1,33},{17,49},{33,1},{49,17},{2,34}... | collective-permute-start | bytes 798728 | tf_op jit(solution)/shard_map/ppermute | solution.py:138
  20.3 2.1 %collective-permute-start = (bf16[1040,128]{1,0:T(8,128)(2,1)S(1)}, bf16[1040,128]{1,0:T(8,128)(2,1)S(1)}, u32[]{:S(2)}, u32[]{:S(2)}) collective-permute-start(bf16[1040,128]{1,0:T(8,128)(2,1)S(1)} %pad_maximum_fusion.refs_0_), channel_id=1, source_target_pairs={{0,16},{16,0},{32,48},{48,32},{1,17},{17,1},{33,49},{49,33},{2,18}... | collective-permute-start | bytes 798728 | tf_op jit(solution)/shard_map/ppermute | solution.py:138
  22.5 0.1 broadcast_in_dim.4
  22.6 0.1 min.14
  22.7 0.1 pad_add_fusion.place_ref.core_ref
  22.7 14.6 %collective-permute-done.2.refs_3_ = bf16[1040,128]{1,0:T(8,128)(2,1)S(1)} collective-permute-done((bf16[1040,128]{1,0:T(8,128)(2,1)S(1)}, bf16[1040,128]{1,0:T(8,128)(2,1)S(1)}, u32[]{:S(2)}, u32[]{:S(2)}) %collective-permute-start.2) | collective-permute-done | bytes 266272 | tf_op jit(solution)/shard_map/ppermute | solution.py:138
  37.4 0.0 collective-permute-done.1.refs_2_
  37.4 3.7 %collective-permute-done.refs_1_ = bf16[1040,128]{1,0:T(8,128)(2,1)S(1)} collective-permute-done((bf16[1040,128]{1,0:T(8,128)(2,1)S(1)}, bf16[1040,128]{1,0:T(8,128)(2,1)S(1)}, u32[]{:S(2)}, u32[]{:S(2)}) %collective-permute-start) | collective-permute-done | bytes 266272 | tf_op jit(solution)/shard_map/ppermute | solution.py:138
  41.1 0.1 maximum_minimum_fusion.index_ref
  41.2 0.0 all-to-all-done.panel_ref
  41.2 1.5 forward_tiles.1
  42.7 3.1 %collective-permute-start.3 = (bf16[32,128,128]{2,1,0:T(8,128)(2,1)S(1)}, bf16[32,128,128]{2,1,0:T(8,128)(2,1)S(1)}, u32[]{:S(2)}, u32[]{:S(2)}) collective-permute-start(bf16[32,128,128]{2,1,0:T(8,128)(2,1)S(1)} %get-tuple-element.16), channel_id=1, source_target_pairs={{0,1},{1,0},{2,3},{3,2},{4,5},{5,4},{6,7},{7,6},{8,9},{9,8},{10,11... | collective-permute-start | bytes 3145736 | tf_op jit(solution)/shard_map/ppermute | solution.py:138
  45.8 2.3 %collective-permute-done.3 = bf16[32,128,128]{2,1,0:T(8,128)(2,1)S(1)} collective-permute-done((bf16[32,128,128]{2,1,0:T(8,128)(2,1)S(1)}, bf16[32,128,128]{2,1,0:T(8,128)(2,1)S(1)}, u32[]{:S(2)}, u32[]{:S(2)}) %collective-permute-start.3) | collective-permute-done | bytes 1048608 | tf_op jit(solution)/shard_map/ppermute | solution.py:138
  48.1 0.4 add_convert_fusion
  48.4 0.0 copy-start
  48.4 0.0 copy-start.3
  48.5 38.3 %all_to_all.25.parts_ref = bf16[32,128,128]{2,1,0:T(8,128)(2,1)S(1)} all-to-all(bf16[32,128,128]{2,1,0:T(8,128)(2,1)S(1)} %add_convert_fusion), channel_id=1, replica_groups=mesh['y_high'=4,'y_low'=2,'x'=4,'z'=8,'core'=2] {'x','z'}, dimensions={0} | all-to-all | bytes 2097152 | tf_op jit(solution)/shard_map/all_to_all | solution.py:196
  86.7 0.0 copy-done
  86.7 1.7 middle.1
  88.4 1.0 copy-done.1
  89.4 7.9 %all-to-all-start.2 = ((bf16[32,128,128]{2,1,0:T(8,128)(2,1)}), bf16[32,128,128]{2,1,0:T(8,128)(2,1)S(1)}, u32[]{:S(2)}, u32[]{:S(2)}) async-start(bf16[32,128,128]{2,1,0:T(8,128)(2,1)} %copy-done.1), calls=%async_computation.2 | async-start | bytes 2097152 | tf_op jit(solution)/shard_map/all_to_all | solution.py:213
  97.4 3.4 %collective-permute-start.4 = (bf16[256,512]{1,0:T(8,128)(2,1)S(1)}, bf16[256,512]{1,0:T(8,128)(2,1)S(1)}, u32[]{:S(2)}, u32[]{:S(2)}) collective-permute-start(bf16[256,512]{1,0:T(8,128)(2,1)S(1)} %get-tuple-element.20), channel_id=1, source_target_pairs={{0,1},{1,0},{2,3},{3,2},{4,5},{5,4},{6,7},{7,6},{8,9},{9,8},{10,11... | collective-permute-start | bytes 786440 | tf_op jit(solution)/shard_map/ppermute | solution.py:138
  100.8 1.1 collective-permute-done.4
  101.9 0.1 add_convert_fusion.1
  102.0 3.0 %collective-permute-start.5 = (bf16[64,512]{1,0:T(8,128)(2,1)S(1)}, bf16[64,512]{1,0:T(8,128)(2,1)S(1)}, u32[]{:S(2)}, u32[]{:S(2)}) collective-permute-start(bf16[64,512]{1,0:T(8,128)(2,1)S(1)} %get-tuple-element.27), channel_id=1, source_target_pairs={{0,128},{128,0},{256,384},{384,256},{1,129},{129,1},{257,385},{385... | collective-permute-start | bytes 196616 | tf_op jit(solution)/shard_map/ppermute | solution.py:138
  105.0 4.2 %collective-permute-start.7 = (bf16[64,512]{1,0:T(8,128)(2,1)S(1)}, bf16[64,512]{1,0:T(8,128)(2,1)S(1)}, u32[]{:S(2)}, u32[]{:S(2)}) collective-permute-start(bf16[64,512]{1,0:T(8,128)(2,1)S(1)} %get-tuple-element.28), channel_id=1, source_target_pairs={{0,384},{128,256},{256,128},{384,0},{1,385},{129,257},{257,129},{3... | collective-permute-start | bytes 196616 | tf_op jit(solution)/shard_map/ppermute | solution.py:138
  109.2 4.2 %collective-permute-start.6 = (bf16[64,512]{1,0:T(8,128)(2,1)S(1)}, bf16[64,512]{1,0:T(8,128)(2,1)S(1)}, u32[]{:S(2)}, u32[]{:S(2)}) collective-permute-start(bf16[64,512]{1,0:T(8,128)(2,1)S(1)} %get-tuple-element.29), channel_id=1, source_target_pairs={{0,256},{128,384},{256,0},{384,128},{1,257},{129,385},{257,1},{385... | collective-permute-start | bytes 196616 | tf_op jit(solution)/shard_map/ppermute | solution.py:138
  113.4 0.0 collective-permute-done.5
  113.4 0.0 collective-permute-done.7
  113.5 4.8 %collective-permute-done.6 = bf16[64,512]{1,0:T(8,128)(2,1)S(1)} collective-permute-done((bf16[64,512]{1,0:T(8,128)(2,1)S(1)}, bf16[64,512]{1,0:T(8,128)(2,1)S(1)}, u32[]{:S(2)}, u32[]{:S(2)}) %collective-permute-start.6) | collective-permute-done | bytes 65568 | tf_op jit(solution)/shard_map/ppermute | solution.py:138
  118.3 3.9 %collective-permute-start.8 = (bf16[64,512]{1,0:T(8,128)(2,1)S(1)}, bf16[64,512]{1,0:T(8,128)(2,1)S(1)}, u32[]{:S(2)}, u32[]{:S(2)}) collective-permute-start(bf16[64,512]{1,0:T(8,128)(2,1)S(1)} %fusion.2), channel_id=1, source_target_pairs={{0,64},{64,0},{1,65},{65,1},{2,66},{66,2},{3,67},{67,3},{4,68},{68... | collective-permute-start | bytes 196616 | tf_op jit(solution)/shard_map/ppermute | solution.py:138
  122.2 1.9 collective-permute-done.8
  124.1 3.4 %collective-permute-start.9 = (bf16[64,512]{1,0:T(8,128)(2,1)S(1)}, bf16[64,512]{1,0:T(8,128)(2,1)S(1)}, u32[]{:S(2)}, u32[]{:S(2)}) collective-permute-start(bf16[64,512]{1,0:T(8,128)(2,1)S(1)} %add_convert_fusion.6), channel_id=1, source_target_pairs={{0,16},{16,0},{32,48},{48,32},{1,17},{17,1},{33,49},{49,33},{2,18}... | collective-permute-start | bytes 196616 | tf_op jit(solution)/shard_map/ppermute | solution.py:138
  127.6 1.6 collective-permute-done.9
  129.2 0.0 all-to-all-done.2.mine_ref
  129.2 5.6 %collective-permute-start.10 = (bf16[32,128,128]{2,1,0:T(8,128)(2,1)S(1)}, bf16[32,128,128]{2,1,0:T(8,128)(2,1)S(1)}, u32[]{:S(2)}, u32[]{:S(2)}) collective-permute-start(bf16[32,128,128]{2,1,0:T(8,128)(2,1)S(1)} %all-to-all-done.2.mine_ref), channel_id=1, source_target_pairs={{0,1},{1,0},{2,3},{3,2},{4,5},{5,4},{6,7},{7,6},{8,9},{9,8},{10,11... | collective-permute-start | bytes 3145736 | tf_op jit(solution)/shard_map/ppermute | solution.py:138
  134.9 2.3 %collective-permute-done.10.other_ref = bf16[32,128,128]{2,1,0:T(8,128)(2,1)S(1)} collective-permute-done((bf16[32,128,128]{2,1,0:T(8,128)(2,1)S(1)}, bf16[32,128,128]{2,1,0:T(8,128)(2,1)S(1)}, u32[]{:S(2)}, u32[]{:S(2)}) %collective-permute-start.10) | collective-permute-done | bytes 1048608 | tf_op jit(solution)/shard_map/ppermute | solution.py:138
  137.1 2.4 %backward_tiles.1 = bf16[32,128,128]{2,1,0:T(8,128)(2,1)} custom-call(s32[2]{0:T(128)S(1)} %pad_add_fusion.place_ref.core_ref, s32[4,24]{1,0:T(4,128)S(1)} %maximum_minimum_fusion.index_ref, bf16[32,128,128]{2,1,0:T(8,128)(2,1)S(1)} %all-to-all-done.2.mine_ref, bf16[32,128,128]{2,1,0:T(8,128)(2,1)S(1)} %collective-permute-done.10.other_ref, ...), custom_call_target="tpu_custom_call" | custom-call | tf_op jit(solution)/shard_map/backward_tiles/pallas_call | solution.py:222
  139.5 7.0 %all-to-all-start.3 = ((bf16[32,128,128]{2,1,0:T(8,128)(2,1)}), bf16[32,128,128]{2,1,0:T(8,128)(2,1)S(1)}, u32[]{:S(2)}, u32[]{:S(2)}) async-start(bf16[32,128,128]{2,1,0:T(8,128)(2,1)} %backward_tiles.1), calls=%async_computation.3 | async-start | bytes 2097152 | tf_op jit(solution)/shard_map/all_to_all | solution.py:232
  146.5 4.9 %collective-permute-start.13 = (bf16[64,512]{1,0:T(8,128)(2,1)S(1)}, bf16[64,512]{1,0:T(8,128)(2,1)S(1)}, u32[]{:S(2)}, u32[]{:S(2)}) collective-permute-start(bf16[64,512]{1,0:T(8,128)(2,1)S(1)} %add_convert_fusion.5), channel_id=1, source_target_pairs={{0,6},{2,4},{4,2},{6,0},{8,14},{10,12},{12,10},{14,8},{1,7},{3,5},... | collective-permute-start | bytes 196616 | tf_op jit(solution)/shard_map/ppermute | solution.py:138
  151.4 1.9 collective-permute-start.12
  153.4 2.5 %collective-permute-start.11 = (bf16[64,512]{1,0:T(8,128)(2,1)S(1)}, bf16[64,512]{1,0:T(8,128)(2,1)S(1)}, u32[]{:S(2)}, u32[]{:S(2)}) collective-permute-start(bf16[64,512]{1,0:T(8,128)(2,1)S(1)} %add_convert_fusion.5), channel_id=1, source_target_pairs={{0,2},{2,0},{4,6},{6,4},{8,10},{10,8},{12,14},{14,12},{1,3},{3,1},... | collective-permute-start | bytes 196616 | tf_op jit(solution)/shard_map/ppermute | solution.py:138
  155.8 0.0 collective-permute-done.13
  155.9 2.5 %collective-permute-done.12 = bf16[64,512]{1,0:T(8,128)(2,1)S(1)} collective-permute-done((bf16[64,512]{1,0:T(8,128)(2,1)S(1)}, bf16[64,512]{1,0:T(8,128)(2,1)S(1)}, u32[]{:S(2)}, u32[]{:S(2)}) %collective-permute-start.12) | collective-permute-done | bytes 65568 | tf_op jit(solution)/shard_map/ppermute | solution.py:138
  158.4 1.2 collective-permute-done.11
  159.6 4.3 %collective-permute-start.14 = (bf16[64,512]{1,0:T(8,128)(2,1)S(1)}, bf16[64,512]{1,0:T(8,128)(2,1)S(1)}, u32[]{:S(2)}, u32[]{:S(2)}) collective-permute-start(bf16[64,512]{1,0:T(8,128)(2,1)S(1)} %add_convert_fusion.4), channel_id=1, source_target_pairs={{0,14},{2,12},{4,10},{6,8},{8,6},{10,4},{12,2},{14,0},{1,15},{3,13... | collective-permute-start | bytes 196616 | tf_op jit(solution)/shard_map/ppermute | solution.py:138
  163.9 2.9 %collective-permute-done.14 = bf16[64,512]{1,0:T(8,128)(2,1)S(1)} collective-permute-done((bf16[64,512]{1,0:T(8,128)(2,1)S(1)}, bf16[64,512]{1,0:T(8,128)(2,1)S(1)}, u32[]{:S(2)}, u32[]{:S(2)}) %collective-permute-start.14) | collective-permute-done | bytes 65568 | tf_op jit(solution)/shard_map/ppermute | solution.py:138
  166.8 2.8 %collective-permute-start.15 = (bf16[64,512]{1,0:T(8,128)(2,1)S(1)}, bf16[64,512]{1,0:T(8,128)(2,1)S(1)}, u32[]{:S(2)}, u32[]{:S(2)}) collective-permute-start(bf16[64,512]{1,0:T(8,128)(2,1)S(1)} %add_convert_fusion.3), channel_id=1, source_target_pairs={{0,48},{16,32},{32,16},{48,0},{1,49},{17,33},{33,17},{49,1},{2,50}... | collective-permute-start | bytes 196616 | tf_op jit(solution)/shard_map/ppermute | solution.py:138
  169.6 4.2 %collective-permute-done.15 = bf16[64,512]{1,0:T(8,128)(2,1)S(1)} collective-permute-done((bf16[64,512]{1,0:T(8,128)(2,1)S(1)}, bf16[64,512]{1,0:T(8,128)(2,1)S(1)}, u32[]{:S(2)}, u32[]{:S(2)}) %collective-permute-start.15) | collective-permute-done | bytes 65568 | tf_op jit(solution)/shard_map/ppermute | solution.py:138
  173.9 0.0 all-to-all-done.3.parts_ref
  173.9 12.6 %all_to_all.26.mine_ref = bf16[4,64,512]{2,1,0:T(8,128)(2,1)S(1)} all-to-all(bf16[4,64,512]{2,1,0:T(8,128)(2,1)S(1)} %broadcast_in_dim.5), channel_id=1, replica_groups=mesh['y_high'=4,'y_low'=2,'x'=4,'z'=8,'core'=2] {'y_high'}, dimensions={0} | all-to-all | bytes 524288 | tf_op jit(solution)/shard_map/all_to_all | solution.py:249
  186.5 6.9 %collective-permute-start.16 = (bf16[4,64,512]{2,1,0:T(8,128)(2,1)S(1)}, bf16[4,64,512]{2,1,0:T(8,128)(2,1)S(1)}, u32[]{:S(2)}, u32[]{:S(2)}) collective-permute-start(bf16[4,64,512]{2,1,0:T(8,128)(2,1)S(1)} %all_to_all.26.mine_ref), channel_id=1, source_target_pairs={{0,1},{1,0},{2,3},{3,2},{4,5},{5,4},{6,7},{7,6},{8,9},{9,8},{10,11... | collective-permute-start | bytes 786440 | tf_op jit(solution)/shard_map/ppermute | solution.py:138
  193.4 1.0 last.1
  194.4 0.2 collective-permute-done.16.other_ref
  194.6 1.6 place_rows.1
  (23 shorter events, 0.2 us)
Async XLA Ops:
  0.6 0.9 copy-start.2
  2.6 10.7 %copy-start.8 = (s32[1,1,8]{2,1,0:T(1,128)S(1)}, s32[1,1,8]{2,1,0:T(1,128)}, u32[]{:S(2)}) copy-start(s32[1,1,8]{2,1,0:T(1,128)} %param.12) | copy-start | bytes 100
  2.6 10.7 %copy-start.6 = (s32[1,1,8]{2,1,0:T(1,128)S(1)}, s32[1,1,8]{2,1,0:T(1,128)}, u32[]{:S(2)}) copy-start(s32[1,1,8]{2,1,0:T(1,128)} %param.14) | copy-start | bytes 100
  2.6 10.7 %copy-start.7 = (s32[1,1,8]{2,1,0:T(1,128)S(1)}, s32[1,1,8]{2,1,0:T(1,128)}, u32[]{:S(2)}) copy-start(s32[1,1,8]{2,1,0:T(1,128)} %param.13) | copy-start | bytes 100
  2.6 10.8 %copy-start.4 = (bf16[1,1,8,128,128]{4,3,2,1,0:T(8,128)(2,1)S(1)}, bf16[1,1,8,128,128]{4,3,2,1,0:T(8,128)(2,1)}, u32[]{:S(2)}) copy-start(bf16[1,1,8,128,128]{4,3,2,1,0:T(8,128)(2,1)} %param.11) | copy-start | bytes 786436
  2.7 19.8 %copy-start.5 = (s32[3]{0:T(128)S(1)}, s32[3]{0:T(128)}, u32[]{:S(2)}) copy-start(s32[3]{0:T(128)} %constant.37.clone) | copy-start | bytes 40
  2.7 38.5 %all-to-all-start = ((bf16[32,128,128]{2,1,0:T(8,128)(2,1)}), bf16[32,128,128]{2,1,0:T(8,128)(2,1)S(1)}, u32[]{:S(2)}, u32[]{:S(2)}) async-start(bf16[32,128,128]{2,1,0:T(8,128)(2,1)} %spread.1), calls=%async_computation | async-start | bytes 2097152 | tf_op jit(solution)/shard_map/all_to_all | solution.py:174
  13.5 23.9 %collective-permute-start.2 = (bf16[1040,128]{1,0:T(8,128)(2,1)S(1)}, bf16[1040,128]{1,0:T(8,128)(2,1)S(1)}, u32[]{:S(2)}, u32[]{:S(2)}) collective-permute-start(bf16[1040,128]{1,0:T(8,128)(2,1)S(1)} %pad_maximum_fusion.refs_0_), channel_id=1, source_target_pairs={{0,48},{16,32},{32,16},{48,0},{1,49},{17,33},{33,17},{49,1},{2,50}... | collective-permute-start | bytes 798728 | tf_op jit(solution)/shard_map/ppermute | solution.py:138
  17.8 19.5 %collective-permute-start.1 = (bf16[1040,128]{1,0:T(8,128)(2,1)S(1)}, bf16[1040,128]{1,0:T(8,128)(2,1)S(1)}, u32[]{:S(2)}, u32[]{:S(2)}) collective-permute-start(bf16[1040,128]{1,0:T(8,128)(2,1)S(1)} %pad_maximum_fusion.refs_0_), channel_id=1, source_target_pairs={{0,32},{16,48},{32,0},{48,16},{1,33},{17,49},{33,1},{49,17},{2,34}... | collective-permute-start | bytes 798728 | tf_op jit(solution)/shard_map/ppermute | solution.py:138
  20.3 20.7 %collective-permute-start = (bf16[1040,128]{1,0:T(8,128)(2,1)S(1)}, bf16[1040,128]{1,0:T(8,128)(2,1)S(1)}, u32[]{:S(2)}, u32[]{:S(2)}) collective-permute-start(bf16[1040,128]{1,0:T(8,128)(2,1)S(1)} %pad_maximum_fusion.refs_0_), channel_id=1, source_target_pairs={{0,16},{16,0},{32,48},{48,32},{1,17},{17,1},{33,49},{49,33},{2,18}... | collective-permute-start | bytes 798728 | tf_op jit(solution)/shard_map/ppermute | solution.py:138
  42.7 5.4 %collective-permute-start.3 = (bf16[32,128,128]{2,1,0:T(8,128)(2,1)S(1)}, bf16[32,128,128]{2,1,0:T(8,128)(2,1)S(1)}, u32[]{:S(2)}, u32[]{:S(2)}) collective-permute-start(bf16[32,128,128]{2,1,0:T(8,128)(2,1)S(1)} %get-tuple-element.16), channel_id=1, source_target_pairs={{0,1},{1,0},{2,3},{3,2},{4,5},{5,4},{6,7},{7,6},{8,9},{9,8},{10,11... | collective-permute-start | bytes 3145736 | tf_op jit(solution)/shard_map/ppermute | solution.py:138
  48.4 38.3 %copy-start = (bf16[512,512]{1,0:T(8,128)(2,1)S(1)}, bf16[512,512]{1,0:T(8,128)(2,1)}, u32[]{:S(2)}) copy-start(bf16[512,512]{1,0:T(8,128)(2,1)} %weight_ref.3) | copy-start | bytes 1572868
  48.4 38.3 %copy-start.3 = (bf16[128,512]{1,0:T(8,128)(2,1)S(1)}, bf16[128,512]{1,0:T(8,128)(2,1)}, u32[]{:S(2)}) copy-start(bf16[128,512]{1,0:T(8,128)(2,1)} %cotangent_ref.1) | copy-start | bytes 393220
  88.4 1.0 copy-start.1
  89.4 39.8 %all-to-all-start.2 = ((bf16[32,128,128]{2,1,0:T(8,128)(2,1)}), bf16[32,128,128]{2,1,0:T(8,128)(2,1)S(1)}, u32[]{:S(2)}, u32[]{:S(2)}) async-start(bf16[32,128,128]{2,1,0:T(8,128)(2,1)} %copy-done.1), calls=%async_computation.2 | async-start | bytes 2097152 | tf_op jit(solution)/shard_map/all_to_all | solution.py:213
  97.4 4.6 %collective-permute-start.4 = (bf16[256,512]{1,0:T(8,128)(2,1)S(1)}, bf16[256,512]{1,0:T(8,128)(2,1)S(1)}, u32[]{:S(2)}, u32[]{:S(2)}) collective-permute-start(bf16[256,512]{1,0:T(8,128)(2,1)S(1)} %get-tuple-element.20), channel_id=1, source_target_pairs={{0,1},{1,0},{2,3},{3,2},{4,5},{5,4},{6,7},{7,6},{8,9},{9,8},{10,11... | collective-permute-start | bytes 786440 | tf_op jit(solution)/shard_map/ppermute | solution.py:138
  102.0 11.4 %collective-permute-start.5 = (bf16[64,512]{1,0:T(8,128)(2,1)S(1)}, bf16[64,512]{1,0:T(8,128)(2,1)S(1)}, u32[]{:S(2)}, u32[]{:S(2)}) collective-permute-start(bf16[64,512]{1,0:T(8,128)(2,1)S(1)} %get-tuple-element.27), channel_id=1, source_target_pairs={{0,128},{128,0},{256,384},{384,256},{1,129},{129,1},{257,385},{385... | collective-permute-start | bytes 196616 | tf_op jit(solution)/shard_map/ppermute | solution.py:138
  105.0 8.4 %collective-permute-start.7 = (bf16[64,512]{1,0:T(8,128)(2,1)S(1)}, bf16[64,512]{1,0:T(8,128)(2,1)S(1)}, u32[]{:S(2)}, u32[]{:S(2)}) collective-permute-start(bf16[64,512]{1,0:T(8,128)(2,1)S(1)} %get-tuple-element.28), channel_id=1, source_target_pairs={{0,384},{128,256},{256,128},{384,0},{1,385},{129,257},{257,129},{3... | collective-permute-start | bytes 196616 | tf_op jit(solution)/shard_map/ppermute | solution.py:138
  109.2 9.0 %collective-permute-start.6 = (bf16[64,512]{1,0:T(8,128)(2,1)S(1)}, bf16[64,512]{1,0:T(8,128)(2,1)S(1)}, u32[]{:S(2)}, u32[]{:S(2)}) collective-permute-start(bf16[64,512]{1,0:T(8,128)(2,1)S(1)} %get-tuple-element.29), channel_id=1, source_target_pairs={{0,256},{128,384},{256,0},{384,128},{1,257},{129,385},{257,1},{385... | collective-permute-start | bytes 196616 | tf_op jit(solution)/shard_map/ppermute | solution.py:138
  118.3 5.8 %collective-permute-start.8 = (bf16[64,512]{1,0:T(8,128)(2,1)S(1)}, bf16[64,512]{1,0:T(8,128)(2,1)S(1)}, u32[]{:S(2)}, u32[]{:S(2)}) collective-permute-start(bf16[64,512]{1,0:T(8,128)(2,1)S(1)} %fusion.2), channel_id=1, source_target_pairs={{0,64},{64,0},{1,65},{65,1},{2,66},{66,2},{3,67},{67,3},{4,68},{68... | collective-permute-start | bytes 196616 | tf_op jit(solution)/shard_map/ppermute | solution.py:138
  124.1 5.1 %collective-permute-start.9 = (bf16[64,512]{1,0:T(8,128)(2,1)S(1)}, bf16[64,512]{1,0:T(8,128)(2,1)S(1)}, u32[]{:S(2)}, u32[]{:S(2)}) collective-permute-start(bf16[64,512]{1,0:T(8,128)(2,1)S(1)} %add_convert_fusion.6), channel_id=1, source_target_pairs={{0,16},{16,0},{32,48},{48,32},{1,17},{17,1},{33,49},{49,33},{2,18}... | collective-permute-start | bytes 196616 | tf_op jit(solution)/shard_map/ppermute | solution.py:138
  129.2 7.9 %collective-permute-start.10 = (bf16[32,128,128]{2,1,0:T(8,128)(2,1)S(1)}, bf16[32,128,128]{2,1,0:T(8,128)(2,1)S(1)}, u32[]{:S(2)}, u32[]{:S(2)}) collective-permute-start(bf16[32,128,128]{2,1,0:T(8,128)(2,1)S(1)} %all-to-all-done.2.mine_ref), channel_id=1, source_target_pairs={{0,1},{1,0},{2,3},{3,2},{4,5},{5,4},{6,7},{7,6},{8,9},{9,8},{10,11... | collective-permute-start | bytes 3145736 | tf_op jit(solution)/shard_map/ppermute | solution.py:138
  139.5 34.4 %all-to-all-start.3 = ((bf16[32,128,128]{2,1,0:T(8,128)(2,1)}), bf16[32,128,128]{2,1,0:T(8,128)(2,1)S(1)}, u32[]{:S(2)}, u32[]{:S(2)}) async-start(bf16[32,128,128]{2,1,0:T(8,128)(2,1)} %backward_tiles.1), calls=%async_computation.3 | async-start | bytes 2097152 | tf_op jit(solution)/shard_map/all_to_all | solution.py:232
  146.5 9.3 %collective-permute-start.13 = (bf16[64,512]{1,0:T(8,128)(2,1)S(1)}, bf16[64,512]{1,0:T(8,128)(2,1)S(1)}, u32[]{:S(2)}, u32[]{:S(2)}) collective-permute-start(bf16[64,512]{1,0:T(8,128)(2,1)S(1)} %add_convert_fusion.5), channel_id=1, source_target_pairs={{0,6},{2,4},{4,2},{6,0},{8,14},{10,12},{12,10},{14,8},{1,7},{3,5},... | collective-permute-start | bytes 196616 | tf_op jit(solution)/shard_map/ppermute | solution.py:138
  151.4 6.9 %collective-permute-start.12 = (bf16[64,512]{1,0:T(8,128)(2,1)S(1)}, bf16[64,512]{1,0:T(8,128)(2,1)S(1)}, u32[]{:S(2)}, u32[]{:S(2)}) collective-permute-start(bf16[64,512]{1,0:T(8,128)(2,1)S(1)} %add_convert_fusion.5), channel_id=1, source_target_pairs={{0,4},{2,6},{4,0},{6,2},{8,12},{10,14},{12,8},{14,10},{1,5},{3,7},... | collective-permute-start | bytes 196616 | tf_op jit(solution)/shard_map/ppermute | solution.py:138
  153.4 6.2 %collective-permute-start.11 = (bf16[64,512]{1,0:T(8,128)(2,1)S(1)}, bf16[64,512]{1,0:T(8,128)(2,1)S(1)}, u32[]{:S(2)}, u32[]{:S(2)}) collective-permute-start(bf16[64,512]{1,0:T(8,128)(2,1)S(1)} %add_convert_fusion.5), channel_id=1, source_target_pairs={{0,2},{2,0},{4,6},{6,4},{8,10},{10,8},{12,14},{14,12},{1,3},{3,1},... | collective-permute-start | bytes 196616 | tf_op jit(solution)/shard_map/ppermute | solution.py:138
  159.6 7.2 %collective-permute-start.14 = (bf16[64,512]{1,0:T(8,128)(2,1)S(1)}, bf16[64,512]{1,0:T(8,128)(2,1)S(1)}, u32[]{:S(2)}, u32[]{:S(2)}) collective-permute-start(bf16[64,512]{1,0:T(8,128)(2,1)S(1)} %add_convert_fusion.4), channel_id=1, source_target_pairs={{0,14},{2,12},{4,10},{6,8},{8,6},{10,4},{12,2},{14,0},{1,15},{3,13... | collective-permute-start | bytes 196616 | tf_op jit(solution)/shard_map/ppermute | solution.py:138
  166.8 7.0 %collective-permute-start.15 = (bf16[64,512]{1,0:T(8,128)(2,1)S(1)}, bf16[64,512]{1,0:T(8,128)(2,1)S(1)}, u32[]{:S(2)}, u32[]{:S(2)}) collective-permute-start(bf16[64,512]{1,0:T(8,128)(2,1)S(1)} %add_convert_fusion.3), channel_id=1, source_target_pairs={{0,48},{16,32},{32,16},{48,0},{1,49},{17,33},{33,17},{49,1},{2,50}... | collective-permute-start | bytes 196616 | tf_op jit(solution)/shard_map/ppermute | solution.py:138
  186.5 8.1 %collective-permute-start.16 = (bf16[4,64,512]{2,1,0:T(8,128)(2,1)S(1)}, bf16[4,64,512]{2,1,0:T(8,128)(2,1)S(1)}, u32[]{:S(2)}, u32[]{:S(2)}) collective-permute-start(bf16[4,64,512]{2,1,0:T(8,128)(2,1)S(1)} %all_to_all.26.mine_ref), channel_id=1, source_target_pairs={{0,1},{1,0},{2,3},{3,2},{4,5},{5,4},{6,7},{7,6},{8,9},{9,8},{10,11... | collective-permute-start | bytes 786440 | tf_op jit(solution)/shard_map/ppermute | solution.py:138

commit v13 on v12

--- a/solution.py
+++ b/solution.py
@@ -7,7 +7,7 @@
 from jax.experimental.pallas import tpu as pltpu
 from jax.sharding import Mesh, PartitionSpec as P
 
-Y_HIGH, Y_LOW, X, Z, CORES = 4, 2, 4, 8, 2
+Y_HIGH, Y_LOW, X, Z, CORES = 2, 4, 4, 8, 2
 Y = Y_HIGH * Y_LOW
 ROW = ("y_high", "y_low", "x")
 COL = ("z", "core")
@@ -125,9 +125,9 @@
 
 def place_rows(place_ref, mine_ref, other_ref, out_ref):
     core = place_ref[0]
-    half, share = WIDTH // CORES, WIDTH // (Y_HIGH * CORES)
+    half, share = WIDTH // CORES, WIDTH // (Y_LOW * CORES)
     scale = 1.0 / math.sqrt(TILE * Y * X * Z * CORES)
-    for y in range(Y_HIGH):
+    for y in range(Y_LOW):
         for side, ref in ((core, mine_ref), (1 - core, other_ref)):
             start = pl.multiple_of(side * half + y * share, share)
             out_ref[pl.ds(start, share), :] = ref[y].astype(F32) * scale
@@ -213,8 +213,8 @@
     grad_mine = lax.all_to_all(grad, ("x", "z"), 0, 0, tiled=True)
     piece = weight_keep.astype(F32) + exchange(weight_send, "core", 1).astype(F32)
     piece = piece.astype(BF16)
-    piece = scatter(piece, "y_high")
-    piece = double(piece, "y_low", 1)
+    piece = scatter(piece, "y_low")
+    piece = double(piece, "y_high", 1)
     piece = double(piece, "x", 1)
     grad_mine, piece = lax.optimization_barrier((grad_mine, piece))
 
@@ -244,9 +244,9 @@
         name="last",
     )(back, weight)
 
-    share = WIDTH // (Y_HIGH * CORES)
-    piece = jnp.broadcast_to(piece[None], (Y_HIGH, share, WIDTH))
-    whole = lax.all_to_all(piece, "y_high", 0, 0, tiled=True)
+    share = WIDTH // (Y_LOW * CORES)
+    piece = jnp.broadcast_to(piece[None], (Y_LOW, share, WIDTH))
+    whole = lax.all_to_all(piece, "y_low", 0, 0, tiled=True)
     weight_grad = pl.pallas_call(
         place_rows,
         in_specs=[smem()] + [vmem()] * 2,

time: 197 us -> 194 us (0.985)
  blocking collectives: 50.9 us -> 47.6 us
    all_to_all x1, blocking collectives: 12.6 us -> 9.31 us  [body(): whole = lax.all_to_all(piece, 'y_low', 0, 0, tiled=True)]
    ppermute x17, starting transfers between devices: 63.1 us -> 60.4 us  [exchange(): return lax.ppermute(array, axis, [(i, i ^ distance) for i in range(size)])]
  transfers between devices with their start and end apart: 20 -> 20, of which waited for: 13 -> 14; matrix products, arithmetic and copies ran while one was open for 0% -> 0% of each run, Pallas kernels for 0% -> 1%
where the time goes in v13:
time: 194 us; the launch traced here: 193 us
  starting transfers between devices  87.3 us (45%)
  blocking collectives  47.6 us (25%)
  waiting for transfers between devices  44.7 us (23%)
  Pallas kernels  9.22 us (5%)
  local copies, waits for them, and re-layouts  2.1 us (1%)
    ppermute x17, starting transfers between devices, exchange(): return lax.ppermute(array, axis, [(i, i ^ distance) for i in range(size)])  60.4 us
    ppermute x17, waiting for transfers between devices, exchange(): return lax.ppermute(array, axis, [(i, i ^ distance) for i in range(size)])  44.7 us
    all_to_all x1, blocking collectives, body(): parts = lax.all_to_all(term, ('x', 'z'), 0, 0, tiled=True)  38.3 us
    all_to_all x1, starting transfers between devices, body(): panel = lax.all_to_all(chunks, ROW, 0, 0, tiled=True)  10.6 us
    all_to_all x1, blocking collectives, body(): whole = lax.all_to_all(piece, 'y_low', 0, 0, tiled=True)  9.31 us
    all_to_all x1, starting transfers between devices, body(): back = lax.all_to_all(back, ROW, 0, 0, tiled=True)  8.26 us
    all_to_all x1, starting transfers between devices, body(): grad_mine = lax.all_to_all(grad, ('x', 'z'), 0, 0, tiled=True)  7.95 us
  transfers between devices with their start and end apart: 20, of which 14 were waited for; matrix products, arithmetic and copies ran while one was open for 0% of the time, Pallas kernels for 1%

profile of v13, /device:TPU:1, one launch (start us, length us, event | category | flops | bytes accessed | tf_op | source)
XLA Modules:
  0.0 192.7 jit_solution(17782817131590123125)
XLA Ops:
  0.6 0.0 copy-start.2
  0.6 0.9 copy-done.2
  1.5 1.1 spread.1
  2.7 0.0 copy-start.5
  2.7 10.6 %all-to-all-start = ((bf16[32,128,128]{2,1,0:T(8,128)(2,1)}), bf16[32,128,128]{2,1,0:T(8,128)(2,1)S(1)}, u32[]{:S(2)}, u32[]{:S(2)}) async-start(bf16[32,128,128]{2,1,0:T(8,128)(2,1)} %spread.1), calls=%async_computation | async-start | bytes 2097152 | tf_op jit(solution)/shard_map/all_to_all | solution.py:174
  13.3 0.0 copy-done.8
  13.3 0.0 copy-done.6
  13.4 0.1 fusion.11
  13.5 4.3 %collective-permute-start.2 = (bf16[1040,128]{1,0:T(8,128)(2,1)S(1)}, bf16[1040,128]{1,0:T(8,128)(2,1)S(1)}, u32[]{:S(2)}, u32[]{:S(2)}) collective-permute-start(bf16[1040,128]{1,0:T(8,128)(2,1)S(1)} %pad_maximum_fusion.refs_0_), channel_id=1, source_target_pairs={{0,48},{16,32},{32,16},{48,0},{1,49},{17,33},{33,17},{49,1},{2,50}... | collective-permute-start | bytes 798728 | tf_op jit(solution)/shard_map/ppermute | solution.py:138
  17.8 2.5 %collective-permute-start.1 = (bf16[1040,128]{1,0:T(8,128)(2,1)S(1)}, bf16[1040,128]{1,0:T(8,128)(2,1)S(1)}, u32[]{:S(2)}, u32[]{:S(2)}) collective-permute-start(bf16[1040,128]{1,0:T(8,128)(2,1)S(1)} %pad_maximum_fusion.refs_0_), channel_id=1, source_target_pairs={{0,32},{16,48},{32,0},{48,16},{1,33},{17,49},{33,1},{49,17},{2,34}... | collective-permute-start | bytes 798728 | tf_op jit(solution)/shard_map/ppermute | solution.py:138
  20.3 2.1 %collective-permute-start = (bf16[1040,128]{1,0:T(8,128)(2,1)S(1)}, bf16[1040,128]{1,0:T(8,128)(2,1)S(1)}, u32[]{:S(2)}, u32[]{:S(2)}) collective-permute-start(bf16[1040,128]{1,0:T(8,128)(2,1)S(1)} %pad_maximum_fusion.refs_0_), channel_id=1, source_target_pairs={{0,16},{16,0},{32,48},{48,32},{1,17},{17,1},{33,49},{49,33},{2,18}... | collective-permute-start | bytes 798728 | tf_op jit(solution)/shard_map/ppermute | solution.py:138
  22.5 0.1 broadcast_in_dim.4
  22.6 0.1 min.14
  22.7 0.1 pad_add_fusion.place_ref.core_ref
  22.7 14.6 %collective-permute-done.2.refs_3_ = bf16[1040,128]{1,0:T(8,128)(2,1)S(1)} collective-permute-done((bf16[1040,128]{1,0:T(8,128)(2,1)S(1)}, bf16[1040,128]{1,0:T(8,128)(2,1)S(1)}, u32[]{:S(2)}, u32[]{:S(2)}) %collective-permute-start.2) | collective-permute-done | bytes 266272 | tf_op jit(solution)/shard_map/ppermute | solution.py:138
  37.4 0.0 collective-permute-done.1.refs_2_
  37.4 3.7 %collective-permute-done.refs_1_ = bf16[1040,128]{1,0:T(8,128)(2,1)S(1)} collective-permute-done((bf16[1040,128]{1,0:T(8,128)(2,1)S(1)}, bf16[1040,128]{1,0:T(8,128)(2,1)S(1)}, u32[]{:S(2)}, u32[]{:S(2)}) %collective-permute-start) | collective-permute-done | bytes 266272 | tf_op jit(solution)/shard_map/ppermute | solution.py:138
  41.1 0.1 maximum_minimum_fusion.index_ref
  41.2 0.0 all-to-all-done.panel_ref
  41.2 1.5 forward_tiles.1
  42.7 3.1 %collective-permute-start.3 = (bf16[32,128,128]{2,1,0:T(8,128)(2,1)S(1)}, bf16[32,128,128]{2,1,0:T(8,128)(2,1)S(1)}, u32[]{:S(2)}, u32[]{:S(2)}) collective-permute-start(bf16[32,128,128]{2,1,0:T(8,128)(2,1)S(1)} %get-tuple-element.16), channel_id=1, source_target_pairs={{0,1},{1,0},{2,3},{3,2},{4,5},{5,4},{6,7},{7,6},{8,9},{9,8},{10,11... | collective-permute-start | bytes 3145736 | tf_op jit(solution)/shard_map/ppermute | solution.py:138
  45.8 2.3 %collective-permute-done.3 = bf16[32,128,128]{2,1,0:T(8,128)(2,1)S(1)} collective-permute-done((bf16[32,128,128]{2,1,0:T(8,128)(2,1)S(1)}, bf16[32,128,128]{2,1,0:T(8,128)(2,1)S(1)}, u32[]{:S(2)}, u32[]{:S(2)}) %collective-permute-start.3) | collective-permute-done | bytes 1048608 | tf_op jit(solution)/shard_map/ppermute | solution.py:138
  48.1 0.4 add_convert_fusion
  48.4 0.0 copy-start
  48.4 0.0 copy-start.3
  48.5 38.3 %all_to_all.25.parts_ref = bf16[32,128,128]{2,1,0:T(8,128)(2,1)S(1)} all-to-all(bf16[32,128,128]{2,1,0:T(8,128)(2,1)S(1)} %add_convert_fusion), channel_id=1, replica_groups=mesh['y_high'=2,'y_low'=4,'x'=4,'z'=8,'core'=2] {'x','z'}, dimensions={0} | all-to-all | bytes 2097152 | tf_op jit(solution)/shard_map/all_to_all | solution.py:196
  86.7 0.0 copy-done
  86.7 1.7 middle.1
  88.4 1.0 copy-done.1
  89.4 7.9 %all-to-all-start.2 = ((bf16[32,128,128]{2,1,0:T(8,128)(2,1)}), bf16[32,128,128]{2,1,0:T(8,128)(2,1)S(1)}, u32[]{:S(2)}, u32[]{:S(2)}) async-start(bf16[32,128,128]{2,1,0:T(8,128)(2,1)} %copy-done.1), calls=%async_computation.2 | async-start | bytes 2097152 | tf_op jit(solution)/shard_map/all_to_all | solution.py:213
  97.4 3.4 %collective-permute-start.4 = (bf16[256,512]{1,0:T(8,128)(2,1)S(1)}, bf16[256,512]{1,0:T(8,128)(2,1)S(1)}, u32[]{:S(2)}, u32[]{:S(2)}) collective-permute-start(bf16[256,512]{1,0:T(8,128)(2,1)S(1)} %get-tuple-element.20), channel_id=1, source_target_pairs={{0,1},{1,0},{2,3},{3,2},{4,5},{5,4},{6,7},{7,6},{8,9},{9,8},{10,11... | collective-permute-start | bytes 786440 | tf_op jit(solution)/shard_map/ppermute | solution.py:138
  100.8 1.1 collective-permute-done.4
  101.9 0.1 add_convert_fusion.1
  102.0 2.2 %collective-permute-start.5 = (bf16[64,512]{1,0:T(8,128)(2,1)S(1)}, bf16[64,512]{1,0:T(8,128)(2,1)S(1)}, u32[]{:S(2)}, u32[]{:S(2)}) collective-permute-start(bf16[64,512]{1,0:T(8,128)(2,1)S(1)} %get-tuple-element.27), channel_id=1, source_target_pairs={{0,64},{64,0},{128,192},{192,128},{1,65},{65,1},{129,193},{193,129... | collective-permute-start | bytes 196616 | tf_op jit(solution)/shard_map/ppermute | solution.py:138
  104.3 3.8 %collective-permute-start.7 = (bf16[64,512]{1,0:T(8,128)(2,1)S(1)}, bf16[64,512]{1,0:T(8,128)(2,1)S(1)}, u32[]{:S(2)}, u32[]{:S(2)}) collective-permute-start(bf16[64,512]{1,0:T(8,128)(2,1)S(1)} %get-tuple-element.28), channel_id=1, source_target_pairs={{0,192},{64,128},{128,64},{192,0},{1,193},{65,129},{129,65},{193,1... | collective-permute-start | bytes 196616 | tf_op jit(solution)/shard_map/ppermute | solution.py:138
  108.1 2.3 %collective-permute-start.6 = (bf16[64,512]{1,0:T(8,128)(2,1)S(1)}, bf16[64,512]{1,0:T(8,128)(2,1)S(1)}, u32[]{:S(2)}, u32[]{:S(2)}) collective-permute-start(bf16[64,512]{1,0:T(8,128)(2,1)S(1)} %get-tuple-element.29), channel_id=1, source_target_pairs={{0,128},{64,192},{128,0},{192,64},{1,129},{65,193},{129,1},{193,65... | collective-permute-start | bytes 196616 | tf_op jit(solution)/shard_map/ppermute | solution.py:138
  110.4 0.0 collective-permute-done.5
  110.4 0.7 collective-permute-done.7
  111.1 3.5 %collective-permute-done.6 = bf16[64,512]{1,0:T(8,128)(2,1)S(1)} collective-permute-done((bf16[64,512]{1,0:T(8,128)(2,1)S(1)}, bf16[64,512]{1,0:T(8,128)(2,1)S(1)}, u32[]{:S(2)}, u32[]{:S(2)}) %collective-permute-start.6) | collective-permute-done | bytes 65568 | tf_op jit(solution)/shard_map/ppermute | solution.py:138
  114.6 5.9 %collective-permute-start.8 = (bf16[64,512]{1,0:T(8,128)(2,1)S(1)}, bf16[64,512]{1,0:T(8,128)(2,1)S(1)}, u32[]{:S(2)}, u32[]{:S(2)}) collective-permute-start(bf16[64,512]{1,0:T(8,128)(2,1)S(1)} %fusion.2), channel_id=1, source_target_pairs={{0,256},{256,0},{1,257},{257,1},{2,258},{258,2},{3,259},{259,3},{4... | collective-permute-start | bytes 196616 | tf_op jit(solution)/shard_map/ppermute | solution.py:138
  120.5 3.3 %collective-permute-done.8 = bf16[64,512]{1,0:T(8,128)(2,1)S(1)} collective-permute-done((bf16[64,512]{1,0:T(8,128)(2,1)S(1)}, bf16[64,512]{1,0:T(8,128)(2,1)S(1)}, u32[]{:S(2)}, u32[]{:S(2)}) %collective-permute-start.8) | collective-permute-done | bytes 65568 | tf_op jit(solution)/shard_map/ppermute | solution.py:138
  123.9 2.8 %collective-permute-start.9 = (bf16[64,512]{1,0:T(8,128)(2,1)S(1)}, bf16[64,512]{1,0:T(8,128)(2,1)S(1)}, u32[]{:S(2)}, u32[]{:S(2)}) collective-permute-start(bf16[64,512]{1,0:T(8,128)(2,1)S(1)} %add_convert_fusion.6), channel_id=1, source_target_pairs={{0,16},{16,0},{32,48},{48,32},{1,17},{17,1},{33,49},{49,33},{2,18}... | collective-permute-start | bytes 196616 | tf_op jit(solution)/shard_map/ppermute | solution.py:138
  126.7 2.2 %collective-permute-done.9 = bf16[64,512]{1,0:T(8,128)(2,1)S(1)} collective-permute-done((bf16[64,512]{1,0:T(8,128)(2,1)S(1)}, bf16[64,512]{1,0:T(8,128)(2,1)S(1)}, u32[]{:S(2)}, u32[]{:S(2)}) %collective-permute-start.9) | collective-permute-done | bytes 65568 | tf_op jit(solution)/shard_map/ppermute | solution.py:138
  128.9 0.0 all-to-all-done.2.mine_ref
  128.9 5.7 %collective-permute-start.10 = (bf16[32,128,128]{2,1,0:T(8,128)(2,1)S(1)}, bf16[32,128,128]{2,1,0:T(8,128)(2,1)S(1)}, u32[]{:S(2)}, u32[]{:S(2)}) collective-permute-start(bf16[32,128,128]{2,1,0:T(8,128)(2,1)S(1)} %all-to-all-done.2.mine_ref), channel_id=1, source_target_pairs={{0,1},{1,0},{2,3},{3,2},{4,5},{5,4},{6,7},{7,6},{8,9},{9,8},{10,11... | collective-permute-start | bytes 3145736 | tf_op jit(solution)/shard_map/ppermute | solution.py:138
  134.6 2.3 %collective-permute-done.10.other_ref = bf16[32,128,128]{2,1,0:T(8,128)(2,1)S(1)} collective-permute-done((bf16[32,128,128]{2,1,0:T(8,128)(2,1)S(1)}, bf16[32,128,128]{2,1,0:T(8,128)(2,1)S(1)}, u32[]{:S(2)}, u32[]{:S(2)}) %collective-permute-start.10) | collective-permute-done | bytes 1048608 | tf_op jit(solution)/shard_map/ppermute | solution.py:138
  136.9 2.4 %backward_tiles.1 = bf16[32,128,128]{2,1,0:T(8,128)(2,1)} custom-call(s32[2]{0:T(128)S(1)} %pad_add_fusion.place_ref.core_ref, s32[4,24]{1,0:T(4,128)S(1)} %maximum_minimum_fusion.index_ref, bf16[32,128,128]{2,1,0:T(8,128)(2,1)S(1)} %all-to-all-done.2.mine_ref, bf16[32,128,128]{2,1,0:T(8,128)(2,1)S(1)} %collective-permute-done.10.other_ref, ...), custom_call_target="tpu_custom_call" | custom-call | tf_op jit(solution)/shard_map/backward_tiles/pallas_call | solution.py:222
  139.3 8.3 %all-to-all-start.3 = ((bf16[32,128,128]{2,1,0:T(8,128)(2,1)}), bf16[32,128,128]{2,1,0:T(8,128)(2,1)S(1)}, u32[]{:S(2)}, u32[]{:S(2)}) async-start(bf16[32,128,128]{2,1,0:T(8,128)(2,1)} %backward_tiles.1), calls=%async_computation.3 | async-start | bytes 2097152 | tf_op jit(solution)/shard_map/all_to_all | solution.py:232
  147.5 4.9 %collective-permute-start.13 = (bf16[64,512]{1,0:T(8,128)(2,1)S(1)}, bf16[64,512]{1,0:T(8,128)(2,1)S(1)}, u32[]{:S(2)}, u32[]{:S(2)}) collective-permute-start(bf16[64,512]{1,0:T(8,128)(2,1)S(1)} %add_convert_fusion.5), channel_id=1, source_target_pairs={{0,6},{2,4},{4,2},{6,0},{8,14},{10,12},{12,10},{14,8},{1,7},{3,5},... | collective-permute-start | bytes 196616 | tf_op jit(solution)/shard_map/ppermute | solution.py:138
  152.4 1.9 collective-permute-start.12
  154.4 2.5 %collective-permute-start.11 = (bf16[64,512]{1,0:T(8,128)(2,1)S(1)}, bf16[64,512]{1,0:T(8,128)(2,1)S(1)}, u32[]{:S(2)}, u32[]{:S(2)}) collective-permute-start(bf16[64,512]{1,0:T(8,128)(2,1)S(1)} %add_convert_fusion.5), channel_id=1, source_target_pairs={{0,2},{2,0},{4,6},{6,4},{8,10},{10,8},{12,14},{14,12},{1,3},{3,1},... | collective-permute-start | bytes 196616 | tf_op jit(solution)/shard_map/ppermute | solution.py:138
  156.8 0.0 collective-permute-done.13
  156.8 2.5 %collective-permute-done.12 = bf16[64,512]{1,0:T(8,128)(2,1)S(1)} collective-permute-done((bf16[64,512]{1,0:T(8,128)(2,1)S(1)}, bf16[64,512]{1,0:T(8,128)(2,1)S(1)}, u32[]{:S(2)}, u32[]{:S(2)}) %collective-permute-start.12) | collective-permute-done | bytes 65568 | tf_op jit(solution)/shard_map/ppermute | solution.py:138
  159.3 1.2 collective-permute-done.11
  160.6 4.3 %collective-permute-start.14 = (bf16[64,512]{1,0:T(8,128)(2,1)S(1)}, bf16[64,512]{1,0:T(8,128)(2,1)S(1)}, u32[]{:S(2)}, u32[]{:S(2)}) collective-permute-start(bf16[64,512]{1,0:T(8,128)(2,1)S(1)} %add_convert_fusion.4), channel_id=1, source_target_pairs={{0,14},{2,12},{4,10},{6,8},{8,6},{10,4},{12,2},{14,0},{1,15},{3,13... | collective-permute-start | bytes 196616 | tf_op jit(solution)/shard_map/ppermute | solution.py:138
  164.9 2.9 %collective-permute-done.14 = bf16[64,512]{1,0:T(8,128)(2,1)S(1)} collective-permute-done((bf16[64,512]{1,0:T(8,128)(2,1)S(1)}, bf16[64,512]{1,0:T(8,128)(2,1)S(1)}, u32[]{:S(2)}, u32[]{:S(2)}) %collective-permute-start.14) | collective-permute-done | bytes 65568 | tf_op jit(solution)/shard_map/ppermute | solution.py:138
  167.8 2.8 %collective-permute-start.15 = (bf16[64,512]{1,0:T(8,128)(2,1)S(1)}, bf16[64,512]{1,0:T(8,128)(2,1)S(1)}, u32[]{:S(2)}, u32[]{:S(2)}) collective-permute-start(bf16[64,512]{1,0:T(8,128)(2,1)S(1)} %add_convert_fusion.3), channel_id=1, source_target_pairs={{0,48},{16,32},{32,16},{48,0},{1,49},{17,33},{33,17},{49,1},{2,50}... | collective-permute-start | bytes 196616 | tf_op jit(solution)/shard_map/ppermute | solution.py:138
  170.6 4.2 %collective-permute-done.15 = bf16[64,512]{1,0:T(8,128)(2,1)S(1)} collective-permute-done((bf16[64,512]{1,0:T(8,128)(2,1)S(1)}, bf16[64,512]{1,0:T(8,128)(2,1)S(1)}, u32[]{:S(2)}, u32[]{:S(2)}) %collective-permute-start.15) | collective-permute-done | bytes 65568 | tf_op jit(solution)/shard_map/ppermute | solution.py:138
  174.9 0.0 all-to-all-done.3.parts_ref
  174.9 9.3 %all_to_all.26.mine_ref = bf16[4,64,512]{2,1,0:T(8,128)(2,1)S(1)} all-to-all(bf16[4,64,512]{2,1,0:T(8,128)(2,1)S(1)} %broadcast_in_dim.5), channel_id=1, replica_groups=mesh['y_high'=2,'y_low'=4,'x'=4,'z'=8,'core'=2] {'y_low'}, dimensions={0} | all-to-all | bytes 524288 | tf_op jit(solution)/shard_map/all_to_all | solution.py:249
  184.2 5.8 %collective-permute-start.16 = (bf16[4,64,512]{2,1,0:T(8,128)(2,1)S(1)}, bf16[4,64,512]{2,1,0:T(8,128)(2,1)S(1)}, u32[]{:S(2)}, u32[]{:S(2)}) collective-permute-start(bf16[4,64,512]{2,1,0:T(8,128)(2,1)S(1)} %all_to_all.26.mine_ref), channel_id=1, source_target_pairs={{0,1},{1,0},{2,3},{3,2},{4,5},{5,4},{6,7},{7,6},{8,9},{9,8},{10,11... | collective-permute-start | bytes 786440 | tf_op jit(solution)/shard_map/ppermute | solution.py:138
  190.0 1.0 last.1
  191.0 0.2 collective-permute-done.16.other_ref
  191.2 1.6 place_rows.1
  (23 shorter events, 0.2 us)
Async XLA Ops:
  0.6 0.9 copy-start.2
  2.6 10.7 %copy-start.8 = (s32[1,1,8]{2,1,0:T(1,128)S(1)}, s32[1,1,8]{2,1,0:T(1,128)}, u32[]{:S(2)}) copy-start(s32[1,1,8]{2,1,0:T(1,128)} %param.12) | copy-start | bytes 100
  2.6 10.7 %copy-start.6 = (s32[1,1,8]{2,1,0:T(1,128)S(1)}, s32[1,1,8]{2,1,0:T(1,128)}, u32[]{:S(2)}) copy-start(s32[1,1,8]{2,1,0:T(1,128)} %param.14) | copy-start | bytes 100
  2.6 10.7 %copy-start.7 = (s32[1,1,8]{2,1,0:T(1,128)S(1)}, s32[1,1,8]{2,1,0:T(1,128)}, u32[]{:S(2)}) copy-start(s32[1,1,8]{2,1,0:T(1,128)} %param.13) | copy-start | bytes 100
  2.6 10.8 %copy-start.4 = (bf16[1,1,8,128,128]{4,3,2,1,0:T(8,128)(2,1)S(1)}, bf16[1,1,8,128,128]{4,3,2,1,0:T(8,128)(2,1)}, u32[]{:S(2)}) copy-start(bf16[1,1,8,128,128]{4,3,2,1,0:T(8,128)(2,1)} %param.11) | copy-start | bytes 786436
  2.7 19.8 %copy-start.5 = (s32[3]{0:T(128)S(1)}, s32[3]{0:T(128)}, u32[]{:S(2)}) copy-start(s32[3]{0:T(128)} %constant.37.clone) | copy-start | bytes 40
  2.7 38.5 %all-to-all-start = ((bf16[32,128,128]{2,1,0:T(8,128)(2,1)}), bf16[32,128,128]{2,1,0:T(8,128)(2,1)S(1)}, u32[]{:S(2)}, u32[]{:S(2)}) async-start(bf16[32,128,128]{2,1,0:T(8,128)(2,1)} %spread.1), calls=%async_computation | async-start | bytes 2097152 | tf_op jit(solution)/shard_map/all_to_all | solution.py:174
  13.5 23.9 %collective-permute-start.2 = (bf16[1040,128]{1,0:T(8,128)(2,1)S(1)}, bf16[1040,128]{1,0:T(8,128)(2,1)S(1)}, u32[]{:S(2)}, u32[]{:S(2)}) collective-permute-start(bf16[1040,128]{1,0:T(8,128)(2,1)S(1)} %pad_maximum_fusion.refs_0_), channel_id=1, source_target_pairs={{0,48},{16,32},{32,16},{48,0},{1,49},{17,33},{33,17},{49,1},{2,50}... | collective-permute-start | bytes 798728 | tf_op jit(solution)/shard_map/ppermute | solution.py:138
  17.8 19.5 %collective-permute-start.1 = (bf16[1040,128]{1,0:T(8,128)(2,1)S(1)}, bf16[1040,128]{1,0:T(8,128)(2,1)S(1)}, u32[]{:S(2)}, u32[]{:S(2)}) collective-permute-start(bf16[1040,128]{1,0:T(8,128)(2,1)S(1)} %pad_maximum_fusion.refs_0_), channel_id=1, source_target_pairs={{0,32},{16,48},{32,0},{48,16},{1,33},{17,49},{33,1},{49,17},{2,34}... | collective-permute-start | bytes 798728 | tf_op jit(solution)/shard_map/ppermute | solution.py:138
  20.3 20.7 %collective-permute-start = (bf16[1040,128]{1,0:T(8,128)(2,1)S(1)}, bf16[1040,128]{1,0:T(8,128)(2,1)S(1)}, u32[]{:S(2)}, u32[]{:S(2)}) collective-permute-start(bf16[1040,128]{1,0:T(8,128)(2,1)S(1)} %pad_maximum_fusion.refs_0_), channel_id=1, source_target_pairs={{0,16},{16,0},{32,48},{48,32},{1,17},{17,1},{33,49},{49,33},{2,18}... | collective-permute-start | bytes 798728 | tf_op jit(solution)/shard_map/ppermute | solution.py:138
  42.7 5.4 %collective-permute-start.3 = (bf16[32,128,128]{2,1,0:T(8,128)(2,1)S(1)}, bf16[32,128,128]{2,1,0:T(8,128)(2,1)S(1)}, u32[]{:S(2)}, u32[]{:S(2)}) collective-permute-start(bf16[32,128,128]{2,1,0:T(8,128)(2,1)S(1)} %get-tuple-element.16), channel_id=1, source_target_pairs={{0,1},{1,0},{2,3},{3,2},{4,5},{5,4},{6,7},{7,6},{8,9},{9,8},{10,11... | collective-permute-start | bytes 3145736 | tf_op jit(solution)/shard_map/ppermute | solution.py:138
  48.4 38.3 %copy-start = (bf16[512,512]{1,0:T(8,128)(2,1)S(1)}, bf16[512,512]{1,0:T(8,128)(2,1)}, u32[]{:S(2)}) copy-start(bf16[512,512]{1,0:T(8,128)(2,1)} %weight_ref.3) | copy-start | bytes 1572868
  48.4 38.3 %copy-start.3 = (bf16[128,512]{1,0:T(8,128)(2,1)S(1)}, bf16[128,512]{1,0:T(8,128)(2,1)}, u32[]{:S(2)}) copy-start(bf16[128,512]{1,0:T(8,128)(2,1)} %cotangent_ref.1) | copy-start | bytes 393220
  88.4 1.0 copy-start.1
  89.4 39.5 %all-to-all-start.2 = ((bf16[32,128,128]{2,1,0:T(8,128)(2,1)}), bf16[32,128,128]{2,1,0:T(8,128)(2,1)S(1)}, u32[]{:S(2)}, u32[]{:S(2)}) async-start(bf16[32,128,128]{2,1,0:T(8,128)(2,1)} %copy-done.1), calls=%async_computation.2 | async-start | bytes 2097152 | tf_op jit(solution)/shard_map/all_to_all | solution.py:213
  97.4 4.6 %collective-permute-start.4 = (bf16[256,512]{1,0:T(8,128)(2,1)S(1)}, bf16[256,512]{1,0:T(8,128)(2,1)S(1)}, u32[]{:S(2)}, u32[]{:S(2)}) collective-permute-start(bf16[256,512]{1,0:T(8,128)(2,1)S(1)} %get-tuple-element.20), channel_id=1, source_target_pairs={{0,1},{1,0},{2,3},{3,2},{4,5},{5,4},{6,7},{7,6},{8,9},{9,8},{10,11... | collective-permute-start | bytes 786440 | tf_op jit(solution)/shard_map/ppermute | solution.py:138
  102.0 8.4 %collective-permute-start.5 = (bf16[64,512]{1,0:T(8,128)(2,1)S(1)}, bf16[64,512]{1,0:T(8,128)(2,1)S(1)}, u32[]{:S(2)}, u32[]{:S(2)}) collective-permute-start(bf16[64,512]{1,0:T(8,128)(2,1)S(1)} %get-tuple-element.27), channel_id=1, source_target_pairs={{0,64},{64,0},{128,192},{192,128},{1,65},{65,1},{129,193},{193,129... | collective-permute-start | bytes 196616 | tf_op jit(solution)/shard_map/ppermute | solution.py:138
  104.3 6.9 %collective-permute-start.7 = (bf16[64,512]{1,0:T(8,128)(2,1)S(1)}, bf16[64,512]{1,0:T(8,128)(2,1)S(1)}, u32[]{:S(2)}, u32[]{:S(2)}) collective-permute-start(bf16[64,512]{1,0:T(8,128)(2,1)S(1)} %get-tuple-element.28), channel_id=1, source_target_pairs={{0,192},{64,128},{128,64},{192,0},{1,193},{65,129},{129,65},{193,1... | collective-permute-start | bytes 196616 | tf_op jit(solution)/shard_map/ppermute | solution.py:138
  108.1 6.5 %collective-permute-start.6 = (bf16[64,512]{1,0:T(8,128)(2,1)S(1)}, bf16[64,512]{1,0:T(8,128)(2,1)S(1)}, u32[]{:S(2)}, u32[]{:S(2)}) collective-permute-start(bf16[64,512]{1,0:T(8,128)(2,1)S(1)} %get-tuple-element.29), channel_id=1, source_target_pairs={{0,128},{64,192},{128,0},{192,64},{1,129},{65,193},{129,1},{193,65... | collective-permute-start | bytes 196616 | tf_op jit(solution)/shard_map/ppermute | solution.py:138
  114.6 9.2 %collective-permute-start.8 = (bf16[64,512]{1,0:T(8,128)(2,1)S(1)}, bf16[64,512]{1,0:T(8,128)(2,1)S(1)}, u32[]{:S(2)}, u32[]{:S(2)}) collective-permute-start(bf16[64,512]{1,0:T(8,128)(2,1)S(1)} %fusion.2), channel_id=1, source_target_pairs={{0,256},{256,0},{1,257},{257,1},{2,258},{258,2},{3,259},{259,3},{4... | collective-permute-start | bytes 196616 | tf_op jit(solution)/shard_map/ppermute | solution.py:138
  123.9 5.0 %collective-permute-start.9 = (bf16[64,512]{1,0:T(8,128)(2,1)S(1)}, bf16[64,512]{1,0:T(8,128)(2,1)S(1)}, u32[]{:S(2)}, u32[]{:S(2)}) collective-permute-start(bf16[64,512]{1,0:T(8,128)(2,1)S(1)} %add_convert_fusion.6), channel_id=1, source_target_pairs={{0,16},{16,0},{32,48},{48,32},{1,17},{17,1},{33,49},{49,33},{2,18}... | collective-permute-start | bytes 196616 | tf_op jit(solution)/shard_map/ppermute | solution.py:138
  128.9 8.0 %collective-permute-start.10 = (bf16[32,128,128]{2,1,0:T(8,128)(2,1)S(1)}, bf16[32,128,128]{2,1,0:T(8,128)(2,1)S(1)}, u32[]{:S(2)}, u32[]{:S(2)}) collective-permute-start(bf16[32,128,128]{2,1,0:T(8,128)(2,1)S(1)} %all-to-all-done.2.mine_ref), channel_id=1, source_target_pairs={{0,1},{1,0},{2,3},{3,2},{4,5},{5,4},{6,7},{7,6},{8,9},{9,8},{10,11... | collective-permute-start | bytes 3145736 | tf_op jit(solution)/shard_map/ppermute | solution.py:138
  139.3 35.6 %all-to-all-start.3 = ((bf16[32,128,128]{2,1,0:T(8,128)(2,1)}), bf16[32,128,128]{2,1,0:T(8,128)(2,1)S(1)}, u32[]{:S(2)}, u32[]{:S(2)}) async-start(bf16[32,128,128]{2,1,0:T(8,128)(2,1)} %backward_tiles.1), calls=%async_computation.3 | async-start | bytes 2097152 | tf_op jit(solution)/shard_map/all_to_all | solution.py:232
  147.5 9.3 %collective-permute-start.13 = (bf16[64,512]{1,0:T(8,128)(2,1)S(1)}, bf16[64,512]{1,0:T(8,128)(2,1)S(1)}, u32[]{:S(2)}, u32[]{:S(2)}) collective-permute-start(bf16[64,512]{1,0:T(8,128)(2,1)S(1)} %add_convert_fusion.5), channel_id=1, source_target_pairs={{0,6},{2,4},{4,2},{6,0},{8,14},{10,12},{12,10},{14,8},{1,7},{3,5},... | collective-permute-start | bytes 196616 | tf_op jit(solution)/shard_map/ppermute | solution.py:138
  152.4 6.9 %collective-permute-start.12 = (bf16[64,512]{1,0:T(8,128)(2,1)S(1)}, bf16[64,512]{1,0:T(8,128)(2,1)S(1)}, u32[]{:S(2)}, u32[]{:S(2)}) collective-permute-start(bf16[64,512]{1,0:T(8,128)(2,1)S(1)} %add_convert_fusion.5), channel_id=1, source_target_pairs={{0,4},{2,6},{4,0},{6,2},{8,12},{10,14},{12,8},{14,10},{1,5},{3,7},... | collective-permute-start | bytes 196616 | tf_op jit(solution)/shard_map/ppermute | solution.py:138
  154.4 6.2 %collective-permute-start.11 = (bf16[64,512]{1,0:T(8,128)(2,1)S(1)}, bf16[64,512]{1,0:T(8,128)(2,1)S(1)}, u32[]{:S(2)}, u32[]{:S(2)}) collective-permute-start(bf16[64,512]{1,0:T(8,128)(2,1)S(1)} %add_convert_fusion.5), channel_id=1, source_target_pairs={{0,2},{2,0},{4,6},{6,4},{8,10},{10,8},{12,14},{14,12},{1,3},{3,1},... | collective-permute-start | bytes 196616 | tf_op jit(solution)/shard_map/ppermute | solution.py:138
  160.6 7.2 %collective-permute-start.14 = (bf16[64,512]{1,0:T(8,128)(2,1)S(1)}, bf16[64,512]{1,0:T(8,128)(2,1)S(1)}, u32[]{:S(2)}, u32[]{:S(2)}) collective-permute-start(bf16[64,512]{1,0:T(8,128)(2,1)S(1)} %add_convert_fusion.4), channel_id=1, source_target_pairs={{0,14},{2,12},{4,10},{6,8},{8,6},{10,4},{12,2},{14,0},{1,15},{3,13... | collective-permute-start | bytes 196616 | tf_op jit(solution)/shard_map/ppermute | solution.py:138
  167.8 7.0 %collective-permute-start.15 = (bf16[64,512]{1,0:T(8,128)(2,1)S(1)}, bf16[64,512]{1,0:T(8,128)(2,1)S(1)}, u32[]{:S(2)}, u32[]{:S(2)}) collective-permute-start(bf16[64,512]{1,0:T(8,128)(2,1)S(1)} %add_convert_fusion.3), channel_id=1, source_target_pairs={{0,48},{16,32},{32,16},{48,0},{1,49},{17,33},{33,17},{49,1},{2,50}... | collective-permute-start | bytes 196616 | tf_op jit(solution)/shard_map/ppermute | solution.py:138
  184.2 6.9 %collective-permute-start.16 = (bf16[4,64,512]{2,1,0:T(8,128)(2,1)S(1)}, bf16[4,64,512]{2,1,0:T(8,128)(2,1)S(1)}, u32[]{:S(2)}, u32[]{:S(2)}) collective-permute-start(bf16[4,64,512]{2,1,0:T(8,128)(2,1)S(1)} %all_to_all.26.mine_ref), channel_id=1, source_target_pairs={{0,1},{1,0},{2,3},{3,2},{4,5},{5,4},{6,7},{7,6},{8,9},{9,8},{10,11... | collective-permute-start | bytes 786440 | tf_op jit(solution)/shard_map/ppermute | solution.py:138

commit v14 on v13

--- a/solution.py
+++ b/solution.py
@@ -129,7 +129,7 @@
     scale = 1.0 / math.sqrt(TILE * Y * X * Z * CORES)
     for y in range(Y_LOW):
         for side, ref in ((core, mine_ref), (1 - core, other_ref)):
-            start = pl.multiple_of(side * half + y * share, share)
+            start = pl.multiple_of(side * half + (y ^ place_ref[2]) * share, share)
             out_ref[pl.ds(start, share), :] = ref[y].astype(F32) * scale
 
 
@@ -138,8 +138,8 @@
     return lax.ppermute(array, axis, [(i, i ^ distance) for i in range(size)])
 
 
-def scatter(array, axis):
-    size, place = lax.axis_size(axis), lax.axis_index(axis)
+def scatter(array, axis, flip):
+    size, place = lax.axis_size(axis), lax.axis_index(axis) ^ flip
     shares = array.reshape(size, array.shape[0] // size, array.shape[1])
 
     def share(distance):
@@ -161,7 +161,8 @@
 
 
 def body(features, weight, cotangent, tile_values, tile_rows, tile_cols, tile_valid):
-    place = jnp.stack([lax.axis_index("core"), lax.axis_index("x")]).astype(jnp.int32)
+    flip = lax.axis_index("y_high") * (Y_LOW - 1)
+    place = jnp.stack([lax.axis_index("core"), lax.axis_index("x"), flip]).astype(jnp.int32)
 
     chunks = pl.pallas_call(
         spread,
@@ -213,8 +214,8 @@
     grad_mine = lax.all_to_all(grad, ("x", "z"), 0, 0, tiled=True)
     piece = weight_keep.astype(F32) + exchange(weight_send, "core", 1).astype(F32)
     piece = piece.astype(BF16)
-    piece = scatter(piece, "y_low")
-    piece = double(piece, "y_high", 1)
+    piece = scatter(piece, "y_low", flip)
+    piece = double(piece, ("y_high", "y_low"), Y - 1)
     piece = double(piece, "x", 1)
     grad_mine, piece = lax.optimization_barrier((grad_mine, piece))
 

time: 194 us -> 191 us (0.985)
  no operation moved by 1% of the time
where the time goes in v14:
time: 191 us; the launch traced here: 190 us
  starting transfers between devices  85.8 us (45%)
  blocking collectives  47.6 us (25%)
  waiting for transfers between devices  43.5 us (23%)
  Pallas kernels  9.23 us (5%)
  local copies, waits for them, and re-layouts  2.1 us (1%)
    ppermute x17, starting transfers between devices, exchange(): return lax.ppermute(array, axis, [(i, i ^ distance) for i in range(size)])  59.7 us
    ppermute x17, waiting for transfers between devices, exchange(): return lax.ppermute(array, axis, [(i, i ^ distance) for i in range(size)])  43.5 us
    all_to_all x1, blocking collectives, body(): parts = lax.all_to_all(term, ('x', 'z'), 0, 0, tiled=True)  38.3 us
    all_to_all x1, starting transfers between devices, body(): panel = lax.all_to_all(chunks, ROW, 0, 0, tiled=True)  10.6 us
    all_to_all x1, blocking collectives, body(): whole = lax.all_to_all(piece, 'y_low', 0, 0, tiled=True)  9.3 us
    all_to_all x1, starting transfers between devices, body(): grad_mine = lax.all_to_all(grad, ('x', 'z'), 0, 0, tiled=True)  7.94 us
    all_to_all x1, starting transfers between devices, body(): back = lax.all_to_all(back, ROW, 0, 0, tiled=True)  7.56 us
  transfers between devices with their start and end apart: 20, of which 14 were waited for; matrix products, arithmetic and copies ran while one was open for 0% of the time, Pallas kernels for 1%

profile of v14, /device:TPU:1, one launch (start us, length us, event | category | flops | bytes accessed | tf_op | source)
XLA Modules:
  0.0 190.0 jit_solution(10041755278572108853)
XLA Ops:
  0.6 0.0 copy-start.2
  0.6 0.9 copy-done.2
  1.5 1.1 spread.1
  2.7 0.0 copy-start.5
  2.7 10.6 %all-to-all-start = ((bf16[32,128,128]{2,1,0:T(8,128)(2,1)}), bf16[32,128,128]{2,1,0:T(8,128)(2,1)S(1)}, u32[]{:S(2)}, u32[]{:S(2)}) async-start(bf16[32,128,128]{2,1,0:T(8,128)(2,1)} %spread.1), calls=%async_computation | async-start | bytes 2097152 | tf_op jit(solution)/shard_map/all_to_all | solution.py:175
  13.3 0.0 copy-done.8
  13.3 0.0 copy-done.6
  13.4 0.1 fusion.11
  13.5 4.3 %collective-permute-start.2 = (bf16[1040,128]{1,0:T(8,128)(2,1)S(1)}, bf16[1040,128]{1,0:T(8,128)(2,1)S(1)}, u32[]{:S(2)}, u32[]{:S(2)}) collective-permute-start(bf16[1040,128]{1,0:T(8,128)(2,1)S(1)} %pad_maximum_fusion.refs_0_), channel_id=1, source_target_pairs={{0,48},{16,32},{32,16},{48,0},{1,49},{17,33},{33,17},{49,1},{2,50}... | collective-permute-start | bytes 798728 | tf_op jit(solution)/shard_map/ppermute | solution.py:138
  17.8 2.5 %collective-permute-start.1 = (bf16[1040,128]{1,0:T(8,128)(2,1)S(1)}, bf16[1040,128]{1,0:T(8,128)(2,1)S(1)}, u32[]{:S(2)}, u32[]{:S(2)}) collective-permute-start(bf16[1040,128]{1,0:T(8,128)(2,1)S(1)} %pad_maximum_fusion.refs_0_), channel_id=1, source_target_pairs={{0,32},{16,48},{32,0},{48,16},{1,33},{17,49},{33,1},{49,17},{2,34}... | collective-permute-start | bytes 798728 | tf_op jit(solution)/shard_map/ppermute | solution.py:138
  20.3 2.1 %collective-permute-start = (bf16[1040,128]{1,0:T(8,128)(2,1)S(1)}, bf16[1040,128]{1,0:T(8,128)(2,1)S(1)}, u32[]{:S(2)}, u32[]{:S(2)}) collective-permute-start(bf16[1040,128]{1,0:T(8,128)(2,1)S(1)} %pad_maximum_fusion.refs_0_), channel_id=1, source_target_pairs={{0,16},{16,0},{32,48},{48,32},{1,17},{17,1},{33,49},{49,33},{2,18}... | collective-permute-start | bytes 798728 | tf_op jit(solution)/shard_map/ppermute | solution.py:138
  22.5 0.1 broadcast_in_dim.4
  22.6 0.1 min.14
  22.7 0.1 pad_add_fusion.place_ref.core_ref
  22.7 14.6 %collective-permute-done.2.refs_3_ = bf16[1040,128]{1,0:T(8,128)(2,1)S(1)} collective-permute-done((bf16[1040,128]{1,0:T(8,128)(2,1)S(1)}, bf16[1040,128]{1,0:T(8,128)(2,1)S(1)}, u32[]{:S(2)}, u32[]{:S(2)}) %collective-permute-start.2) | collective-permute-done | bytes 266272 | tf_op jit(solution)/shard_map/ppermute | solution.py:138
  37.4 0.0 collective-permute-done.1.refs_2_
  37.4 3.7 %collective-permute-done.refs_1_ = bf16[1040,128]{1,0:T(8,128)(2,1)S(1)} collective-permute-done((bf16[1040,128]{1,0:T(8,128)(2,1)S(1)}, bf16[1040,128]{1,0:T(8,128)(2,1)S(1)}, u32[]{:S(2)}, u32[]{:S(2)}) %collective-permute-start) | collective-permute-done | bytes 266272 | tf_op jit(solution)/shard_map/ppermute | solution.py:138
  41.1 0.1 maximum_minimum_fusion.index_ref
  41.2 0.0 all-to-all-done.panel_ref
  41.2 1.5 forward_tiles.1
  42.7 3.1 %collective-permute-start.3 = (bf16[32,128,128]{2,1,0:T(8,128)(2,1)S(1)}, bf16[32,128,128]{2,1,0:T(8,128)(2,1)S(1)}, u32[]{:S(2)}, u32[]{:S(2)}) collective-permute-start(bf16[32,128,128]{2,1,0:T(8,128)(2,1)S(1)} %get-tuple-element.16), channel_id=1, source_target_pairs={{0,1},{1,0},{2,3},{3,2},{4,5},{5,4},{6,7},{7,6},{8,9},{9,8},{10,11... | collective-permute-start | bytes 3145736 | tf_op jit(solution)/shard_map/ppermute | solution.py:138
  45.8 2.3 %collective-permute-done.3 = bf16[32,128,128]{2,1,0:T(8,128)(2,1)S(1)} collective-permute-done((bf16[32,128,128]{2,1,0:T(8,128)(2,1)S(1)}, bf16[32,128,128]{2,1,0:T(8,128)(2,1)S(1)}, u32[]{:S(2)}, u32[]{:S(2)}) %collective-permute-start.3) | collective-permute-done | bytes 1048608 | tf_op jit(solution)/shard_map/ppermute | solution.py:138
  48.1 0.4 add_convert_fusion
  48.4 0.0 copy-start
  48.4 0.0 copy-start.3
  48.5 38.3 %all_to_all.25.parts_ref = bf16[32,128,128]{2,1,0:T(8,128)(2,1)S(1)} all-to-all(bf16[32,128,128]{2,1,0:T(8,128)(2,1)S(1)} %add_convert_fusion), channel_id=1, replica_groups=mesh['y_high'=2,'y_low'=4,'x'=4,'z'=8,'core'=2] {'x','z'}, dimensions={0} | all-to-all | bytes 2097152 | tf_op jit(solution)/shard_map/all_to_all | solution.py:197
  86.7 0.0 copy-done
  86.7 1.7 middle.1
  88.4 1.0 copy-done.1
  89.4 7.9 %all-to-all-start.2 = ((bf16[32,128,128]{2,1,0:T(8,128)(2,1)}), bf16[32,128,128]{2,1,0:T(8,128)(2,1)S(1)}, u32[]{:S(2)}, u32[]{:S(2)}) async-start(bf16[32,128,128]{2,1,0:T(8,128)(2,1)} %copy-done.1), calls=%async_computation.2 | async-start | bytes 2097152 | tf_op jit(solution)/shard_map/all_to_all | solution.py:214
  97.3 3.4 %collective-permute-start.4 = (bf16[256,512]{1,0:T(8,128)(2,1)S(1)}, bf16[256,512]{1,0:T(8,128)(2,1)S(1)}, u32[]{:S(2)}, u32[]{:S(2)}) collective-permute-start(bf16[256,512]{1,0:T(8,128)(2,1)S(1)} %get-tuple-element.20), channel_id=1, source_target_pairs={{0,1},{1,0},{2,3},{3,2},{4,5},{5,4},{6,7},{7,6},{8,9},{9,8},{10,11... | collective-permute-start | bytes 786440 | tf_op jit(solution)/shard_map/ppermute | solution.py:138
  100.8 1.1 collective-permute-done.4
  101.9 0.1 add_convert_fusion.1
  102.0 2.2 %collective-permute-start.5 = (bf16[64,512]{1,0:T(8,128)(2,1)S(1)}, bf16[64,512]{1,0:T(8,128)(2,1)S(1)}, u32[]{:S(2)}, u32[]{:S(2)}) collective-permute-start(bf16[64,512]{1,0:T(8,128)(2,1)S(1)} %get-tuple-element.27), channel_id=1, source_target_pairs={{0,64},{64,0},{128,192},{192,128},{1,65},{65,1},{129,193},{193,129... | collective-permute-start | bytes 196616 | tf_op jit(solution)/shard_map/ppermute | solution.py:138
  104.3 3.8 %collective-permute-start.7 = (bf16[64,512]{1,0:T(8,128)(2,1)S(1)}, bf16[64,512]{1,0:T(8,128)(2,1)S(1)}, u32[]{:S(2)}, u32[]{:S(2)}) collective-permute-start(bf16[64,512]{1,0:T(8,128)(2,1)S(1)} %get-tuple-element.28), channel_id=1, source_target_pairs={{0,192},{64,128},{128,64},{192,0},{1,193},{65,129},{129,65},{193,1... | collective-permute-start | bytes 196616 | tf_op jit(solution)/shard_map/ppermute | solution.py:138
  108.1 2.3 %collective-permute-start.6 = (bf16[64,512]{1,0:T(8,128)(2,1)S(1)}, bf16[64,512]{1,0:T(8,128)(2,1)S(1)}, u32[]{:S(2)}, u32[]{:S(2)}) collective-permute-start(bf16[64,512]{1,0:T(8,128)(2,1)S(1)} %get-tuple-element.29), channel_id=1, source_target_pairs={{0,128},{64,192},{128,0},{192,64},{1,129},{65,193},{129,1},{193,65... | collective-permute-start | bytes 196616 | tf_op jit(solution)/shard_map/ppermute | solution.py:138
  110.4 0.0 collective-permute-done.5
  110.4 0.7 collective-permute-done.7
  111.1 3.5 %collective-permute-done.6 = bf16[64,512]{1,0:T(8,128)(2,1)S(1)} collective-permute-done((bf16[64,512]{1,0:T(8,128)(2,1)S(1)}, bf16[64,512]{1,0:T(8,128)(2,1)S(1)}, u32[]{:S(2)}, u32[]{:S(2)}) %collective-permute-start.6) | collective-permute-done | bytes 65568 | tf_op jit(solution)/shard_map/ppermute | solution.py:138
  114.6 4.5 %collective-permute-start.8 = (bf16[64,512]{1,0:T(8,128)(2,1)S(1)}, bf16[64,512]{1,0:T(8,128)(2,1)S(1)}, u32[]{:S(2)}, u32[]{:S(2)}) collective-permute-start(bf16[64,512]{1,0:T(8,128)(2,1)S(1)} %fusion.2), channel_id=1, source_target_pairs={{0,448},{64,384},{128,320},{192,256},{256,192},{320,128},{384,64},... | collective-permute-start | bytes 196616 | tf_op jit(solution)/shard_map/ppermute | solution.py:138
  119.2 2.7 %collective-permute-done.8 = bf16[64,512]{1,0:T(8,128)(2,1)S(1)} collective-permute-done((bf16[64,512]{1,0:T(8,128)(2,1)S(1)}, bf16[64,512]{1,0:T(8,128)(2,1)S(1)}, u32[]{:S(2)}, u32[]{:S(2)}) %collective-permute-start.8) | collective-permute-done | bytes 65568 | tf_op jit(solution)/shard_map/ppermute | solution.py:138
  121.9 3.4 %collective-permute-start.9 = (bf16[64,512]{1,0:T(8,128)(2,1)S(1)}, bf16[64,512]{1,0:T(8,128)(2,1)S(1)}, u32[]{:S(2)}, u32[]{:S(2)}) collective-permute-start(bf16[64,512]{1,0:T(8,128)(2,1)S(1)} %add_convert_fusion.6), channel_id=1, source_target_pairs={{0,16},{16,0},{32,48},{48,32},{1,17},{17,1},{33,49},{49,33},{2,18}... | collective-permute-start | bytes 196616 | tf_op jit(solution)/shard_map/ppermute | solution.py:138
  125.3 1.6 collective-permute-done.9
  126.9 0.0 all-to-all-done.2.mine_ref
  127.0 5.7 %collective-permute-start.10 = (bf16[32,128,128]{2,1,0:T(8,128)(2,1)S(1)}, bf16[32,128,128]{2,1,0:T(8,128)(2,1)S(1)}, u32[]{:S(2)}, u32[]{:S(2)}) collective-permute-start(bf16[32,128,128]{2,1,0:T(8,128)(2,1)S(1)} %all-to-all-done.2.mine_ref), channel_id=1, source_target_pairs={{0,1},{1,0},{2,3},{3,2},{4,5},{5,4},{6,7},{7,6},{8,9},{9,8},{10,11... | collective-permute-start | bytes 3145736 | tf_op jit(solution)/shard_map/ppermute | solution.py:138
  132.6 2.3 %collective-permute-done.10.other_ref = bf16[32,128,128]{2,1,0:T(8,128)(2,1)S(1)} collective-permute-done((bf16[32,128,128]{2,1,0:T(8,128)(2,1)S(1)}, bf16[32,128,128]{2,1,0:T(8,128)(2,1)S(1)}, u32[]{:S(2)}, u32[]{:S(2)}) %collective-permute-start.10) | collective-permute-done | bytes 1048608 | tf_op jit(solution)/shard_map/ppermute | solution.py:138
  134.9 2.4 %backward_tiles.1 = bf16[32,128,128]{2,1,0:T(8,128)(2,1)} custom-call(s32[3]{0:T(128)S(1)} %pad_add_fusion.place_ref.core_ref, s32[4,24]{1,0:T(4,128)S(1)} %maximum_minimum_fusion.index_ref, bf16[32,128,128]{2,1,0:T(8,128)(2,1)S(1)} %all-to-all-done.2.mine_ref, bf16[32,128,128]{2,1,0:T(8,128)(2,1)S(1)} %collective-permute-done.10.other_ref, ...), custom_call_target="tpu_custom_call" | custom-call | tf_op jit(solution)/shard_map/backward_tiles/pallas_call | solution.py:223
  137.3 7.6 %all-to-all-start.3 = ((bf16[32,128,128]{2,1,0:T(8,128)(2,1)}), bf16[32,128,128]{2,1,0:T(8,128)(2,1)S(1)}, u32[]{:S(2)}, u32[]{:S(2)}) async-start(bf16[32,128,128]{2,1,0:T(8,128)(2,1)} %backward_tiles.1), calls=%async_computation.3 | async-start | bytes 2097152 | tf_op jit(solution)/shard_map/all_to_all | solution.py:233
  144.8 4.9 %collective-permute-start.13 = (bf16[64,512]{1,0:T(8,128)(2,1)S(1)}, bf16[64,512]{1,0:T(8,128)(2,1)S(1)}, u32[]{:S(2)}, u32[]{:S(2)}) collective-permute-start(bf16[64,512]{1,0:T(8,128)(2,1)S(1)} %add_convert_fusion.5), channel_id=1, source_target_pairs={{0,6},{2,4},{4,2},{6,0},{8,14},{10,12},{12,10},{14,8},{1,7},{3,5},... | collective-permute-start | bytes 196616 | tf_op jit(solution)/shard_map/ppermute | solution.py:138
  149.7 1.9 %collective-permute-start.12 = (bf16[64,512]{1,0:T(8,128)(2,1)S(1)}, bf16[64,512]{1,0:T(8,128)(2,1)S(1)}, u32[]{:S(2)}, u32[]{:S(2)}) collective-permute-start(bf16[64,512]{1,0:T(8,128)(2,1)S(1)} %add_convert_fusion.5), channel_id=1, source_target_pairs={{0,4},{2,6},{4,0},{6,2},{8,12},{10,14},{12,8},{14,10},{1,5},{3,7},... | collective-permute-start | bytes 196616 | tf_op jit(solution)/shard_map/ppermute | solution.py:138
  151.7 2.5 %collective-permute-start.11 = (bf16[64,512]{1,0:T(8,128)(2,1)S(1)}, bf16[64,512]{1,0:T(8,128)(2,1)S(1)}, u32[]{:S(2)}, u32[]{:S(2)}) collective-permute-start(bf16[64,512]{1,0:T(8,128)(2,1)S(1)} %add_convert_fusion.5), channel_id=1, source_target_pairs={{0,2},{2,0},{4,6},{6,4},{8,10},{10,8},{12,14},{14,12},{1,3},{3,1},... | collective-permute-start | bytes 196616 | tf_op jit(solution)/shard_map/ppermute | solution.py:138
  154.1 0.0 collective-permute-done.13
  154.1 2.5 %collective-permute-done.12 = bf16[64,512]{1,0:T(8,128)(2,1)S(1)} collective-permute-done((bf16[64,512]{1,0:T(8,128)(2,1)S(1)}, bf16[64,512]{1,0:T(8,128)(2,1)S(1)}, u32[]{:S(2)}, u32[]{:S(2)}) %collective-permute-start.12) | collective-permute-done | bytes 65568 | tf_op jit(solution)/shard_map/ppermute | solution.py:138
  156.6 1.2 collective-permute-done.11
  157.9 4.3 %collective-permute-start.14 = (bf16[64,512]{1,0:T(8,128)(2,1)S(1)}, bf16[64,512]{1,0:T(8,128)(2,1)S(1)}, u32[]{:S(2)}, u32[]{:S(2)}) collective-permute-start(bf16[64,512]{1,0:T(8,128)(2,1)S(1)} %add_convert_fusion.4), channel_id=1, source_target_pairs={{0,14},{2,12},{4,10},{6,8},{8,6},{10,4},{12,2},{14,0},{1,15},{3,13... | collective-permute-start | bytes 196616 | tf_op jit(solution)/shard_map/ppermute | solution.py:138
  162.2 2.9 %collective-permute-done.14 = bf16[64,512]{1,0:T(8,128)(2,1)S(1)} collective-permute-done((bf16[64,512]{1,0:T(8,128)(2,1)S(1)}, bf16[64,512]{1,0:T(8,128)(2,1)S(1)}, u32[]{:S(2)}, u32[]{:S(2)}) %collective-permute-start.14) | collective-permute-done | bytes 65568 | tf_op jit(solution)/shard_map/ppermute | solution.py:138
  165.1 2.8 %collective-permute-start.15 = (bf16[64,512]{1,0:T(8,128)(2,1)S(1)}, bf16[64,512]{1,0:T(8,128)(2,1)S(1)}, u32[]{:S(2)}, u32[]{:S(2)}) collective-permute-start(bf16[64,512]{1,0:T(8,128)(2,1)S(1)} %add_convert_fusion.3), channel_id=1, source_target_pairs={{0,48},{16,32},{32,16},{48,0},{1,49},{17,33},{33,17},{49,1},{2,50}... | collective-permute-start | bytes 196616 | tf_op jit(solution)/shard_map/ppermute | solution.py:138
  167.9 4.2 %collective-permute-done.15 = bf16[64,512]{1,0:T(8,128)(2,1)S(1)} collective-permute-done((bf16[64,512]{1,0:T(8,128)(2,1)S(1)}, bf16[64,512]{1,0:T(8,128)(2,1)S(1)}, u32[]{:S(2)}, u32[]{:S(2)}) %collective-permute-start.15) | collective-permute-done | bytes 65568 | tf_op jit(solution)/shard_map/ppermute | solution.py:138
  172.2 0.0 all-to-all-done.3.parts_ref
  172.2 9.3 %all_to_all.26.mine_ref = bf16[4,64,512]{2,1,0:T(8,128)(2,1)S(1)} all-to-all(bf16[4,64,512]{2,1,0:T(8,128)(2,1)S(1)} %broadcast_in_dim.5), channel_id=1, replica_groups=mesh['y_high'=2,'y_low'=4,'x'=4,'z'=8,'core'=2] {'y_low'}, dimensions={0} | all-to-all | bytes 524288 | tf_op jit(solution)/shard_map/all_to_all | solution.py:250
  181.5 5.8 %collective-permute-start.16 = (bf16[4,64,512]{2,1,0:T(8,128)(2,1)S(1)}, bf16[4,64,512]{2,1,0:T(8,128)(2,1)S(1)}, u32[]{:S(2)}, u32[]{:S(2)}) collective-permute-start(bf16[4,64,512]{2,1,0:T(8,128)(2,1)S(1)} %all_to_all.26.mine_ref), channel_id=1, source_target_pairs={{0,1},{1,0},{2,3},{3,2},{4,5},{5,4},{6,7},{7,6},{8,9},{9,8},{10,11... | collective-permute-start | bytes 786440 | tf_op jit(solution)/shard_map/ppermute | solution.py:138
  187.3 1.0 last.1
  188.3 0.2 collective-permute-done.16.other_ref
  188.5 1.6 place_rows.1
  (23 shorter events, 0.2 us)
Async XLA Ops:
  0.6 0.9 copy-start.2
  2.6 10.7 %copy-start.8 = (s32[1,1,8]{2,1,0:T(1,128)S(1)}, s32[1,1,8]{2,1,0:T(1,128)}, u32[]{:S(2)}) copy-start(s32[1,1,8]{2,1,0:T(1,128)} %param.12) | copy-start | bytes 100
  2.6 10.7 %copy-start.6 = (s32[1,1,8]{2,1,0:T(1,128)S(1)}, s32[1,1,8]{2,1,0:T(1,128)}, u32[]{:S(2)}) copy-start(s32[1,1,8]{2,1,0:T(1,128)} %param.14) | copy-start | bytes 100
  2.6 10.7 %copy-start.7 = (s32[1,1,8]{2,1,0:T(1,128)S(1)}, s32[1,1,8]{2,1,0:T(1,128)}, u32[]{:S(2)}) copy-start(s32[1,1,8]{2,1,0:T(1,128)} %param.13) | copy-start | bytes 100
  2.6 10.8 %copy-start.4 = (bf16[1,1,8,128,128]{4,3,2,1,0:T(8,128)(2,1)S(1)}, bf16[1,1,8,128,128]{4,3,2,1,0:T(8,128)(2,1)}, u32[]{:S(2)}) copy-start(bf16[1,1,8,128,128]{4,3,2,1,0:T(8,128)(2,1)} %param.11) | copy-start | bytes 786436
  2.7 19.8 %copy-start.5 = (s32[3]{0:T(128)S(1)}, s32[3]{0:T(128)}, u32[]{:S(2)}) copy-start(s32[3]{0:T(128)} %constant.41.clone) | copy-start | bytes 40
  2.7 38.5 %all-to-all-start = ((bf16[32,128,128]{2,1,0:T(8,128)(2,1)}), bf16[32,128,128]{2,1,0:T(8,128)(2,1)S(1)}, u32[]{:S(2)}, u32[]{:S(2)}) async-start(bf16[32,128,128]{2,1,0:T(8,128)(2,1)} %spread.1), calls=%async_computation | async-start | bytes 2097152 | tf_op jit(solution)/shard_map/all_to_all | solution.py:175
  13.5 23.9 %collective-permute-start.2 = (bf16[1040,128]{1,0:T(8,128)(2,1)S(1)}, bf16[1040,128]{1,0:T(8,128)(2,1)S(1)}, u32[]{:S(2)}, u32[]{:S(2)}) collective-permute-start(bf16[1040,128]{1,0:T(8,128)(2,1)S(1)} %pad_maximum_fusion.refs_0_), channel_id=1, source_target_pairs={{0,48},{16,32},{32,16},{48,0},{1,49},{17,33},{33,17},{49,1},{2,50}... | collective-permute-start | bytes 798728 | tf_op jit(solution)/shard_map/ppermute | solution.py:138
  17.8 19.5 %collective-permute-start.1 = (bf16[1040,128]{1,0:T(8,128)(2,1)S(1)}, bf16[1040,128]{1,0:T(8,128)(2,1)S(1)}, u32[]{:S(2)}, u32[]{:S(2)}) collective-permute-start(bf16[1040,128]{1,0:T(8,128)(2,1)S(1)} %pad_maximum_fusion.refs_0_), channel_id=1, source_target_pairs={{0,32},{16,48},{32,0},{48,16},{1,33},{17,49},{33,1},{49,17},{2,34}... | collective-permute-start | bytes 798728 | tf_op jit(solution)/shard_map/ppermute | solution.py:138
  20.3 20.7 %collective-permute-start = (bf16[1040,128]{1,0:T(8,128)(2,1)S(1)}, bf16[1040,128]{1,0:T(8,128)(2,1)S(1)}, u32[]{:S(2)}, u32[]{:S(2)}) collective-permute-start(bf16[1040,128]{1,0:T(8,128)(2,1)S(1)} %pad_maximum_fusion.refs_0_), channel_id=1, source_target_pairs={{0,16},{16,0},{32,48},{48,32},{1,17},{17,1},{33,49},{49,33},{2,18}... | collective-permute-start | bytes 798728 | tf_op jit(solution)/shard_map/ppermute | solution.py:138
  42.7 5.4 %collective-permute-start.3 = (bf16[32,128,128]{2,1,0:T(8,128)(2,1)S(1)}, bf16[32,128,128]{2,1,0:T(8,128)(2,1)S(1)}, u32[]{:S(2)}, u32[]{:S(2)}) collective-permute-start(bf16[32,128,128]{2,1,0:T(8,128)(2,1)S(1)} %get-tuple-element.16), channel_id=1, source_target_pairs={{0,1},{1,0},{2,3},{3,2},{4,5},{5,4},{6,7},{7,6},{8,9},{9,8},{10,11... | collective-permute-start | bytes 3145736 | tf_op jit(solution)/shard_map/ppermute | solution.py:138
  48.4 38.3 %copy-start = (bf16[512,512]{1,0:T(8,128)(2,1)S(1)}, bf16[512,512]{1,0:T(8,128)(2,1)}, u32[]{:S(2)}) copy-start(bf16[512,512]{1,0:T(8,128)(2,1)} %weight_ref.3) | copy-start | bytes 1572868
  48.4 38.3 %copy-start.3 = (bf16[128,512]{1,0:T(8,128)(2,1)S(1)}, bf16[128,512]{1,0:T(8,128)(2,1)}, u32[]{:S(2)}) copy-start(bf16[128,512]{1,0:T(8,128)(2,1)} %cotangent_ref.1) | copy-start | bytes 393220
  88.4 1.0 copy-start.1
  89.4 37.5 %all-to-all-start.2 = ((bf16[32,128,128]{2,1,0:T(8,128)(2,1)}), bf16[32,128,128]{2,1,0:T(8,128)(2,1)S(1)}, u32[]{:S(2)}, u32[]{:S(2)}) async-start(bf16[32,128,128]{2,1,0:T(8,128)(2,1)} %copy-done.1), calls=%async_computation.2 | async-start | bytes 2097152 | tf_op jit(solution)/shard_map/all_to_all | solution.py:214
  97.3 4.6 %collective-permute-start.4 = (bf16[256,512]{1,0:T(8,128)(2,1)S(1)}, bf16[256,512]{1,0:T(8,128)(2,1)S(1)}, u32[]{:S(2)}, u32[]{:S(2)}) collective-permute-start(bf16[256,512]{1,0:T(8,128)(2,1)S(1)} %get-tuple-element.20), channel_id=1, source_target_pairs={{0,1},{1,0},{2,3},{3,2},{4,5},{5,4},{6,7},{7,6},{8,9},{9,8},{10,11... | collective-permute-start | bytes 786440 | tf_op jit(solution)/shard_map/ppermute | solution.py:138
  102.0 8.4 %collective-permute-start.5 = (bf16[64,512]{1,0:T(8,128)(2,1)S(1)}, bf16[64,512]{1,0:T(8,128)(2,1)S(1)}, u32[]{:S(2)}, u32[]{:S(2)}) collective-permute-start(bf16[64,512]{1,0:T(8,128)(2,1)S(1)} %get-tuple-element.27), channel_id=1, source_target_pairs={{0,64},{64,0},{128,192},{192,128},{1,65},{65,1},{129,193},{193,129... | collective-permute-start | bytes 196616 | tf_op jit(solution)/shard_map/ppermute | solution.py:138
  104.3 6.9 %collective-permute-start.7 = (bf16[64,512]{1,0:T(8,128)(2,1)S(1)}, bf16[64,512]{1,0:T(8,128)(2,1)S(1)}, u32[]{:S(2)}, u32[]{:S(2)}) collective-permute-start(bf16[64,512]{1,0:T(8,128)(2,1)S(1)} %get-tuple-element.28), channel_id=1, source_target_pairs={{0,192},{64,128},{128,64},{192,0},{1,193},{65,129},{129,65},{193,1... | collective-permute-start | bytes 196616 | tf_op jit(solution)/shard_map/ppermute | solution.py:138
  108.1 6.5 %collective-permute-start.6 = (bf16[64,512]{1,0:T(8,128)(2,1)S(1)}, bf16[64,512]{1,0:T(8,128)(2,1)S(1)}, u32[]{:S(2)}, u32[]{:S(2)}) collective-permute-start(bf16[64,512]{1,0:T(8,128)(2,1)S(1)} %get-tuple-element.29), channel_id=1, source_target_pairs={{0,128},{64,192},{128,0},{192,64},{1,129},{65,193},{129,1},{193,65... | collective-permute-start | bytes 196616 | tf_op jit(solution)/shard_map/ppermute | solution.py:138
  114.6 7.2 %collective-permute-start.8 = (bf16[64,512]{1,0:T(8,128)(2,1)S(1)}, bf16[64,512]{1,0:T(8,128)(2,1)S(1)}, u32[]{:S(2)}, u32[]{:S(2)}) collective-permute-start(bf16[64,512]{1,0:T(8,128)(2,1)S(1)} %fusion.2), channel_id=1, source_target_pairs={{0,448},{64,384},{128,320},{192,256},{256,192},{320,128},{384,64},... | collective-permute-start | bytes 196616 | tf_op jit(solution)/shard_map/ppermute | solution.py:138
  121.9 5.0 %collective-permute-start.9 = (bf16[64,512]{1,0:T(8,128)(2,1)S(1)}, bf16[64,512]{1,0:T(8,128)(2,1)S(1)}, u32[]{:S(2)}, u32[]{:S(2)}) collective-permute-start(bf16[64,512]{1,0:T(8,128)(2,1)S(1)} %add_convert_fusion.6), channel_id=1, source_target_pairs={{0,16},{16,0},{32,48},{48,32},{1,17},{17,1},{33,49},{49,33},{2,18}... | collective-permute-start | bytes 196616 | tf_op jit(solution)/shard_map/ppermute | solution.py:138
  127.0 7.9 %collective-permute-start.10 = (bf16[32,128,128]{2,1,0:T(8,128)(2,1)S(1)}, bf16[32,128,128]{2,1,0:T(8,128)(2,1)S(1)}, u32[]{:S(2)}, u32[]{:S(2)}) collective-permute-start(bf16[32,128,128]{2,1,0:T(8,128)(2,1)S(1)} %all-to-all-done.2.mine_ref), channel_id=1, source_target_pairs={{0,1},{1,0},{2,3},{3,2},{4,5},{5,4},{6,7},{7,6},{8,9},{9,8},{10,11... | collective-permute-start | bytes 3145736 | tf_op jit(solution)/shard_map/ppermute | solution.py:138
  137.3 34.9 %all-to-all-start.3 = ((bf16[32,128,128]{2,1,0:T(8,128)(2,1)}), bf16[32,128,128]{2,1,0:T(8,128)(2,1)S(1)}, u32[]{:S(2)}, u32[]{:S(2)}) async-start(bf16[32,128,128]{2,1,0:T(8,128)(2,1)} %backward_tiles.1), calls=%async_computation.3 | async-start | bytes 2097152 | tf_op jit(solution)/shard_map/all_to_all | solution.py:233
  144.8 9.3 %collective-permute-start.13 = (bf16[64,512]{1,0:T(8,128)(2,1)S(1)}, bf16[64,512]{1,0:T(8,128)(2,1)S(1)}, u32[]{:S(2)}, u32[]{:S(2)}) collective-permute-start(bf16[64,512]{1,0:T(8,128)(2,1)S(1)} %add_convert_fusion.5), channel_id=1, source_target_pairs={{0,6},{2,4},{4,2},{6,0},{8,14},{10,12},{12,10},{14,8},{1,7},{3,5},... | collective-permute-start | bytes 196616 | tf_op jit(solution)/shard_map/ppermute | solution.py:138
  149.7 6.9 %collective-permute-start.12 = (bf16[64,512]{1,0:T(8,128)(2,1)S(1)}, bf16[64,512]{1,0:T(8,128)(2,1)S(1)}, u32[]{:S(2)}, u32[]{:S(2)}) collective-permute-start(bf16[64,512]{1,0:T(8,128)(2,1)S(1)} %add_convert_fusion.5), channel_id=1, source_target_pairs={{0,4},{2,6},{4,0},{6,2},{8,12},{10,14},{12,8},{14,10},{1,5},{3,7},... | collective-permute-start | bytes 196616 | tf_op jit(solution)/shard_map/ppermute | solution.py:138
  151.7 6.2 %collective-permute-start.11 = (bf16[64,512]{1,0:T(8,128)(2,1)S(1)}, bf16[64,512]{1,0:T(8,128)(2,1)S(1)}, u32[]{:S(2)}, u32[]{:S(2)}) collective-permute-start(bf16[64,512]{1,0:T(8,128)(2,1)S(1)} %add_convert_fusion.5), channel_id=1, source_target_pairs={{0,2},{2,0},{4,6},{6,4},{8,10},{10,8},{12,14},{14,12},{1,3},{3,1},... | collective-permute-start | bytes 196616 | tf_op jit(solution)/shard_map/ppermute | solution.py:138
  157.9 7.2 %collective-permute-start.14 = (bf16[64,512]{1,0:T(8,128)(2,1)S(1)}, bf16[64,512]{1,0:T(8,128)(2,1)S(1)}, u32[]{:S(2)}, u32[]{:S(2)}) collective-permute-start(bf16[64,512]{1,0:T(8,128)(2,1)S(1)} %add_convert_fusion.4), channel_id=1, source_target_pairs={{0,14},{2,12},{4,10},{6,8},{8,6},{10,4},{12,2},{14,0},{1,15},{3,13... | collective-permute-start | bytes 196616 | tf_op jit(solution)/shard_map/ppermute | solution.py:138
  165.1 7.0 %collective-permute-start.15 = (bf16[64,512]{1,0:T(8,128)(2,1)S(1)}, bf16[64,512]{1,0:T(8,128)(2,1)S(1)}, u32[]{:S(2)}, u32[]{:S(2)}) collective-permute-start(bf16[64,512]{1,0:T(8,128)(2,1)S(1)} %add_convert_fusion.3), channel_id=1, source_target_pairs={{0,48},{16,32},{32,16},{48,0},{1,49},{17,33},{33,17},{49,1},{2,50}... | collective-permute-start | bytes 196616 | tf_op jit(solution)/shard_map/ppermute | solution.py:138
  181.5 7.0 %collective-permute-start.16 = (bf16[4,64,512]{2,1,0:T(8,128)(2,1)S(1)}, bf16[4,64,512]{2,1,0:T(8,128)(2,1)S(1)}, u32[]{:S(2)}, u32[]{:S(2)}) collective-permute-start(bf16[4,64,512]{2,1,0:T(8,128)(2,1)S(1)} %all_to_all.26.mine_ref), channel_id=1, source_target_pairs={{0,1},{1,0},{2,3},{3,2},{4,5},{5,4},{6,7},{7,6},{8,9},{9,8},{10,11... | collective-permute-start | bytes 786440 | tf_op jit(solution)/shard_map/ppermute | solution.py:138

commit v15 on v14

--- a/solution.py
+++ b/solution.py
@@ -1,3 +1,4 @@
+import functools
 import math
 
 import jax
@@ -34,11 +35,20 @@
     return pl.BlockSpec(memory_space=pltpu.SMEM)
 
 
-def spread(features_ref, out_ref):
-    for chunk in range(X):
-        piece = features_ref[:, chunk * CHUNK : (chunk + 1) * CHUNK]
-        for y in range(Y):
-            out_ref[y * X + chunk] = piece
+def spread(places, in_ref, out_ref):
+    for place, chunk in enumerate(places):
+        out_ref[place] = in_ref[:, chunk * CHUNK : (chunk + 1) * CHUNK]
+
+
+def spread_chunks(array, places, name):
+    return pl.pallas_call(
+        functools.partial(spread, places),
+        in_specs=[vmem()],
+        out_specs=vmem(),
+        out_shape=jax.ShapeDtypeStruct((len(places), TILE, CHUNK), BF16),
+        compiler_params=params(),
+        name=name,
+    )(array)
 
 
 def forward_tiles(place_ref, index_ref, panel_ref, *refs):
@@ -76,10 +86,7 @@
     sig = jax.nn.sigmoid(aggregated)
     act_ref[...] = (aggregated * sig).astype(BF16)
     grad = (cotangent_ref[...].astype(F32) * sig * (1.0 + aggregated * (1.0 - sig))).astype(BF16)
-    for chunk in range(X):
-        piece = grad[:, chunk * CHUNK : (chunk + 1) * CHUNK]
-        for z in range(Z):
-            grad_ref[chunk * Z + z] = piece
+    grad_ref[...] = grad
     weight_part = lax.dot_general(
         high, grad, (((0,), (0,)), ((), ())), preferred_element_type=F32
     ).astype(BF16)
@@ -164,14 +171,7 @@
     flip = lax.axis_index("y_high") * (Y_LOW - 1)
     place = jnp.stack([lax.axis_index("core"), lax.axis_index("x"), flip]).astype(jnp.int32)
 
-    chunks = pl.pallas_call(
-        spread,
-        in_specs=[vmem()],
-        out_specs=vmem(),
-        out_shape=jax.ShapeDtypeStruct((COL_TILES, TILE, CHUNK), BF16),
-        compiler_params=params(),
-        name="spread",
-    )(features)
+    chunks = spread_chunks(features, [at % X for at in range(COL_TILES)], "spread_features")
     panel = lax.all_to_all(chunks, ROW, 0, 0, tiled=True)
 
     index = jnp.concatenate(
@@ -203,7 +203,7 @@
         out_specs=[vmem()] * 4,
         out_shape=[
             jax.ShapeDtypeStruct((TILE, WIDTH), BF16),
-            jax.ShapeDtypeStruct((X * Z, TILE, CHUNK), BF16),
+            jax.ShapeDtypeStruct((TILE, WIDTH), BF16),
             jax.ShapeDtypeStruct((half, WIDTH), BF16),
             jax.ShapeDtypeStruct((half, WIDTH), BF16),
         ],
@@ -211,9 +211,10 @@
         name="middle",
     )(place, parts, weight, cotangent)
 
+    grad = spread_chunks(grad, [at // Z for at in range(X * Z)], "spread_grad")
+    piece = weight_keep.astype(F32) + exchange(weight_send, "core", 1).astype(F32)
+    grad, piece = lax.optimization_barrier((grad, piece.astype(BF16)))
     grad_mine = lax.all_to_all(grad, ("x", "z"), 0, 0, tiled=True)
-    piece = weight_keep.astype(F32) + exchange(weight_send, "core", 1).astype(F32)
-    piece = piece.astype(BF16)
     piece = scatter(piece, "y_low", flip)
     piece = double(piece, ("y_high", "y_low"), Y - 1)
     piece = double(piece, "x", 1)

time: 191 us -> 190 us (level)
  starting transfers between devices: 85.8 us -> 83.8 us
    all_to_all x1, starting transfers between devices: 7.94 us -> 4.84 us  [body(): grad_mine = lax.all_to_all(grad, ('x', 'z'), 0, 0, tiled=True)]
  transfers between devices with their start and end apart: 20 -> 20, of which waited for: 14 -> 13; matrix products, arithmetic and copies ran while one was open for 0% -> 0% of each run, Pallas kernels for 1% -> 1%
where the time goes in v15:
time: 190 us; the launch traced here: 189 us
  starting transfers between devices  83.8 us (44%)
  blocking collectives  47.6 us (25%)
  waiting for transfers between devices  44.4 us (23%)
  Pallas kernels  10.3 us (5%)
    ppermute x17, starting transfers between devices, exchange(): return lax.ppermute(array, axis, [(i, i ^ distance) for i in range(size)])  61.3 us
    ppermute x17, waiting for transfers between devices, exchange(): return lax.ppermute(array, axis, [(i, i ^ distance) for i in range(size)])  44.4 us
    all_to_all x1, blocking collectives, body(): parts = lax.all_to_all(term, ('x', 'z'), 0, 0, tiled=True)  38.3 us
    all_to_all x1, starting transfers between devices, body(): panel = lax.all_to_all(chunks, ROW, 0, 0, tiled=True)  10.6 us
    all_to_all x1, blocking collectives, body(): whole = lax.all_to_all(piece, 'y_low', 0, 0, tiled=True)  9.3 us
    all_to_all x1, starting transfers between devices, body(): back = lax.all_to_all(back, ROW, 0, 0, tiled=True)  7.03 us
    all_to_all x1, starting transfers between devices, body(): grad_mine = lax.all_to_all(grad, ('x', 'z'), 0, 0, tiled=True)  4.84 us
  transfers between devices with their start and end apart: 20, of which 13 were waited for; matrix products, arithmetic and copies ran while one was open for 0% of the time, Pallas kernels for 1%

profile of v15, /device:TPU:1, one launch (start us, length us, event | category | flops | bytes accessed | tf_op | source)
XLA Modules:
  0.0 189.0 jit_solution(11553813289215444210)
XLA Ops:
  0.6 0.0 copy-start.1
  0.6 0.9 copy-done.1
  1.5 1.1 spread_features.1
  2.7 0.0 copy-start.4
  2.7 10.6 %all-to-all-start = ((bf16[32,128,128]{2,1,0:T(8,128)(2,1)}), bf16[32,128,128]{2,1,0:T(8,128)(2,1)S(1)}, u32[]{:S(2)}, u32[]{:S(2)}) async-start(bf16[32,128,128]{2,1,0:T(8,128)(2,1)} %spread_features.1), calls=%async_computation | async-start | bytes 2097152 | tf_op jit(solution)/shard_map/all_to_all | solution.py:175
  13.3 0.0 copy-done.7
  13.3 0.0 copy-done.5
  13.3 0.0 copy-done.6
  13.4 0.1 fusion.11
  13.5 4.3 %collective-permute-start.2 = (bf16[1040,128]{1,0:T(8,128)(2,1)S(1)}, bf16[1040,128]{1,0:T(8,128)(2,1)S(1)}, u32[]{:S(2)}, u32[]{:S(2)}) collective-permute-start(bf16[1040,128]{1,0:T(8,128)(2,1)S(1)} %pad_maximum_fusion.refs_0_), channel_id=1, source_target_pairs={{0,48},{16,32},{32,16},{48,0},{1,49},{17,33},{33,17},{49,1},{2,50}... | collective-permute-start | bytes 798728 | tf_op jit(solution)/shard_map/ppermute | solution.py:145
  17.8 2.5 %collective-permute-start.1 = (bf16[1040,128]{1,0:T(8,128)(2,1)S(1)}, bf16[1040,128]{1,0:T(8,128)(2,1)S(1)}, u32[]{:S(2)}, u32[]{:S(2)}) collective-permute-start(bf16[1040,128]{1,0:T(8,128)(2,1)S(1)} %pad_maximum_fusion.refs_0_), channel_id=1, source_target_pairs={{0,32},{16,48},{32,0},{48,16},{1,33},{17,49},{33,1},{49,17},{2,34}... | collective-permute-start | bytes 798728 | tf_op jit(solution)/shard_map/ppermute | solution.py:145
  20.3 2.1 %collective-permute-start = (bf16[1040,128]{1,0:T(8,128)(2,1)S(1)}, bf16[1040,128]{1,0:T(8,128)(2,1)S(1)}, u32[]{:S(2)}, u32[]{:S(2)}) collective-permute-start(bf16[1040,128]{1,0:T(8,128)(2,1)S(1)} %pad_maximum_fusion.refs_0_), channel_id=1, source_target_pairs={{0,16},{16,0},{32,48},{48,32},{1,17},{17,1},{33,49},{49,33},{2,18}... | collective-permute-start | bytes 798728 | tf_op jit(solution)/shard_map/ppermute | solution.py:145
  22.5 0.1 broadcast_in_dim.4
  22.6 0.1 min.14
  22.7 0.1 pad_add_fusion.place_ref.core_ref
  22.7 14.6 %collective-permute-done.2.refs_3_ = bf16[1040,128]{1,0:T(8,128)(2,1)S(1)} collective-permute-done((bf16[1040,128]{1,0:T(8,128)(2,1)S(1)}, bf16[1040,128]{1,0:T(8,128)(2,1)S(1)}, u32[]{:S(2)}, u32[]{:S(2)}) %collective-permute-start.2) | collective-permute-done | bytes 266272 | tf_op jit(solution)/shard_map/ppermute | solution.py:145
  37.4 0.0 collective-permute-done.1.refs_2_
  37.4 3.7 %collective-permute-done.refs_1_ = bf16[1040,128]{1,0:T(8,128)(2,1)S(1)} collective-permute-done((bf16[1040,128]{1,0:T(8,128)(2,1)S(1)}, bf16[1040,128]{1,0:T(8,128)(2,1)S(1)}, u32[]{:S(2)}, u32[]{:S(2)}) %collective-permute-start) | collective-permute-done | bytes 266272 | tf_op jit(solution)/shard_map/ppermute | solution.py:145
  41.1 0.1 maximum_minimum_fusion.index_ref
  41.2 0.0 all-to-all-done.panel_ref
  41.2 1.5 forward_tiles.1
  42.7 3.1 %collective-permute-start.3 = (bf16[32,128,128]{2,1,0:T(8,128)(2,1)S(1)}, bf16[32,128,128]{2,1,0:T(8,128)(2,1)S(1)}, u32[]{:S(2)}, u32[]{:S(2)}) collective-permute-start(bf16[32,128,128]{2,1,0:T(8,128)(2,1)S(1)} %get-tuple-element.18), channel_id=1, source_target_pairs={{0,1},{1,0},{2,3},{3,2},{4,5},{5,4},{6,7},{7,6},{8,9},{9,8},{10,11... | collective-permute-start | bytes 3145736 | tf_op jit(solution)/shard_map/ppermute | solution.py:145
  45.8 2.3 %collective-permute-done.3 = bf16[32,128,128]{2,1,0:T(8,128)(2,1)S(1)} collective-permute-done((bf16[32,128,128]{2,1,0:T(8,128)(2,1)S(1)}, bf16[32,128,128]{2,1,0:T(8,128)(2,1)S(1)}, u32[]{:S(2)}, u32[]{:S(2)}) %collective-permute-start.3) | collective-permute-done | bytes 1048608 | tf_op jit(solution)/shard_map/ppermute | solution.py:145
  48.1 0.4 add_convert_fusion
  48.4 0.0 copy-start
  48.5 0.0 copy-start.2
  48.5 38.3 %all_to_all.25.parts_ref = bf16[32,128,128]{2,1,0:T(8,128)(2,1)S(1)} all-to-all(bf16[32,128,128]{2,1,0:T(8,128)(2,1)S(1)} %add_convert_fusion), channel_id=1, replica_groups=mesh['y_high'=2,'y_low'=4,'x'=4,'z'=8,'core'=2] {'x','z'}, dimensions={0} | all-to-all | bytes 2097152 | tf_op jit(solution)/shard_map/all_to_all | solution.py:197
  86.7 1.6 middle.1
  88.4 6.2 %collective-permute-start.4 = (bf16[256,512]{1,0:T(8,128)(2,1)S(1)}, bf16[256,512]{1,0:T(8,128)(2,1)S(1)}, u32[]{:S(2)}, u32[]{:S(2)}) collective-permute-start(bf16[256,512]{1,0:T(8,128)(2,1)S(1)} %get-tuple-element.22), channel_id=1, source_target_pairs={{0,1},{1,0},{2,3},{3,2},{4,5},{5,4},{6,7},{7,6},{8,9},{9,8},{10,11... | collective-permute-start | bytes 786440 | tf_op jit(solution)/shard_map/ppermute | solution.py:145
  94.6 1.1 spread_grad.1
  95.7 0.0 collective-permute-done.4
  95.8 0.1 add_convert_fusion.1
  95.8 4.8 %all-to-all-start.2 = ((bf16[32,128,128]{2,1,0:T(8,128)(2,1)}), bf16[32,128,128]{2,1,0:T(8,128)(2,1)S(1)}, u32[]{:S(2)}, u32[]{:S(2)}) async-start(bf16[32,128,128]{2,1,0:T(8,128)(2,1)} %spread_grad.1), calls=%async_computation.2 | async-start | bytes 2097152 | tf_op jit(solution)/shard_map/all_to_all | solution.py:217
  100.7 2.2 %collective-permute-start.5 = (bf16[64,512]{1,0:T(8,128)(2,1)S(1)}, bf16[64,512]{1,0:T(8,128)(2,1)S(1)}, u32[]{:S(2)}, u32[]{:S(2)}) collective-permute-start(bf16[64,512]{1,0:T(8,128)(2,1)S(1)} %get-tuple-element.31), channel_id=1, source_target_pairs={{0,64},{64,0},{128,192},{192,128},{1,65},{65,1},{129,193},{193,129... | collective-permute-start | bytes 196616 | tf_op jit(solution)/shard_map/ppermute | solution.py:145
  103.0 3.8 %collective-permute-start.7 = (bf16[64,512]{1,0:T(8,128)(2,1)S(1)}, bf16[64,512]{1,0:T(8,128)(2,1)S(1)}, u32[]{:S(2)}, u32[]{:S(2)}) collective-permute-start(bf16[64,512]{1,0:T(8,128)(2,1)S(1)} %get-tuple-element.32), channel_id=1, source_target_pairs={{0,192},{64,128},{128,64},{192,0},{1,193},{65,129},{129,65},{193,1... | collective-permute-start | bytes 196616 | tf_op jit(solution)/shard_map/ppermute | solution.py:145
  106.8 2.3 %collective-permute-start.6 = (bf16[64,512]{1,0:T(8,128)(2,1)S(1)}, bf16[64,512]{1,0:T(8,128)(2,1)S(1)}, u32[]{:S(2)}, u32[]{:S(2)}) collective-permute-start(bf16[64,512]{1,0:T(8,128)(2,1)S(1)} %get-tuple-element.33), channel_id=1, source_target_pairs={{0,128},{64,192},{128,0},{192,64},{1,129},{65,193},{129,1},{193,65... | collective-permute-start | bytes 196616 | tf_op jit(solution)/shard_map/ppermute | solution.py:145
  109.2 0.0 collective-permute-done.5
  109.2 0.6 collective-permute-done.7
  109.8 3.5 %collective-permute-done.6 = bf16[64,512]{1,0:T(8,128)(2,1)S(1)} collective-permute-done((bf16[64,512]{1,0:T(8,128)(2,1)S(1)}, bf16[64,512]{1,0:T(8,128)(2,1)S(1)}, u32[]{:S(2)}, u32[]{:S(2)}) %collective-permute-start.6) | collective-permute-done | bytes 65568 | tf_op jit(solution)/shard_map/ppermute | solution.py:145
  113.4 3.8 %collective-permute-start.8 = (bf16[64,512]{1,0:T(8,128)(2,1)S(1)}, bf16[64,512]{1,0:T(8,128)(2,1)S(1)}, u32[]{:S(2)}, u32[]{:S(2)}) collective-permute-start(bf16[64,512]{1,0:T(8,128)(2,1)S(1)} %fusion.2), channel_id=1, source_target_pairs={{0,448},{64,384},{128,320},{192,256},{256,192},{320,128},{384,64},... | collective-permute-start | bytes 196616 | tf_op jit(solution)/shard_map/ppermute | solution.py:145
  117.2 3.4 %collective-permute-done.8 = bf16[64,512]{1,0:T(8,128)(2,1)S(1)} collective-permute-done((bf16[64,512]{1,0:T(8,128)(2,1)S(1)}, bf16[64,512]{1,0:T(8,128)(2,1)S(1)}, u32[]{:S(2)}, u32[]{:S(2)}) %collective-permute-start.8) | collective-permute-done | bytes 65568 | tf_op jit(solution)/shard_map/ppermute | solution.py:145
  120.6 2.9 %collective-permute-start.9 = (bf16[64,512]{1,0:T(8,128)(2,1)S(1)}, bf16[64,512]{1,0:T(8,128)(2,1)S(1)}, u32[]{:S(2)}, u32[]{:S(2)}) collective-permute-start(bf16[64,512]{1,0:T(8,128)(2,1)S(1)} %add_convert_fusion.6), channel_id=1, source_target_pairs={{0,16},{16,0},{32,48},{48,32},{1,17},{17,1},{33,49},{49,33},{2,18}... | collective-permute-start | bytes 196616 | tf_op jit(solution)/shard_map/ppermute | solution.py:145
  123.5 3.0 %collective-permute-done.9 = bf16[64,512]{1,0:T(8,128)(2,1)S(1)} collective-permute-done((bf16[64,512]{1,0:T(8,128)(2,1)S(1)}, bf16[64,512]{1,0:T(8,128)(2,1)S(1)}, u32[]{:S(2)}, u32[]{:S(2)}) %collective-permute-start.9) | collective-permute-done | bytes 65568 | tf_op jit(solution)/shard_map/ppermute | solution.py:145
  126.5 0.0 all-to-all-done.2.mine_ref
  126.5 5.6 %collective-permute-start.10 = (bf16[32,128,128]{2,1,0:T(8,128)(2,1)S(1)}, bf16[32,128,128]{2,1,0:T(8,128)(2,1)S(1)}, u32[]{:S(2)}, u32[]{:S(2)}) collective-permute-start(bf16[32,128,128]{2,1,0:T(8,128)(2,1)S(1)} %all-to-all-done.2.mine_ref), channel_id=1, source_target_pairs={{0,1},{1,0},{2,3},{3,2},{4,5},{5,4},{6,7},{7,6},{8,9},{9,8},{10,11... | collective-permute-start | bytes 3145736 | tf_op jit(solution)/shard_map/ppermute | solution.py:145
  132.2 2.3 %collective-permute-done.10.other_ref = bf16[32,128,128]{2,1,0:T(8,128)(2,1)S(1)} collective-permute-done((bf16[32,128,128]{2,1,0:T(8,128)(2,1)S(1)}, bf16[32,128,128]{2,1,0:T(8,128)(2,1)S(1)}, u32[]{:S(2)}, u32[]{:S(2)}) %collective-permute-start.10) | collective-permute-done | bytes 1048608 | tf_op jit(solution)/shard_map/ppermute | solution.py:145
  134.4 2.4 %backward_tiles.1 = bf16[32,128,128]{2,1,0:T(8,128)(2,1)} custom-call(s32[3]{0:T(128)S(1)} %pad_add_fusion.place_ref.core_ref, s32[4,24]{1,0:T(4,128)S(1)} %maximum_minimum_fusion.index_ref, bf16[32,128,128]{2,1,0:T(8,128)(2,1)S(1)} %all-to-all-done.2.mine_ref, bf16[32,128,128]{2,1,0:T(8,128)(2,1)S(1)} %collective-permute-done.10.other_ref, ...), custom_call_target="tpu_custom_call" | custom-call | tf_op jit(solution)/shard_map/backward_tiles/pallas_call | solution.py:224
  136.8 7.0 %all-to-all-start.3 = ((bf16[32,128,128]{2,1,0:T(8,128)(2,1)}), bf16[32,128,128]{2,1,0:T(8,128)(2,1)S(1)}, u32[]{:S(2)}, u32[]{:S(2)}) async-start(bf16[32,128,128]{2,1,0:T(8,128)(2,1)} %backward_tiles.1), calls=%async_computation.3 | async-start | bytes 2097152 | tf_op jit(solution)/shard_map/all_to_all | solution.py:234
  143.8 4.9 %collective-permute-start.13 = (bf16[64,512]{1,0:T(8,128)(2,1)S(1)}, bf16[64,512]{1,0:T(8,128)(2,1)S(1)}, u32[]{:S(2)}, u32[]{:S(2)}) collective-permute-start(bf16[64,512]{1,0:T(8,128)(2,1)S(1)} %add_convert_fusion.5), channel_id=1, source_target_pairs={{0,6},{2,4},{4,2},{6,0},{8,14},{10,12},{12,10},{14,8},{1,7},{3,5},... | collective-permute-start | bytes 196616 | tf_op jit(solution)/shard_map/ppermute | solution.py:145
  148.7 1.9 %collective-permute-start.12 = (bf16[64,512]{1,0:T(8,128)(2,1)S(1)}, bf16[64,512]{1,0:T(8,128)(2,1)S(1)}, u32[]{:S(2)}, u32[]{:S(2)}) collective-permute-start(bf16[64,512]{1,0:T(8,128)(2,1)S(1)} %add_convert_fusion.5), channel_id=1, source_target_pairs={{0,4},{2,6},{4,0},{6,2},{8,12},{10,14},{12,8},{14,10},{1,5},{3,7},... | collective-permute-start | bytes 196616 | tf_op jit(solution)/shard_map/ppermute | solution.py:145
  150.7 2.5 %collective-permute-start.11 = (bf16[64,512]{1,0:T(8,128)(2,1)S(1)}, bf16[64,512]{1,0:T(8,128)(2,1)S(1)}, u32[]{:S(2)}, u32[]{:S(2)}) collective-permute-start(bf16[64,512]{1,0:T(8,128)(2,1)S(1)} %add_convert_fusion.5), channel_id=1, source_target_pairs={{0,2},{2,0},{4,6},{6,4},{8,10},{10,8},{12,14},{14,12},{1,3},{3,1},... | collective-permute-start | bytes 196616 | tf_op jit(solution)/shard_map/ppermute | solution.py:145
  153.1 0.0 collective-permute-done.13
  153.1 2.5 %collective-permute-done.12 = bf16[64,512]{1,0:T(8,128)(2,1)S(1)} collective-permute-done((bf16[64,512]{1,0:T(8,128)(2,1)S(1)}, bf16[64,512]{1,0:T(8,128)(2,1)S(1)}, u32[]{:S(2)}, u32[]{:S(2)}) %collective-permute-start.12) | collective-permute-done | bytes 65568 | tf_op jit(solution)/shard_map/ppermute | solution.py:145
  155.6 1.2 collective-permute-done.11
  156.9 4.3 %collective-permute-start.14 = (bf16[64,512]{1,0:T(8,128)(2,1)S(1)}, bf16[64,512]{1,0:T(8,128)(2,1)S(1)}, u32[]{:S(2)}, u32[]{:S(2)}) collective-permute-start(bf16[64,512]{1,0:T(8,128)(2,1)S(1)} %add_convert_fusion.4), channel_id=1, source_target_pairs={{0,14},{2,12},{4,10},{6,8},{8,6},{10,4},{12,2},{14,0},{1,15},{3,13... | collective-permute-start | bytes 196616 | tf_op jit(solution)/shard_map/ppermute | solution.py:145
  161.2 2.9 %collective-permute-done.14 = bf16[64,512]{1,0:T(8,128)(2,1)S(1)} collective-permute-done((bf16[64,512]{1,0:T(8,128)(2,1)S(1)}, bf16[64,512]{1,0:T(8,128)(2,1)S(1)}, u32[]{:S(2)}, u32[]{:S(2)}) %collective-permute-start.14) | collective-permute-done | bytes 65568 | tf_op jit(solution)/shard_map/ppermute | solution.py:145
  164.1 2.8 %collective-permute-start.15 = (bf16[64,512]{1,0:T(8,128)(2,1)S(1)}, bf16[64,512]{1,0:T(8,128)(2,1)S(1)}, u32[]{:S(2)}, u32[]{:S(2)}) collective-permute-start(bf16[64,512]{1,0:T(8,128)(2,1)S(1)} %add_convert_fusion.3), channel_id=1, source_target_pairs={{0,48},{16,32},{32,16},{48,0},{1,49},{17,33},{33,17},{49,1},{2,50}... | collective-permute-start | bytes 196616 | tf_op jit(solution)/shard_map/ppermute | solution.py:145
  166.9 4.2 %collective-permute-done.15 = bf16[64,512]{1,0:T(8,128)(2,1)S(1)} collective-permute-done((bf16[64,512]{1,0:T(8,128)(2,1)S(1)}, bf16[64,512]{1,0:T(8,128)(2,1)S(1)}, u32[]{:S(2)}, u32[]{:S(2)}) %collective-permute-start.15) | collective-permute-done | bytes 65568 | tf_op jit(solution)/shard_map/ppermute | solution.py:145
  171.2 0.0 all-to-all-done.3.parts_ref
  171.2 9.3 %all_to_all.26.mine_ref = bf16[4,64,512]{2,1,0:T(8,128)(2,1)S(1)} all-to-all(bf16[4,64,512]{2,1,0:T(8,128)(2,1)S(1)} %broadcast_in_dim.5), channel_id=1, replica_groups=mesh['y_high'=2,'y_low'=4,'x'=4,'z'=8,'core'=2] {'y_low'}, dimensions={0} | all-to-all | bytes 524288 | tf_op jit(solution)/shard_map/all_to_all | solution.py:251
  180.5 5.8 %collective-permute-start.16 = (bf16[4,64,512]{2,1,0:T(8,128)(2,1)S(1)}, bf16[4,64,512]{2,1,0:T(8,128)(2,1)S(1)}, u32[]{:S(2)}, u32[]{:S(2)}) collective-permute-start(bf16[4,64,512]{2,1,0:T(8,128)(2,1)S(1)} %all_to_all.26.mine_ref), channel_id=1, source_target_pairs={{0,1},{1,0},{2,3},{3,2},{4,5},{5,4},{6,7},{7,6},{8,9},{9,8},{10,11... | collective-permute-start | bytes 786440 | tf_op jit(solution)/shard_map/ppermute | solution.py:145
  186.3 1.0 last.1
  187.3 0.2 collective-permute-done.16.other_ref
  187.5 1.6 place_rows.1
  (22 shorter events, 0.2 us)
Async XLA Ops:
  0.6 0.9 copy-start.1
  2.6 10.7 %copy-start.7 = (s32[1,1,8]{2,1,0:T(1,128)S(1)}, s32[1,1,8]{2,1,0:T(1,128)}, u32[]{:S(2)}) copy-start(s32[1,1,8]{2,1,0:T(1,128)} %param.12) | copy-start | bytes 100
  2.6 10.7 %copy-start.5 = (s32[1,1,8]{2,1,0:T(1,128)S(1)}, s32[1,1,8]{2,1,0:T(1,128)}, u32[]{:S(2)}) copy-start(s32[1,1,8]{2,1,0:T(1,128)} %param.14) | copy-start | bytes 100
  2.6 10.7 %copy-start.6 = (s32[1,1,8]{2,1,0:T(1,128)S(1)}, s32[1,1,8]{2,1,0:T(1,128)}, u32[]{:S(2)}) copy-start(s32[1,1,8]{2,1,0:T(1,128)} %param.13) | copy-start | bytes 100
  2.6 10.8 %copy-start.3 = (bf16[1,1,8,128,128]{4,3,2,1,0:T(8,128)(2,1)S(1)}, bf16[1,1,8,128,128]{4,3,2,1,0:T(8,128)(2,1)}, u32[]{:S(2)}) copy-start(bf16[1,1,8,128,128]{4,3,2,1,0:T(8,128)(2,1)} %param.11) | copy-start | bytes 786436
  2.7 19.8 %copy-start.4 = (s32[3]{0:T(128)S(1)}, s32[3]{0:T(128)}, u32[]{:S(2)}) copy-start(s32[3]{0:T(128)} %constant.41.clone) | copy-start | bytes 40
  2.7 38.5 %all-to-all-start = ((bf16[32,128,128]{2,1,0:T(8,128)(2,1)}), bf16[32,128,128]{2,1,0:T(8,128)(2,1)S(1)}, u32[]{:S(2)}, u32[]{:S(2)}) async-start(bf16[32,128,128]{2,1,0:T(8,128)(2,1)} %spread_features.1), calls=%async_computation | async-start | bytes 2097152 | tf_op jit(solution)/shard_map/all_to_all | solution.py:175
  13.5 23.9 %collective-permute-start.2 = (bf16[1040,128]{1,0:T(8,128)(2,1)S(1)}, bf16[1040,128]{1,0:T(8,128)(2,1)S(1)}, u32[]{:S(2)}, u32[]{:S(2)}) collective-permute-start(bf16[1040,128]{1,0:T(8,128)(2,1)S(1)} %pad_maximum_fusion.refs_0_), channel_id=1, source_target_pairs={{0,48},{16,32},{32,16},{48,0},{1,49},{17,33},{33,17},{49,1},{2,50}... | collective-permute-start | bytes 798728 | tf_op jit(solution)/shard_map/ppermute | solution.py:145
  17.8 19.5 %collective-permute-start.1 = (bf16[1040,128]{1,0:T(8,128)(2,1)S(1)}, bf16[1040,128]{1,0:T(8,128)(2,1)S(1)}, u32[]{:S(2)}, u32[]{:S(2)}) collective-permute-start(bf16[1040,128]{1,0:T(8,128)(2,1)S(1)} %pad_maximum_fusion.refs_0_), channel_id=1, source_target_pairs={{0,32},{16,48},{32,0},{48,16},{1,33},{17,49},{33,1},{49,17},{2,34}... | collective-permute-start | bytes 798728 | tf_op jit(solution)/shard_map/ppermute | solution.py:145
  20.3 20.7 %collective-permute-start = (bf16[1040,128]{1,0:T(8,128)(2,1)S(1)}, bf16[1040,128]{1,0:T(8,128)(2,1)S(1)}, u32[]{:S(2)}, u32[]{:S(2)}) collective-permute-start(bf16[1040,128]{1,0:T(8,128)(2,1)S(1)} %pad_maximum_fusion.refs_0_), channel_id=1, source_target_pairs={{0,16},{16,0},{32,48},{48,32},{1,17},{17,1},{33,49},{49,33},{2,18}... | collective-permute-start | bytes 798728 | tf_op jit(solution)/shard_map/ppermute | solution.py:145
  42.7 5.4 %collective-permute-start.3 = (bf16[32,128,128]{2,1,0:T(8,128)(2,1)S(1)}, bf16[32,128,128]{2,1,0:T(8,128)(2,1)S(1)}, u32[]{:S(2)}, u32[]{:S(2)}) collective-permute-start(bf16[32,128,128]{2,1,0:T(8,128)(2,1)S(1)} %get-tuple-element.18), channel_id=1, source_target_pairs={{0,1},{1,0},{2,3},{3,2},{4,5},{5,4},{6,7},{7,6},{8,9},{9,8},{10,11... | collective-permute-start | bytes 3145736 | tf_op jit(solution)/shard_map/ppermute | solution.py:145
  48.4 38.3 %copy-start = (bf16[512,512]{1,0:T(8,128)(2,1)S(1)}, bf16[512,512]{1,0:T(8,128)(2,1)}, u32[]{:S(2)}) copy-start(bf16[512,512]{1,0:T(8,128)(2,1)} %weight_ref.3) | copy-start | bytes 1572868
  48.5 38.3 %copy-start.2 = (bf16[128,512]{1,0:T(8,128)(2,1)S(1)}, bf16[128,512]{1,0:T(8,128)(2,1)}, u32[]{:S(2)}) copy-start(bf16[128,512]{1,0:T(8,128)(2,1)} %cotangent_ref.1) | copy-start | bytes 393220
  88.4 7.4 %collective-permute-start.4 = (bf16[256,512]{1,0:T(8,128)(2,1)S(1)}, bf16[256,512]{1,0:T(8,128)(2,1)S(1)}, u32[]{:S(2)}, u32[]{:S(2)}) collective-permute-start(bf16[256,512]{1,0:T(8,128)(2,1)S(1)} %get-tuple-element.22), channel_id=1, source_target_pairs={{0,1},{1,0},{2,3},{3,2},{4,5},{5,4},{6,7},{7,6},{8,9},{9,8},{10,11... | collective-permute-start | bytes 786440 | tf_op jit(solution)/shard_map/ppermute | solution.py:145
  95.8 30.7 %all-to-all-start.2 = ((bf16[32,128,128]{2,1,0:T(8,128)(2,1)}), bf16[32,128,128]{2,1,0:T(8,128)(2,1)S(1)}, u32[]{:S(2)}, u32[]{:S(2)}) async-start(bf16[32,128,128]{2,1,0:T(8,128)(2,1)} %spread_grad.1), calls=%async_computation.2 | async-start | bytes 2097152 | tf_op jit(solution)/shard_map/all_to_all | solution.py:217
  100.7 8.4 %collective-permute-start.5 = (bf16[64,512]{1,0:T(8,128)(2,1)S(1)}, bf16[64,512]{1,0:T(8,128)(2,1)S(1)}, u32[]{:S(2)}, u32[]{:S(2)}) collective-permute-start(bf16[64,512]{1,0:T(8,128)(2,1)S(1)} %get-tuple-element.31), channel_id=1, source_target_pairs={{0,64},{64,0},{128,192},{192,128},{1,65},{65,1},{129,193},{193,129... | collective-permute-start | bytes 196616 | tf_op jit(solution)/shard_map/ppermute | solution.py:145
  103.0 6.8 %collective-permute-start.7 = (bf16[64,512]{1,0:T(8,128)(2,1)S(1)}, bf16[64,512]{1,0:T(8,128)(2,1)S(1)}, u32[]{:S(2)}, u32[]{:S(2)}) collective-permute-start(bf16[64,512]{1,0:T(8,128)(2,1)S(1)} %get-tuple-element.32), channel_id=1, source_target_pairs={{0,192},{64,128},{128,64},{192,0},{1,193},{65,129},{129,65},{193,1... | collective-permute-start | bytes 196616 | tf_op jit(solution)/shard_map/ppermute | solution.py:145
  106.8 6.5 %collective-permute-start.6 = (bf16[64,512]{1,0:T(8,128)(2,1)S(1)}, bf16[64,512]{1,0:T(8,128)(2,1)S(1)}, u32[]{:S(2)}, u32[]{:S(2)}) collective-permute-start(bf16[64,512]{1,0:T(8,128)(2,1)S(1)} %get-tuple-element.33), channel_id=1, source_target_pairs={{0,128},{64,192},{128,0},{192,64},{1,129},{65,193},{129,1},{193,65... | collective-permute-start | bytes 196616 | tf_op jit(solution)/shard_map/ppermute | solution.py:145
  113.4 7.2 %collective-permute-start.8 = (bf16[64,512]{1,0:T(8,128)(2,1)S(1)}, bf16[64,512]{1,0:T(8,128)(2,1)S(1)}, u32[]{:S(2)}, u32[]{:S(2)}) collective-permute-start(bf16[64,512]{1,0:T(8,128)(2,1)S(1)} %fusion.2), channel_id=1, source_target_pairs={{0,448},{64,384},{128,320},{192,256},{256,192},{320,128},{384,64},... | collective-permute-start | bytes 196616 | tf_op jit(solution)/shard_map/ppermute | solution.py:145
  120.6 5.9 %collective-permute-start.9 = (bf16[64,512]{1,0:T(8,128)(2,1)S(1)}, bf16[64,512]{1,0:T(8,128)(2,1)S(1)}, u32[]{:S(2)}, u32[]{:S(2)}) collective-permute-start(bf16[64,512]{1,0:T(8,128)(2,1)S(1)} %add_convert_fusion.6), channel_id=1, source_target_pairs={{0,16},{16,0},{32,48},{48,32},{1,17},{17,1},{33,49},{49,33},{2,18}... | collective-permute-start | bytes 196616 | tf_op jit(solution)/shard_map/ppermute | solution.py:145
  126.5 7.9 %collective-permute-start.10 = (bf16[32,128,128]{2,1,0:T(8,128)(2,1)S(1)}, bf16[32,128,128]{2,1,0:T(8,128)(2,1)S(1)}, u32[]{:S(2)}, u32[]{:S(2)}) collective-permute-start(bf16[32,128,128]{2,1,0:T(8,128)(2,1)S(1)} %all-to-all-done.2.mine_ref), channel_id=1, source_target_pairs={{0,1},{1,0},{2,3},{3,2},{4,5},{5,4},{6,7},{7,6},{8,9},{9,8},{10,11... | collective-permute-start | bytes 3145736 | tf_op jit(solution)/shard_map/ppermute | solution.py:145
  136.8 34.4 %all-to-all-start.3 = ((bf16[32,128,128]{2,1,0:T(8,128)(2,1)}), bf16[32,128,128]{2,1,0:T(8,128)(2,1)S(1)}, u32[]{:S(2)}, u32[]{:S(2)}) async-start(bf16[32,128,128]{2,1,0:T(8,128)(2,1)} %backward_tiles.1), calls=%async_computation.3 | async-start | bytes 2097152 | tf_op jit(solution)/shard_map/all_to_all | solution.py:234
  143.8 9.3 %collective-permute-start.13 = (bf16[64,512]{1,0:T(8,128)(2,1)S(1)}, bf16[64,512]{1,0:T(8,128)(2,1)S(1)}, u32[]{:S(2)}, u32[]{:S(2)}) collective-permute-start(bf16[64,512]{1,0:T(8,128)(2,1)S(1)} %add_convert_fusion.5), channel_id=1, source_target_pairs={{0,6},{2,4},{4,2},{6,0},{8,14},{10,12},{12,10},{14,8},{1,7},{3,5},... | collective-permute-start | bytes 196616 | tf_op jit(solution)/shard_map/ppermute | solution.py:145
  148.7 6.9 %collective-permute-start.12 = (bf16[64,512]{1,0:T(8,128)(2,1)S(1)}, bf16[64,512]{1,0:T(8,128)(2,1)S(1)}, u32[]{:S(2)}, u32[]{:S(2)}) collective-permute-start(bf16[64,512]{1,0:T(8,128)(2,1)S(1)} %add_convert_fusion.5), channel_id=1, source_target_pairs={{0,4},{2,6},{4,0},{6,2},{8,12},{10,14},{12,8},{14,10},{1,5},{3,7},... | collective-permute-start | bytes 196616 | tf_op jit(solution)/shard_map/ppermute | solution.py:145
  150.7 6.2 %collective-permute-start.11 = (bf16[64,512]{1,0:T(8,128)(2,1)S(1)}, bf16[64,512]{1,0:T(8,128)(2,1)S(1)}, u32[]{:S(2)}, u32[]{:S(2)}) collective-permute-start(bf16[64,512]{1,0:T(8,128)(2,1)S(1)} %add_convert_fusion.5), channel_id=1, source_target_pairs={{0,2},{2,0},{4,6},{6,4},{8,10},{10,8},{12,14},{14,12},{1,3},{3,1},... | collective-permute-start | bytes 196616 | tf_op jit(solution)/shard_map/ppermute | solution.py:145
  156.9 7.2 %collective-permute-start.14 = (bf16[64,512]{1,0:T(8,128)(2,1)S(1)}, bf16[64,512]{1,0:T(8,128)(2,1)S(1)}, u32[]{:S(2)}, u32[]{:S(2)}) collective-permute-start(bf16[64,512]{1,0:T(8,128)(2,1)S(1)} %add_convert_fusion.4), channel_id=1, source_target_pairs={{0,14},{2,12},{4,10},{6,8},{8,6},{10,4},{12,2},{14,0},{1,15},{3,13... | collective-permute-start | bytes 196616 | tf_op jit(solution)/shard_map/ppermute | solution.py:145
  164.1 7.0 %collective-permute-start.15 = (bf16[64,512]{1,0:T(8,128)(2,1)S(1)}, bf16[64,512]{1,0:T(8,128)(2,1)S(1)}, u32[]{:S(2)}, u32[]{:S(2)}) collective-permute-start(bf16[64,512]{1,0:T(8,128)(2,1)S(1)} %add_convert_fusion.3), channel_id=1, source_target_pairs={{0,48},{16,32},{32,16},{48,0},{1,49},{17,33},{33,17},{49,1},{2,50}... | collective-permute-start | bytes 196616 | tf_op jit(solution)/shard_map/ppermute | solution.py:145
  180.5 6.9 %collective-permute-start.16 = (bf16[4,64,512]{2,1,0:T(8,128)(2,1)S(1)}, bf16[4,64,512]{2,1,0:T(8,128)(2,1)S(1)}, u32[]{:S(2)}, u32[]{:S(2)}) collective-permute-start(bf16[4,64,512]{2,1,0:T(8,128)(2,1)S(1)} %all_to_all.26.mine_ref), channel_id=1, source_target_pairs={{0,1},{1,0},{2,3},{3,2},{4,5},{5,4},{6,7},{7,6},{8,9},{9,8},{10,11... | collective-permute-start | bytes 786440 | tf_op jit(solution)/shard_map/ppermute | solution.py:145

commit v16 on v15

--- a/solution.py
+++ b/solution.py
@@ -35,17 +35,23 @@
     return pl.BlockSpec(memory_space=pltpu.SMEM)
 
 
-def spread(places, in_ref, out_ref):
+def spread(places, in_ref, out_ref, sems):
+    copies = []
     for place, chunk in enumerate(places):
-        out_ref[place] = in_ref[:, chunk * CHUNK : (chunk + 1) * CHUNK]
+        piece = in_ref.at[:, pl.ds(chunk * CHUNK, CHUNK)]
+        copies.append(pltpu.make_async_copy(piece, out_ref.at[place], sems.at[place]))
+        copies[-1].start()
+    for copy in copies:
+        copy.wait()
 
 
 def spread_chunks(array, places, name):
     return pl.pallas_call(
         functools.partial(spread, places),
         in_specs=[vmem()],
-        out_specs=vmem(),
+        out_specs=pl.BlockSpec(memory_space=pl.ANY),
         out_shape=jax.ShapeDtypeStruct((len(places), TILE, CHUNK), BF16),
+        scratch_shapes=[pltpu.SemaphoreType.DMA((len(places),))],
         compiler_params=params(),
         name=name,
     )(array)
@@ -97,7 +103,7 @@
 
 
 def backward_tiles(place_ref, index_ref, mine_ref, other_ref, *refs):
-    tiles_refs, (out_ref, total) = refs[:X], refs[X:]
+    tiles_refs, (out_ref, total, done, sems) = refs[:X], refs[X:]
     core = place_ref[0]
     total[...] = jnp.zeros_like(total)
     for step in range(X):
@@ -113,8 +119,14 @@
                 tile, panel, (((0,), (0,)), ((), ())), preferred_element_type=F32
             )
             total[col] += jnp.where(valid > 0, product, 0.0)
-    for tile in range(COL_TILES):
-        out_ref[tile] = total[tile].astype(BF16)
+    copies = []
+    for group in range(0, COL_TILES, X):
+        done[group : group + X] = total[group : group + X].astype(BF16)
+        here = pl.ds(group, X)
+        copies.append(pltpu.make_async_copy(done.at[here], out_ref.at[here], sems.at[group // X]))
+        copies[-1].start()
+    for copy in copies:
+        copy.wait()
 
 
 def last(parts_ref, weight_ref, out_ref):
@@ -130,14 +142,20 @@
     ).astype(BF16)
 
 
-def place_rows(place_ref, mine_ref, other_ref, out_ref):
+def place_rows(place_ref, mine_ref, other_ref, out_ref, held, sems):
     core = place_ref[0]
     half, share = WIDTH // CORES, WIDTH // (Y_LOW * CORES)
     scale = 1.0 / math.sqrt(TILE * Y * X * Z * CORES)
+    copies = []
     for y in range(Y_LOW):
         for side, ref in ((core, mine_ref), (1 - core, other_ref)):
             start = pl.multiple_of(side * half + (y ^ place_ref[2]) * share, share)
-            out_ref[pl.ds(start, share), :] = ref[y].astype(F32) * scale
+            at = len(copies)
+            held[at] = ref[y].astype(F32) * scale
+            copies.append(pltpu.make_async_copy(held.at[at], out_ref.at[pl.ds(start, share), :], sems.at[at]))
+            copies[-1].start()
+    for copy in copies:
+        copy.wait()
 
 
 def exchange(array, axis, distance):
@@ -224,9 +242,13 @@
     back = pl.pallas_call(
         backward_tiles,
         in_specs=[smem(), smem()] + [vmem()] * (2 + X),
-        out_specs=vmem(),
+        out_specs=pl.BlockSpec(memory_space=pl.ANY),
         out_shape=jax.ShapeDtypeStruct((COL_TILES, TILE, CHUNK), BF16),
-        scratch_shapes=[pltpu.VMEM((COL_TILES, TILE, CHUNK), F32)],
+        scratch_shapes=[
+            pltpu.VMEM((COL_TILES, TILE, CHUNK), F32),
+            pltpu.VMEM((COL_TILES, TILE, CHUNK), BF16),
+            pltpu.SemaphoreType.DMA((Y,)),
+        ],
         compiler_params=params(),
         name="backward_tiles",
     )(place, index, grad_mine, grad_other, *tiles)
@@ -252,8 +274,12 @@
     weight_grad = pl.pallas_call(
         place_rows,
         in_specs=[smem()] + [vmem()] * 2,
-        out_specs=vmem(),
+        out_specs=pl.BlockSpec(memory_space=pl.ANY),
         out_shape=jax.ShapeDtypeStruct((WIDTH, WIDTH), F32),
+        scratch_shapes=[
+            pltpu.VMEM((Y_LOW * CORES, share, WIDTH), F32),
+            pltpu.SemaphoreType.DMA((Y_LOW * CORES,)),
+        ],
         compiler_params=params(),
         name="place_rows",
     )(place, whole, exchange(whole, "core", 1))

time: 190 us -> 190 us (level)
  no operation moved by 1% of the time
where the time goes in v16:
time: 190 us; the launch traced here: 189 us
  starting transfers between devices  83.8 us (44%)
  blocking collectives  47.6 us (25%)
  waiting for transfers between devices  44.2 us (23%)
  Pallas kernels  10.5 us (6%)
    ppermute x17, starting transfers between devices, exchange(): return lax.ppermute(array, axis, [(i, i ^ distance) for i in range(size)])  61.4 us
    ppermute x17, waiting for transfers between devices, exchange(): return lax.ppermute(array, axis, [(i, i ^ distance) for i in range(size)])  44.2 us
    all_to_all x1, blocking collectives, body(): parts = lax.all_to_all(term, ('x', 'z'), 0, 0, tiled=True)  38.3 us
    all_to_all x1, starting transfers between devices, body(): panel = lax.all_to_all(chunks, ROW, 0, 0, tiled=True)  10.6 us
    all_to_all x1, blocking collectives, body(): whole = lax.all_to_all(piece, 'y_low', 0, 0, tiled=True)  9.3 us
    all_to_all x1, starting transfers between devices, body(): back = lax.all_to_all(back, ROW, 0, 0, tiled=True)  6.93 us
    all_to_all x1, starting transfers between devices, body(): grad_mine = lax.all_to_all(grad, ('x', 'z'), 0, 0, tiled=True)  4.84 us
  transfers between devices with their start and end apart: 20, of which 13 were waited for; matrix products, arithmetic and copies ran while one was open for 0% of the time, Pallas kernels for 1%

profile of v16, /device:TPU:1, one launch (start us, length us, event | category | flops | bytes accessed | tf_op | source)
XLA Modules:
  0.0 189.2 jit_solution(14945363701580957434)
XLA Ops:
  0.6 0.9 copy-done.1
  1.5 1.2 spread_features.1
  2.8 0.0 copy-start.7
  2.8 0.0 copy-start.5
  2.8 0.0 copy-start.6
  2.8 0.0 copy-start.3
  2.8 0.0 copy-start.4
  2.8 10.6 %all-to-all-start = ((bf16[32,128,128]{2,1,0:T(8,128)(2,1)}), bf16[32,128,128]{2,1,0:T(8,128)(2,1)S(1)}, u32[]{:S(2)}, u32[]{:S(2)}) async-start(bf16[32,128,128]{2,1,0:T(8,128)(2,1)} %spread_features.1), calls=%async_computation | async-start | bytes 2097152 | tf_op jit(solution)/shard_map/all_to_all | solution.py:193
  13.5 0.1 fusion.11
  13.6 4.3 %collective-permute-start.2 = (bf16[1040,128]{1,0:T(8,128)(2,1)S(1)}, bf16[1040,128]{1,0:T(8,128)(2,1)S(1)}, u32[]{:S(2)}, u32[]{:S(2)}) collective-permute-start(bf16[1040,128]{1,0:T(8,128)(2,1)S(1)} %pad_maximum_fusion.refs_0_), channel_id=1, source_target_pairs={{0,48},{16,32},{32,16},{48,0},{1,49},{17,33},{33,17},{49,1},{2,50}... | collective-permute-start | bytes 798728 | tf_op jit(solution)/shard_map/ppermute | solution.py:163
  18.0 2.5 %collective-permute-start.1 = (bf16[1040,128]{1,0:T(8,128)(2,1)S(1)}, bf16[1040,128]{1,0:T(8,128)(2,1)S(1)}, u32[]{:S(2)}, u32[]{:S(2)}) collective-permute-start(bf16[1040,128]{1,0:T(8,128)(2,1)S(1)} %pad_maximum_fusion.refs_0_), channel_id=1, source_target_pairs={{0,32},{16,48},{32,0},{48,16},{1,33},{17,49},{33,1},{49,17},{2,34}... | collective-permute-start | bytes 798728 | tf_op jit(solution)/shard_map/ppermute | solution.py:163
  20.5 2.1 %collective-permute-start = (bf16[1040,128]{1,0:T(8,128)(2,1)S(1)}, bf16[1040,128]{1,0:T(8,128)(2,1)S(1)}, u32[]{:S(2)}, u32[]{:S(2)}) collective-permute-start(bf16[1040,128]{1,0:T(8,128)(2,1)S(1)} %pad_maximum_fusion.refs_0_), channel_id=1, source_target_pairs={{0,16},{16,0},{32,48},{48,32},{1,17},{17,1},{33,49},{49,33},{2,18}... | collective-permute-start | bytes 798728 | tf_op jit(solution)/shard_map/ppermute | solution.py:163
  22.7 0.1 broadcast_in_dim.4
  22.7 0.1 min.14
  22.8 0.1 pad_add_fusion.place_ref.core_ref
  22.9 14.6 %collective-permute-done.2.refs_3_ = bf16[1040,128]{1,0:T(8,128)(2,1)S(1)} collective-permute-done((bf16[1040,128]{1,0:T(8,128)(2,1)S(1)}, bf16[1040,128]{1,0:T(8,128)(2,1)S(1)}, u32[]{:S(2)}, u32[]{:S(2)}) %collective-permute-start.2) | collective-permute-done | bytes 266272 | tf_op jit(solution)/shard_map/ppermute | solution.py:163
  37.5 0.0 collective-permute-done.1.refs_2_
  37.5 3.7 %collective-permute-done.refs_1_ = bf16[1040,128]{1,0:T(8,128)(2,1)S(1)} collective-permute-done((bf16[1040,128]{1,0:T(8,128)(2,1)S(1)}, bf16[1040,128]{1,0:T(8,128)(2,1)S(1)}, u32[]{:S(2)}, u32[]{:S(2)}) %collective-permute-start) | collective-permute-done | bytes 266272 | tf_op jit(solution)/shard_map/ppermute | solution.py:163
  41.2 0.1 maximum_minimum_fusion.index_ref
  41.3 0.0 all-to-all-done.panel_ref
  41.3 1.5 forward_tiles.1
  42.8 3.1 %collective-permute-start.3 = (bf16[32,128,128]{2,1,0:T(8,128)(2,1)S(1)}, bf16[32,128,128]{2,1,0:T(8,128)(2,1)S(1)}, u32[]{:S(2)}, u32[]{:S(2)}) collective-permute-start(bf16[32,128,128]{2,1,0:T(8,128)(2,1)S(1)} %get-tuple-element.18), channel_id=1, source_target_pairs={{0,1},{1,0},{2,3},{3,2},{4,5},{5,4},{6,7},{7,6},{8,9},{9,8},{10,11... | collective-permute-start | bytes 3145736 | tf_op jit(solution)/shard_map/ppermute | solution.py:163
  45.9 2.3 %collective-permute-done.3 = bf16[32,128,128]{2,1,0:T(8,128)(2,1)S(1)} collective-permute-done((bf16[32,128,128]{2,1,0:T(8,128)(2,1)S(1)}, bf16[32,128,128]{2,1,0:T(8,128)(2,1)S(1)}, u32[]{:S(2)}, u32[]{:S(2)}) %collective-permute-start.3) | collective-permute-done | bytes 1048608 | tf_op jit(solution)/shard_map/ppermute | solution.py:163
  48.2 0.4 add_convert_fusion
  48.6 0.0 copy-start
  48.6 0.0 copy-start.2
  48.6 38.3 %all_to_all.25.parts_ref = bf16[32,128,128]{2,1,0:T(8,128)(2,1)S(1)} all-to-all(bf16[32,128,128]{2,1,0:T(8,128)(2,1)S(1)} %add_convert_fusion), channel_id=1, replica_groups=mesh['y_high'=2,'y_low'=4,'x'=4,'z'=8,'core'=2] {'x','z'}, dimensions={0} | all-to-all | bytes 2097152 | tf_op jit(solution)/shard_map/all_to_all | solution.py:215
  86.9 1.6 middle.1
  88.5 6.3 %collective-permute-start.4 = (bf16[256,512]{1,0:T(8,128)(2,1)S(1)}, bf16[256,512]{1,0:T(8,128)(2,1)S(1)}, u32[]{:S(2)}, u32[]{:S(2)}) collective-permute-start(bf16[256,512]{1,0:T(8,128)(2,1)S(1)} %get-tuple-element.22), channel_id=1, source_target_pairs={{0,1},{1,0},{2,3},{3,2},{4,5},{5,4},{6,7},{7,6},{8,9},{9,8},{10,11... | collective-permute-start | bytes 786440 | tf_op jit(solution)/shard_map/ppermute | solution.py:163
  94.8 1.2 spread_grad.1
  96.0 0.0 collective-permute-done.4
  96.0 0.1 add_convert_fusion.1
  96.1 4.8 %all-to-all-start.2 = ((bf16[32,128,128]{2,1,0:T(8,128)(2,1)}), bf16[32,128,128]{2,1,0:T(8,128)(2,1)S(1)}, u32[]{:S(2)}, u32[]{:S(2)}) async-start(bf16[32,128,128]{2,1,0:T(8,128)(2,1)} %spread_grad.1), calls=%async_computation.2 | async-start | bytes 2097152 | tf_op jit(solution)/shard_map/all_to_all | solution.py:235
  101.0 2.2 %collective-permute-start.5 = (bf16[64,512]{1,0:T(8,128)(2,1)S(1)}, bf16[64,512]{1,0:T(8,128)(2,1)S(1)}, u32[]{:S(2)}, u32[]{:S(2)}) collective-permute-start(bf16[64,512]{1,0:T(8,128)(2,1)S(1)} %get-tuple-element.31), channel_id=1, source_target_pairs={{0,64},{64,0},{128,192},{192,128},{1,65},{65,1},{129,193},{193,129... | collective-permute-start | bytes 196616 | tf_op jit(solution)/shard_map/ppermute | solution.py:163
  103.2 3.8 %collective-permute-start.7 = (bf16[64,512]{1,0:T(8,128)(2,1)S(1)}, bf16[64,512]{1,0:T(8,128)(2,1)S(1)}, u32[]{:S(2)}, u32[]{:S(2)}) collective-permute-start(bf16[64,512]{1,0:T(8,128)(2,1)S(1)} %get-tuple-element.32), channel_id=1, source_target_pairs={{0,192},{64,128},{128,64},{192,0},{1,193},{65,129},{129,65},{193,1... | collective-permute-start | bytes 196616 | tf_op jit(solution)/shard_map/ppermute | solution.py:163
  107.1 2.3 %collective-permute-start.6 = (bf16[64,512]{1,0:T(8,128)(2,1)S(1)}, bf16[64,512]{1,0:T(8,128)(2,1)S(1)}, u32[]{:S(2)}, u32[]{:S(2)}) collective-permute-start(bf16[64,512]{1,0:T(8,128)(2,1)S(1)} %get-tuple-element.33), channel_id=1, source_target_pairs={{0,128},{64,192},{128,0},{192,64},{1,129},{65,193},{129,1},{193,65... | collective-permute-start | bytes 196616 | tf_op jit(solution)/shard_map/ppermute | solution.py:163
  109.4 0.0 collective-permute-done.5
  109.4 0.7 collective-permute-done.7
  110.1 3.5 %collective-permute-done.6 = bf16[64,512]{1,0:T(8,128)(2,1)S(1)} collective-permute-done((bf16[64,512]{1,0:T(8,128)(2,1)S(1)}, bf16[64,512]{1,0:T(8,128)(2,1)S(1)}, u32[]{:S(2)}, u32[]{:S(2)}) %collective-permute-start.6) | collective-permute-done | bytes 65568 | tf_op jit(solution)/shard_map/ppermute | solution.py:163
  113.6 3.8 %collective-permute-start.8 = (bf16[64,512]{1,0:T(8,128)(2,1)S(1)}, bf16[64,512]{1,0:T(8,128)(2,1)S(1)}, u32[]{:S(2)}, u32[]{:S(2)}) collective-permute-start(bf16[64,512]{1,0:T(8,128)(2,1)S(1)} %fusion.2), channel_id=1, source_target_pairs={{0,448},{64,384},{128,320},{192,256},{256,192},{320,128},{384,64},... | collective-permute-start | bytes 196616 | tf_op jit(solution)/shard_map/ppermute | solution.py:163
  117.5 3.4 %collective-permute-done.8 = bf16[64,512]{1,0:T(8,128)(2,1)S(1)} collective-permute-done((bf16[64,512]{1,0:T(8,128)(2,1)S(1)}, bf16[64,512]{1,0:T(8,128)(2,1)S(1)}, u32[]{:S(2)}, u32[]{:S(2)}) %collective-permute-start.8) | collective-permute-done | bytes 65568 | tf_op jit(solution)/shard_map/ppermute | solution.py:163
  120.9 3.1 %collective-permute-start.9 = (bf16[64,512]{1,0:T(8,128)(2,1)S(1)}, bf16[64,512]{1,0:T(8,128)(2,1)S(1)}, u32[]{:S(2)}, u32[]{:S(2)}) collective-permute-start(bf16[64,512]{1,0:T(8,128)(2,1)S(1)} %add_convert_fusion.6), channel_id=1, source_target_pairs={{0,16},{16,0},{32,48},{48,32},{1,17},{17,1},{33,49},{49,33},{2,18}... | collective-permute-start | bytes 196616 | tf_op jit(solution)/shard_map/ppermute | solution.py:163
  124.0 2.8 %collective-permute-done.9 = bf16[64,512]{1,0:T(8,128)(2,1)S(1)} collective-permute-done((bf16[64,512]{1,0:T(8,128)(2,1)S(1)}, bf16[64,512]{1,0:T(8,128)(2,1)S(1)}, u32[]{:S(2)}, u32[]{:S(2)}) %collective-permute-start.9) | collective-permute-done | bytes 65568 | tf_op jit(solution)/shard_map/ppermute | solution.py:163
  126.9 0.0 all-to-all-done.2.mine_ref
  126.9 5.5 %collective-permute-start.10 = (bf16[32,128,128]{2,1,0:T(8,128)(2,1)S(1)}, bf16[32,128,128]{2,1,0:T(8,128)(2,1)S(1)}, u32[]{:S(2)}, u32[]{:S(2)}) collective-permute-start(bf16[32,128,128]{2,1,0:T(8,128)(2,1)S(1)} %all-to-all-done.2.mine_ref), channel_id=1, source_target_pairs={{0,1},{1,0},{2,3},{3,2},{4,5},{5,4},{6,7},{7,6},{8,9},{9,8},{10,11... | collective-permute-start | bytes 3145736 | tf_op jit(solution)/shard_map/ppermute | solution.py:163
  132.4 2.3 %collective-permute-done.10.other_ref = bf16[32,128,128]{2,1,0:T(8,128)(2,1)S(1)} collective-permute-done((bf16[32,128,128]{2,1,0:T(8,128)(2,1)S(1)}, bf16[32,128,128]{2,1,0:T(8,128)(2,1)S(1)}, u32[]{:S(2)}, u32[]{:S(2)}) %collective-permute-start.10) | collective-permute-done | bytes 1048608 | tf_op jit(solution)/shard_map/ppermute | solution.py:163
  134.7 2.3 %backward_tiles.1 = bf16[32,128,128]{2,1,0:T(8,128)(2,1)} custom-call(s32[3]{0:T(128)S(1)} %pad_add_fusion.place_ref.core_ref, s32[4,24]{1,0:T(4,128)S(1)} %maximum_minimum_fusion.index_ref, bf16[32,128,128]{2,1,0:T(8,128)(2,1)S(1)} %all-to-all-done.2.mine_ref, bf16[32,128,128]{2,1,0:T(8,128)(2,1)S(1)} %collective-permute-done.10.other_ref, ...), custom_call_target="tpu_custom_call" | custom-call | tf_op jit(solution)/shard_map/backward_tiles/pallas_call | solution.py:242
  137.0 6.9 %all-to-all-start.3 = ((bf16[32,128,128]{2,1,0:T(8,128)(2,1)}), bf16[32,128,128]{2,1,0:T(8,128)(2,1)S(1)}, u32[]{:S(2)}, u32[]{:S(2)}) async-start(bf16[32,128,128]{2,1,0:T(8,128)(2,1)} %backward_tiles.1), calls=%async_computation.3 | async-start | bytes 2097152 | tf_op jit(solution)/shard_map/all_to_all | solution.py:256
  144.0 4.9 %collective-permute-start.13 = (bf16[64,512]{1,0:T(8,128)(2,1)S(1)}, bf16[64,512]{1,0:T(8,128)(2,1)S(1)}, u32[]{:S(2)}, u32[]{:S(2)}) collective-permute-start(bf16[64,512]{1,0:T(8,128)(2,1)S(1)} %add_convert_fusion.5), channel_id=1, source_target_pairs={{0,6},{2,4},{4,2},{6,0},{8,14},{10,12},{12,10},{14,8},{1,7},{3,5},... | collective-permute-start | bytes 196616 | tf_op jit(solution)/shard_map/ppermute | solution.py:163
  148.9 1.9 %collective-permute-start.12 = (bf16[64,512]{1,0:T(8,128)(2,1)S(1)}, bf16[64,512]{1,0:T(8,128)(2,1)S(1)}, u32[]{:S(2)}, u32[]{:S(2)}) collective-permute-start(bf16[64,512]{1,0:T(8,128)(2,1)S(1)} %add_convert_fusion.5), channel_id=1, source_target_pairs={{0,4},{2,6},{4,0},{6,2},{8,12},{10,14},{12,8},{14,10},{1,5},{3,7},... | collective-permute-start | bytes 196616 | tf_op jit(solution)/shard_map/ppermute | solution.py:163
  150.8 2.5 %collective-permute-start.11 = (bf16[64,512]{1,0:T(8,128)(2,1)S(1)}, bf16[64,512]{1,0:T(8,128)(2,1)S(1)}, u32[]{:S(2)}, u32[]{:S(2)}) collective-permute-start(bf16[64,512]{1,0:T(8,128)(2,1)S(1)} %add_convert_fusion.5), channel_id=1, source_target_pairs={{0,2},{2,0},{4,6},{6,4},{8,10},{10,8},{12,14},{14,12},{1,3},{3,1},... | collective-permute-start | bytes 196616 | tf_op jit(solution)/shard_map/ppermute | solution.py:163
  153.3 0.0 collective-permute-done.13
  153.3 2.5 %collective-permute-done.12 = bf16[64,512]{1,0:T(8,128)(2,1)S(1)} collective-permute-done((bf16[64,512]{1,0:T(8,128)(2,1)S(1)}, bf16[64,512]{1,0:T(8,128)(2,1)S(1)}, u32[]{:S(2)}, u32[]{:S(2)}) %collective-permute-start.12) | collective-permute-done | bytes 65568 | tf_op jit(solution)/shard_map/ppermute | solution.py:163
  155.8 1.2 collective-permute-done.11
  157.0 4.3 %collective-permute-start.14 = (bf16[64,512]{1,0:T(8,128)(2,1)S(1)}, bf16[64,512]{1,0:T(8,128)(2,1)S(1)}, u32[]{:S(2)}, u32[]{:S(2)}) collective-permute-start(bf16[64,512]{1,0:T(8,128)(2,1)S(1)} %add_convert_fusion.4), channel_id=1, source_target_pairs={{0,14},{2,12},{4,10},{6,8},{8,6},{10,4},{12,2},{14,0},{1,15},{3,13... | collective-permute-start | bytes 196616 | tf_op jit(solution)/shard_map/ppermute | solution.py:163
  161.3 2.9 %collective-permute-done.14 = bf16[64,512]{1,0:T(8,128)(2,1)S(1)} collective-permute-done((bf16[64,512]{1,0:T(8,128)(2,1)S(1)}, bf16[64,512]{1,0:T(8,128)(2,1)S(1)}, u32[]{:S(2)}, u32[]{:S(2)}) %collective-permute-start.14) | collective-permute-done | bytes 65568 | tf_op jit(solution)/shard_map/ppermute | solution.py:163
  164.3 2.8 %collective-permute-start.15 = (bf16[64,512]{1,0:T(8,128)(2,1)S(1)}, bf16[64,512]{1,0:T(8,128)(2,1)S(1)}, u32[]{:S(2)}, u32[]{:S(2)}) collective-permute-start(bf16[64,512]{1,0:T(8,128)(2,1)S(1)} %add_convert_fusion.3), channel_id=1, source_target_pairs={{0,48},{16,32},{32,16},{48,0},{1,49},{17,33},{33,17},{49,1},{2,50}... | collective-permute-start | bytes 196616 | tf_op jit(solution)/shard_map/ppermute | solution.py:163
  167.1 4.2 %collective-permute-done.15 = bf16[64,512]{1,0:T(8,128)(2,1)S(1)} collective-permute-done((bf16[64,512]{1,0:T(8,128)(2,1)S(1)}, bf16[64,512]{1,0:T(8,128)(2,1)S(1)}, u32[]{:S(2)}, u32[]{:S(2)}) %collective-permute-start.15) | collective-permute-done | bytes 65568 | tf_op jit(solution)/shard_map/ppermute | solution.py:163
  171.3 0.0 all-to-all-done.3.parts_ref
  171.3 9.3 %all_to_all.26.mine_ref = bf16[4,64,512]{2,1,0:T(8,128)(2,1)S(1)} all-to-all(bf16[4,64,512]{2,1,0:T(8,128)(2,1)S(1)} %broadcast_in_dim.5), channel_id=1, replica_groups=mesh['y_high'=2,'y_low'=4,'x'=4,'z'=8,'core'=2] {'y_low'}, dimensions={0} | all-to-all | bytes 524288 | tf_op jit(solution)/shard_map/all_to_all | solution.py:273
  180.6 5.8 %collective-permute-start.16 = (bf16[4,64,512]{2,1,0:T(8,128)(2,1)S(1)}, bf16[4,64,512]{2,1,0:T(8,128)(2,1)S(1)}, u32[]{:S(2)}, u32[]{:S(2)}) collective-permute-start(bf16[4,64,512]{2,1,0:T(8,128)(2,1)S(1)} %all_to_all.26.mine_ref), channel_id=1, source_target_pairs={{0,1},{1,0},{2,3},{3,2},{4,5},{5,4},{6,7},{7,6},{8,9},{9,8},{10,11... | collective-permute-start | bytes 786440 | tf_op jit(solution)/shard_map/ppermute | solution.py:163
  186.5 1.0 last.1
  187.4 0.2 collective-permute-done.16.other_ref
  187.6 1.6 place_rows.1
  (22 shorter events, 0.2 us)
Async XLA Ops:
  0.6 0.9 copy-start.1
  2.8 10.7 %copy-start.7 = (s32[1,1,8]{2,1,0:T(1,128)S(1)}, s32[1,1,8]{2,1,0:T(1,128)}, u32[]{:S(2)}) copy-start(s32[1,1,8]{2,1,0:T(1,128)} %param.12) | copy-start | bytes 100
  2.8 10.7 %copy-start.5 = (s32[1,1,8]{2,1,0:T(1,128)S(1)}, s32[1,1,8]{2,1,0:T(1,128)}, u32[]{:S(2)}) copy-start(s32[1,1,8]{2,1,0:T(1,128)} %param.14) | copy-start | bytes 100
  2.8 10.7 %copy-start.6 = (s32[1,1,8]{2,1,0:T(1,128)S(1)}, s32[1,1,8]{2,1,0:T(1,128)}, u32[]{:S(2)}) copy-start(s32[1,1,8]{2,1,0:T(1,128)} %param.13) | copy-start | bytes 100
  2.8 10.8 %copy-start.3 = (bf16[1,1,8,128,128]{4,3,2,1,0:T(8,128)(2,1)S(1)}, bf16[1,1,8,128,128]{4,3,2,1,0:T(8,128)(2,1)}, u32[]{:S(2)}) copy-start(bf16[1,1,8,128,128]{4,3,2,1,0:T(8,128)(2,1)} %param.11) | copy-start | bytes 786436
  2.8 19.8 %copy-start.4 = (s32[3]{0:T(128)S(1)}, s32[3]{0:T(128)}, u32[]{:S(2)}) copy-start(s32[3]{0:T(128)} %constant.41.clone) | copy-start | bytes 40
  2.8 38.5 %all-to-all-start = ((bf16[32,128,128]{2,1,0:T(8,128)(2,1)}), bf16[32,128,128]{2,1,0:T(8,128)(2,1)S(1)}, u32[]{:S(2)}, u32[]{:S(2)}) async-start(bf16[32,128,128]{2,1,0:T(8,128)(2,1)} %spread_features.1), calls=%async_computation | async-start | bytes 2097152 | tf_op jit(solution)/shard_map/all_to_all | solution.py:193
  13.6 23.9 %collective-permute-start.2 = (bf16[1040,128]{1,0:T(8,128)(2,1)S(1)}, bf16[1040,128]{1,0:T(8,128)(2,1)S(1)}, u32[]{:S(2)}, u32[]{:S(2)}) collective-permute-start(bf16[1040,128]{1,0:T(8,128)(2,1)S(1)} %pad_maximum_fusion.refs_0_), channel_id=1, source_target_pairs={{0,48},{16,32},{32,16},{48,0},{1,49},{17,33},{33,17},{49,1},{2,50}... | collective-permute-start | bytes 798728 | tf_op jit(solution)/shard_map/ppermute | solution.py:163
  18.0 19.5 %collective-permute-start.1 = (bf16[1040,128]{1,0:T(8,128)(2,1)S(1)}, bf16[1040,128]{1,0:T(8,128)(2,1)S(1)}, u32[]{:S(2)}, u32[]{:S(2)}) collective-permute-start(bf16[1040,128]{1,0:T(8,128)(2,1)S(1)} %pad_maximum_fusion.refs_0_), channel_id=1, source_target_pairs={{0,32},{16,48},{32,0},{48,16},{1,33},{17,49},{33,1},{49,17},{2,34}... | collective-permute-start | bytes 798728 | tf_op jit(solution)/shard_map/ppermute | solution.py:163
  20.5 20.7 %collective-permute-start = (bf16[1040,128]{1,0:T(8,128)(2,1)S(1)}, bf16[1040,128]{1,0:T(8,128)(2,1)S(1)}, u32[]{:S(2)}, u32[]{:S(2)}) collective-permute-start(bf16[1040,128]{1,0:T(8,128)(2,1)S(1)} %pad_maximum_fusion.refs_0_), channel_id=1, source_target_pairs={{0,16},{16,0},{32,48},{48,32},{1,17},{17,1},{33,49},{49,33},{2,18}... | collective-permute-start | bytes 798728 | tf_op jit(solution)/shard_map/ppermute | solution.py:163
  42.8 5.4 %collective-permute-start.3 = (bf16[32,128,128]{2,1,0:T(8,128)(2,1)S(1)}, bf16[32,128,128]{2,1,0:T(8,128)(2,1)S(1)}, u32[]{:S(2)}, u32[]{:S(2)}) collective-permute-start(bf16[32,128,128]{2,1,0:T(8,128)(2,1)S(1)} %get-tuple-element.18), channel_id=1, source_target_pairs={{0,1},{1,0},{2,3},{3,2},{4,5},{5,4},{6,7},{7,6},{8,9},{9,8},{10,11... | collective-permute-start | bytes 3145736 | tf_op jit(solution)/shard_map/ppermute | solution.py:163
  48.6 38.3 %copy-start = (bf16[512,512]{1,0:T(8,128)(2,1)S(1)}, bf16[512,512]{1,0:T(8,128)(2,1)}, u32[]{:S(2)}) copy-start(bf16[512,512]{1,0:T(8,128)(2,1)} %weight_ref.3) | copy-start | bytes 1572868
  48.6 38.3 %copy-start.2 = (bf16[128,512]{1,0:T(8,128)(2,1)S(1)}, bf16[128,512]{1,0:T(8,128)(2,1)}, u32[]{:S(2)}) copy-start(bf16[128,512]{1,0:T(8,128)(2,1)} %cotangent_ref.1) | copy-start | bytes 393220
  88.5 7.5 %collective-permute-start.4 = (bf16[256,512]{1,0:T(8,128)(2,1)S(1)}, bf16[256,512]{1,0:T(8,128)(2,1)S(1)}, u32[]{:S(2)}, u32[]{:S(2)}) collective-permute-start(bf16[256,512]{1,0:T(8,128)(2,1)S(1)} %get-tuple-element.22), channel_id=1, source_target_pairs={{0,1},{1,0},{2,3},{3,2},{4,5},{5,4},{6,7},{7,6},{8,9},{9,8},{10,11... | collective-permute-start | bytes 786440 | tf_op jit(solution)/shard_map/ppermute | solution.py:163
  96.1 30.8 %all-to-all-start.2 = ((bf16[32,128,128]{2,1,0:T(8,128)(2,1)}), bf16[32,128,128]{2,1,0:T(8,128)(2,1)S(1)}, u32[]{:S(2)}, u32[]{:S(2)}) async-start(bf16[32,128,128]{2,1,0:T(8,128)(2,1)} %spread_grad.1), calls=%async_computation.2 | async-start | bytes 2097152 | tf_op jit(solution)/shard_map/all_to_all | solution.py:235
  101.0 8.4 %collective-permute-start.5 = (bf16[64,512]{1,0:T(8,128)(2,1)S(1)}, bf16[64,512]{1,0:T(8,128)(2,1)S(1)}, u32[]{:S(2)}, u32[]{:S(2)}) collective-permute-start(bf16[64,512]{1,0:T(8,128)(2,1)S(1)} %get-tuple-element.31), channel_id=1, source_target_pairs={{0,64},{64,0},{128,192},{192,128},{1,65},{65,1},{129,193},{193,129... | collective-permute-start | bytes 196616 | tf_op jit(solution)/shard_map/ppermute | solution.py:163
  103.2 6.8 %collective-permute-start.7 = (bf16[64,512]{1,0:T(8,128)(2,1)S(1)}, bf16[64,512]{1,0:T(8,128)(2,1)S(1)}, u32[]{:S(2)}, u32[]{:S(2)}) collective-permute-start(bf16[64,512]{1,0:T(8,128)(2,1)S(1)} %get-tuple-element.32), channel_id=1, source_target_pairs={{0,192},{64,128},{128,64},{192,0},{1,193},{65,129},{129,65},{193,1... | collective-permute-start | bytes 196616 | tf_op jit(solution)/shard_map/ppermute | solution.py:163
  107.1 6.5 %collective-permute-start.6 = (bf16[64,512]{1,0:T(8,128)(2,1)S(1)}, bf16[64,512]{1,0:T(8,128)(2,1)S(1)}, u32[]{:S(2)}, u32[]{:S(2)}) collective-permute-start(bf16[64,512]{1,0:T(8,128)(2,1)S(1)} %get-tuple-element.33), channel_id=1, source_target_pairs={{0,128},{64,192},{128,0},{192,64},{1,129},{65,193},{129,1},{193,65... | collective-permute-start | bytes 196616 | tf_op jit(solution)/shard_map/ppermute | solution.py:163
  113.6 7.2 %collective-permute-start.8 = (bf16[64,512]{1,0:T(8,128)(2,1)S(1)}, bf16[64,512]{1,0:T(8,128)(2,1)S(1)}, u32[]{:S(2)}, u32[]{:S(2)}) collective-permute-start(bf16[64,512]{1,0:T(8,128)(2,1)S(1)} %fusion.2), channel_id=1, source_target_pairs={{0,448},{64,384},{128,320},{192,256},{256,192},{320,128},{384,64},... | collective-permute-start | bytes 196616 | tf_op jit(solution)/shard_map/ppermute | solution.py:163
  120.9 6.0 %collective-permute-start.9 = (bf16[64,512]{1,0:T(8,128)(2,1)S(1)}, bf16[64,512]{1,0:T(8,128)(2,1)S(1)}, u32[]{:S(2)}, u32[]{:S(2)}) collective-permute-start(bf16[64,512]{1,0:T(8,128)(2,1)S(1)} %add_convert_fusion.6), channel_id=1, source_target_pairs={{0,16},{16,0},{32,48},{48,32},{1,17},{17,1},{33,49},{49,33},{2,18}... | collective-permute-start | bytes 196616 | tf_op jit(solution)/shard_map/ppermute | solution.py:163
  126.9 7.8 %collective-permute-start.10 = (bf16[32,128,128]{2,1,0:T(8,128)(2,1)S(1)}, bf16[32,128,128]{2,1,0:T(8,128)(2,1)S(1)}, u32[]{:S(2)}, u32[]{:S(2)}) collective-permute-start(bf16[32,128,128]{2,1,0:T(8,128)(2,1)S(1)} %all-to-all-done.2.mine_ref), channel_id=1, source_target_pairs={{0,1},{1,0},{2,3},{3,2},{4,5},{5,4},{6,7},{7,6},{8,9},{9,8},{10,11... | collective-permute-start | bytes 3145736 | tf_op jit(solution)/shard_map/ppermute | solution.py:163
  137.0 34.3 %all-to-all-start.3 = ((bf16[32,128,128]{2,1,0:T(8,128)(2,1)}), bf16[32,128,128]{2,1,0:T(8,128)(2,1)S(1)}, u32[]{:S(2)}, u32[]{:S(2)}) async-start(bf16[32,128,128]{2,1,0:T(8,128)(2,1)} %backward_tiles.1), calls=%async_computation.3 | async-start | bytes 2097152 | tf_op jit(solution)/shard_map/all_to_all | solution.py:256
  144.0 9.3 %collective-permute-start.13 = (bf16[64,512]{1,0:T(8,128)(2,1)S(1)}, bf16[64,512]{1,0:T(8,128)(2,1)S(1)}, u32[]{:S(2)}, u32[]{:S(2)}) collective-permute-start(bf16[64,512]{1,0:T(8,128)(2,1)S(1)} %add_convert_fusion.5), channel_id=1, source_target_pairs={{0,6},{2,4},{4,2},{6,0},{8,14},{10,12},{12,10},{14,8},{1,7},{3,5},... | collective-permute-start | bytes 196616 | tf_op jit(solution)/shard_map/ppermute | solution.py:163
  148.9 6.9 %collective-permute-start.12 = (bf16[64,512]{1,0:T(8,128)(2,1)S(1)}, bf16[64,512]{1,0:T(8,128)(2,1)S(1)}, u32[]{:S(2)}, u32[]{:S(2)}) collective-permute-start(bf16[64,512]{1,0:T(8,128)(2,1)S(1)} %add_convert_fusion.5), channel_id=1, source_target_pairs={{0,4},{2,6},{4,0},{6,2},{8,12},{10,14},{12,8},{14,10},{1,5},{3,7},... | collective-permute-start | bytes 196616 | tf_op jit(solution)/shard_map/ppermute | solution.py:163
  150.8 6.2 %collective-permute-start.11 = (bf16[64,512]{1,0:T(8,128)(2,1)S(1)}, bf16[64,512]{1,0:T(8,128)(2,1)S(1)}, u32[]{:S(2)}, u32[]{:S(2)}) collective-permute-start(bf16[64,512]{1,0:T(8,128)(2,1)S(1)} %add_convert_fusion.5), channel_id=1, source_target_pairs={{0,2},{2,0},{4,6},{6,4},{8,10},{10,8},{12,14},{14,12},{1,3},{3,1},... | collective-permute-start | bytes 196616 | tf_op jit(solution)/shard_map/ppermute | solution.py:163
  157.0 7.2 %collective-permute-start.14 = (bf16[64,512]{1,0:T(8,128)(2,1)S(1)}, bf16[64,512]{1,0:T(8,128)(2,1)S(1)}, u32[]{:S(2)}, u32[]{:S(2)}) collective-permute-start(bf16[64,512]{1,0:T(8,128)(2,1)S(1)} %add_convert_fusion.4), channel_id=1, source_target_pairs={{0,14},{2,12},{4,10},{6,8},{8,6},{10,4},{12,2},{14,0},{1,15},{3,13... | collective-permute-start | bytes 196616 | tf_op jit(solution)/shard_map/ppermute | solution.py:163
  164.3 7.0 %collective-permute-start.15 = (bf16[64,512]{1,0:T(8,128)(2,1)S(1)}, bf16[64,512]{1,0:T(8,128)(2,1)S(1)}, u32[]{:S(2)}, u32[]{:S(2)}) collective-permute-start(bf16[64,512]{1,0:T(8,128)(2,1)S(1)} %add_convert_fusion.3), channel_id=1, source_target_pairs={{0,48},{16,32},{32,16},{48,0},{1,49},{17,33},{33,17},{49,1},{2,50}... | collective-permute-start | bytes 196616 | tf_op jit(solution)/shard_map/ppermute | solution.py:163
  180.6 7.0 %collective-permute-start.16 = (bf16[4,64,512]{2,1,0:T(8,128)(2,1)S(1)}, bf16[4,64,512]{2,1,0:T(8,128)(2,1)S(1)}, u32[]{:S(2)}, u32[]{:S(2)}) collective-permute-start(bf16[4,64,512]{2,1,0:T(8,128)(2,1)S(1)} %all_to_all.26.mine_ref), channel_id=1, source_target_pairs={{0,1},{1,0},{2,3},{3,2},{4,5},{5,4},{6,7},{7,6},{8,9},{9,8},{10,11... | collective-permute-start | bytes 786440 | tf_op jit(solution)/shard_map/ppermute | solution.py:163

commit v17 on v15

--- a/solution.py
+++ b/solution.py
@@ -130,14 +130,13 @@
     ).astype(BF16)
 
 
-def place_rows(place_ref, mine_ref, other_ref, out_ref):
-    core = place_ref[0]
+def place_rows(place_ref, pieces_ref, out_ref):
     half, share = WIDTH // CORES, WIDTH // (Y_LOW * CORES)
     scale = 1.0 / math.sqrt(TILE * Y * X * Z * CORES)
     for y in range(Y_LOW):
-        for side, ref in ((core, mine_ref), (1 - core, other_ref)):
-            start = pl.multiple_of(side * half + (y ^ place_ref[2]) * share, share)
-            out_ref[pl.ds(start, share), :] = ref[y].astype(F32) * scale
+        for core in range(CORES):
+            start = pl.multiple_of(core * half + (y ^ place_ref[2]) * share, share)
+            out_ref[pl.ds(start, share), :] = pieces_ref[y * CORES + core].astype(F32) * scale
 
 
 def exchange(array, axis, distance):
@@ -247,16 +246,16 @@
     )(back, weight)
 
     share = WIDTH // (Y_LOW * CORES)
-    piece = jnp.broadcast_to(piece[None], (Y_LOW, share, WIDTH))
-    whole = lax.all_to_all(piece, "y_low", 0, 0, tiled=True)
+    piece = jnp.broadcast_to(piece[None], (Y_LOW * CORES, share, WIDTH))
+    whole = lax.all_to_all(piece, ("y_low", "core"), 0, 0, tiled=True)
     weight_grad = pl.pallas_call(
         place_rows,
-        in_specs=[smem()] + [vmem()] * 2,
+        in_specs=[smem(), vmem()],
         out_specs=vmem(),
         out_shape=jax.ShapeDtypeStruct((WIDTH, WIDTH), F32),
         compiler_params=params(),
         name="place_rows",
-    )(place, whole, exchange(whole, "core", 1))
+    )(place, whole)
     return (activations, input_grad, weight_grad)
 
 

time: 190 us -> 195 us (1.026)
  waiting for transfers between devices: 44.4 us -> 57.7 us
  blocking collectives: 47.6 us -> 38.3 us
    all_to_all x0 -> x1, waiting for transfers between devices: none -> 13.5 us  [body(): whole = lax.all_to_all(piece, ('y_low', 'core'), 0, 0, tiled=True)]
    all_to_all x1 -> x0, blocking collectives: 9.3 us -> none  [body(): whole = lax.all_to_all(piece, 'y_low', 0, 0, tiled=True)]
    all_to_all x0 -> x1, starting transfers between devices: none -> 6.28 us  [body(): whole = lax.all_to_all(piece, ('y_low', 'core'), 0, 0, tiled=True)]
    ppermute x17 -> x16, starting transfers between devices: 61.3 us -> 55.5 us  [exchange(): return lax.ppermute(array, axis, [(i, i ^ distance) for i in range(size)])]
    ppermute x17 -> x16, waiting for transfers between devices: 44.4 us -> 44.2 us  [exchange(): return lax.ppermute(array, axis, [(i, i ^ distance) for i in range(size)])]
where the time goes in v17:
time: 195 us; the launch traced here: 194 us
  starting transfers between devices  84.3 us (43%)
  waiting for transfers between devices  57.7 us (30%)
  blocking collectives  38.3 us (20%)
  Pallas kernels  10.3 us (5%)
  local copies, waits for them, and re-layouts  1.95 us (1%)
    ppermute x16, starting transfers between devices, exchange(): return lax.ppermute(array, axis, [(i, i ^ distance) for i in range(size)])  55.5 us
    ppermute x16, waiting for transfers between devices, exchange(): return lax.ppermute(array, axis, [(i, i ^ distance) for i in range(size)])  44.2 us
    all_to_all x1, blocking collectives, body(): parts = lax.all_to_all(term, ('x', 'z'), 0, 0, tiled=True)  38.3 us
    all_to_all x1, waiting for transfers between devices, body(): whole = lax.all_to_all(piece, ('y_low', 'core'), 0, 0, tiled=True)  13.5 us
    all_to_all x1, starting transfers between devices, body(): panel = lax.all_to_all(chunks, ROW, 0, 0, tiled=True)  10.6 us
    all_to_all x1, starting transfers between devices, body(): back = lax.all_to_all(back, ROW, 0, 0, tiled=True)  7.03 us
    all_to_all x1, starting transfers between devices, body(): whole = lax.all_to_all(piece, ('y_low', 'core'), 0, 0, tiled=True)  6.28 us
    all_to_all x1, starting transfers between devices, body(): grad_mine = lax.all_to_all(grad, ('x', 'z'), 0, 0, tiled=True)  4.84 us
  transfers between devices with their start and end apart: 20, of which 13 were waited for; matrix products, arithmetic and copies ran while one was open for 0% of the time, Pallas kernels for 1%

profile of v17, /device:TPU:1, one launch (start us, length us, event | category | flops | bytes accessed | tf_op | source)
XLA Modules:
  0.0 194.4 jit_solution(6188682353242485321)
XLA Ops:
  0.6 0.0 copy-start.1
  0.6 0.9 copy-done.1
  1.5 1.1 spread_features.1
  2.7 0.0 copy-start.4
  2.7 10.6 %all-to-all-start = ((bf16[32,128,128]{2,1,0:T(8,128)(2,1)}), bf16[32,128,128]{2,1,0:T(8,128)(2,1)S(1)}, u32[]{:S(2)}, u32[]{:S(2)}) async-start(bf16[32,128,128]{2,1,0:T(8,128)(2,1)} %spread_features.1), calls=%async_computation | async-start | bytes 2097152 | tf_op jit(solution)/shard_map/all_to_all | solution.py:174
  13.3 0.0 copy-done.7
  13.4 0.1 fusion.11
  13.5 0.0 copy-done.3
  13.5 4.3 %collective-permute-start.2 = (bf16[1040,128]{1,0:T(8,128)(2,1)S(1)}, bf16[1040,128]{1,0:T(8,128)(2,1)S(1)}, u32[]{:S(2)}, u32[]{:S(2)}) collective-permute-start(bf16[1040,128]{1,0:T(8,128)(2,1)S(1)} %pad_maximum_fusion.refs_0_), channel_id=1, source_target_pairs={{0,48},{16,32},{32,16},{48,0},{1,49},{17,33},{33,17},{49,1},{2,50}... | collective-permute-start | bytes 798728 | tf_op jit(solution)/shard_map/ppermute | solution.py:144
  17.8 2.5 %collective-permute-start.1 = (bf16[1040,128]{1,0:T(8,128)(2,1)S(1)}, bf16[1040,128]{1,0:T(8,128)(2,1)S(1)}, u32[]{:S(2)}, u32[]{:S(2)}) collective-permute-start(bf16[1040,128]{1,0:T(8,128)(2,1)S(1)} %pad_maximum_fusion.refs_0_), channel_id=1, source_target_pairs={{0,32},{16,48},{32,0},{48,16},{1,33},{17,49},{33,1},{49,17},{2,34}... | collective-permute-start | bytes 798728 | tf_op jit(solution)/shard_map/ppermute | solution.py:144
  20.3 2.1 %collective-permute-start = (bf16[1040,128]{1,0:T(8,128)(2,1)S(1)}, bf16[1040,128]{1,0:T(8,128)(2,1)S(1)}, u32[]{:S(2)}, u32[]{:S(2)}) collective-permute-start(bf16[1040,128]{1,0:T(8,128)(2,1)S(1)} %pad_maximum_fusion.refs_0_), channel_id=1, source_target_pairs={{0,16},{16,0},{32,48},{48,32},{1,17},{17,1},{33,49},{49,33},{2,18}... | collective-permute-start | bytes 798728 | tf_op jit(solution)/shard_map/ppermute | solution.py:144
  22.5 0.0 copy-done.4
  22.5 0.1 broadcast_in_dim.4
  22.6 0.1 min.14
  22.7 0.1 pad_add_fusion.place_ref.core_ref
  22.7 14.6 %collective-permute-done.2.refs_3_ = bf16[1040,128]{1,0:T(8,128)(2,1)S(1)} collective-permute-done((bf16[1040,128]{1,0:T(8,128)(2,1)S(1)}, bf16[1040,128]{1,0:T(8,128)(2,1)S(1)}, u32[]{:S(2)}, u32[]{:S(2)}) %collective-permute-start.2) | collective-permute-done | bytes 266272 | tf_op jit(solution)/shard_map/ppermute | solution.py:144
  37.4 0.0 collective-permute-done.1.refs_2_
  37.4 3.7 %collective-permute-done.refs_1_ = bf16[1040,128]{1,0:T(8,128)(2,1)S(1)} collective-permute-done((bf16[1040,128]{1,0:T(8,128)(2,1)S(1)}, bf16[1040,128]{1,0:T(8,128)(2,1)S(1)}, u32[]{:S(2)}, u32[]{:S(2)}) %collective-permute-start) | collective-permute-done | bytes 266272 | tf_op jit(solution)/shard_map/ppermute | solution.py:144
  41.1 0.1 maximum_minimum_fusion.index_ref
  41.2 0.0 all-to-all-done.panel_ref
  41.2 1.5 forward_tiles.1
  42.7 3.1 %collective-permute-start.3 = (bf16[32,128,128]{2,1,0:T(8,128)(2,1)S(1)}, bf16[32,128,128]{2,1,0:T(8,128)(2,1)S(1)}, u32[]{:S(2)}, u32[]{:S(2)}) collective-permute-start(bf16[32,128,128]{2,1,0:T(8,128)(2,1)S(1)} %get-tuple-element.18), channel_id=1, source_target_pairs={{0,1},{1,0},{2,3},{3,2},{4,5},{5,4},{6,7},{7,6},{8,9},{9,8},{10,11... | collective-permute-start | bytes 3145736 | tf_op jit(solution)/shard_map/ppermute | solution.py:144
  45.8 2.3 %collective-permute-done.3 = bf16[32,128,128]{2,1,0:T(8,128)(2,1)S(1)} collective-permute-done((bf16[32,128,128]{2,1,0:T(8,128)(2,1)S(1)}, bf16[32,128,128]{2,1,0:T(8,128)(2,1)S(1)}, u32[]{:S(2)}, u32[]{:S(2)}) %collective-permute-start.3) | collective-permute-done | bytes 1048608 | tf_op jit(solution)/shard_map/ppermute | solution.py:144
  48.1 0.4 add_convert_fusion
  48.4 0.0 copy-start
  48.5 0.0 copy-start.2
  48.5 38.3 %all_to_all.25.parts_ref = bf16[32,128,128]{2,1,0:T(8,128)(2,1)S(1)} all-to-all(bf16[32,128,128]{2,1,0:T(8,128)(2,1)S(1)} %add_convert_fusion), channel_id=1, replica_groups=mesh['y_high'=2,'y_low'=4,'x'=4,'z'=8,'core'=2] {'x','z'}, dimensions={0} | all-to-all | bytes 2097152 | tf_op jit(solution)/shard_map/all_to_all | solution.py:196
  86.7 1.6 middle.1
  88.4 6.2 %collective-permute-start.4 = (bf16[256,512]{1,0:T(8,128)(2,1)S(1)}, bf16[256,512]{1,0:T(8,128)(2,1)S(1)}, u32[]{:S(2)}, u32[]{:S(2)}) collective-permute-start(bf16[256,512]{1,0:T(8,128)(2,1)S(1)} %get-tuple-element.22), channel_id=1, source_target_pairs={{0,1},{1,0},{2,3},{3,2},{4,5},{5,4},{6,7},{7,6},{8,9},{9,8},{10,11... | collective-permute-start | bytes 786440 | tf_op jit(solution)/shard_map/ppermute | solution.py:144
  94.6 1.1 spread_grad.1
  95.7 0.0 collective-permute-done.4
  95.8 0.1 add_convert_fusion.1
  95.8 4.8 %all-to-all-start.2 = ((bf16[32,128,128]{2,1,0:T(8,128)(2,1)}), bf16[32,128,128]{2,1,0:T(8,128)(2,1)S(1)}, u32[]{:S(2)}, u32[]{:S(2)}) async-start(bf16[32,128,128]{2,1,0:T(8,128)(2,1)} %spread_grad.1), calls=%async_computation.2 | async-start | bytes 2097152 | tf_op jit(solution)/shard_map/all_to_all | solution.py:216
  100.7 2.2 %collective-permute-start.5 = (bf16[64,512]{1,0:T(8,128)(2,1)S(1)}, bf16[64,512]{1,0:T(8,128)(2,1)S(1)}, u32[]{:S(2)}, u32[]{:S(2)}) collective-permute-start(bf16[64,512]{1,0:T(8,128)(2,1)S(1)} %get-tuple-element.31), channel_id=1, source_target_pairs={{0,64},{64,0},{128,192},{192,128},{1,65},{65,1},{129,193},{193,129... | collective-permute-start | bytes 196616 | tf_op jit(solution)/shard_map/ppermute | solution.py:144
  103.0 3.8 %collective-permute-start.7 = (bf16[64,512]{1,0:T(8,128)(2,1)S(1)}, bf16[64,512]{1,0:T(8,128)(2,1)S(1)}, u32[]{:S(2)}, u32[]{:S(2)}) collective-permute-start(bf16[64,512]{1,0:T(8,128)(2,1)S(1)} %get-tuple-element.32), channel_id=1, source_target_pairs={{0,192},{64,128},{128,64},{192,0},{1,193},{65,129},{129,65},{193,1... | collective-permute-start | bytes 196616 | tf_op jit(solution)/shard_map/ppermute | solution.py:144
  106.8 2.3 %collective-permute-start.6 = (bf16[64,512]{1,0:T(8,128)(2,1)S(1)}, bf16[64,512]{1,0:T(8,128)(2,1)S(1)}, u32[]{:S(2)}, u32[]{:S(2)}) collective-permute-start(bf16[64,512]{1,0:T(8,128)(2,1)S(1)} %get-tuple-element.33), channel_id=1, source_target_pairs={{0,128},{64,192},{128,0},{192,64},{1,129},{65,193},{129,1},{193,65... | collective-permute-start | bytes 196616 | tf_op jit(solution)/shard_map/ppermute | solution.py:144
  109.2 0.0 collective-permute-done.5
  109.2 0.6 collective-permute-done.7
  109.8 3.5 %collective-permute-done.6 = bf16[64,512]{1,0:T(8,128)(2,1)S(1)} collective-permute-done((bf16[64,512]{1,0:T(8,128)(2,1)S(1)}, bf16[64,512]{1,0:T(8,128)(2,1)S(1)}, u32[]{:S(2)}, u32[]{:S(2)}) %collective-permute-start.6) | collective-permute-done | bytes 65568 | tf_op jit(solution)/shard_map/ppermute | solution.py:144
  113.4 3.8 %collective-permute-start.8 = (bf16[64,512]{1,0:T(8,128)(2,1)S(1)}, bf16[64,512]{1,0:T(8,128)(2,1)S(1)}, u32[]{:S(2)}, u32[]{:S(2)}) collective-permute-start(bf16[64,512]{1,0:T(8,128)(2,1)S(1)} %fusion.2), channel_id=1, source_target_pairs={{0,448},{64,384},{128,320},{192,256},{256,192},{320,128},{384,64},... | collective-permute-start | bytes 196616 | tf_op jit(solution)/shard_map/ppermute | solution.py:144
  117.2 3.4 %collective-permute-done.8 = bf16[64,512]{1,0:T(8,128)(2,1)S(1)} collective-permute-done((bf16[64,512]{1,0:T(8,128)(2,1)S(1)}, bf16[64,512]{1,0:T(8,128)(2,1)S(1)}, u32[]{:S(2)}, u32[]{:S(2)}) %collective-permute-start.8) | collective-permute-done | bytes 65568 | tf_op jit(solution)/shard_map/ppermute | solution.py:144
  120.6 2.9 %collective-permute-start.9 = (bf16[64,512]{1,0:T(8,128)(2,1)S(1)}, bf16[64,512]{1,0:T(8,128)(2,1)S(1)}, u32[]{:S(2)}, u32[]{:S(2)}) collective-permute-start(bf16[64,512]{1,0:T(8,128)(2,1)S(1)} %add_convert_fusion.6), channel_id=1, source_target_pairs={{0,16},{16,0},{32,48},{48,32},{1,17},{17,1},{33,49},{49,33},{2,18}... | collective-permute-start | bytes 196616 | tf_op jit(solution)/shard_map/ppermute | solution.py:144
  123.5 3.0 %collective-permute-done.9 = bf16[64,512]{1,0:T(8,128)(2,1)S(1)} collective-permute-done((bf16[64,512]{1,0:T(8,128)(2,1)S(1)}, bf16[64,512]{1,0:T(8,128)(2,1)S(1)}, u32[]{:S(2)}, u32[]{:S(2)}) %collective-permute-start.9) | collective-permute-done | bytes 65568 | tf_op jit(solution)/shard_map/ppermute | solution.py:144
  126.5 0.0 all-to-all-done.2.mine_ref
  126.5 5.6 %collective-permute-start.10 = (bf16[32,128,128]{2,1,0:T(8,128)(2,1)S(1)}, bf16[32,128,128]{2,1,0:T(8,128)(2,1)S(1)}, u32[]{:S(2)}, u32[]{:S(2)}) collective-permute-start(bf16[32,128,128]{2,1,0:T(8,128)(2,1)S(1)} %all-to-all-done.2.mine_ref), channel_id=1, source_target_pairs={{0,1},{1,0},{2,3},{3,2},{4,5},{5,4},{6,7},{7,6},{8,9},{9,8},{10,11... | collective-permute-start | bytes 3145736 | tf_op jit(solution)/shard_map/ppermute | solution.py:144
  132.2 2.3 %collective-permute-done.10.other_ref = bf16[32,128,128]{2,1,0:T(8,128)(2,1)S(1)} collective-permute-done((bf16[32,128,128]{2,1,0:T(8,128)(2,1)S(1)}, bf16[32,128,128]{2,1,0:T(8,128)(2,1)S(1)}, u32[]{:S(2)}, u32[]{:S(2)}) %collective-permute-start.10) | collective-permute-done | bytes 1048608 | tf_op jit(solution)/shard_map/ppermute | solution.py:144
  134.4 2.4 %backward_tiles.1 = bf16[32,128,128]{2,1,0:T(8,128)(2,1)} custom-call(s32[3]{0:T(128)S(1)} %pad_add_fusion.place_ref.core_ref, s32[4,24]{1,0:T(4,128)S(1)} %maximum_minimum_fusion.index_ref, bf16[32,128,128]{2,1,0:T(8,128)(2,1)S(1)} %all-to-all-done.2.mine_ref, bf16[32,128,128]{2,1,0:T(8,128)(2,1)S(1)} %collective-permute-done.10.other_ref, ...), custom_call_target="tpu_custom_call" | custom-call | tf_op jit(solution)/shard_map/backward_tiles/pallas_call | solution.py:223
  136.8 7.0 %all-to-all-start.3 = ((bf16[32,128,128]{2,1,0:T(8,128)(2,1)}), bf16[32,128,128]{2,1,0:T(8,128)(2,1)S(1)}, u32[]{:S(2)}, u32[]{:S(2)}) async-start(bf16[32,128,128]{2,1,0:T(8,128)(2,1)} %backward_tiles.1), calls=%async_computation.3 | async-start | bytes 2097152 | tf_op jit(solution)/shard_map/all_to_all | solution.py:233
  143.8 4.9 %collective-permute-start.13 = (bf16[64,512]{1,0:T(8,128)(2,1)S(1)}, bf16[64,512]{1,0:T(8,128)(2,1)S(1)}, u32[]{:S(2)}, u32[]{:S(2)}) collective-permute-start(bf16[64,512]{1,0:T(8,128)(2,1)S(1)} %add_convert_fusion.5), channel_id=1, source_target_pairs={{0,6},{2,4},{4,2},{6,0},{8,14},{10,12},{12,10},{14,8},{1,7},{3,5},... | collective-permute-start | bytes 196616 | tf_op jit(solution)/shard_map/ppermute | solution.py:144
  148.7 1.9 collective-permute-start.12
  150.7 2.5 %collective-permute-start.11 = (bf16[64,512]{1,0:T(8,128)(2,1)S(1)}, bf16[64,512]{1,0:T(8,128)(2,1)S(1)}, u32[]{:S(2)}, u32[]{:S(2)}) collective-permute-start(bf16[64,512]{1,0:T(8,128)(2,1)S(1)} %add_convert_fusion.5), channel_id=1, source_target_pairs={{0,2},{2,0},{4,6},{6,4},{8,10},{10,8},{12,14},{14,12},{1,3},{3,1},... | collective-permute-start | bytes 196616 | tf_op jit(solution)/shard_map/ppermute | solution.py:144
  153.1 0.0 collective-permute-done.13
  153.1 2.5 %collective-permute-done.12 = bf16[64,512]{1,0:T(8,128)(2,1)S(1)} collective-permute-done((bf16[64,512]{1,0:T(8,128)(2,1)S(1)}, bf16[64,512]{1,0:T(8,128)(2,1)S(1)}, u32[]{:S(2)}, u32[]{:S(2)}) %collective-permute-start.12) | collective-permute-done | bytes 65568 | tf_op jit(solution)/shard_map/ppermute | solution.py:144
  155.6 1.2 collective-permute-done.11
  156.9 4.3 %collective-permute-start.14 = (bf16[64,512]{1,0:T(8,128)(2,1)S(1)}, bf16[64,512]{1,0:T(8,128)(2,1)S(1)}, u32[]{:S(2)}, u32[]{:S(2)}) collective-permute-start(bf16[64,512]{1,0:T(8,128)(2,1)S(1)} %add_convert_fusion.4), channel_id=1, source_target_pairs={{0,14},{2,12},{4,10},{6,8},{8,6},{10,4},{12,2},{14,0},{1,15},{3,13... | collective-permute-start | bytes 196616 | tf_op jit(solution)/shard_map/ppermute | solution.py:144
  161.2 2.9 %collective-permute-done.14 = bf16[64,512]{1,0:T(8,128)(2,1)S(1)} collective-permute-done((bf16[64,512]{1,0:T(8,128)(2,1)S(1)}, bf16[64,512]{1,0:T(8,128)(2,1)S(1)}, u32[]{:S(2)}, u32[]{:S(2)}) %collective-permute-start.14) | collective-permute-done | bytes 65568 | tf_op jit(solution)/shard_map/ppermute | solution.py:144
  164.1 2.8 %collective-permute-start.15 = (bf16[64,512]{1,0:T(8,128)(2,1)S(1)}, bf16[64,512]{1,0:T(8,128)(2,1)S(1)}, u32[]{:S(2)}, u32[]{:S(2)}) collective-permute-start(bf16[64,512]{1,0:T(8,128)(2,1)S(1)} %add_convert_fusion.3), channel_id=1, source_target_pairs={{0,48},{16,32},{32,16},{48,0},{1,49},{17,33},{33,17},{49,1},{2,50}... | collective-permute-start | bytes 196616 | tf_op jit(solution)/shard_map/ppermute | solution.py:144
  166.9 4.2 %collective-permute-done.15 = bf16[64,512]{1,0:T(8,128)(2,1)S(1)} collective-permute-done((bf16[64,512]{1,0:T(8,128)(2,1)S(1)}, bf16[64,512]{1,0:T(8,128)(2,1)S(1)}, u32[]{:S(2)}, u32[]{:S(2)}) %collective-permute-start.15) | collective-permute-done | bytes 65568 | tf_op jit(solution)/shard_map/ppermute | solution.py:144
  171.2 0.0 all-to-all-done.3.parts_ref
  171.2 0.8 broadcast_in_dim.5
  172.0 6.3 %all-to-all-start.4 = ((bf16[8,64,512]{2,1,0:T(8,128)(2,1)}), bf16[8,64,512]{2,1,0:T(8,128)(2,1)S(1)}, u32[]{:S(2)}, u32[]{:S(2)}) async-start(bf16[8,64,512]{2,1,0:T(8,128)(2,1)} %broadcast_in_dim.5), calls=%async_computation.4 | async-start | bytes 1048576 | tf_op jit(solution)/shard_map/all_to_all | solution.py:250
  178.3 1.0 last.1
  179.3 13.5 %all-to-all-done.4.pieces_ref = bf16[8,64,512]{2,1,0:T(8,128)(2,1)S(1)} async-done(((bf16[8,64,512]{2,1,0:T(8,128)(2,1)}), bf16[8,64,512]{2,1,0:T(8,128)(2,1)S(1)}, u32[]{:S(2)}, u32[]{:S(2)}) %all-to-all-start.4) | async-done | bytes 524320 | tf_op jit(solution)/shard_map/all_to_all | solution.py:250
  192.8 1.6 place_rows.1
  (21 shorter events, 0.2 us)
Async XLA Ops:
  0.6 0.9 copy-start.1
  2.6 10.7 %copy-start.7 = (s32[1,1,8]{2,1,0:T(1,128)S(1)}, s32[1,1,8]{2,1,0:T(1,128)}, u32[]{:S(2)}) copy-start(s32[1,1,8]{2,1,0:T(1,128)} %param.12) | copy-start | bytes 100
  2.6 10.7 %copy-start.5 = (s32[1,1,8]{2,1,0:T(1,128)S(1)}, s32[1,1,8]{2,1,0:T(1,128)}, u32[]{:S(2)}) copy-start(s32[1,1,8]{2,1,0:T(1,128)} %param.14) | copy-start | bytes 100
  2.6 10.7 %copy-start.6 = (s32[1,1,8]{2,1,0:T(1,128)S(1)}, s32[1,1,8]{2,1,0:T(1,128)}, u32[]{:S(2)}) copy-start(s32[1,1,8]{2,1,0:T(1,128)} %param.13) | copy-start | bytes 100
  2.6 10.8 %copy-start.3 = (bf16[1,1,8,128,128]{4,3,2,1,0:T(8,128)(2,1)S(1)}, bf16[1,1,8,128,128]{4,3,2,1,0:T(8,128)(2,1)}, u32[]{:S(2)}) copy-start(bf16[1,1,8,128,128]{4,3,2,1,0:T(8,128)(2,1)} %param.11) | copy-start | bytes 786436
  2.7 19.8 %copy-start.4 = (s32[3]{0:T(128)S(1)}, s32[3]{0:T(128)}, u32[]{:S(2)}) copy-start(s32[3]{0:T(128)} %constant.41.clone) | copy-start | bytes 40
  2.7 38.5 %all-to-all-start = ((bf16[32,128,128]{2,1,0:T(8,128)(2,1)}), bf16[32,128,128]{2,1,0:T(8,128)(2,1)S(1)}, u32[]{:S(2)}, u32[]{:S(2)}) async-start(bf16[32,128,128]{2,1,0:T(8,128)(2,1)} %spread_features.1), calls=%async_computation | async-start | bytes 2097152 | tf_op jit(solution)/shard_map/all_to_all | solution.py:174
  13.5 23.9 %collective-permute-start.2 = (bf16[1040,128]{1,0:T(8,128)(2,1)S(1)}, bf16[1040,128]{1,0:T(8,128)(2,1)S(1)}, u32[]{:S(2)}, u32[]{:S(2)}) collective-permute-start(bf16[1040,128]{1,0:T(8,128)(2,1)S(1)} %pad_maximum_fusion.refs_0_), channel_id=1, source_target_pairs={{0,48},{16,32},{32,16},{48,0},{1,49},{17,33},{33,17},{49,1},{2,50}... | collective-permute-start | bytes 798728 | tf_op jit(solution)/shard_map/ppermute | solution.py:144
  17.8 19.5 %collective-permute-start.1 = (bf16[1040,128]{1,0:T(8,128)(2,1)S(1)}, bf16[1040,128]{1,0:T(8,128)(2,1)S(1)}, u32[]{:S(2)}, u32[]{:S(2)}) collective-permute-start(bf16[1040,128]{1,0:T(8,128)(2,1)S(1)} %pad_maximum_fusion.refs_0_), channel_id=1, source_target_pairs={{0,32},{16,48},{32,0},{48,16},{1,33},{17,49},{33,1},{49,17},{2,34}... | collective-permute-start | bytes 798728 | tf_op jit(solution)/shard_map/ppermute | solution.py:144
  20.3 20.7 %collective-permute-start = (bf16[1040,128]{1,0:T(8,128)(2,1)S(1)}, bf16[1040,128]{1,0:T(8,128)(2,1)S(1)}, u32[]{:S(2)}, u32[]{:S(2)}) collective-permute-start(bf16[1040,128]{1,0:T(8,128)(2,1)S(1)} %pad_maximum_fusion.refs_0_), channel_id=1, source_target_pairs={{0,16},{16,0},{32,48},{48,32},{1,17},{17,1},{33,49},{49,33},{2,18}... | collective-permute-start | bytes 798728 | tf_op jit(solution)/shard_map/ppermute | solution.py:144
  42.7 5.4 %collective-permute-start.3 = (bf16[32,128,128]{2,1,0:T(8,128)(2,1)S(1)}, bf16[32,128,128]{2,1,0:T(8,128)(2,1)S(1)}, u32[]{:S(2)}, u32[]{:S(2)}) collective-permute-start(bf16[32,128,128]{2,1,0:T(8,128)(2,1)S(1)} %get-tuple-element.18), channel_id=1, source_target_pairs={{0,1},{1,0},{2,3},{3,2},{4,5},{5,4},{6,7},{7,6},{8,9},{9,8},{10,11... | collective-permute-start | bytes 3145736 | tf_op jit(solution)/shard_map/ppermute | solution.py:144
  48.4 38.3 %copy-start = (bf16[512,512]{1,0:T(8,128)(2,1)S(1)}, bf16[512,512]{1,0:T(8,128)(2,1)}, u32[]{:S(2)}) copy-start(bf16[512,512]{1,0:T(8,128)(2,1)} %weight_ref.3) | copy-start | bytes 1572868
  48.5 38.3 %copy-start.2 = (bf16[128,512]{1,0:T(8,128)(2,1)S(1)}, bf16[128,512]{1,0:T(8,128)(2,1)}, u32[]{:S(2)}) copy-start(bf16[128,512]{1,0:T(8,128)(2,1)} %cotangent_ref.1) | copy-start | bytes 393220
  88.4 7.4 %collective-permute-start.4 = (bf16[256,512]{1,0:T(8,128)(2,1)S(1)}, bf16[256,512]{1,0:T(8,128)(2,1)S(1)}, u32[]{:S(2)}, u32[]{:S(2)}) collective-permute-start(bf16[256,512]{1,0:T(8,128)(2,1)S(1)} %get-tuple-element.22), channel_id=1, source_target_pairs={{0,1},{1,0},{2,3},{3,2},{4,5},{5,4},{6,7},{7,6},{8,9},{9,8},{10,11... | collective-permute-start | bytes 786440 | tf_op jit(solution)/shard_map/ppermute | solution.py:144
  95.8 30.7 %all-to-all-start.2 = ((bf16[32,128,128]{2,1,0:T(8,128)(2,1)}), bf16[32,128,128]{2,1,0:T(8,128)(2,1)S(1)}, u32[]{:S(2)}, u32[]{:S(2)}) async-start(bf16[32,128,128]{2,1,0:T(8,128)(2,1)} %spread_grad.1), calls=%async_computation.2 | async-start | bytes 2097152 | tf_op jit(solution)/shard_map/all_to_all | solution.py:216
  100.7 8.4 %collective-permute-start.5 = (bf16[64,512]{1,0:T(8,128)(2,1)S(1)}, bf16[64,512]{1,0:T(8,128)(2,1)S(1)}, u32[]{:S(2)}, u32[]{:S(2)}) collective-permute-start(bf16[64,512]{1,0:T(8,128)(2,1)S(1)} %get-tuple-element.31), channel_id=1, source_target_pairs={{0,64},{64,0},{128,192},{192,128},{1,65},{65,1},{129,193},{193,129... | collective-permute-start | bytes 196616 | tf_op jit(solution)/shard_map/ppermute | solution.py:144
  103.0 6.8 %collective-permute-start.7 = (bf16[64,512]{1,0:T(8,128)(2,1)S(1)}, bf16[64,512]{1,0:T(8,128)(2,1)S(1)}, u32[]{:S(2)}, u32[]{:S(2)}) collective-permute-start(bf16[64,512]{1,0:T(8,128)(2,1)S(1)} %get-tuple-element.32), channel_id=1, source_target_pairs={{0,192},{64,128},{128,64},{192,0},{1,193},{65,129},{129,65},{193,1... | collective-permute-start | bytes 196616 | tf_op jit(solution)/shard_map/ppermute | solution.py:144
  106.8 6.5 %collective-permute-start.6 = (bf16[64,512]{1,0:T(8,128)(2,1)S(1)}, bf16[64,512]{1,0:T(8,128)(2,1)S(1)}, u32[]{:S(2)}, u32[]{:S(2)}) collective-permute-start(bf16[64,512]{1,0:T(8,128)(2,1)S(1)} %get-tuple-element.33), channel_id=1, source_target_pairs={{0,128},{64,192},{128,0},{192,64},{1,129},{65,193},{129,1},{193,65... | collective-permute-start | bytes 196616 | tf_op jit(solution)/shard_map/ppermute | solution.py:144
  113.4 7.2 %collective-permute-start.8 = (bf16[64,512]{1,0:T(8,128)(2,1)S(1)}, bf16[64,512]{1,0:T(8,128)(2,1)S(1)}, u32[]{:S(2)}, u32[]{:S(2)}) collective-permute-start(bf16[64,512]{1,0:T(8,128)(2,1)S(1)} %fusion.2), channel_id=1, source_target_pairs={{0,448},{64,384},{128,320},{192,256},{256,192},{320,128},{384,64},... | collective-permute-start | bytes 196616 | tf_op jit(solution)/shard_map/ppermute | solution.py:144
  120.6 5.9 %collective-permute-start.9 = (bf16[64,512]{1,0:T(8,128)(2,1)S(1)}, bf16[64,512]{1,0:T(8,128)(2,1)S(1)}, u32[]{:S(2)}, u32[]{:S(2)}) collective-permute-start(bf16[64,512]{1,0:T(8,128)(2,1)S(1)} %add_convert_fusion.6), channel_id=1, source_target_pairs={{0,16},{16,0},{32,48},{48,32},{1,17},{17,1},{33,49},{49,33},{2,18}... | collective-permute-start | bytes 196616 | tf_op jit(solution)/shard_map/ppermute | solution.py:144
  126.5 7.9 %collective-permute-start.10 = (bf16[32,128,128]{2,1,0:T(8,128)(2,1)S(1)}, bf16[32,128,128]{2,1,0:T(8,128)(2,1)S(1)}, u32[]{:S(2)}, u32[]{:S(2)}) collective-permute-start(bf16[32,128,128]{2,1,0:T(8,128)(2,1)S(1)} %all-to-all-done.2.mine_ref), channel_id=1, source_target_pairs={{0,1},{1,0},{2,3},{3,2},{4,5},{5,4},{6,7},{7,6},{8,9},{9,8},{10,11... | collective-permute-start | bytes 3145736 | tf_op jit(solution)/shard_map/ppermute | solution.py:144
  136.8 34.4 %all-to-all-start.3 = ((bf16[32,128,128]{2,1,0:T(8,128)(2,1)}), bf16[32,128,128]{2,1,0:T(8,128)(2,1)S(1)}, u32[]{:S(2)}, u32[]{:S(2)}) async-start(bf16[32,128,128]{2,1,0:T(8,128)(2,1)} %backward_tiles.1), calls=%async_computation.3 | async-start | bytes 2097152 | tf_op jit(solution)/shard_map/all_to_all | solution.py:233
  143.8 9.3 %collective-permute-start.13 = (bf16[64,512]{1,0:T(8,128)(2,1)S(1)}, bf16[64,512]{1,0:T(8,128)(2,1)S(1)}, u32[]{:S(2)}, u32[]{:S(2)}) collective-permute-start(bf16[64,512]{1,0:T(8,128)(2,1)S(1)} %add_convert_fusion.5), channel_id=1, source_target_pairs={{0,6},{2,4},{4,2},{6,0},{8,14},{10,12},{12,10},{14,8},{1,7},{3,5},... | collective-permute-start | bytes 196616 | tf_op jit(solution)/shard_map/ppermute | solution.py:144
  148.7 6.9 %collective-permute-start.12 = (bf16[64,512]{1,0:T(8,128)(2,1)S(1)}, bf16[64,512]{1,0:T(8,128)(2,1)S(1)}, u32[]{:S(2)}, u32[]{:S(2)}) collective-permute-start(bf16[64,512]{1,0:T(8,128)(2,1)S(1)} %add_convert_fusion.5), channel_id=1, source_target_pairs={{0,4},{2,6},{4,0},{6,2},{8,12},{10,14},{12,8},{14,10},{1,5},{3,7},... | collective-permute-start | bytes 196616 | tf_op jit(solution)/shard_map/ppermute | solution.py:144
  150.7 6.2 %collective-permute-start.11 = (bf16[64,512]{1,0:T(8,128)(2,1)S(1)}, bf16[64,512]{1,0:T(8,128)(2,1)S(1)}, u32[]{:S(2)}, u32[]{:S(2)}) collective-permute-start(bf16[64,512]{1,0:T(8,128)(2,1)S(1)} %add_convert_fusion.5), channel_id=1, source_target_pairs={{0,2},{2,0},{4,6},{6,4},{8,10},{10,8},{12,14},{14,12},{1,3},{3,1},... | collective-permute-start | bytes 196616 | tf_op jit(solution)/shard_map/ppermute | solution.py:144
  156.9 7.2 %collective-permute-start.14 = (bf16[64,512]{1,0:T(8,128)(2,1)S(1)}, bf16[64,512]{1,0:T(8,128)(2,1)S(1)}, u32[]{:S(2)}, u32[]{:S(2)}) collective-permute-start(bf16[64,512]{1,0:T(8,128)(2,1)S(1)} %add_convert_fusion.4), channel_id=1, source_target_pairs={{0,14},{2,12},{4,10},{6,8},{8,6},{10,4},{12,2},{14,0},{1,15},{3,13... | collective-permute-start | bytes 196616 | tf_op jit(solution)/shard_map/ppermute | solution.py:144
  164.1 7.0 %collective-permute-start.15 = (bf16[64,512]{1,0:T(8,128)(2,1)S(1)}, bf16[64,512]{1,0:T(8,128)(2,1)S(1)}, u32[]{:S(2)}, u32[]{:S(2)}) collective-permute-start(bf16[64,512]{1,0:T(8,128)(2,1)S(1)} %add_convert_fusion.3), channel_id=1, source_target_pairs={{0,48},{16,32},{32,16},{48,0},{1,49},{17,33},{33,17},{49,1},{2,50}... | collective-permute-start | bytes 196616 | tf_op jit(solution)/shard_map/ppermute | solution.py:144
  172.0 20.8 %all-to-all-start.4 = ((bf16[8,64,512]{2,1,0:T(8,128)(2,1)}), bf16[8,64,512]{2,1,0:T(8,128)(2,1)S(1)}, u32[]{:S(2)}, u32[]{:S(2)}) async-start(bf16[8,64,512]{2,1,0:T(8,128)(2,1)} %broadcast_in_dim.5), calls=%async_computation.4 | async-start | bytes 1048576 | tf_op jit(solution)/shard_map/all_to_all | solution.py:250
